TPU v7x, 128 devices: a whole 4x4x4 slice. The times are simulated.
128 devices in a mesh: replica: 2 (over x_hi), fsdp: 64 (over x_lo, y, z, core).
Axes of the slice: x: 4 (x_hi: 2, x_lo: 2; x = x_hi * 2 + x_lo), y: 4, z: 4, core: 2. Of those that a mesh axis runs over, the one named last changes fastest.
Arguments:
- tokens: bfloat16 [16384, 2048], P(('replica', 'fsdp')), may hold values from -6 to 6
- doc_ids: int32 [16384], P(('replica', 'fsdp')), may hold values from 0 to 31, as said below
- first_gain: bfloat16 [2048], P('fsdp'), may hold values from 0.5 to 1.5
- query_weight: bfloat16 [2048, 2048], P('fsdp'), may hold values from -0.125 to 0.125
- key_weight: bfloat16 [2048, 256], P('fsdp'), may hold values from -0.125 to 0.125
- value_weight: bfloat16 [2048, 256], P('fsdp'), may hold values from -0.125 to 0.125
- out_weight: bfloat16 [2048, 2048], P('fsdp'), may hold values from -0.5 to 0.5
- second_gain: bfloat16 [2048], P('fsdp'), may hold values from 0.5 to 1.5
- gate_weight: bfloat16 [2048, 5632], P('fsdp'), may hold values from -0.125 to 0.125
- up_weight: bfloat16 [2048, 5632], P('fsdp'), may hold values from -0.125 to 0.125
- down_weight: bfloat16 [5632, 2048], P('fsdp'), may hold values from -0.078125 to 0.078125
- cotangent: bfloat16 [16384, 2048], P(('replica', 'fsdp')), may hold values from -6 to 6
Outputs:
- output: bfloat16 [16384, 2048], P(('replica', 'fsdp'))
- tokens_grad: float32 [16384, 2048], P(('replica', 'fsdp'))
- first_gain_grad: float32 [2048], P('fsdp')
- query_grad: float32 [2048, 2048], P('fsdp')
- key_grad: float32 [2048, 256], P('fsdp')
- value_grad: float32 [2048, 256], P('fsdp')
- out_grad: float32 [2048, 2048], P('fsdp')
- second_gain_grad: float32 [2048], P('fsdp')
- gate_grad: float32 [2048, 5632], P('fsdp')
- up_grad: float32 [2048, 5632], P('fsdp')
- down_grad: float32 [5632, 2048], P('fsdp')
Inputs may be any that keep to these rules, and one draw needn't show every extreme that they name: `doc_ids`: within each aligned block of 128 tokens (one device's), ids start at 0 and rise by 0 or 1 from one token to the next, rising only at positions that are multiples of 4 within the block; a sequence is the tokens of one block that share an id; in some block all 128 tokens form one sequence.
All inputs are finite; a program needn't handle non-finite values.
Results may differ from a plain program's by a relative error of at most 0.015.
Values may be sent and summed in bfloat16 or wider, within the bound.
No kernel may reach another device: no remote copies, remote signals or barrier semaphores. Data moves between devices by JAX's collectives and lax.ppermute only.
A program may use at most 576 MiB of HBM per device.

v0:
```python
import jax
import jax.numpy as jnp
from jax import lax
from jax.sharding import PartitionSpec as P

D = 2048
HEADS = 32
KV_HEADS = 4
HDIM = 64
FF = 5632
GROUP = 8


norm_eps = 1e-05


def turn(u):
    half = u.shape[-1] // 2
    return jnp.concatenate([-u[..., half:], u[..., :half]], axis=-1)


def turn_back(u):
    half = u.shape[-1] // 2
    return jnp.concatenate([u[..., half:], -u[..., :half]], axis=-1)


def times_t(left, right):
    return lax.dot_general(
        left, right, (((1,), (1,)), ((), ())), preferred_element_type=jnp.float32
    )


def t_times(left, right):
    return lax.dot_general(
        left, right, (((0,), (0,)), ((), ())), preferred_element_type=jnp.float32
    )


def rms_scale(rows):
    return lax.rsqrt(jnp.mean(rows * rows, axis=-1, keepdims=True) + norm_eps)


def norm_back(rows, scale, gain, upstream):
    gain_term = jnp.sum(upstream * rows * scale, axis=0)
    inner = upstream * gain
    rows_grad = scale * inner - rows * (scale * scale * scale) * jnp.mean(
        inner * rows, axis=-1, keepdims=True
    )
    return (rows_grad, gain_term)


def rotary(doc_ids, width):
    count = doc_ids.shape[0]
    order = jnp.arange(count)
    same = doc_ids[:, None] == doc_ids[None, :]
    earlier = order[None, :] < order[:, None]
    place = jnp.sum(jnp.where(same & earlier, 1.0, 0.0), axis=1).astype(jnp.float32)
    half = width // 2
    inverse = 10000.0 ** (jnp.arange(half, dtype=jnp.float32) * (-2.0 / width))
    angle = place[:, None] * inverse[None, :]
    angle = jnp.concatenate([angle, angle], axis=-1)
    allowed = same & (order[None, :] <= order[:, None])
    return (jnp.cos(angle), jnp.sin(angle), allowed)


def score_block(grouped, rot_keys, allowed):
    scores = jnp.einsum(
        "ikgd,jkd->kgij", grouped, rot_keys, preferred_element_type=jnp.float32
    ) * HDIM ** (-0.5)
    return jnp.where(allowed, scores, -1e30)


def on_device(
    tokens,
    doc_ids,
    first_gain,
    query_weight,
    key_weight,
    value_weight,
    out_weight,
    second_gain,
    gate_weight,
    up_weight,
    down_weight,
    cotangent,
):
    count = tokens.shape[0]
    cosine, sine, allowed = rotary(doc_ids, HDIM)
    full_query, full_key, full_value, full_first = (
        lax.all_gather(query_weight, "fsdp", axis=0, tiled=True),
        lax.all_gather(key_weight, "fsdp", axis=0, tiled=True),
        lax.all_gather(value_weight, "fsdp", axis=0, tiled=True),
        lax.all_gather(first_gain, "fsdp", axis=0, tiled=True),
    )
    rows = tokens.astype(jnp.float32)
    first_scale = rms_scale(rows)
    normed = (rows * first_scale * full_first.astype(jnp.float32)).astype(jnp.bfloat16)
    queries = jnp.dot(normed, full_query, preferred_element_type=jnp.float32).reshape(
        count, HEADS, HDIM
    )
    keys = jnp.dot(normed, full_key, preferred_element_type=jnp.float32).reshape(
        count, KV_HEADS, HDIM
    )
    values = (
        jnp.dot(normed, full_value, preferred_element_type=jnp.float32)
        .astype(jnp.bfloat16)
        .reshape(count, KV_HEADS, HDIM)
    )
    rot_queries = (queries * cosine[:, None] + turn(queries) * sine[:, None]).astype(jnp.bfloat16)
    rot_keys = (keys * cosine[:, None] + turn(keys) * sine[:, None]).astype(jnp.bfloat16)
    grouped = rot_queries.reshape(count, KV_HEADS, GROUP, HDIM)
    scores = score_block(grouped, rot_keys, allowed)
    peak = jnp.max(scores, axis=-1, keepdims=True)
    expo = jnp.exp(scores - peak)
    total = jnp.sum(expo, axis=-1, keepdims=True)
    probs = expo / total
    log_total = peak + jnp.log(total)
    mixed = jnp.einsum(
        "kgij,jkd->ikgd", probs.astype(jnp.bfloat16), values, preferred_element_type=jnp.float32
    )
    mixed = mixed.reshape(count, D).astype(jnp.bfloat16)
    full_out = lax.all_gather(out_weight, "fsdp", axis=0, tiled=True)
    midway = rows + jnp.dot(mixed, full_out, preferred_element_type=jnp.float32)
    full_gate, full_up, full_second = (
        lax.all_gather(gate_weight, "fsdp", axis=0, tiled=True),
        lax.all_gather(up_weight, "fsdp", axis=0, tiled=True),
        lax.all_gather(second_gain, "fsdp", axis=0, tiled=True),
    )
    second_scale = rms_scale(midway)
    normed_two = (midway * second_scale * full_second.astype(jnp.float32)).astype(jnp.bfloat16)
    gate_act = jnp.dot(normed_two, full_gate, preferred_element_type=jnp.float32)
    up_act = jnp.dot(normed_two, full_up, preferred_element_type=jnp.float32)
    sigmoid_gate = jax.nn.sigmoid(gate_act)
    silu_gate = gate_act * sigmoid_gate
    hidden = (silu_gate * up_act).astype(jnp.bfloat16)
    full_down = lax.all_gather(down_weight, "fsdp", axis=0, tiled=True)
    output = (midway + jnp.dot(hidden, full_down, preferred_element_type=jnp.float32)).astype(
        jnp.bfloat16
    )
    grad_out = cotangent.astype(jnp.float32)
    down_back = lax.all_gather(down_weight, "fsdp", axis=0, tiled=True)
    grad_hidden = times_t(cotangent, down_back)
    part = hidden
    down_part = lax.psum_scatter(t_times(part, cotangent), "fsdp", scatter_dimension=0, tiled=True)
    grad_gate = (
        grad_hidden * up_act * (sigmoid_gate * (1.0 + gate_act * (1.0 - sigmoid_gate)))
    ).astype(jnp.bfloat16)
    grad_up = (grad_hidden * silu_gate).astype(jnp.bfloat16)
    gate_back, up_back, second_back = (
        lax.all_gather(gate_weight, "fsdp", axis=0, tiled=True),
        lax.all_gather(up_weight, "fsdp", axis=0, tiled=True),
        lax.all_gather(second_gain, "fsdp", axis=0, tiled=True),
    )
    grad_two = times_t(grad_gate, gate_back) + times_t(grad_up, up_back)
    part = normed_two
    feed_part = lax.psum_scatter(
        jnp.concatenate([t_times(part, grad_gate), t_times(part, grad_up)], axis=1),
        "fsdp",
        scatter_dimension=0,
        tiled=True,
    )
    mid_grad, second_term = norm_back(
        midway, second_scale, second_back.astype(jnp.float32), grad_two
    )
    grad_mid = grad_out + mid_grad
    grad_attn = grad_mid.astype(jnp.bfloat16)
    out_back = lax.all_gather(out_weight, "fsdp", axis=0, tiled=True)
    grad_mixed = times_t(grad_attn, out_back).astype(jnp.bfloat16)
    part = mixed
    out_part = lax.psum_scatter(t_times(part, grad_attn), "fsdp", scatter_dimension=0, tiled=True)
    grad_heads = grad_mixed.reshape(count, KV_HEADS, GROUP, HDIM)
    again_scores = score_block(grouped, rot_keys, allowed)
    again_probs = jnp.exp(again_scores - log_total)
    grad_probs = jnp.einsum(
        "ikgd,jkd->kgij", grad_heads, values, preferred_element_type=jnp.float32
    )
    delta = jnp.sum(again_probs * grad_probs, axis=-1, keepdims=True)
    grad_scores = (again_probs * (grad_probs - delta)).astype(jnp.bfloat16)
    grad_rot_queries = jnp.einsum(
        "kgij,jkd->ikgd", grad_scores, rot_keys, preferred_element_type=jnp.float32
    ) * HDIM ** (-0.5)
    grad_rot_keys = jnp.einsum(
        "kgij,ikgd->jkd", grad_scores, grouped, preferred_element_type=jnp.float32
    ) * HDIM ** (-0.5)
    grad_values = jnp.einsum(
        "kgij,ikgd->jkd",
        again_probs.astype(jnp.bfloat16),
        grad_heads,
        preferred_element_type=jnp.float32,
    )
    grad_rot_queries = grad_rot_queries.reshape(count, HEADS, HDIM)
    grad_queries = (
        (grad_rot_queries * cosine[:, None] + turn_back(grad_rot_queries * sine[:, None]))
        .reshape(count, D)
        .astype(jnp.bfloat16)
    )
    grad_keys = (
        (grad_rot_keys * cosine[:, None] + turn_back(grad_rot_keys * sine[:, None]))
        .reshape(count, KV_HEADS * HDIM)
        .astype(jnp.bfloat16)
    )
    grad_values = grad_values.reshape(count, KV_HEADS * HDIM).astype(jnp.bfloat16)
    query_back, key_back, value_back, first_back = (
        lax.all_gather(query_weight, "fsdp", axis=0, tiled=True),
        lax.all_gather(key_weight, "fsdp", axis=0, tiled=True),
        lax.all_gather(value_weight, "fsdp", axis=0, tiled=True),
        lax.all_gather(first_gain, "fsdp", axis=0, tiled=True),
    )
    grad_one = (
        times_t(grad_queries, query_back)
        + times_t(grad_keys, key_back)
        + times_t(grad_values, value_back)
    )
    rows_grad, first_term = norm_back(rows, first_scale, first_back.astype(jnp.float32), grad_one)
    tokens_grad = grad_mid + rows_grad
    query_term = t_times(normed, grad_queries)
    key_term = t_times(normed, grad_keys)
    value_term = t_times(normed, grad_values)
    query_part, key_part, value_part, first_part, second_part = (
        lax.psum_scatter(query_term, "fsdp", scatter_dimension=0, tiled=True),
        lax.psum_scatter(key_term, "fsdp", scatter_dimension=0, tiled=True),
        lax.psum_scatter(value_term, "fsdp", scatter_dimension=0, tiled=True),
        lax.psum_scatter(first_term, "fsdp", scatter_dimension=0, tiled=True),
        lax.psum_scatter(second_term, "fsdp", scatter_dimension=0, tiled=True),
    )
    summed = (
        lax.psum(query_part.astype(jnp.bfloat16), "replica").astype(jnp.float32),
        lax.psum(key_part.astype(jnp.bfloat16), "replica").astype(jnp.float32),
        lax.psum(value_part.astype(jnp.bfloat16), "replica").astype(jnp.float32),
        lax.psum(out_part.astype(jnp.bfloat16), "replica").astype(jnp.float32),
        lax.psum(first_part.astype(jnp.bfloat16), "replica").astype(jnp.float32),
        lax.psum(second_part.astype(jnp.bfloat16), "replica").astype(jnp.float32),
        lax.psum(feed_part.astype(jnp.bfloat16), "replica").astype(jnp.float32),
        lax.psum(down_part.astype(jnp.bfloat16), "replica").astype(jnp.float32),
    )
    query_grad, key_grad, value_grad, out_grad, first_grad, second_grad, feed_grad, down_grad = (
        summed
    )
    gate_grad = feed_grad[:, :FF]
    up_grad = feed_grad[:, FF:]
    return (
        output,
        tokens_grad,
        first_grad,
        query_grad,
        key_grad,
        value_grad,
        out_grad,
        second_grad,
        gate_grad,
        up_grad,
        down_grad,
    )


def solution(mesh):
    in_specs = (
        P(("replica", "fsdp"), None),
        P(("replica", "fsdp")),
        P("fsdp"),
        P("fsdp", None),
        P("fsdp", None),
        P("fsdp", None),
        P("fsdp", None),
        P("fsdp"),
        P("fsdp", None),
        P("fsdp", None),
        P("fsdp", None),
        P(("replica", "fsdp"), None),
    )
    out_specs = (
        P(("replica", "fsdp"), None),
        P(("replica", "fsdp"), None),
        P("fsdp"),
        P("fsdp", None),
        P("fsdp", None),
        P("fsdp", None),
        P("fsdp", None),
        P("fsdp"),
        P("fsdp", None),
        P("fsdp", None),
        P("fsdp", None),
    )
    return jax.shard_map(
        on_device, mesh=mesh, in_specs=in_specs, out_specs=out_specs, check_vma=False
    )
```

profile of v0, /device:TPU:1, one launch (start us, length us, event | category | flops | bytes accessed | tf_op | source)
XLA Modules:
  0.0 3027.6 jit_solution(16748704550298543855)
XLA Ops:
  15.6 143.2 %all-reduce.5 = (bf16[2048]{0:T(1024)(128)(2,1)S(1)}, bf16[2048]{0:T(1024)(128)(2,1)S(1)}) all-reduce(bf16[2048]{0:T(1024)(128)(2,1)S(1)} %dynamic-update-slice, bf16[2048]{0:T(1024)(128)(2,1)S(1)} %dynamic-update-slice.1), channel_id=1, replica_groups=mesh['replica'=2,'fsdp'=64] {'fsdp'}, use_global_device_ids=true, to_apply=%add | all-reduce | flops 4096 | bytes 16384
  164.9 52.2 %all-gather.10.cloned.1.call-done = bf16[2048,256]{1,0:T(8,128)(2,1)} async-done(((bf16[32,256]{1,0:T(8,128)(2,1)}), bf16[2048,256]{1,0:T(8,128)(2,1)}) %all-gather.10.cloned.1.call-update) | async-done | bytes 1048592 | tf_op jit(solution)/shard_map/all_gather | solution.py:91
  219.0 110.4 %all-gather.12.cloned.1.call-done = bf16[2048,2048]{1,0:T(8,128)(2,1)} async-done(((bf16[32,2048]{1,0:T(8,128)(2,1)}), bf16[2048,2048]{1,0:T(8,128)(2,1)}) %all-gather.12.cloned.1.call-update) | async-done | bytes 8388624 | tf_op jit(solution)/shard_map/all_gather | solution.py:90
  338.8 102.3 %all-gather.14.cloned.1.call-done = bf16[2048,2048]{1,0:T(8,128)(2,1)} async-done(((bf16[32,2048]{1,0:T(8,128)(2,1)}), bf16[2048,2048]{1,0:T(8,128)(2,1)}) %all-gather.14.cloned.1.call-update) | async-done | bytes 8388624 | tf_op jit(solution)/shard_map/all_gather | solution.py:122
  447.0 129.5 %all-gather.18.cloned.1.call-done = bf16[2048,5632]{1,0:T(8,128)(2,1)} async-done(((bf16[32,5632]{1,0:T(8,128)(2,1)}), bf16[2048,5632]{1,0:T(8,128)(2,1)}) %all-gather.18.cloned.1.call-update) | async-done | bytes 23068688 | tf_op jit(solution)/shard_map/all_gather | solution.py:126
  576.5 12.3 fusion.49
  588.8 123.4 %all-gather.16.cloned.1.call-done = bf16[2048,5632]{1,0:T(8,128)(2,1)} async-done(((bf16[32,5632]{1,0:T(8,128)(2,1)}), bf16[2048,5632]{1,0:T(8,128)(2,1)}) %all-gather.16.cloned.1.call-update) | async-done | bytes 23068688 | tf_op jit(solution)/shard_map/all_gather | solution.py:125
  712.2 12.9 fusion.48
  725.1 123.0 %all-gather.20.cloned.1.call-done = bf16[5632,2048]{1,0:T(8,128)(2,1)} async-done(((bf16[88,2048]{1,0:T(8,128)(2,1)}), bf16[5632,2048]{1,0:T(8,128)(2,1)}) %all-gather.20.cloned.1.call-update) | async-done | bytes 23068688 | tf_op jit(solution)/shard_map/all_gather | solution.py:136
  848.1 15.2 multiply_convert_fusion
  863.3 13.0 fusion.50
  876.3 13.9 multiply_reduce_fusion
  924.8 18.1 fusion.54
  943.1 19.6 fusion.53
  962.7 18.2 fusion.52
  980.9 60.3 %pad_maximum_fusion = f32[2048,11264]{1,0:T(8,128)} fusion(f32[2048,5632]{1,0:T(8,128)} %fusion.53, f32[2048,5632]{1,0:T(8,128)} %fusion.52), kind=kLoop, calls=%fused_computation | loop fusion | flops 23068672 | bytes 184549376 | tf_op jit(solution)/shard_map/concatenate | solution.py:157
  1057.1 273.9 %all-reduce.4 = (bf16[2048]{0:T(1024)(128)(2,1)S(1)}, bf16[2048]{0:T(1024)(128)(2,1)S(1)}) all-reduce(f32[2048]{0:T(1024)S(1)} %get-tuple-element.13, f32[2048]{0:T(1024)S(1)} %copy-done.27), channel_id=2, replica_groups=mesh['replica'=2,'fsdp'=64] {'fsdp'}, use_global_device_ids=true, to_apply=%region_9.10.clone | all-reduce | flops 4096 | bytes 24576
  1334.4 181.7 %reduce-scatter.7.cloned.1.call-done = f32[32,2048]{1,0:T(8,128)} async-done(((f32[2048,2048]{1,0:T(8,128)}), f32[32,2048]{1,0:T(8,128)}) %reduce-scatter.7.cloned.1.call-update) | async-done | bytes 262160 | tf_op jit(solution)/shard_map/reduce_scatter | solution.py:220
  1517.7 360.4 %reduce-scatter.17.cloned.1.call-done = f32[88,2048]{1,0:T(8,128)} async-done(((f32[5632,2048]{1,0:T(8,128)}), f32[88,2048]{1,0:T(8,128)}) %reduce-scatter.17.cloned.1.call-update) | async-done | bytes 720912 | tf_op jit(solution)/shard_map/reduce_scatter | solution.py:144
  1880.0 501.4 %reduce-scatter.15.cloned.1.call-done = f32[32,11264]{1,0:T(8,128)} async-done(((f32[2048,11264]{1,0:T(8,128)}), f32[32,11264]{1,0:T(8,128)}) %reduce-scatter.15.cloned.1.call-update) | async-done | bytes 1441808 | tf_op jit(solution)/shard_map/reduce_scatter | solution.py:156
  2383.7 11.5 fusion.1
  2395.2 271.2 %reduce-scatter.11.cloned.1.call-done = f32[32,256]{1,0:T(8,128)} async-done(((f32[2048,256]{1,0:T(8,128)}), f32[32,256]{1,0:T(8,128)}) %reduce-scatter.11.cloned.1.call-update) | async-done | bytes 32784 | tf_op jit(solution)/shard_map/reduce_scatter | solution.py:222
  2667.2 285.4 %reduce-scatter.9.cloned.1.call-done = f32[32,256]{1,0:T(8,128)} async-done(((f32[2048,256]{1,0:T(8,128)}), f32[32,256]{1,0:T(8,128)}) %reduce-scatter.9.cloned.1.call-update) | async-done | bytes 32784 | tf_op jit(solution)/shard_map/reduce_scatter | solution.py:221
  2965.0 48.2 %all-reduce.10.cloned.1.call-done = (bf16[32,2048]{1,0:T(8,128)(2,1)}, bf16[32,2048]{1,0:T(8,128)(2,1)}, bf16[32,11264]{1,0:T(8,128)(2,1)}, bf16[88,2048]{1,0:T(8,128)(2,1)}) async-done(((bf16[32,2048]{1,0:T(8,128)(2,1)}, bf16[32,2048]{1,0:T(8,128)(2,1)}, bf16[32,11264]{1,0:T(8,128)(2,1)}, bf16[88,2048]{1,0:T(8,128)(2,1)}), (bf16[32,2048]{1,0:T(8,128)(2,1)}, bf16[32,2048]{1,0:T(8,128)(2,1)}, ...) | async-done | bytes 1343504 | tf_op jit(solution)/shard_map/psum | solution.py:227
  (158 shorter events, 110.3 us)
Async XLA Ops:
  7.2 210.0 %copy-start.2 = (bf16[128,2048]{1,0:T(8,128)(2,1)S(1)}, bf16[128,2048]{1,0:T(8,128)(2,1)}, u32[]{:S(2)}) copy-start(bf16[128,2048]{1,0:T(8,128)(2,1)} %param.12) | copy-start | bytes 1572868
  7.2 155.9 %all-gather.8.cloned.1.call-start = ((), (), s32[]{:S(2)}) async-start(), calls=%async_computation.6 | async-start | bytes 1064960 | tf_op jit(solution)/shard_map/all_gather | solution.py:92
  7.9 209.2 %all-gather.10.cloned.1.call-start = ((), (), s32[]{:S(2)}) async-start(), calls=%async_computation.7 | async-start | bytes 1064960 | tf_op jit(solution)/shard_map/all_gather | solution.py:91
  8.7 320.7 %all-gather.12.cloned.1.call-start = ((), (), s32[]{:S(2)}) async-start(), calls=%async_computation.8 | async-start | bytes 8519680 | tf_op jit(solution)/shard_map/all_gather | solution.py:90
  9.4 431.7 %all-gather.14.cloned.1.call-start = ((), (), s32[]{:S(2)}) async-start(), calls=%async_computation.9 | async-start | bytes 8519680 | tf_op jit(solution)/shard_map/all_gather | solution.py:122
  10.0 566.5 %all-gather.18.cloned.1.call-start = ((), (), s32[]{:S(2)}) async-start(), calls=%async_computation.11 | async-start | bytes 23429120 | tf_op jit(solution)/shard_map/all_gather | solution.py:126
  10.6 701.6 %all-gather.16.cloned.1.call-start = ((), (), s32[]{:S(2)}) async-start(), calls=%async_computation.10 | async-start | bytes 23429120 | tf_op jit(solution)/shard_map/all_gather | solution.py:125
  11.1 836.9 %all-gather.20.cloned.1.call-start = ((), (), s32[]{:S(2)}) async-start(), calls=%async_computation.12 | async-start | bytes 23429120 | tf_op jit(solution)/shard_map/all_gather | solution.py:136
  11.9 1320.7 %reduce-scatter.13.cloned.1.call-start = ((), (), s32[]{:S(2)}) async-start(), calls=%async_computation.16 | async-start | bytes 17039360 | tf_op jit(solution)/shard_map/reduce_scatter | solution.py:170
  337.9 574.5 %copy-start = (f32[4,8,128,128]{2,3,1,0:T(8,128)}, f32[4,8,128,128]{2,3,1,0:T(8,128)S(1)}, u32[]{:S(2)}) copy-start(f32[4,8,128,128]{2,3,1,0:T(8,128)S(1)} %get-tuple-element.51) | copy-start | bytes 6291460
  338.8 107.1 %copy-start.18 = (bf16[4,64,8,128]{3,1,2,0:T(8,128)(2,1)}, bf16[4,64,8,128]{3,1,2,0:T(8,128)(2,1)S(1)}, u32[]{:S(2)}) copy-start(bf16[4,64,8,128]{3,1,2,0:T(8,128)(2,1)S(1)} %convolution_convert_fusion.1) | copy-start | bytes 1572868
  863.3 13.0 copy-start.4
  901.1 615.0 %reduce-scatter.7.cloned.1.call-start = ((), (), s32[]{:S(2)}) async-start(), calls=%async_computation.13 | async-start | bytes 17039360 | tf_op jit(solution)/shard_map/reduce_scatter | solution.py:220
  901.3 11.1 copy-start.23
  923.3 954.8 %reduce-scatter.17.cloned.1.call-start = ((), (), s32[]{:S(2)}) async-start(), calls=%async_computation.18 | async-start | bytes 46858240 | tf_op jit(solution)/shard_map/reduce_scatter | solution.py:144
  942.9 19.8 copy-start.8
  942.9 1438.5 %reduce-scatter.15.cloned.1.call-start = ((), (), s32[]{:S(2)}) async-start(), calls=%async_computation.17 | async-start | bytes 93716480 | tf_op jit(solution)/shard_map/reduce_scatter | solution.py:156
  1041.3 1625.1 %reduce-scatter.11.cloned.1.call-start = ((), (), s32[]{:S(2)}) async-start(), calls=%async_computation.15 | async-start | bytes 2129920 | tf_op jit(solution)/shard_map/reduce_scatter | solution.py:222
  1045.5 1907.1 %reduce-scatter.9.cloned.1.call-start = ((), (), s32[]{:S(2)}) async-start(), calls=%async_computation.14 | async-start | bytes 2129920 | tf_op jit(solution)/shard_map/reduce_scatter | solution.py:221
  1048.0 1965.2 %all-reduce.10.cloned.1.call-start = ((), (), s32[]{:S(2)}) async-start(), calls=%async_computation.19 | async-start | bytes 2686976 | tf_op jit(solution)/shard_map/psum | solution.py:227
  1055.2 275.9 %copy-start.7 = (f32[128,2048]{1,0:T(8,128)S(1)}, f32[128,2048]{1,0:T(8,128)}, u32[]{:S(2)}) copy-start(f32[128,2048]{1,0:T(8,128)} %copy-done.6) | copy-start | bytes 3145732
  1055.3 275.9 %copy-start.28 = (f32[128]{0:T(128)S(1)}, f32[128]{0:T(128)}, u32[]{:S(2)}) copy-start(f32[128]{0:T(128)} %get-tuple-element.46) | copy-start | bytes 1540
  1332.6 1051.1 %copy-start.5 = (f32[128,2048]{1,0:T(8,128)S(1)}, f32[128,2048]{1,0:T(8,128)}, u32[]{:S(2)}) copy-start(f32[128,2048]{1,0:T(8,128)} %copy-done.3) | copy-start | bytes 3145732
  1332.6 1051.1 %copy-start.12 = (bf16[128,5632]{1,0:T(8,128)(2,1)S(1)}, bf16[128,5632]{1,0:T(8,128)(2,1)}, u32[]{:S(2)}) copy-start(bf16[128,5632]{1,0:T(8,128)(2,1)} %get-tuple-element.29) | copy-start | bytes 4325380
  (19 other events, 36.1 us)
Sparse Core Ops, SparseCore 0:
  9.7 105.1 all-gather.7
  116.6 100.4 all-gather.9
  218.9 110.4 all-gather.11
  331.0 110.1 all-gather.13
  442.7 133.7 all-gather.17
  578.0 134.1 all-gather.15
  713.9 134.1 all-gather.19
  901.2 304.8 reduce-scatter.12
  1208.5 307.5 reduce-scatter.6
  1518.3 359.7 reduce-scatter.16
  1880.5 500.7 reduce-scatter.14
  2383.6 282.7 reduce-scatter.10
  2668.9 283.6 reduce-scatter.8
  2956.2 56.9 all-reduce.9
where the time goes:
time: 3040 us; the launch traced here: 3030 us
  waiting for transfers between devices  2290 us (75%)
  blocking collectives  427 us (14%)
  matrix products  189 us (6%)
  other arithmetic  86.2 us (3%)
    reduce_scatter x1, waiting for transfers between devices, on_device(): lax.psum_scatter(jnp.concatenate([t_times(part, grad_gate), t_times(part,...  501 us
    unnamed x2, blocking collectives  417 us
    reduce_scatter x1, waiting for transfers between devices, on_device(): lax.psum_scatter(t_times(part, cotangent), 'fsdp', scatter_dimension=0, t...  360 us
    reduce_scatter x1, waiting for transfers between devices, on_device(): lax.psum_scatter(key_term, 'fsdp', scatter_dimension=0, tiled=True)  285 us
    reduce_scatter x1, waiting for transfers between devices, on_device(): lax.psum_scatter(value_term, 'fsdp', scatter_dimension=0, tiled=True)  271 us
    reduce_scatter x1, waiting for transfers between devices, on_device(): lax.psum_scatter(query_term, 'fsdp', scatter_dimension=0, tiled=True)  182 us
    all_gather x1, waiting for transfers between devices, on_device(): lax.all_gather(up_weight, 'fsdp', axis=0, tiled=True)  129 us
    all_gather x1, waiting for transfers between devices, on_device(): lax.all_gather(gate_weight, 'fsdp', axis=0, tiled=True)  123 us
  transfers between devices with their start and end apart: 14, of which 12 were waited for; matrix products, arithmetic and copies ran while one was open for 7% of the time, Pallas kernels for 0%

commit v1 on v0

v1 whole, which is shorter than its diff:
```python
import jax
import jax.numpy as jnp
from jax import lax
from jax.sharding import Mesh, PartitionSpec as P

D = 2048
HEADS = 32
KV_HEADS = 4
HDIM = 64
FF = 5632
CAP = 128
TP = 8
LOCAL_HEADS = HEADS // TP
LOCAL_FF = FF // TP
SEGMENT = LOCAL_FF // 4
PADDED = 192
WIDE = 4 * PADDED
BF16 = jnp.bfloat16
F32 = jnp.float32

norm_eps = 1e-05

RING = ("xh", "xl")
SWAP = [(0, 1), (1, 0)]


def turn(u):
    half = u.shape[-1] // 2
    return jnp.concatenate([-u[..., half:], u[..., :half]], axis=-1)


def turn_back(u):
    half = u.shape[-1] // 2
    return jnp.concatenate([u[..., half:], -u[..., :half]], axis=-1)


def times(left, right):
    return jnp.dot(left, right, preferred_element_type=F32)


def times_t(left, right):
    return lax.dot_general(left, right, (((1,), (1,)), ((), ())), preferred_element_type=F32)


def t_times(left, right):
    return lax.dot_general(left, right, (((0,), (0,)), ((), ())), preferred_element_type=F32)


def rms_scale(rows):
    return lax.rsqrt(jnp.mean(rows * rows, axis=-1, keepdims=True) + norm_eps)


def norm_back(rows, scale, inner):
    return scale * inner - rows * (scale * scale * scale) * jnp.mean(
        inner * rows, axis=-1, keepdims=True
    )


def rotary(ids):
    order = jnp.arange(CAP)
    same = ids[:, :, None] == ids[:, None, :]
    earlier = order[None, :] < order[:, None]
    place = jnp.sum(jnp.where(same & earlier[None], 1.0, 0.0), axis=2).astype(F32)
    half = HDIM // 2
    inverse = 10000.0 ** (jnp.arange(half, dtype=F32) * (-2.0 / HDIM))
    angle = place[..., None] * inverse
    angle = jnp.concatenate([angle, angle], axis=-1)
    allowed = same & (order[None, :] <= order[:, None])[None]
    return jnp.cos(angle), jnp.sin(angle), allowed


def from_ring(item, step):
    return lax.ppermute(item, RING, [(i, (i - step) % 4) for i in range(4)])


def to_ring(item, step):
    return lax.ppermute(item, RING, [(i, (i + step) % 4) for i in range(4)])


def swap(item, axis):
    return lax.ppermute(item, axis, SWAP)


def share(item):
    mine = [item] + [from_ring(item, step) for step in (1, 2, 3)]
    return jnp.concatenate(mine + [swap(part, "c") for part in mine], axis=0)


def collect(left, right, product):
    far = product(left[4 * CAP :], right).astype(BF16)
    near = product(left[: 4 * CAP], right)
    near = near + swap(far, "c").astype(F32)
    total = near[:CAP]
    for step in (1, 2, 3):
        total = total + to_ring(near[step * CAP : (step + 1) * CAP].astype(BF16), step).astype(F32)
    return total


def spread_columns(chunks, xl, c):
    mine = [jnp.where(c == 0, pair[0], pair[1]) for pair in chunks]
    away = [jnp.where(c == 0, pair[1], pair[0]) for pair in chunks]
    came = swap(jnp.concatenate(away, axis=0), "c")
    rows = mine[0].shape[0]
    both = []
    for k in range(2):
        other = came[k * rows : (k + 1) * rows]
        both.append(
            jnp.concatenate(
                [jnp.where(c == 0, mine[k], other), jnp.where(c == 0, other, mine[k])], axis=0
            )
        )
    kept = jnp.where(xl == 0, both[0], both[1])
    came = swap(jnp.where(xl == 0, both[1], both[0]), "xl")
    return jnp.stack([jnp.where(xl == 0, kept, came), jnp.where(xl == 0, came, kept)])


def return_columns(item, xl, c):
    kept = jnp.where(xl == 0, item[0], item[1])
    came = swap(jnp.where(xl == 0, item[1], item[0]), "xl")
    first = jnp.where(xl == 0, kept, came)
    second = jnp.where(xl == 0, came, kept)
    rows = first.shape[0] // 2
    both = jnp.stack([first, second])
    mine = jnp.where(c == 0, both[:, :rows], both[:, rows:])
    came = swap(jnp.where(c == 0, both[:, rows:], both[:, :rows]), "c")
    zero = jnp.where(c == 0, mine, came)
    one = jnp.where(c == 0, came, mine)
    return zero, one


def column_part(item, width, xh):
    out = []
    for k in range(2):
        start = 2 * width * k
        out.append(
            jnp.where(
                xh == 0, item[:, start : start + width], item[:, start + width : start + 2 * width]
            )
        )
    return out


def on_device(
    tokens,
    doc_ids,
    first_gain,
    query_weight,
    key_weight,
    value_weight,
    out_weight,
    second_gain,
    gate_weight,
    up_weight,
    down_weight,
    cotangent,
):
    xh, xl, y, z, c = (lax.axis_index(name) for name in ("xh", "xl", "y", "z", "c"))
    first_col = first_gain.astype(F32)[:, None]
    second_col = second_gain.astype(F32)[:, None]

    def scaled(item, gain):
        return (item.astype(F32) * gain).astype(BF16)

    q_parts = column_part(scaled(query_weight, first_col), 512, xh)
    k_parts = column_part(scaled(key_weight, first_col), 64, xh)
    v_parts = column_part(scaled(value_weight, first_col), 64, xh)
    chunks = [
        [
            jnp.concatenate([q_parts[k][:, 256 * j : 256 * (j + 1)], k_parts[k], v_parts[k]], axis=1)
            for j in range(2)
        ]
        for k in range(2)
    ]
    qkv_full = lax.all_gather(spread_columns(chunks, xl, c), ("y", "z"), axis=1, tiled=True)
    qkv_full = qkv_full.reshape(D, 384)

    source = 2 * xh + c
    pair_rows = jnp.concatenate([out_weight, down_weight], axis=0)
    came = swap(pair_rows, "c")
    low = jnp.where(c == 0, pair_rows, came)
    high = jnp.where(c == 0, came, pair_rows)
    out_pair = jnp.concatenate([low[:32], high[:32]], axis=0).reshape(4, 16, D)
    down_pair = jnp.concatenate([low[32:], high[32:], jnp.zeros((16, D), BF16)], axis=0)
    quarters = jnp.concatenate([out_pair, down_pair.reshape(4, 48, D)], axis=1)
    piece = lax.dynamic_index_in_dim(quarters, y, 0, keepdims=False)
    for step in (1, 2, 3):
        sent = lax.dynamic_index_in_dim(quarters, (y + step) % 4, 0, keepdims=False)
        pairs = []
        for a in range(2):
            for b in range(4):
                for e in range(2):
                    if b == 2 * a + e:
                        pairs.append(((a * 4 + b) * 2 + e, (a * 4 + (b + step) % 4) * 2 + e))
        came = lax.ppermute(sent, ("xh", "y", "c"), pairs)
        piece = jnp.where((source + step) % 4 == y, came, piece)
    out_full = lax.all_gather(piece[:16], ("z", "y"), axis=0, tiled=True)

    g_parts = column_part(scaled(gate_weight, second_col), 1408, xh)
    u_parts = column_part(scaled(up_weight, second_col), 1408, xh)

    def widened(item):
        item = item.reshape(32, 8, SEGMENT)
        item = jnp.pad(item, ((0, 0), (0, 0), (0, PADDED - SEGMENT)))
        return item.reshape(32, 2 * WIDE)

    chunks = []
    for k in range(2):
        g_wide, u_wide = widened(g_parts[k]), widened(u_parts[k])
        chunks.append(
            [
                jnp.concatenate(
                    [g_wide[:, j * WIDE : (j + 1) * WIDE], u_wide[:, j * WIDE : (j + 1) * WIDE]], axis=1
                )
                for j in range(2)
            ]
        )
    feed_full = lax.all_gather(spread_columns(chunks, xl, c), ("y", "z"), axis=1, tiled=True)
    feed_full = feed_full.reshape(D, 2 * WIDE)
    down_full = lax.all_gather(piece[16:], ("z", "y"), axis=0, tiled=True)

    ids = share(doc_ids[None])
    cosine, sine, allowed = rotary(ids)
    cosine = cosine.reshape(TP * CAP, 1, HDIM)
    sine = sine.reshape(TP * CAP, 1, HDIM)
    rows = tokens.astype(F32)
    first_scale = rms_scale(rows)
    normed = share((rows * first_scale).astype(BF16))
    qkv = times(normed, qkv_full)
    queries = qkv[:, :256].reshape(TP * CAP, LOCAL_HEADS, HDIM)
    keys = qkv[:, 256:320].reshape(TP * CAP, 1, HDIM)
    values = qkv[:, 320:].astype(BF16).reshape(TP, CAP, HDIM)
    rot_queries = (queries * cosine + turn(queries) * sine).astype(BF16)
    rot_queries = rot_queries.reshape(TP, CAP, LOCAL_HEADS, HDIM)
    rot_keys = (keys * cosine + turn(keys) * sine).astype(BF16).reshape(TP, CAP, HDIM)
    scores = jnp.einsum("bigd,bjd->bgij", rot_queries, rot_keys, preferred_element_type=F32)
    scores = jnp.where(allowed[:, None], scores * HDIM ** (-0.5), -1e30)
    peak = jnp.max(scores, axis=-1, keepdims=True)
    expo = jnp.exp(scores - peak)
    probs = expo / jnp.sum(expo, axis=-1, keepdims=True)
    probs_low = probs.astype(BF16)
    mixed = jnp.einsum("bgij,bjd->bigd", probs_low, values, preferred_element_type=F32)
    mixed = mixed.reshape(TP * CAP, LOCAL_HEADS * HDIM).astype(BF16)
    midway = rows + collect(mixed, out_full, times)

    second_scale = rms_scale(midway)
    normed_two = share((midway * second_scale).astype(BF16))
    upstream = share(cotangent)
    gate_act = times(normed_two, feed_full[:, :WIDE])
    up_act = times(normed_two, feed_full[:, WIDE:])
    sigmoid_gate = jax.nn.sigmoid(gate_act)
    silu_gate = gate_act * sigmoid_gate
    hidden = (silu_gate * up_act).astype(BF16)
    grad_hidden = times_t(upstream, down_full)
    grad_gate = grad_hidden * up_act * (sigmoid_gate * (1.0 + gate_act * (1.0 - sigmoid_gate)))
    grad_up = grad_hidden * silu_gate
    grad_feed = jnp.concatenate([grad_gate.astype(BF16), grad_up.astype(BF16)], axis=1)
    inner_two = collect(grad_feed, feed_full, times_t)
    grad_mid = cotangent.astype(F32) + norm_back(midway, second_scale, inner_two)
    output = (midway + collect(hidden, down_full, times)).astype(BF16)

    feed_term = t_times(normed_two, grad_feed).astype(BF16).reshape(2, D // 2, 2 * WIDE)
    feed_part = lax.psum_scatter(feed_term, ("y", "z"), scatter_dimension=1, tiled=True)
    down_term = t_times(hidden, upstream).astype(BF16)
    down_part = lax.psum_scatter(down_term, ("z", "y"), scatter_dimension=0, tiled=True)

    grad_attn = share(grad_mid.astype(BF16))
    grad_mixed = times_t(grad_attn, out_full).astype(BF16)
    out_term = t_times(mixed, grad_attn).astype(BF16)
    out_part = lax.psum_scatter(out_term, ("z", "y"), scatter_dimension=0, tiled=True)
    grad_heads = grad_mixed.reshape(TP, CAP, LOCAL_HEADS, HDIM)
    grad_probs = jnp.einsum("bigd,bjd->bgij", grad_heads, values, preferred_element_type=F32)
    delta = jnp.sum(probs * grad_probs, axis=-1, keepdims=True)
    grad_scores = (probs * (grad_probs - delta)).astype(BF16)
    grad_rot_queries = jnp.einsum("bgij,bjd->bigd", grad_scores, rot_keys, preferred_element_type=F32)
    grad_rot_keys = jnp.einsum("bgij,bigd->bjd", grad_scores, rot_queries, preferred_element_type=F32)
    grad_values = jnp.einsum("bgij,bigd->bjd", probs_low, grad_heads, preferred_element_type=F32)
    grad_rot_queries = (grad_rot_queries * HDIM ** (-0.5)).reshape(TP * CAP, LOCAL_HEADS, HDIM)
    grad_rot_keys = (grad_rot_keys * HDIM ** (-0.5)).reshape(TP * CAP, 1, HDIM)
    grad_queries = grad_rot_queries * cosine + turn_back(grad_rot_queries * sine)
    grad_keys = grad_rot_keys * cosine + turn_back(grad_rot_keys * sine)
    grad_qkv = jnp.concatenate(
        [
            grad_queries.reshape(TP * CAP, LOCAL_HEADS * HDIM).astype(BF16),
            grad_keys.reshape(TP * CAP, HDIM).astype(BF16),
            grad_values.reshape(TP * CAP, HDIM).astype(BF16),
        ],
        axis=1,
    )
    qkv_term = t_times(normed, grad_qkv).astype(BF16).reshape(2, D // 2, 384)
    qkv_part = lax.psum_scatter(qkv_term, ("y", "z"), scatter_dimension=1, tiled=True)
    inner_one = collect(grad_qkv, qkv_full, times_t)
    tokens_grad = grad_mid + norm_back(rows, first_scale, inner_one)

    def both_halves(item):
        came = swap(item, "xh")
        return jnp.where(xh == 0, item, came), jnp.where(xh == 0, came, item)

    zero, one = return_columns(qkv_part, xl, c)
    pair_kv = (zero[:, :, 256:].astype(F32) + one[:, :, 256:].astype(F32)).astype(BF16)
    pack = jnp.concatenate([zero[:, :, :256], one[:, :, :256], pair_kv], axis=2)
    halves = both_halves(pack)
    query_raw = jnp.concatenate(
        [halves[h][k][:, :512] for k in range(2) for h in range(2)], axis=1
    ).astype(F32)
    key_raw = jnp.concatenate(
        [halves[h][k][:, 512:576] for k in range(2) for h in range(2)], axis=1
    ).astype(F32)
    value_raw = jnp.concatenate(
        [halves[h][k][:, 576:] for k in range(2) for h in range(2)], axis=1
    ).astype(F32)
    first_grad = (
        jnp.sum(query_raw * query_weight.astype(F32), axis=1)
        + jnp.sum(key_raw * key_weight.astype(F32), axis=1)
        + jnp.sum(value_raw * value_weight.astype(F32), axis=1)
    )

    def narrowed(item):
        item = item.reshape(32, 4, PADDED)[:, :, :SEGMENT]
        return item.reshape(32, LOCAL_FF)

    zero, one = return_columns(feed_part, xl, c)
    halves = both_halves(jnp.stack([zero, one]))

    def feed_columns(start):
        return jnp.concatenate(
            [
                narrowed(halves[h][j, k, :, start : start + WIDE])
                for k in range(2)
                for h in range(2)
                for j in range(2)
            ],
            axis=1,
        ).astype(F32)

    gate_raw = feed_columns(0)
    up_raw = feed_columns(WIDE)
    second_grad = jnp.sum(gate_raw * gate_weight.astype(F32), axis=1) + jnp.sum(
        up_raw * up_weight.astype(F32), axis=1
    )

    piece = jnp.concatenate([out_part, down_part], axis=0)
    parts = [piece]
    for step in (1, 2, 3):
        pairs = []
        for a in range(2):
            for b in range(4):
                for e in range(2):
                    if b == 2 * a + e:
                        pairs.append(((a * 4 + (b + step) % 4) * 2 + e, (a * 4 + b) * 2 + e))
        parts.append(lax.ppermute(piece, ("xh", "y", "c"), pairs))
    ordered = []
    for q in range(4):
        item = parts[0]
        for step in (1, 2, 3):
            item = jnp.where((y + step) % 4 == q, parts[step], item)
        ordered.append(item)
    out_rows = jnp.concatenate([item[:16] for item in ordered], axis=0)
    down_rows = jnp.concatenate([item[16:] for item in ordered], axis=0)
    low = jnp.concatenate([out_rows[:32], down_rows[:88]], axis=0)
    high = jnp.concatenate([out_rows[32:], down_rows[88:176]], axis=0)
    came = swap(jnp.where(c == 0, high, low), "c")
    owned = jnp.where(y % 2 == c, jnp.where(c == 0, low, high), came)
    came = swap(owned, "xh")
    owned = jnp.where(y // 2 == xh, owned, came).astype(F32)

    return (
        output,
        tokens_grad,
        first_grad,
        query_raw * first_col,
        key_raw * first_col,
        value_raw * first_col,
        owned[:32],
        second_grad,
        gate_raw * second_col,
        up_raw * second_col,
        owned[32:],
    )


def solution(mesh):
    fine = Mesh(mesh.devices.reshape(2, 2, 4, 4, 2), ("xh", "xl", "y", "z", "c"))
    everyone = ("xh", "xl", "y", "z", "c")
    group = ("xl", "y", "z", "c")
    in_specs = (
        P(everyone, None),
        P(everyone),
        P(group),
        P(group, None),
        P(group, None),
        P(group, None),
        P(group, None),
        P(group),
        P(group, None),
        P(group, None),
        P(group, None),
        P(everyone, None),
    )
    out_specs = (
        P(everyone, None),
        P(everyone, None),
        P(group),
        P(group, None),
        P(group, None),
        P(group, None),
        P(group, None),
        P(group),
        P(group, None),
        P(group, None),
        P(group, None),
    )
    return jax.shard_map(
        on_device, mesh=fine, in_specs=in_specs, out_specs=out_specs, check_vma=False
    )
```

time: 3040 us -> 701 us (0.23)
  waiting for transfers between devices: 2290 us -> 365 us
  blocking collectives: 427 us -> 0 us
  starting transfers between devices: 0.94 us -> 131 us
  matrix products: 189 us -> 92.5 us
  other arithmetic: 86.2 us -> 36.9 us
  local copies, waits for them, and re-layouts: 15.3 us -> 50.7 us
    reduce_scatter x6 -> x4, waiting for transfers between devices: 1600 us -> 234 us  [the longest x1 77.7 us: on_device(): lax.psum_scatter(down_term, ('z', 'y'), scatter_dimension=0, tiled=True)]
    all_gather x7 -> x4, waiting for transfers between devices: 641 us -> 20.3 us  [the longest x1 12.8 us: on_device(): down_full = lax.all_gather(piece[16:], ('z', 'y'), axis=0, tiled=True)]
    unnamed x2 -> x0, blocking collectives: 417 us -> none
    ppermute x0 -> x70, starting transfers between devices: none -> 130 us  [the longest x37 88.3 us: swap(): return lax.ppermute(item, axis, SWAP)]
    ppermute x0 -> x70, waiting for transfers between devices: none -> 110 us  [the longest x15 41.4 us: from_ring(): return lax.ppermute(item, RING, [(i, (i - step) % 4) for i in range(4)])]
    concatenate x1 -> x8, other arithmetic: 60.3 us -> 1.73 us  [the longest x1 0.74 us: rotary(): angle = jnp.concatenate([angle, angle], axis=-1)]
    dot_general x7 -> x4, matrix products: 76.1 us -> 24.5 us  [t_times(): lax.dot_general(left, right, (((0,), (0,)), ((), ())), preferred_element_...]
    psum x1 -> x0, waiting for transfers between devices: 48.2 us -> none  [on_device(): lax.psum(query_part.astype(jnp.bfloat16), 'replica').astype(jnp.float32)]
  transfers between devices with their start and end apart: 14 -> 78, of which waited for: 12 -> 26; matrix products, arithmetic and copies ran while one was open for 7% -> 21% of each run, Pallas kernels for 0% -> 0%
where the time goes in v1:
time: 701 us; the launch traced here: 692 us
  waiting for transfers between devices  365 us (52%)
  starting transfers between devices  131 us (19%)
  matrix products  92.5 us (13%)
  local copies, waits for them, and re-layouts  50.7 us (7%)
  other arithmetic  36.9 us (5%)
  between operations  16 us (2%)
    ppermute x37, starting transfers between devices, swap(): return lax.ppermute(item, axis, SWAP)  88.3 us
    reduce_scatter x1, waiting for transfers between devices, on_device(): lax.psum_scatter(down_term, ('z', 'y'), scatter_dimension=0, tiled=True)  77.7 us
    reduce_scatter x1, waiting for transfers between devices, on_device(): lax.psum_scatter(feed_term, ('y', 'z'), scatter_dimension=1, tiled=True)  68.4 us
    reduce_scatter x1, waiting for transfers between devices, on_device(): lax.psum_scatter(qkv_term, ('y', 'z'), scatter_dimension=1, tiled=True)  68.1 us
    ppermute x15, waiting for transfers between devices, from_ring(): return lax.ppermute(item, RING, [(i, (i - step) % 4) for i in range(4)])  41.4 us
    ppermute x12, waiting for transfers between devices, to_ring(): return lax.ppermute(item, RING, [(i, (i + step) % 4) for i in range(4)])  35.3 us
    ppermute x37, waiting for transfers between devices, swap(): return lax.ppermute(item, axis, SWAP)  33.4 us
    dot_general x6, matrix products, times_t(): lax.dot_general(left, right, (((1,), (1,)), ((), ())), preferred_element_...  31 us
  transfers between devices with their start and end apart: 78, of which 26 were waited for; matrix products, arithmetic and copies ran while one was open for 21% of the time, Pallas kernels for 0%

profile of v1, /device:TPU:1, one launch (start us, length us, event | category | flops | bytes accessed | tf_op | source)
XLA Modules:
  0.0 691.7 jit_solution(7901807521043347433)
XLA Ops:
  61.6 8.0 %collective-permute-done.2 = bf16[128,2048]{1,0:T(8,128)(2,1)S(1)} collective-permute-done((bf16[128,2048]{1,0:T(8,128)(2,1)S(1)}, bf16[128,2048]{1,0:T(8,128)(2,1)S(1)}, u32[]{:S(2)}, u32[]{:S(2)}) %collective-permute-start.2) | collective-permute-done | bytes 524320 | tf_op jit(solution)/shard_map/ppermute | solution.py:73
  70.8 11.0 %collective-permute-done.1 = bf16[128,2048]{1,0:T(8,128)(2,1)S(1)} collective-permute-done((bf16[128,2048]{1,0:T(8,128)(2,1)S(1)}, bf16[128,2048]{1,0:T(8,128)(2,1)S(1)}, u32[]{:S(2)}, u32[]{:S(2)}) %collective-permute-start.1) | collective-permute-done | bytes 524320 | tf_op jit(solution)/shard_map/ppermute | solution.py:73
  103.4 7.5 %all-gather.7.cloned.1.call-done = bf16[256,2048]{1,0:T(8,128)(2,1)} async-done(((bf16[16,2048]{1,0:T(8,128)(2,1)}), bf16[256,2048]{1,0:T(8,128)(2,1)}) %all-gather.7.cloned.1.call-update) | async-done | bytes 1048592 | tf_op jit(solution)/shard_map/all_gather | solution.py:196
  122.3 9.0 %collective-permute-done.39 = bf16[128,2048]{1,0:T(8,128)(2,1)} collective-permute-done((bf16[128,2048]{1,0:T(8,128)(2,1)S(1)}, bf16[128,2048]{1,0:T(8,128)(2,1)}, u32[]{:S(2)}, u32[]{:S(2)}) %collective-permute-start.39) | collective-permute-done | bytes 524320 | tf_op jit(solution)/shard_map/ppermute | solution.py:73
  148.0 8.8 %collective-permute-start.42 = (bf16[128,2048]{1,0:T(8,128)(2,1)}, bf16[128,2048]{1,0:T(8,128)(2,1)S(1)}, u32[]{:S(2)}, u32[]{:S(2)}) collective-permute-start(bf16[128,2048]{1,0:T(8,128)(2,1)} %collective-permute-done.38), channel_id=1, source_target_pairs={{0,1},{1,0},{2,3},{3,2},{4,5},{5,4},{6,7},{7,6},{8,9},{9,8},{10,11... | collective-permute-start | bytes 1572872 | tf_op jit(solution)/shard_map/ppermute | solution.py:81
  169.4 7.6 %collective-permute-start.27 = (bf16[128,2048]{1,0:T(8,128)(2,1)S(1)}, bf16[128,2048]{1,0:T(8,128)(2,1)S(1)}, u32[]{:S(2)}, u32[]{:S(2)}) collective-permute-start(bf16[128,2048]{1,0:T(8,128)(2,1)S(1)} %get-tuple-element.15), channel_id=1, source_target_pairs={{0,1},{1,0},{2,3},{3,2},{4,5},{5,4},{6,7},{7,6},{8,9},{9,8},{10,11... | collective-permute-start | bytes 1572872 | tf_op jit(solution)/shard_map/ppermute | solution.py:81
  177.3 12.6 %collective-permute-start.30 = (bf16[128,2048]{1,0:T(8,128)(2,1)S(1)}, bf16[128,2048]{1,0:T(8,128)(2,1)S(1)}, u32[]{:S(2)}, u32[]{:S(2)}) collective-permute-start(bf16[128,2048]{1,0:T(8,128)(2,1)S(1)} %collective-permute-done.26), channel_id=1, source_target_pairs={{0,1},{1,0},{2,3},{3,2},{4,5},{5,4},{6,7},{7,6},{8,9},{9,8},{10,11... | collective-permute-start | bytes 1572872 | tf_op jit(solution)/shard_map/ppermute | solution.py:81
  196.9 8.5 %fusion.1 = f32[1024,768]{0,1:T(8,128)} fusion(bf16[1024,2048]{1,0:T(8,128)(2,1)} %constant_dynamic-update-slice_fusion.10, bf16[2048,1536]{1,0:T(8,128)(2,1)} %bitcast.325), kind=kOutput, calls=%fused_computation.12 | convolution fusion | flops 3221225472 | bytes 10485760 | tf_op jit(solution)/shard_map/dot_general | solution.py:38
  205.5 7.4 %fusion.3 = f32[1024,768]{0,1:T(8,128)} fusion(bf16[1024,2048]{1,0:T(8,128)(2,1)} %constant_dynamic-update-slice_fusion.10, bf16[2048,1536]{1,0:T(8,128)(2,1)S(1)} %bitcast.327), kind=kOutput, calls=%fused_computation.14 | convolution fusion | flops 3221225472 | bytes 10485760 | tf_op jit(solution)/shard_map/dot_general | solution.py:38
  212.9 12.8 %all-gather.11.cloned.1.call-done = bf16[768,2048]{1,0:T(8,128)(2,1)} async-done(((bf16[48,2048]{1,0:T(8,128)(2,1)}), bf16[768,2048]{1,0:T(8,128)(2,1)}) %all-gather.11.cloned.1.call-update) | async-done | bytes 3145744 | tf_op jit(solution)/shard_map/all_gather | solution.py:219
  225.7 9.6 %multiply_convert_fusion = (bf16[1024,768]{0,1:T(8,128)(2,1)S(1)}, bf16[1024,768]{0,1:T(8,128)(2,1)S(1)}, bf16[1024,768]{0,1:T(8,128)(2,1)S(1)}) fusion(f32[1024,768]{0,1:T(8,128)} %fusion.3, f32[1024,768]{0,1:T(8,128)} %fusion.1, bf16[1024,2048]{1,0:T(8,128)(2,1)} %constant_dynamic-update-slice_fusion.18, bf16[768,2048]{1,0:T(8,128)(2,1)} %all-gather.11.cloned.1.call-done), kind=kOutput, calls=%fused_computation.16 | convolution fusion | flops 3233021952 | bytes 18350080 | tf_op jit(solution)/shard_map/dot_general | solution.py:42
  238.4 7.8 %convolution_convert_fusion.4 = bf16[512,2048]{1,0:T(8,128)(2,1)} fusion(bf16[2048,1536]{1,0:T(8,128)(2,1)} %bitcast.326, bf16[1024,768]{0,1:T(8,128)(2,1)S(1)} %get-tuple-element.21, bf16[1024,768]{0,1:T(8,128)(2,1)S(1)} %get-tuple-element.20), kind=kOutput, calls=%fused_computation.23 | convolution fusion | flops 3225419776 | bytes 11534336 | tf_op jit(solution)/shard_map/dot_general | solution.py:42
  265.2 10.7 %collective-permute-done.35 = bf16[128,2048]{1,0:T(8,128)(2,1)S(1)} collective-permute-done((bf16[128,2048]{1,0:T(8,128)(2,1)S(1)}, bf16[128,2048]{1,0:T(8,128)(2,1)S(1)}, u32[]{:S(2)}, u32[]{:S(2)}) %collective-permute-start.35) | collective-permute-done | bytes 524320 | tf_op jit(solution)/shard_map/ppermute | solution.py:77
  276.0 10.3 %collective-permute-done.45 = bf16[128,2048]{1,0:T(8,128)(2,1)S(1)} collective-permute-done((bf16[128,2048]{1,0:T(8,128)(2,1)S(1)}, bf16[128,2048]{1,0:T(8,128)(2,1)S(1)}, u32[]{:S(2)}, u32[]{:S(2)}) %collective-permute-start.45) | collective-permute-done | bytes 524320 | tf_op jit(solution)/shard_map/ppermute | solution.py:77
  286.2 12.2 %collective-permute-done.46 = bf16[128,2048]{1,0:T(8,128)(2,1)S(1)} collective-permute-done((bf16[128,2048]{1,0:T(8,128)(2,1)S(1)}, bf16[128,2048]{1,0:T(8,128)(2,1)S(1)}, u32[]{:S(2)}, u32[]{:S(2)}) %collective-permute-start.46) | collective-permute-done | bytes 524320 | tf_op jit(solution)/shard_map/ppermute | solution.py:77
  306.8 9.6 %collective-permute-done.50 = bf16[128,2048]{1,0:T(8,128)(2,1)S(1)} collective-permute-done((bf16[128,2048]{1,0:T(8,128)(2,1)S(1)}, bf16[128,2048]{1,0:T(8,128)(2,1)S(1)}, u32[]{:S(2)}, u32[]{:S(2)}) %collective-permute-start.50) | collective-permute-done | bytes 524320 | tf_op jit(solution)/shard_map/ppermute | solution.py:73
  316.4 12.0 %collective-permute-start.54 = (bf16[128,2048]{1,0:T(8,128)(2,1)S(1)}, bf16[128,2048]{1,0:T(8,128)(2,1)S(1)}, u32[]{:S(2)}, u32[]{:S(2)}) collective-permute-start(bf16[128,2048]{1,0:T(8,128)(2,1)S(1)} %collective-permute-done.50), channel_id=1, source_target_pairs={{0,1},{1,0},{2,3},{3,2},{4,5},{5,4},{6,7},{7,6},{8,9},{9,8},{10,11... | collective-permute-start | bytes 1572872 | tf_op jit(solution)/shard_map/ppermute | solution.py:81
  336.1 7.7 %convolution_convert_fusion.1 = bf16[768,2048]{1,0:T(8,128)(2,1)} fusion(bf16[1024,768]{0,1:T(8,128)(2,1)} %copy-done.11, bf16[1024,2048]{1,0:T(8,128)(2,1)} %constant_dynamic-update-slice_fusion.18), kind=kOutput, calls=%fused_computation.11 | convolution fusion | flops 3222798336 | bytes 8912896 | tf_op jit(solution)/shard_map/dot_general | solution.py:46
  360.2 10.7 %convolution_convert_fusion = bf16[2048,1536]{1,0:T(8,128)(2,1)} fusion(bf16[1024,2048]{1,0:T(8,128)(2,1)} %constant_dynamic-update-slice_fusion.10, bf16[1024,768]{0,1:T(8,128)(2,1)S(1)} %copy-done.42, bf16[1024,768]{0,1:T(8,128)(2,1)} %copy-done.43), kind=kOutput, calls=%fused_computation.1 | convolution fusion | flops 6451888128 | bytes 13631488 | tf_op jit(solution)/shard_map/dot_general | solution.py:46
  385.2 19.9 %reduce-scatter.7.cloned.1.call-done = bf16[16,2048]{1,0:T(8,128)(2,1)} async-done(((bf16[256,2048]{1,0:T(8,128)(2,1)}), bf16[16,2048]{1,0:T(8,128)(2,1)}) %reduce-scatter.7.cloned.1.call-update) | async-done | bytes 65552 | tf_op jit(solution)/shard_map/reduce_scatter | solution.py:269
  405.9 77.7 %reduce-scatter.9.cloned.1.call-done = bf16[48,2048]{1,0:T(8,128)(2,1)} async-done(((bf16[768,2048]{1,0:T(8,128)(2,1)}), bf16[48,2048]{1,0:T(8,128)(2,1)}) %reduce-scatter.9.cloned.1.call-update) | async-done | bytes 196624 | tf_op jit(solution)/shard_map/reduce_scatter | solution.py:264
  492.0 68.1 %reduce-scatter.5.cloned.1.call-done = bf16[2,64,384]{2,1,0:T(8,128)(2,1)} async-done(((bf16[2,1024,384]{2,1,0:T(8,128)(2,1)}), bf16[2,64,384]{2,1,0:T(8,128)(2,1)}) %reduce-scatter.5.cloned.1.call-update) | async-done | bytes 98320 | tf_op jit(solution)/shard_map/reduce_scatter | solution.py:290
  577.0 68.4 %reduce-scatter.11.cloned.1.call-done = bf16[2,64,1536]{2,1,0:T(8,128)(2,1)} async-done(((bf16[2,1024,1536]{2,1,0:T(8,128)(2,1)}), bf16[2,64,1536]{2,1,0:T(8,128)(2,1)}) %reduce-scatter.11.cloned.1.call-update) | async-done | bytes 393232 | tf_op jit(solution)/shard_map/reduce_scatter | solution.py:262
  659.4 10.4 %collective-permute-done.66 = bf16[120,2048]{1,0:T(8,128)(2,1)S(1)} collective-permute-done((bf16[120,2048]{1,0:T(8,128)(2,1)S(1)}, bf16[120,2048]{1,0:T(8,128)(2,1)S(1)}, u32[]{:S(2)}, u32[]{:S(2)}) %collective-permute-start.66) | collective-permute-done | bytes 491552 | tf_op jit(solution)/shard_map/ppermute | solution.py:81
  (480 shorter events, 247.2 us)
Async XLA Ops:
  7.2 82.7 %all-gather.5.cloned.1.call-start = ((), (), s32[]{:S(2)}) async-start(), calls=%async_computation.4 | async-start | bytes 1671168 | tf_op jit(solution)/shard_map/all_gather | solution.py:174
  19.9 91.0 %all-gather.7.cloned.1.call-start = ((), (), s32[]{:S(2)}) async-start(), calls=%async_computation.5 | async-start | bytes 1114112 | tf_op jit(solution)/shard_map/all_gather | solution.py:196
  32.6 164.4 %all-gather.9.cloned.1.call-start = ((), (), s32[]{:S(2)}) async-start(), calls=%async_computation.6 | async-start | bytes 6684672 | tf_op jit(solution)/shard_map/all_gather | solution.py:217
  40.1 185.6 %all-gather.11.cloned.1.call-start = ((), (), s32[]{:S(2)}) async-start(), calls=%async_computation.7 | async-start | bytes 3342336 | tf_op jit(solution)/shard_map/all_gather | solution.py:219
  53.5 33.0 %collective-permute-start.3 = (bf16[128,2048]{1,0:T(8,128)(2,1)S(1)}, bf16[128,2048]{1,0:T(8,128)(2,1)S(1)}, u32[]{:S(2)}, u32[]{:S(2)}) collective-permute-start(bf16[128,2048]{1,0:T(8,128)(2,1)S(1)} %get-tuple-element.19), channel_id=1, source_target_pairs={{0,1},{1,0},{2,3},{3,2},{4,5},{5,4},{6,7},{7,6},{8,9},{9,8},{10,11... | collective-permute-start | bytes 1572872 | tf_op jit(solution)/shard_map/ppermute | solution.py:81
  56.0 25.8 %collective-permute-start.1 = (bf16[128,2048]{1,0:T(8,128)(2,1)S(1)}, bf16[128,2048]{1,0:T(8,128)(2,1)S(1)}, u32[]{:S(2)}, u32[]{:S(2)}) collective-permute-start(bf16[128,2048]{1,0:T(8,128)(2,1)S(1)} %get-tuple-element.19), channel_id=1, source_target_pairs={{0,64},{32,96},{64,0},{96,32},{1,65},{33,97},{65,1},{97,33},{2,66}... | collective-permute-start | bytes 1572872 | tf_op jit(solution)/shard_map/ppermute | solution.py:73
  120.7 27.4 %collective-permute-start.40 = (bf16[128,2048]{1,0:T(8,128)(2,1)S(1)}, bf16[128,2048]{1,0:T(8,128)(2,1)}, u32[]{:S(2)}, u32[]{:S(2)}) collective-permute-start(bf16[128,2048]{1,0:T(8,128)(2,1)S(1)} %copy-done.9), channel_id=1, source_target_pairs={{0,1},{1,0},{2,3},{3,2},{4,5},{5,4},{6,7},{7,6},{8,9},{9,8},{10,11... | collective-permute-start | bytes 1572872 | tf_op jit(solution)/shard_map/ppermute | solution.py:81
  131.4 36.2 %collective-permute-start.43 = (bf16[128,2048]{1,0:T(8,128)(2,1)}, bf16[128,2048]{1,0:T(8,128)(2,1)}, u32[]{:S(2)}, u32[]{:S(2)}) collective-permute-start(bf16[128,2048]{1,0:T(8,128)(2,1)} %collective-permute-done.39), channel_id=1, source_target_pairs={{0,1},{1,0},{2,3},{3,2},{4,5},{5,4},{6,7},{7,6},{8,9},{9,8},{10,11... | collective-permute-start | bytes 1572872 | tf_op jit(solution)/shard_map/ppermute | solution.py:81
  134.5 270.6 %reduce-scatter.7.cloned.1.call-start = ((), (), s32[]{:S(2)}) async-start(), calls=%async_computation.9 | async-start | bytes 1114112 | tf_op jit(solution)/shard_map/reduce_scatter | solution.py:269
  163.2 26.8 %collective-permute-start.25 = (bf16[128,2048]{1,0:T(8,128)(2,1)S(1)}, bf16[128,2048]{1,0:T(8,128)(2,1)S(1)}, u32[]{:S(2)}, u32[]{:S(2)}) collective-permute-start(bf16[128,2048]{1,0:T(8,128)(2,1)S(1)} %get-tuple-element.15), channel_id=1, source_target_pairs={{0,64},{32,96},{64,0},{96,32},{1,65},{33,97},{65,1},{97,33},{2,66}... | collective-permute-start | bytes 1572872 | tf_op jit(solution)/shard_map/ppermute | solution.py:73
  258.9 27.3 %collective-permute-start.45 = (bf16[128,2048]{1,0:T(8,128)(2,1)S(1)}, bf16[128,2048]{1,0:T(8,128)(2,1)S(1)}, u32[]{:S(2)}, u32[]{:S(2)}) collective-permute-start(bf16[128,2048]{1,0:T(8,128)(2,1)S(1)} %get-tuple-element.26), channel_id=1, source_target_pairs={{0,32},{32,64},{64,96},{96,0},{1,33},{33,65},{65,97},{97,1},{2,34}... | collective-permute-start | bytes 1572872 | tf_op jit(solution)/shard_map/ppermute | solution.py:77
  259.3 27.0 %collective-permute-start.47 = (bf16[128,2048]{1,0:T(8,128)(2,1)S(1)}, bf16[128,2048]{1,0:T(8,128)(2,1)S(1)}, u32[]{:S(2)}, u32[]{:S(2)}) collective-permute-start(bf16[128,2048]{1,0:T(8,128)(2,1)S(1)} %get-tuple-element.27), channel_id=1, source_target_pairs={{0,96},{32,0},{64,32},{96,64},{1,97},{33,1},{65,33},{97,65},{2,98}... | collective-permute-start | bytes 1572872 | tf_op jit(solution)/shard_map/ppermute | solution.py:77
  263.8 34.7 %collective-permute-start.46 = (bf16[128,2048]{1,0:T(8,128)(2,1)S(1)}, bf16[128,2048]{1,0:T(8,128)(2,1)S(1)}, u32[]{:S(2)}, u32[]{:S(2)}) collective-permute-start(bf16[128,2048]{1,0:T(8,128)(2,1)S(1)} %get-tuple-element.28), channel_id=1, source_target_pairs={{0,64},{32,96},{64,0},{96,32},{1,65},{33,97},{65,1},{97,33},{2,66}... | collective-permute-start | bytes 1572872 | tf_op jit(solution)/shard_map/ppermute | solution.py:77
  302.2 26.3 %collective-permute-start.49 = (bf16[128,2048]{1,0:T(8,128)(2,1)S(1)}, bf16[128,2048]{1,0:T(8,128)(2,1)S(1)}, u32[]{:S(2)}, u32[]{:S(2)}) collective-permute-start(bf16[128,2048]{1,0:T(8,128)(2,1)S(1)} %get-tuple-element.12), channel_id=1, source_target_pairs={{0,64},{32,96},{64,0},{96,32},{1,65},{33,97},{65,1},{97,33},{2,66}... | collective-permute-start | bytes 1572872 | tf_op jit(solution)/shard_map/ppermute | solution.py:73
  336.0 147.6 %reduce-scatter.9.cloned.1.call-start = ((), (), s32[]{:S(2)}) async-start(), calls=%async_computation.10 | async-start | bytes 3342336 | tf_op jit(solution)/shard_map/reduce_scatter | solution.py:264
  343.8 216.3 %reduce-scatter.5.cloned.1.call-start = ((), (), s32[]{:S(2)}) async-start(), calls=%async_computation.8 | async-start | bytes 1671168 | tf_op jit(solution)/shard_map/reduce_scatter | solution.py:290
  360.0 285.5 %reduce-scatter.11.cloned.1.call-start = ((), (), s32[]{:S(2)}) async-start(), calls=%async_computation.11 | async-start | bytes 6684672 | tf_op jit(solution)/shard_map/reduce_scatter | solution.py:262
  382.5 104.8 %collective-permute-start.56 = (bf16[128,2048]{1,0:T(8,128)(2,1)}, bf16[128,2048]{1,0:T(8,128)(2,1)S(1)}, u32[]{:S(2)}, u32[]{:S(2)}) collective-permute-start(bf16[128,2048]{1,0:T(8,128)(2,1)} %get-tuple-element.23), channel_id=1, source_target_pairs={{0,32},{32,64},{64,96},{96,0},{1,33},{33,65},{65,97},{97,1},{2,34}... | collective-permute-start | bytes 1572872 | tf_op jit(solution)/shard_map/ppermute | solution.py:77
  382.5 107.9 %collective-permute-start.58 = (bf16[128,2048]{1,0:T(8,128)(2,1)}, bf16[128,2048]{1,0:T(8,128)(2,1)S(1)}, u32[]{:S(2)}, u32[]{:S(2)}) collective-permute-start(bf16[128,2048]{1,0:T(8,128)(2,1)} %get-tuple-element.24), channel_id=1, source_target_pairs={{0,96},{32,0},{64,32},{96,64},{1,97},{33,1},{65,33},{97,65},{2,98}... | collective-permute-start | bytes 1572872 | tf_op jit(solution)/shard_map/ppermute | solution.py:77
  385.2 105.2 %collective-permute-start.57 = (bf16[128,2048]{1,0:T(8,128)(2,1)}, bf16[128,2048]{1,0:T(8,128)(2,1)S(1)}, u32[]{:S(2)}, u32[]{:S(2)}) collective-permute-start(bf16[128,2048]{1,0:T(8,128)(2,1)} %get-tuple-element.25), channel_id=1, source_target_pairs={{0,64},{32,96},{64,0},{96,32},{1,65},{33,97},{65,1},{97,33},{2,66}... | collective-permute-start | bytes 1572872 | tf_op jit(solution)/shard_map/ppermute | solution.py:77
  484.6 83.1 %collective-permute-start.64 = (bf16[64,2048]{1,0:T(8,128)(2,1)S(1)}, bf16[64,2048]{1,0:T(8,128)(2,1)}, u32[]{:S(2)}, u32[]{:S(2)}) collective-permute-start(bf16[64,2048]{1,0:T(8,128)(2,1)S(1)} %constant_dynamic-update-slice_fusion.34), channel_id=1, source_target_pairs={{8,0},{17,9},{88,80},{65,89},{10,2},{19,11},{90,82},{67,91},{12,4}... | collective-permute-start | bytes 786440 | tf_op jit(solution)/shard_map/ppermute | solution.py:350
  485.9 81.7 %collective-permute-start.63 = (bf16[64,2048]{1,0:T(8,128)(2,1)S(1)}, bf16[64,2048]{1,0:T(8,128)(2,1)}, u32[]{:S(2)}, u32[]{:S(2)}) collective-permute-start(bf16[64,2048]{1,0:T(8,128)(2,1)S(1)} %constant_dynamic-update-slice_fusion.34), channel_id=1, source_target_pairs={{16,0},{25,9},{64,80},{73,89},{18,2},{27,11},{66,82},{75,91},{20,4... | collective-permute-start | bytes 786440 | tf_op jit(solution)/shard_map/ppermute | solution.py:350
  487.3 80.4 %collective-permute-start.62 = (bf16[64,2048]{1,0:T(8,128)(2,1)S(1)}, bf16[64,2048]{1,0:T(8,128)(2,1)}, u32[]{:S(2)}, u32[]{:S(2)}) collective-permute-start(bf16[64,2048]{1,0:T(8,128)(2,1)S(1)} %constant_dynamic-update-slice_fusion.34), channel_id=1, source_target_pairs={{24,0},{1,9},{72,80},{81,89},{26,2},{3,11},{74,82},{83,91},{28,4},... | collective-permute-start | bytes 786440 | tf_op jit(solution)/shard_map/ppermute | solution.py:350
  572.1 83.1 %collective-permute-start.65 = (bf16[120,2048]{1,0:T(8,128)(2,1)S(1)}, bf16[120,2048]{1,0:T(8,128)(2,1)S(1)}, u32[]{:S(2)}, u32[]{:S(2)}) collective-permute-start(bf16[120,2048]{1,0:T(8,128)(2,1)S(1)} %broadcast_select_fusion), channel_id=1, source_target_pairs={{0,1},{1,0},{2,3},{3,2},{4,5},{5,4},{6,7},{7,6},{8,9},{9,8},{10,11... | collective-permute-start | bytes 1474568 | tf_op jit(solution)/shard_map/ppermute | solution.py:81
  (100 other events, 1544.2 us)
Sparse Core Ops, SparseCore 0:
  20.0 46.5 all-gather.4
  69.3 41.4 all-gather.6
  113.6 62.0 all-gather.8
  178.2 47.3 all-gather.10
  336.1 68.9 reduce-scatter.6
  408.6 74.9 reduce-scatter.8
  487.2 72.9 reduce-scatter.4
  564.0 81.4 reduce-scatter.10

commit v2 on v1

--- a/solution.py
+++ b/solution.py
@@ -11,10 +11,7 @@
 CAP = 128
 TP = 8
 LOCAL_HEADS = HEADS // TP
-LOCAL_FF = FF // TP
-SEGMENT = LOCAL_FF // 4
-PADDED = 192
-WIDE = 4 * PADDED
+WIDE = 768
 BF16 = jnp.bfloat16
 F32 = jnp.float32
 
@@ -114,18 +111,63 @@
     return jnp.stack([jnp.where(xl == 0, kept, came), jnp.where(xl == 0, came, kept)])
 
 
-def return_columns(item, xl, c):
-    kept = jnp.where(xl == 0, item[0], item[1])
-    came = swap(jnp.where(xl == 0, item[1], item[0]), "xl")
-    first = jnp.where(xl == 0, kept, came)
-    second = jnp.where(xl == 0, came, kept)
-    rows = first.shape[0] // 2
-    both = jnp.stack([first, second])
-    mine = jnp.where(c == 0, both[:, :rows], both[:, rows:])
-    came = swap(jnp.where(c == 0, both[:, rows:], both[:, :rows]), "c")
-    zero = jnp.where(c == 0, mine, came)
-    one = jnp.where(c == 0, came, mine)
-    return zero, one
+def return_columns(item, xh, xl, c, reduce):
+    rows = item.shape[1] // 2
+    mine = jnp.where(c == 0, item[:, :rows], item[:, rows:])
+    came = swap(jnp.where(c == 0, item[:, rows:], item[:, :rows]), "c")
+    both = reduce(jnp.where(c == 0, mine, came), jnp.where(c == 0, came, mine))
+    here = jnp.where(xl == 0, both[0], both[1])
+    there = jnp.where(xl == 0, both[1], both[0])
+    parts = [here, to_ring(there, 1), to_ring(here, 2), to_ring(there, 3)]
+    spot = 2 * xh + xl
+    stacked = jnp.stack(parts)
+    return [
+        [
+            lax.dynamic_index_in_dim(stacked, (spot - (2 * h + k)) % 4, 0, keepdims=False)
+            for h in range(2)
+        ]
+        for k in range(2)
+    ]
+
+
+def gather_four(item, axis, spot, dim):
+    shape = item.shape[:dim] + (4,) + item.shape[dim:]
+    out = jnp.zeros(shape, item.dtype)
+    out = lax.dynamic_update_index_in_dim(out, item, spot, dim)
+    for step in (1, 2, 3):
+        came = lax.ppermute(item, axis, [(i, (i - step) % 4) for i in range(4)])
+        out = lax.dynamic_update_index_in_dim(out, came, (spot + step) % 4, dim)
+    return out
+
+
+def scatter_four(item, axis, spot, dim):
+    total = lax.dynamic_index_in_dim(item, spot, dim, keepdims=False).astype(F32)
+    for step in (1, 2, 3):
+        sent = lax.dynamic_index_in_dim(item, (spot + step) % 4, dim, keepdims=False)
+        total = total + lax.ppermute(sent, axis, [(i, (i + step) % 4) for i in range(4)]).astype(F32)
+    return total
+
+
+def row_pairs(step, back):
+    pairs = []
+    for h in range(2):
+        for e in range(2):
+            first = 2 * h + e
+            one = (h * 4 + first) * 2 + e
+            other = (h * 4 + (first + step) % 4) * 2 + e
+            pairs.append((other, one) if back else (one, other))
+    return pairs
+
+
+def after(item, *others):
+    return lax.optimization_barrier((item,) + others)[0]
+
+
+def order_of_columns(xh):
+    place = jnp.arange(768)
+    core, owner, row = place // 384, (place % 384) // 48, place % 48
+    origin = jnp.where(row < 44, 176 * owner + 88 * core + 44 * xh + row, -1)
+    return (jnp.arange(1408)[:, None] == origin[None, :]).astype(BF16)
 
 
 def column_part(item, width, xh):
@@ -171,52 +213,45 @@
         ]
         for k in range(2)
     ]
-    qkv_full = lax.all_gather(spread_columns(chunks, xl, c), ("y", "z"), axis=1, tiled=True)
-    qkv_full = qkv_full.reshape(D, 384)
+    spread = spread_columns(chunks, xl, c)
+    qkv_full = gather_four(gather_four(spread, "z", z, 1), "y", y, 1).reshape(D, 384)
 
     source = 2 * xh + c
-    pair_rows = jnp.concatenate([out_weight, down_weight], axis=0)
-    came = swap(pair_rows, "c")
-    low = jnp.where(c == 0, pair_rows, came)
-    high = jnp.where(c == 0, came, pair_rows)
-    out_pair = jnp.concatenate([low[:32], high[:32]], axis=0).reshape(4, 16, D)
-    down_pair = jnp.concatenate([low[32:], high[32:], jnp.zeros((16, D), BF16)], axis=0)
-    quarters = jnp.concatenate([out_pair, down_pair.reshape(4, 48, D)], axis=1)
+    came = swap(out_weight, "c")
+    out_pair = jnp.concatenate(
+        [jnp.where(c == 0, out_weight, came), jnp.where(c == 0, came, out_weight)], axis=0
+    )
+    quarters = out_pair.reshape(4, 16, D)
     piece = lax.dynamic_index_in_dim(quarters, y, 0, keepdims=False)
     for step in (1, 2, 3):
         sent = lax.dynamic_index_in_dim(quarters, (y + step) % 4, 0, keepdims=False)
-        pairs = []
-        for a in range(2):
-            for b in range(4):
-                for e in range(2):
-                    if b == 2 * a + e:
-                        pairs.append(((a * 4 + b) * 2 + e, (a * 4 + (b + step) % 4) * 2 + e))
-        came = lax.ppermute(sent, ("xh", "y", "c"), pairs)
+        came = lax.ppermute(sent, ("xh", "y", "c"), row_pairs(step, False))
         piece = jnp.where((source + step) % 4 == y, came, piece)
-    out_full = lax.all_gather(piece[:16], ("z", "y"), axis=0, tiled=True)
-
-    g_parts = column_part(scaled(gate_weight, second_col), 1408, xh)
-    u_parts = column_part(scaled(up_weight, second_col), 1408, xh)
-
-    def widened(item):
-        item = item.reshape(32, 8, SEGMENT)
-        item = jnp.pad(item, ((0, 0), (0, 0), (0, PADDED - SEGMENT)))
-        return item.reshape(32, 2 * WIDE)
-
-    chunks = []
-    for k in range(2):
-        g_wide, u_wide = widened(g_parts[k]), widened(u_parts[k])
-        chunks.append(
-            [
-                jnp.concatenate(
-                    [g_wide[:, j * WIDE : (j + 1) * WIDE], u_wide[:, j * WIDE : (j + 1) * WIDE]], axis=1
-                )
-                for j in range(2)
-            ]
-        )
+    out_full = gather_four(gather_four(piece, "y", y, 0), "z", z, 0).reshape(256, D)
+
+    wide = jnp.stack([scaled(gate_weight, second_col), scaled(up_weight, second_col)])
+    blocks = jnp.concatenate([wide[:, :, 1408 * k : 1408 * (k + 1)] for k in range(4)], axis=0)
+    sorted_columns = times(blocks.reshape(256, 1408), order_of_columns(xh)).astype(BF16)
+    sorted_columns = sorted_columns.reshape(2, 2, 2, 32, 768)
+    chunks = [
+        [
+            jnp.concatenate(
+                [
+                    sorted_columns[k, h, item, :, 384 * j : 384 * (j + 1)]
+                    for item in range(2)
+                    for h in range(2)
+                ],
+                axis=1,
+            )
+            for j in range(2)
+        ]
+        for k in range(2)
+    ]
     feed_full = lax.all_gather(spread_columns(chunks, xl, c), ("y", "z"), axis=1, tiled=True)
     feed_full = feed_full.reshape(D, 2 * WIDE)
-    down_full = lax.all_gather(piece[16:], ("z", "y"), axis=0, tiled=True)
+    down_half = jnp.where(xh == 0, down_weight[:44], down_weight[44:])
+    down_half = jnp.pad(down_half, ((0, 4), (0, 0)))
+    down_full = lax.all_gather(down_half, ("y", "z"), axis=0, tiled=True)
 
     ids = share(doc_ids[None])
     cosine, sine, allowed = rotary(ids)
@@ -225,6 +260,7 @@
     rows = tokens.astype(F32)
     first_scale = rms_scale(rows)
     normed = share((rows * first_scale).astype(BF16))
+    upstream = share(after(cotangent, normed))
     qkv = times(normed, qkv_full)
     queries = qkv[:, :256].reshape(TP * CAP, LOCAL_HEADS, HDIM)
     keys = qkv[:, 256:320].reshape(TP * CAP, 1, HDIM)
@@ -244,7 +280,6 @@
 
     second_scale = rms_scale(midway)
     normed_two = share((midway * second_scale).astype(BF16))
-    upstream = share(cotangent)
     gate_act = times(normed_two, feed_full[:, :WIDE])
     up_act = times(normed_two, feed_full[:, WIDE:])
     sigmoid_gate = jax.nn.sigmoid(gate_act)
@@ -256,17 +291,27 @@
     grad_feed = jnp.concatenate([grad_gate.astype(BF16), grad_up.astype(BF16)], axis=1)
     inner_two = collect(grad_feed, feed_full, times_t)
     grad_mid = cotangent.astype(F32) + norm_back(midway, second_scale, inner_two)
-    output = (midway + collect(hidden, down_full, times)).astype(BF16)
-
-    feed_term = t_times(normed_two, grad_feed).astype(BF16).reshape(2, D // 2, 2 * WIDE)
-    feed_part = lax.psum_scatter(feed_term, ("y", "z"), scatter_dimension=1, tiled=True)
-    down_term = t_times(hidden, upstream).astype(BF16)
-    down_part = lax.psum_scatter(down_term, ("z", "y"), scatter_dimension=0, tiled=True)
+    feed_term = t_times(normed_two, grad_feed).astype(BF16).reshape(2, 16, 64, 2 * WIDE)
+    feed_term = feed_term.swapaxes(0, 1).reshape(16, 128, 2 * WIDE)
+    down_term = t_times(hidden, upstream).astype(BF16).reshape(16, 48, D)
+    corner = jnp.concatenate(
+        [down_term[:, 16 * k : 16 * (k + 1), 2 * WIDE :] for k in range(3)], axis=2
+    )
+    pack = jnp.concatenate([feed_term, down_term[:, :, : 2 * WIDE], corner], axis=1)
+    pack = pack.reshape(16 * 192, 2 * WIDE)
+    pack = lax.psum_scatter(pack, ("y", "z"), scatter_dimension=0, tiled=True)
+    feed_part = pack[:128].reshape(2, 64, 2 * WIDE)
+    corner = pack[176:]
+    corner = jnp.concatenate([corner[:, 512 * k : 512 * (k + 1)] for k in range(3)], axis=0)
+    down_part = jnp.concatenate([pack[128:176], corner], axis=1)
 
     grad_attn = share(grad_mid.astype(BF16))
     grad_mixed = times_t(grad_attn, out_full).astype(BF16)
     out_term = t_times(mixed, grad_attn).astype(BF16)
-    out_part = lax.psum_scatter(out_term, ("z", "y"), scatter_dimension=0, tiled=True)
+    out_part = scatter_four(out_term.reshape(4, 4, 16, D), "z", z, 0).astype(BF16)
+    out_part = scatter_four(out_part, "y", y, 0).astype(BF16)
+    output = midway + collect(after(hidden, grad_attn), down_full, times)
+    output = output.astype(BF16)
     grad_heads = grad_mixed.reshape(TP, CAP, LOCAL_HEADS, HDIM)
     grad_probs = jnp.einsum("bigd,bjd->bgij", grad_heads, values, preferred_element_type=F32)
     delta = jnp.sum(probs * grad_probs, axis=-1, keepdims=True)
@@ -287,81 +332,75 @@
         axis=1,
     )
     qkv_term = t_times(normed, grad_qkv).astype(BF16).reshape(2, D // 2, 384)
-    qkv_part = lax.psum_scatter(qkv_term, ("y", "z"), scatter_dimension=1, tiled=True)
+    qkv_part = scatter_four(qkv_term.reshape(2, 4, 4, 64, 384), "y", y, 1).astype(BF16)
+    qkv_part = scatter_four(qkv_part, "z", z, 1).astype(BF16)
     inner_one = collect(grad_qkv, qkv_full, times_t)
     tokens_grad = grad_mid + norm_back(rows, first_scale, inner_one)
 
-    def both_halves(item):
-        came = swap(item, "xh")
-        return jnp.where(xh == 0, item, came), jnp.where(xh == 0, came, item)
-
-    zero, one = return_columns(qkv_part, xl, c)
-    pair_kv = (zero[:, :, 256:].astype(F32) + one[:, :, 256:].astype(F32)).astype(BF16)
-    pack = jnp.concatenate([zero[:, :, :256], one[:, :, :256], pair_kv], axis=2)
-    halves = both_halves(pack)
-    query_raw = jnp.concatenate(
-        [halves[h][k][:, :512] for k in range(2) for h in range(2)], axis=1
-    ).astype(F32)
-    key_raw = jnp.concatenate(
-        [halves[h][k][:, 512:576] for k in range(2) for h in range(2)], axis=1
-    ).astype(F32)
-    value_raw = jnp.concatenate(
-        [halves[h][k][:, 576:] for k in range(2) for h in range(2)], axis=1
-    ).astype(F32)
+    def with_pair(zero, one):
+        pair = zero[:, :, 256:].astype(F32) + one[:, :, 256:].astype(F32)
+        return jnp.concatenate([zero[:, :, :256], one[:, :, :256], pair.astype(BF16)], axis=2)
+
+    parts = return_columns(qkv_part, xh, xl, c, with_pair)
+
+    def joined(start, end):
+        return jnp.concatenate(
+            [parts[k][h][:, start:end] for k in range(2) for h in range(2)], axis=1
+        ).astype(F32)
+
+    query_raw, key_raw, value_raw = joined(0, 512), joined(512, 576), joined(576, 640)
     first_grad = (
         jnp.sum(query_raw * query_weight.astype(F32), axis=1)
         + jnp.sum(key_raw * key_weight.astype(F32), axis=1)
         + jnp.sum(value_raw * value_weight.astype(F32), axis=1)
     )
 
-    def narrowed(item):
-        item = item.reshape(32, 4, PADDED)[:, :, :SEGMENT]
-        return item.reshape(32, LOCAL_FF)
-
-    zero, one = return_columns(feed_part, xl, c)
-    halves = both_halves(jnp.stack([zero, one]))
-
-    def feed_columns(start):
-        return jnp.concatenate(
-            [
-                narrowed(halves[h][j, k, :, start : start + WIDE])
-                for k in range(2)
-                for h in range(2)
-                for j in range(2)
-            ],
-            axis=1,
-        ).astype(F32)
-
-    gate_raw = feed_columns(0)
-    up_raw = feed_columns(WIDE)
+    parts = return_columns(
+        feed_part, xh, xl, c, lambda zero, one: jnp.concatenate([zero, one], axis=2)
+    )
+    shuffle = jnp.concatenate([order_of_columns(0), order_of_columns(1)], axis=1)
+    rows_of = []
+    for item in range(2):
+        for k in range(2):
+            for half in range(2):
+                start = item * WIDE + half * 384
+                rows_of.append(
+                    jnp.concatenate(
+                        [
+                            parts[k][h][:, e * 2 * WIDE + start : e * 2 * WIDE + start + 384]
+                            for h in range(2)
+                            for e in range(2)
+                        ],
+                        axis=1,
+                    )
+                )
+    unsorted = times_t(jnp.concatenate(rows_of, axis=0), shuffle).reshape(2, 4, 32, 1408)
+    gate_raw = jnp.concatenate([unsorted[0, k] for k in range(4)], axis=1)
+    up_raw = jnp.concatenate([unsorted[1, k] for k in range(4)], axis=1)
     second_grad = jnp.sum(gate_raw * gate_weight.astype(F32), axis=1) + jnp.sum(
         up_raw * up_weight.astype(F32), axis=1
     )
 
-    piece = jnp.concatenate([out_part, down_part], axis=0)
-    parts = [piece]
+    came = swap(down_part, "xh")
+    down_grad = jnp.concatenate(
+        [jnp.where(xh == 0, down_part, came)[:44], jnp.where(xh == 0, came, down_part)[:44]], axis=0
+    ).astype(F32)
+
+    parts = [out_part]
     for step in (1, 2, 3):
-        pairs = []
-        for a in range(2):
-            for b in range(4):
-                for e in range(2):
-                    if b == 2 * a + e:
-                        pairs.append(((a * 4 + (b + step) % 4) * 2 + e, (a * 4 + b) * 2 + e))
-        parts.append(lax.ppermute(piece, ("xh", "y", "c"), pairs))
+        parts.append(lax.ppermute(out_part, ("xh", "y", "c"), row_pairs(step, True)))
     ordered = []
     for q in range(4):
         item = parts[0]
         for step in (1, 2, 3):
             item = jnp.where((y + step) % 4 == q, parts[step], item)
         ordered.append(item)
-    out_rows = jnp.concatenate([item[:16] for item in ordered], axis=0)
-    down_rows = jnp.concatenate([item[16:] for item in ordered], axis=0)
-    low = jnp.concatenate([out_rows[:32], down_rows[:88]], axis=0)
-    high = jnp.concatenate([out_rows[32:], down_rows[88:176]], axis=0)
+    low = jnp.concatenate(ordered[:2], axis=0)
+    high = jnp.concatenate(ordered[2:], axis=0)
     came = swap(jnp.where(c == 0, high, low), "c")
     owned = jnp.where(y % 2 == c, jnp.where(c == 0, low, high), came)
     came = swap(owned, "xh")
-    owned = jnp.where(y // 2 == xh, owned, came).astype(F32)
+    out_grad = jnp.where(y // 2 == xh, owned, came).astype(F32)
 
     return (
         output,
@@ -370,11 +409,11 @@
         query_raw * first_col,
         key_raw * first_col,
         value_raw * first_col,
-        owned[:32],
+        out_grad,
         second_grad,
         gate_raw * second_col,
         up_raw * second_col,
-        owned[32:],
+        down_grad,
     )
 
 

time: 701 us -> 571 us (0.81)
  waiting for transfers between devices: 365 us -> 231 us
  other arithmetic: 36.9 us -> 48.3 us
    reduce_scatter x4 -> x1, waiting for transfers between devices: 234 us -> 0.01 us  [on_device(): pack = lax.psum_scatter(pack, ('y', 'z'), scatter_dimension=0, tiled=True)]
    ppermute x6 -> x30, waiting for transfers between devices: 0.23 us -> 87.4 us  [the longest x12 54.5 us: gather_four(): came = lax.ppermute(item, axis, [(i, (i - step) % 4) for i in range(4)])]
    ppermute x12 -> x18, waiting for transfers between devices: 35.3 us -> 84.2 us  [to_ring(): return lax.ppermute(item, RING, [(i, (i + step) % 4) for i in range(4)])]
    ppermute x37 -> x34, starting transfers between devices: 88.3 us -> 49.3 us  [swap(): return lax.ppermute(item, axis, SWAP)]
    ppermute x6 -> x30, starting transfers between devices: 8.41 us -> 35.6 us  [the longest x12 17.4 us: gather_four(): came = lax.ppermute(item, axis, [(i, (i - step) % 4) for i in range(4)])]
    all_gather x2 -> x1, waiting for transfers between devices: 20.3 us -> 0.01 us  [on_device(): down_full = lax.all_gather(down_half, ('y', 'z'), axis=0, tiled=True)]
    ppermute x37 -> x34, waiting for transfers between devices: 33.4 us -> 21.7 us  [swap(): return lax.ppermute(item, axis, SWAP)]
    ppermute x12 -> x18, starting transfers between devices: 14.5 us -> 24.8 us  [to_ring(): return lax.ppermute(item, RING, [(i, (i + step) % 4) for i in range(4)])]
  transfers between devices with their start and end apart: 78 -> 100, of which waited for: 26 -> 45; matrix products, arithmetic and copies ran while one was open for 21% -> 27% of each run, Pallas kernels for 0% -> 0%
where the time goes in v2:
time: 571 us; the launch traced here: 561 us
  waiting for transfers between devices  231 us (40%)
  starting transfers between devices  125 us (22%)
  matrix products  93.5 us (16%)
  other arithmetic  48.3 us (8%)
  local copies, waits for them, and re-layouts  47.1 us (8%)
  between operations  16.1 us (3%)
    ppermute x18, waiting for transfers between devices, to_ring(): return lax.ppermute(item, RING, [(i, (i + step) % 4) for i in range(4)])  84.2 us
    ppermute x12, waiting for transfers between devices, gather_four(): came = lax.ppermute(item, axis, [(i, (i - step) % 4) for i in range(4)])  54.5 us
    ppermute x34, starting transfers between devices, swap(): return lax.ppermute(item, axis, SWAP)  49.3 us
    ppermute x15, waiting for transfers between devices, from_ring(): return lax.ppermute(item, RING, [(i, (i - step) % 4) for i in range(4)])  37.6 us
    dot_general x7, matrix products, times_t(): lax.dot_general(left, right, (((1,), (1,)), ((), ())), preferred_element_...  34.5 us
    ppermute x12, waiting for transfers between devices, scatter_four(): lax.ppermute(sent, axis, [(i, (i + step) % 4) for i in range(4)])  32.8 us
    dot_general x8, matrix products, times(): return jnp.dot(left, right, preferred_element_type=F32)  29.7 us
    unnamed x152, local copies, waits for them, and re-layouts  24.9 us
  transfers between devices with their start and end apart: 100, of which 45 were waited for; matrix products, arithmetic and copies ran while one was open for 27% of the time, Pallas kernels for 0%

profile of v2, /device:TPU:1, one launch (start us, length us, event | category | flops | bytes accessed | tf_op | source)
XLA Modules:
  0.0 561.3 jit_solution(1761370885668894891)
XLA Ops:
  30.9 12.5 %collective-permute-done.8 = bf16[64,384]{1,0:T(8,128)(2,1)S(1)} collective-permute-done((bf16[64,384]{1,0:T(8,128)(2,1)S(1)}, bf16[64,384]{1,0:T(8,128)(2,1)S(1)}, u32[]{:S(2)}, u32[]{:S(2)}) %collective-permute-start.8) | collective-permute-done | bytes 49184 | tf_op jit(solution)/shard_map/ppermute | solution.py:78
  67.7 6.5 %collective-permute-done.11 = bf16[2,64,384]{2,1,0:T(8,128)(2,1)S(1)} collective-permute-done((bf16[2,64,384]{2,1,0:T(8,128)(2,1)S(1)}, bf16[2,64,384]{2,1,0:T(8,128)(2,1)S(1)}, u32[]{:S(2)}, u32[]{:S(2)}) %collective-permute-start.11) | collective-permute-done | bytes 98336 | tf_op jit(solution)/shard_map/ppermute | solution.py:138
  89.5 9.2 %collective-permute-done.29 = bf16[4,16,2048]{2,1,0:T(8,128)(2,1)S(1)} collective-permute-done((bf16[4,16,2048]{2,1,0:T(8,128)(2,1)S(1)}, bf16[4,16,2048]{2,1,0:T(8,128)(2,1)S(1)}, u32[]{:S(2)}, u32[]{:S(2)}) %collective-permute-start.29) | collective-permute-done | bytes 262176 | tf_op jit(solution)/shard_map/ppermute | solution.py:138
  99.1 12.9 %collective-permute-done.30 = bf16[4,16,2048]{2,1,0:T(8,128)(2,1)S(1)} collective-permute-done((bf16[4,16,2048]{2,1,0:T(8,128)(2,1)S(1)}, bf16[4,16,2048]{2,1,0:T(8,128)(2,1)S(1)}, u32[]{:S(2)}, u32[]{:S(2)}) %collective-permute-start.30) | collective-permute-done | bytes 262176 | tf_op jit(solution)/shard_map/ppermute | solution.py:138
  113.6 13.1 %collective-permute-done.31 = bf16[4,16,2048]{2,1,0:T(8,128)(2,1)S(1)} collective-permute-done((bf16[4,16,2048]{2,1,0:T(8,128)(2,1)S(1)}, bf16[4,16,2048]{2,1,0:T(8,128)(2,1)S(1)}, u32[]{:S(2)}, u32[]{:S(2)}) %collective-permute-start.31) | collective-permute-done | bytes 262176 | tf_op jit(solution)/shard_map/ppermute | solution.py:138
  137.2 9.1 %collective-permute-start.6 = (bf16[128,2048]{1,0:T(8,128)(2,1)S(1)}, bf16[128,2048]{1,0:T(8,128)(2,1)S(1)}, u32[]{:S(2)}, u32[]{:S(2)}) collective-permute-start(bf16[128,2048]{1,0:T(8,128)(2,1)S(1)} %collective-permute-done.2), channel_id=1, source_target_pairs={{0,1},{1,0},{2,3},{3,2},{4,5},{5,4},{6,7},{7,6},{8,9},{9,8},{10,11... | collective-permute-start | bytes 1572872 | tf_op jit(solution)/shard_map/ppermute | solution.py:78
  170.3 6.6 %collective-permute-done.45 = bf16[128,2048]{1,0:T(8,128)(2,1)} collective-permute-done((bf16[128,2048]{1,0:T(8,128)(2,1)}, bf16[128,2048]{1,0:T(8,128)(2,1)}, u32[]{:S(2)}, u32[]{:S(2)}) %collective-permute-start.45) | collective-permute-done | bytes 524320 | tf_op jit(solution)/shard_map/ppermute | solution.py:70
  183.6 6.7 %collective-permute-start.33 = (bf16[128,2048]{1,0:T(8,128)(2,1)S(1)}, bf16[128,2048]{1,0:T(8,128)(2,1)S(1)}, u32[]{:S(2)}, u32[]{:S(2)}) collective-permute-start(bf16[128,2048]{1,0:T(8,128)(2,1)S(1)} %get-tuple-element.41), channel_id=1, source_target_pairs={{0,32},{32,64},{64,96},{96,0},{1,33},{33,65},{65,97},{97,1},{2,34}... | collective-permute-start | bytes 1572872 | tf_op jit(solution)/shard_map/ppermute | solution.py:74
  203.1 11.8 %collective-permute-done.33 = bf16[128,2048]{1,0:T(8,128)(2,1)S(1)} collective-permute-done((bf16[128,2048]{1,0:T(8,128)(2,1)S(1)}, bf16[128,2048]{1,0:T(8,128)(2,1)S(1)}, u32[]{:S(2)}, u32[]{:S(2)}) %collective-permute-start.33) | collective-permute-done | bytes 524320 | tf_op jit(solution)/shard_map/ppermute | solution.py:74
  221.0 9.0 %collective-permute-done.36 = bf16[128,2048]{1,0:T(8,128)(2,1)S(1)} collective-permute-done((bf16[128,2048]{1,0:T(8,128)(2,1)S(1)}, bf16[128,2048]{1,0:T(8,128)(2,1)S(1)}, u32[]{:S(2)}, u32[]{:S(2)}) %collective-permute-start.36) | collective-permute-done | bytes 524320 | tf_op jit(solution)/shard_map/ppermute | solution.py:70
  235.4 8.2 %collective-permute-done.38 = bf16[128,2048]{1,0:T(8,128)(2,1)S(1)} collective-permute-done((bf16[128,2048]{1,0:T(8,128)(2,1)S(1)}, bf16[128,2048]{1,0:T(8,128)(2,1)S(1)}, u32[]{:S(2)}, u32[]{:S(2)}) %collective-permute-start.38) | collective-permute-done | bytes 524320 | tf_op jit(solution)/shard_map/ppermute | solution.py:70
  248.6 8.4 %fusion.8 = f32[1024,768]{0,1:T(8,128)} fusion(bf16[1024,2048]{1,0:T(8,128)(2,1)} %constant_dynamic-update-slice_fusion.8, bf16[2048,1536]{1,0:T(8,128)(2,1)} %bitcast.415), kind=kOutput, calls=%fused_computation.23 | convolution fusion | flops 3221225472 | bytes 10485760 | tf_op jit(solution)/shard_map/dot_general | solution.py:35
  257.0 7.4 %fusion.6 = f32[1024,768]{0,1:T(8,128)} fusion(bf16[1024,2048]{1,0:T(8,128)(2,1)} %constant_dynamic-update-slice_fusion.8, bf16[2048,1536]{1,0:T(8,128)(2,1)S(1)} %bitcast.418), kind=kOutput, calls=%fused_computation.21 | convolution fusion | flops 3221225472 | bytes 10485760 | tf_op jit(solution)/shard_map/dot_general | solution.py:35
  264.4 9.5 %multiply_convert_fusion = (bf16[1024,768]{0,1:T(8,128)(2,1)S(1)}, bf16[1024,768]{0,1:T(8,128)(2,1)S(1)}, bf16[1024,768]{0,1:T(8,128)(2,1)S(1)}) fusion(f32[1024,768]{0,1:T(8,128)} %fusion.8, f32[1024,768]{0,1:T(8,128)} %fusion.6, bf16[1024,2048]{1,0:T(8,128)(2,1)} %copy-done.37, bf16[768,2048]{1,0:T(8,128)(2,1)} %all-gather.5.cloned.1.call-done), kind=kOutput, calls=%fused_computation.25 | convolution fusion | flops 3233021952 | bytes 18350080 | tf_op jit(solution)/shard_map/dot_general | solution.py:39
  273.9 9.6 %convolution_convert_fusion.5 = bf16[512,2048]{1,0:T(8,128)(2,1)} fusion(bf16[2048,1536]{1,0:T(8,128)(2,1)} %bitcast.416, bf16[1024,768]{0,1:T(8,128)(2,1)S(1)} %get-tuple-element.27, bf16[1024,768]{0,1:T(8,128)(2,1)S(1)} %get-tuple-element.26), kind=kOutput, calls=%fused_computation.33 | convolution fusion | flops 3225419776 | bytes 11534336 | tf_op jit(solution)/shard_map/dot_general | solution.py:39
  287.4 11.7 %convolution_convert_fusion = bf16[2048,1536]{1,0:T(8,128)(2,1)S(1)} fusion(bf16[1024,2048]{1,0:T(8,128)(2,1)} %constant_dynamic-update-slice_fusion.8, bf16[1024,768]{0,1:T(8,128)(2,1)S(1)} %get-tuple-element.26, bf16[1024,768]{0,1:T(8,128)(2,1)S(1)} %get-tuple-element.27), kind=kOutput, calls=%fused_computation.6 | convolution fusion | flops 6451888128 | bytes 13631488 | tf_op jit(solution)/shard_map/dot_general | solution.py:43
  300.9 9.3 %fusion.183 = (bf16[512,2048]{1,0:T(8,128)(2,1)S(1)}, f32[512,2048]{1,0:T(8,128)}) fusion(bf16[512,2048]{1,0:T(8,128)(2,1)} %collective-permute-done.52, bf16[2048,1536]{1,0:T(8,128)(2,1)} %bitcast.417, bf16[1024,768]{0,1:T(8,128)(2,1)} %copy-done.59, bf16[1024,768]{0,1:T(8,128)(2,1)} %copy-done.58), kind=kOutput, calls=%fused_computation.474 | convolution fusion | flops 3227516928 | bytes 17825792 | tf_op jit(solution)/shard_map/dot_general | solution.py:39
  314.1 9.9 %maximum_maximum_fusion = bf16[16,192,1536]{2,1,0:T(8,128)(2,1)} fusion(bf16[16,16,512]{2,1,0:T(8,128)(2,1)S(1)} %get-tuple-element.30, bf16[16,16,512]{2,1,0:T(8,128)(2,1)S(1)} %get-tuple-element.31, bf16[16,16,512]{2,1,0:T(8,128)(2,1)S(1)} %get-tuple-element.29, bf16[16,48,1536]{2,1,0:T(8,128)(2,1)S(1)} %slice.748, bf16[16,128,1536]{2,1,0:T(8,128)(2,1)S(1)} %bitcast.363), kind=kLoop, calls=%fused_computation.1 | loop fusion | flops 47185920 | bytes 18874368 | tf_op jit(solution)/shard_map/concatenate | solution.py:300
  324.0 12.2 %collective-permute-done.55 = bf16[128,2048]{1,0:T(8,128)(2,1)} collective-permute-done((bf16[128,2048]{1,0:T(8,128)(2,1)}, bf16[128,2048]{1,0:T(8,128)(2,1)}, u32[]{:S(2)}, u32[]{:S(2)}) %collective-permute-start.55) | collective-permute-done | bytes 524320 | tf_op jit(solution)/shard_map/ppermute | solution.py:74
  367.9 6.8 %collective-permute-done.58 = bf16[128,2048]{1,0:T(8,128)(2,1)} collective-permute-done((bf16[128,2048]{1,0:T(8,128)(2,1)}, bf16[128,2048]{1,0:T(8,128)(2,1)}, u32[]{:S(2)}, u32[]{:S(2)}) %collective-permute-start.58) | collective-permute-done | bytes 524320 | tf_op jit(solution)/shard_map/ppermute | solution.py:70
  440.9 10.3 %collective-permute-done.71 = bf16[2,4,64,384]{3,2,1,0:T(8,128)(2,1)S(1)} collective-permute-done((bf16[2,4,64,384]{3,2,1,0:T(8,128)(2,1)S(1)}, bf16[2,4,64,384]{3,2,1,0:T(8,128)(2,1)S(1)}, u32[]{:S(2)}, u32[]{:S(2)}) %collective-permute-start.71) | collective-permute-done | bytes 393248 | tf_op jit(solution)/shard_map/ppermute | solution.py:147
  488.9 17.4 %collective-permute-done.68 = bf16[128,2048]{1,0:T(8,128)(2,1)S(1)} collective-permute-done((bf16[128,2048]{1,0:T(8,128)(2,1)S(1)}, bf16[128,2048]{1,0:T(8,128)(2,1)S(1)}, u32[]{:S(2)}, u32[]{:S(2)}) %collective-permute-start.68) | collective-permute-done | bytes 524320 | tf_op jit(solution)/shard_map/ppermute | solution.py:74
  511.4 14.2 %collective-permute-done.64 = bf16[128,2048]{1,0:T(8,128)(2,1)S(1)} collective-permute-done((bf16[128,2048]{1,0:T(8,128)(2,1)S(1)}, bf16[128,2048]{1,0:T(8,128)(2,1)S(1)}, u32[]{:S(2)}, u32[]{:S(2)}) %collective-permute-start.64) | collective-permute-done | bytes 524320 | tf_op jit(solution)/shard_map/ppermute | solution.py:74
  542.0 6.2 %collective-permute-done.94 = bf16[32,3072]{1,0:T(8,128)(2,1)S(1)} collective-permute-done((bf16[32,3072]{1,0:T(8,128)(2,1)S(1)}, bf16[32,3072]{1,0:T(8,128)(2,1)S(1)}, u32[]{:S(2)}, u32[]{:S(2)}) %collective-permute-start.94) | collective-permute-done | bytes 196640 | tf_op jit(solution)/shard_map/ppermute | solution.py:74
  (528 shorter events, 306.6 us)
Async XLA Ops:
  7.2 241.4 %all-gather.3.cloned.1.call-start = ((), (), s32[]{:S(2)}) async-start(), calls=%async_computation.1 | async-start | bytes 6684672 | tf_op jit(solution)/shard_map/all_gather | solution.py:250
  17.2 109.6 %collective-permute-start = (bf16[128,2048]{1,0:T(8,128)(2,1)}, bf16[128,2048]{1,0:T(8,128)(2,1)}, u32[]{:S(2)}, u32[]{:S(2)}) collective-permute-start(bf16[128,2048]{1,0:T(8,128)(2,1)} %get-tuple-element.23), channel_id=1, source_target_pairs={{0,96},{32,0},{64,32},{96,64},{1,97},{33,1},{65,33},{97,65},{2,98}... | collective-permute-start | bytes 1572872 | tf_op jit(solution)/shard_map/ppermute | solution.py:70
  24.7 104.0 %collective-permute-start.1 = (bf16[128,2048]{1,0:T(8,128)(2,1)}, bf16[128,2048]{1,0:T(8,128)(2,1)}, u32[]{:S(2)}, u32[]{:S(2)}) collective-permute-start(bf16[128,2048]{1,0:T(8,128)(2,1)} %get-tuple-element.23), channel_id=1, source_target_pairs={{0,64},{32,96},{64,0},{96,32},{1,65},{33,97},{65,1},{97,33},{2,66}... | collective-permute-start | bytes 1572872 | tf_op jit(solution)/shard_map/ppermute | solution.py:70
  51.2 213.2 %all-gather.5.cloned.1.call-start = ((), (), s32[]{:S(2)}) async-start(), calls=%async_computation.2 | async-start | bytes 3342336 | tf_op jit(solution)/shard_map/all_gather | solution.py:254
  51.3 79.7 %collective-permute-start.2 = (bf16[128,2048]{1,0:T(8,128)(2,1)}, bf16[128,2048]{1,0:T(8,128)(2,1)S(1)}, u32[]{:S(2)}, u32[]{:S(2)}) collective-permute-start(bf16[128,2048]{1,0:T(8,128)(2,1)} %get-tuple-element.23), channel_id=1, source_target_pairs={{0,32},{32,64},{64,96},{96,0},{1,33},{33,65},{65,97},{97,1},{2,34}... | collective-permute-start | bytes 1572872 | tf_op jit(solution)/shard_map/ppermute | solution.py:70
  51.7 85.4 %collective-permute-start.3 = (bf16[128,2048]{1,0:T(8,128)(2,1)}, bf16[128,2048]{1,0:T(8,128)(2,1)S(1)}, u32[]{:S(2)}, u32[]{:S(2)}) collective-permute-start(bf16[128,2048]{1,0:T(8,128)(2,1)} %get-tuple-element.23), channel_id=1, source_target_pairs={{0,1},{1,0},{2,3},{3,2},{4,5},{5,4},{6,7},{7,6},{8,9},{9,8},{10,11... | collective-permute-start | bytes 1572872 | tf_op jit(solution)/shard_map/ppermute | solution.py:78
  165.0 363.3 %reduce-scatter.2.cloned.1.call-start = ((), (), s32[]{:S(2)}) async-start(), calls=%async_computation.3 | async-start | bytes 10027008 | tf_op jit(solution)/shard_map/reduce_scatter | solution.py:302
  167.3 25.7 %collective-permute-start.47 = (bf16[128,2048]{1,0:T(8,128)(2,1)}, bf16[128,2048]{1,0:T(8,128)(2,1)S(1)}, u32[]{:S(2)}, u32[]{:S(2)}) collective-permute-start(bf16[128,2048]{1,0:T(8,128)(2,1)} %param.23), channel_id=1, source_target_pairs={{0,32},{32,64},{64,96},{96,0},{1,33},{33,65},{65,97},{97,1},{2,34}... | collective-permute-start | bytes 1572872 | tf_op jit(solution)/shard_map/ppermute | solution.py:70
  168.2 25.6 %collective-permute-start.48 = (bf16[128,2048]{1,0:T(8,128)(2,1)}, bf16[128,2048]{1,0:T(8,128)(2,1)S(1)}, u32[]{:S(2)}, u32[]{:S(2)}) collective-permute-start(bf16[128,2048]{1,0:T(8,128)(2,1)} %param.23), channel_id=1, source_target_pairs={{0,1},{1,0},{2,3},{3,2},{4,5},{5,4},{6,7},{7,6},{8,9},{9,8},{10,11... | collective-permute-start | bytes 1572872 | tf_op jit(solution)/shard_map/ppermute | solution.py:78
  183.6 31.3 %collective-permute-start.33 = (bf16[128,2048]{1,0:T(8,128)(2,1)S(1)}, bf16[128,2048]{1,0:T(8,128)(2,1)S(1)}, u32[]{:S(2)}, u32[]{:S(2)}) collective-permute-start(bf16[128,2048]{1,0:T(8,128)(2,1)S(1)} %get-tuple-element.41), channel_id=1, source_target_pairs={{0,32},{32,64},{64,96},{96,0},{1,33},{33,65},{65,97},{97,1},{2,34}... | collective-permute-start | bytes 1572872 | tf_op jit(solution)/shard_map/ppermute | solution.py:74
  193.0 23.9 %collective-permute-start.49 = (bf16[128,2048]{1,0:T(8,128)(2,1)}, bf16[128,2048]{1,0:T(8,128)(2,1)S(1)}, u32[]{:S(2)}, u32[]{:S(2)}) collective-permute-start(bf16[128,2048]{1,0:T(8,128)(2,1)} %collective-permute-done.45), channel_id=1, source_target_pairs={{0,1},{1,0},{2,3},{3,2},{4,5},{5,4},{6,7},{7,6},{8,9},{9,8},{10,11... | collective-permute-start | bytes 1572872 | tf_op jit(solution)/shard_map/ppermute | solution.py:78
  193.7 25.1 %collective-permute-start.50 = (bf16[128,2048]{1,0:T(8,128)(2,1)S(1)}, bf16[128,2048]{1,0:T(8,128)(2,1)S(1)}, u32[]{:S(2)}, u32[]{:S(2)}) collective-permute-start(bf16[128,2048]{1,0:T(8,128)(2,1)S(1)} %collective-permute-done.46), channel_id=1, source_target_pairs={{0,1},{1,0},{2,3},{3,2},{4,5},{5,4},{6,7},{7,6},{8,9},{9,8},{10,11... | collective-permute-start | bytes 1572872 | tf_op jit(solution)/shard_map/ppermute | solution.py:78
  218.9 24.8 %collective-permute-start.38 = (bf16[128,2048]{1,0:T(8,128)(2,1)S(1)}, bf16[128,2048]{1,0:T(8,128)(2,1)S(1)}, u32[]{:S(2)}, u32[]{:S(2)}) collective-permute-start(bf16[128,2048]{1,0:T(8,128)(2,1)S(1)} %get-tuple-element.19), channel_id=1, source_target_pairs={{0,32},{32,64},{64,96},{96,0},{1,33},{33,65},{65,97},{97,1},{2,34}... | collective-permute-start | bytes 1572872 | tf_op jit(solution)/shard_map/ppermute | solution.py:70
  219.3 25.8 %collective-permute-start.39 = (bf16[128,2048]{1,0:T(8,128)(2,1)S(1)}, bf16[128,2048]{1,0:T(8,128)(2,1)S(1)}, u32[]{:S(2)}, u32[]{:S(2)}) collective-permute-start(bf16[128,2048]{1,0:T(8,128)(2,1)S(1)} %get-tuple-element.19), channel_id=1, source_target_pairs={{0,1},{1,0},{2,3},{3,2},{4,5},{5,4},{6,7},{7,6},{8,9},{9,8},{10,11... | collective-permute-start | bytes 1572872 | tf_op jit(solution)/shard_map/ppermute | solution.py:78
  311.4 24.8 %collective-permute-start.55 = (bf16[128,2048]{1,0:T(8,128)(2,1)}, bf16[128,2048]{1,0:T(8,128)(2,1)}, u32[]{:S(2)}, u32[]{:S(2)}) collective-permute-start(bf16[128,2048]{1,0:T(8,128)(2,1)} %get-tuple-element.39), channel_id=1, source_target_pairs={{0,96},{32,0},{64,32},{96,64},{1,97},{33,1},{65,33},{97,65},{2,98}... | collective-permute-start | bytes 1572872 | tf_op jit(solution)/shard_map/ppermute | solution.py:74
  313.5 26.3 %collective-permute-start.53 = (bf16[128,2048]{1,0:T(8,128)(2,1)}, bf16[128,2048]{1,0:T(8,128)(2,1)}, u32[]{:S(2)}, u32[]{:S(2)}) collective-permute-start(bf16[128,2048]{1,0:T(8,128)(2,1)} %get-tuple-element.38), channel_id=1, source_target_pairs={{0,32},{32,64},{64,96},{96,0},{1,33},{33,65},{65,97},{97,1},{2,34}... | collective-permute-start | bytes 1572872 | tf_op jit(solution)/shard_map/ppermute | solution.py:74
  348.2 26.6 %collective-permute-start.58 = (bf16[128,2048]{1,0:T(8,128)(2,1)}, bf16[128,2048]{1,0:T(8,128)(2,1)}, u32[]{:S(2)}, u32[]{:S(2)}) collective-permute-start(bf16[128,2048]{1,0:T(8,128)(2,1)} %get-tuple-element.16), channel_id=1, source_target_pairs={{0,32},{32,64},{64,96},{96,0},{1,33},{33,65},{65,97},{97,1},{2,34}... | collective-permute-start | bytes 1572872 | tf_op jit(solution)/shard_map/ppermute | solution.py:70
  353.1 24.0 %collective-permute-start.59 = (bf16[128,2048]{1,0:T(8,128)(2,1)}, bf16[128,2048]{1,0:T(8,128)(2,1)S(1)}, u32[]{:S(2)}, u32[]{:S(2)}) collective-permute-start(bf16[128,2048]{1,0:T(8,128)(2,1)} %get-tuple-element.16), channel_id=1, source_target_pairs={{0,1},{1,0},{2,3},{3,2},{4,5},{5,4},{6,7},{7,6},{8,9},{9,8},{10,11... | collective-permute-start | bytes 1572872 | tf_op jit(solution)/shard_map/ppermute | solution.py:78
  383.7 93.7 %collective-permute-start.63 = (bf16[512,2048]{1,0:T(8,128)(2,1)}, bf16[512,2048]{1,0:T(8,128)(2,1)}, u32[]{:S(2)}, u32[]{:S(2)}) collective-permute-start(bf16[512,2048]{1,0:T(8,128)(2,1)} %convolution_convert_fusion.4), channel_id=1, source_target_pairs={{0,1},{1,0},{2,3},{3,2},{4,5},{5,4},{6,7},{7,6},{8,9},{9,8},{10,11... | collective-permute-start | bytes 6291464 | tf_op jit(solution)/shard_map/ppermute | solution.py:78
  405.0 68.9 %collective-permute-start.67 = (bf16[512,2048]{1,0:T(8,128)(2,1)S(1)}, bf16[512,2048]{1,0:T(8,128)(2,1)S(1)}, u32[]{:S(2)}, u32[]{:S(2)}) collective-permute-start(bf16[512,2048]{1,0:T(8,128)(2,1)S(1)} %convolution_convert_fusion.3), channel_id=1, source_target_pairs={{0,1},{1,0},{2,3},{3,2},{4,5},{5,4},{6,7},{7,6},{8,9},{9,8},{10,11... | collective-permute-start | bytes 6291464 | tf_op jit(solution)/shard_map/ppermute | solution.py:78
  477.2 29.2 %collective-permute-start.68 = (bf16[128,2048]{1,0:T(8,128)(2,1)S(1)}, bf16[128,2048]{1,0:T(8,128)(2,1)S(1)}, u32[]{:S(2)}, u32[]{:S(2)}) collective-permute-start(bf16[128,2048]{1,0:T(8,128)(2,1)S(1)} %get-tuple-element.32), channel_id=1, source_target_pairs={{0,32},{32,64},{64,96},{96,0},{1,33},{33,65},{65,97},{97,1},{2,34}... | collective-permute-start | bytes 1572872 | tf_op jit(solution)/shard_map/ppermute | solution.py:74
  481.0 27.8 %collective-permute-start.66 = (bf16[128,2048]{1,0:T(8,128)(2,1)S(1)}, bf16[128,2048]{1,0:T(8,128)(2,1)S(1)}, u32[]{:S(2)}, u32[]{:S(2)}) collective-permute-start(bf16[128,2048]{1,0:T(8,128)(2,1)S(1)} %get-tuple-element.36), channel_id=1, source_target_pairs={{0,96},{32,0},{64,32},{96,64},{1,97},{33,1},{65,33},{97,65},{2,98}... | collective-permute-start | bytes 1572872 | tf_op jit(solution)/shard_map/ppermute | solution.py:74
  483.6 27.8 %collective-permute-start.65 = (bf16[128,2048]{1,0:T(8,128)(2,1)S(1)}, bf16[128,2048]{1,0:T(8,128)(2,1)S(1)}, u32[]{:S(2)}, u32[]{:S(2)}) collective-permute-start(bf16[128,2048]{1,0:T(8,128)(2,1)S(1)} %get-tuple-element.37), channel_id=1, source_target_pairs={{0,64},{32,96},{64,0},{96,32},{1,65},{33,97},{65,1},{97,33},{2,66}... | collective-permute-start | bytes 1572872 | tf_op jit(solution)/shard_map/ppermute | solution.py:74
  486.3 39.3 %collective-permute-start.64 = (bf16[128,2048]{1,0:T(8,128)(2,1)S(1)}, bf16[128,2048]{1,0:T(8,128)(2,1)S(1)}, u32[]{:S(2)}, u32[]{:S(2)}) collective-permute-start(bf16[128,2048]{1,0:T(8,128)(2,1)S(1)} %get-tuple-element.35), channel_id=1, source_target_pairs={{0,32},{32,64},{64,96},{96,0},{1,33},{33,65},{65,97},{97,1},{2,34}... | collective-permute-start | bytes 1572872 | tf_op jit(solution)/shard_map/ppermute | solution.py:74
  (136 other events, 1501.8 us)
Sparse Core Ops, SparseCore 0:
  51.3 76.3 all-gather.2
  165.1 45.4 all-gather.4
  324.1 87.1 reduce-scatter.1

commit v3 on v2

--- a/solution.py
+++ b/solution.py
@@ -1,16 +1,15 @@
 import jax
 import jax.numpy as jnp
+import ml_dtypes
+import numpy as np
 from jax import lax
+from jax.experimental import pallas as pl
+from jax.experimental.pallas import tpu as pltpu
 from jax.sharding import Mesh, PartitionSpec as P
 
 D = 2048
-HEADS = 32
-KV_HEADS = 4
 HDIM = 64
-FF = 5632
 CAP = 128
-TP = 8
-LOCAL_HEADS = HEADS // TP
 WIDE = 768
 BF16 = jnp.bfloat16
 F32 = jnp.float32
@@ -21,14 +20,526 @@
 SWAP = [(0, 1), (1, 0)]
 
 
-def turn(u):
-    half = u.shape[-1] // 2
-    return jnp.concatenate([-u[..., half:], u[..., :half]], axis=-1)
-
-
-def turn_back(u):
-    half = u.shape[-1] // 2
-    return jnp.concatenate([u[..., half:], -u[..., :half]], axis=-1)
+def dot_nn(left, right):
+    return lax.dot_general(left, right, (((1,), (0,)), ((), ())), preferred_element_type=F32)
+
+
+def dot_nt(left, right):
+    return lax.dot_general(left, right, (((1,), (1,)), ((), ())), preferred_element_type=F32)
+
+
+def dot_tn(left, right):
+    return lax.dot_general(left, right, (((0,), (0,)), ((), ())), preferred_element_type=F32)
+
+
+ANY = pl.BlockSpec(memory_space=pl.ANY)
+
+
+def part_copies(parts, whole, sems):
+    copies, start = [], 0
+    for k, part in enumerate(parts):
+        rows = min(part.shape[0] // CAP, 2) * CAP
+        copies.append(
+            pltpu.make_async_copy(part.at[pl.ds(0, rows)], whole.at[pl.ds(start, rows)], sems.at[k])
+        )
+        start += rows
+    return copies
+
+
+def feed_copies(packed, feed, sems):
+    copies = []
+    for k in range(16):
+        for h in range(2):
+            copies.append(
+                pltpu.make_async_copy(
+                    packed.at[pl.ds(192 * k + 64 * h, 64)],
+                    feed.at[pl.ds(1024 * h + 64 * k, 64)],
+                    sems.at[2 * k + h],
+                )
+            )
+    return copies
+
+
+def down_copies(packed, down, sems):
+    copies = []
+    for k in range(16):
+        copies.append(
+            pltpu.make_async_copy(
+                packed.at[pl.ds(192 * k + 128, 48)],
+                down.at[pl.ds(48 * k, 48), pl.ds(0, 1536)],
+                sems.at[4 * k],
+            )
+        )
+        for h in range(3):
+            copies.append(
+                pltpu.make_async_copy(
+                    packed.at[pl.ds(192 * k + 176, 16), pl.ds(512 * h, 512)],
+                    down.at[pl.ds(48 * k + 16 * h, 16), pl.ds(1536, 512)],
+                    sems.at[4 * k + 1 + h],
+                )
+            )
+    return copies
+
+
+def feed_kernel(*refs):
+    x_parts, c_parts, packed = refs[:7], refs[7:14], refs[14]
+    hidden, grads, far, near = refs[15:19]
+    x, c, feed, down, x_sems, c_sems, f_sems, d_sems = refs[19:]
+    step = pl.program_id(0)
+
+    @pl.when(step == 0)
+    def _():
+        first = part_copies(x_parts, x, x_sems)
+        second = feed_copies(packed, feed, f_sems)
+        third = part_copies(c_parts, c, c_sems)
+        fourth = down_copies(packed, down, d_sems)
+        for group in (first, second, third, fourth):
+            for copy in group:
+                copy.start()
+        for copy in first + second:
+            copy.wait()
+
+    rows = pl.ds(pl.multiple_of(((step + 2) % 4) * 256, 256), 256)
+    block = x[rows, :]
+    gate = dot_nn(block, feed[:, :WIDE])
+    up = dot_nn(block, feed[:, WIDE:])
+
+    @pl.when(step == 0)
+    def _():
+        third = part_copies(c_parts, c, c_sems)
+        fourth = down_copies(packed, down, d_sems)
+        for copy in third + fourth:
+            copy.wait()
+
+    back = dot_nt(c[rows, :], down[...])
+    sig = jax.nn.sigmoid(gate)
+    silu = gate * sig
+    hidden[...] = (silu * up).astype(BF16)
+    grad_gate = (back * up * (sig * (1.0 + gate * (1.0 - sig)))).astype(BF16)
+    grad_up = (back * silu).astype(BF16)
+    grads[:, :WIDE] = grad_gate
+    grads[:, WIDE:] = grad_up
+    inner = dot_nt(grads[...], feed[...])
+
+    @pl.when(step < 2)
+    def _():
+        far[...] = inner.astype(BF16)
+
+    @pl.when(step >= 2)
+    def _():
+        near[...] = inner
+
+
+def feed_forward(x_parts, c_parts, packed):
+    row = lambda i: ((i + 2) % 4, 0)
+    return pl.pallas_call(
+        feed_kernel,
+        grid=(4,),
+        in_specs=[ANY] * 15,
+        out_specs=[
+            pl.BlockSpec((256, WIDE), row),
+            pl.BlockSpec((256, 2 * WIDE), row),
+            pl.BlockSpec((256, D), lambda i: (jnp.minimum(i, 1), 0)),
+            pl.BlockSpec((256, D), lambda i: (jnp.maximum(i - 2, 0), 0)),
+        ],
+        out_shape=[
+            jax.ShapeDtypeStruct((1024, WIDE), BF16),
+            jax.ShapeDtypeStruct((1024, 2 * WIDE), BF16),
+            jax.ShapeDtypeStruct((512, D), BF16),
+            jax.ShapeDtypeStruct((512, D), F32),
+        ],
+        scratch_shapes=[
+            pltpu.VMEM((1024, D), BF16),
+            pltpu.VMEM((1024, D), BF16),
+            pltpu.VMEM((D, 2 * WIDE), BF16),
+            pltpu.VMEM((WIDE, D), BF16),
+            pltpu.SemaphoreType.DMA((7,)),
+            pltpu.SemaphoreType.DMA((7,)),
+            pltpu.SemaphoreType.DMA((32,)),
+            pltpu.SemaphoreType.DMA((64,)),
+        ],
+        compiler_params=pltpu.CompilerParams(vmem_limit_bytes=50 * 1024 * 1024),
+        cost_estimate=pl.CostEstimate(
+            flops=2 * 1024 * D * WIDE * 5, bytes_accessed=28 * 2**20, transcendentals=1024 * WIDE
+        ),
+    )(*x_parts, *c_parts, packed)
+
+
+def grads_kernel(*refs):
+    x_parts, c_parts, hidden_hbm, grads_hbm = refs[:7], refs[7:14], refs[14], refs[15]
+    out = refs[16]
+    x, c, hidden, grads, pack, x_sems, c_sems, in_sems, sems = refs[17:]
+    first = part_copies(x_parts, x, x_sems)
+    second = part_copies(c_parts, c, c_sems)
+    loads = [
+        pltpu.make_async_copy(grads_hbm, grads, in_sems.at[0]),
+        pltpu.make_async_copy(hidden_hbm, hidden, in_sems.at[1]),
+    ]
+    for copy in first + loads + second:
+        copy.start()
+    for copy in first + loads[:1]:
+        copy.wait()
+    stores = []
+
+    def store(row, rows):
+        copy = pltpu.make_async_copy(
+            pack.at[pl.ds(row, rows)], out.at[pl.ds(row, rows)], sems.at[len(stores)]
+        )
+        copy.start()
+        stores.append(copy)
+
+    for k in range(8):
+        tile = dot_tn(x[:, 256 * k : 256 * (k + 1)], grads[...]).astype(BF16)
+        half, spot = k // 4, (k % 4) * 4
+        for j in range(4):
+            row = 192 * (spot + j) + 64 * half
+            pack[row : row + 64, :] = tile[64 * j : 64 * (j + 1)]
+            store(row, 64)
+    for copy in second + loads[1:]:
+        copy.wait()
+    for k in range(2):
+        tile = dot_tn(hidden[:, 384 * k : 384 * (k + 1)], c[...]).astype(BF16)
+        for j in range(8):
+            row = 192 * (8 * k + j) + 128
+            piece = tile[48 * j : 48 * (j + 1)]
+            pack[row : row + 48, :] = piece[:, :1536]
+            for h in range(3):
+                pack[row + 48 : row + 64, 512 * h : 512 * (h + 1)] = piece[
+                    16 * h : 16 * (h + 1), 1536:
+                ]
+            store(row, 64)
+    for copy in stores:
+        copy.wait()
+
+
+def feed_grads(x_parts, c_parts, hidden, grads):
+    return pl.pallas_call(
+        grads_kernel,
+        in_specs=[ANY] * 16,
+        out_specs=ANY,
+        out_shape=jax.ShapeDtypeStruct((3072, 1536), BF16),
+        scratch_shapes=[
+            pltpu.VMEM((1024, D), BF16),
+            pltpu.VMEM((1024, D), BF16),
+            pltpu.VMEM((1024, WIDE), BF16),
+            pltpu.VMEM((1024, 2 * WIDE), BF16),
+            pltpu.VMEM((3072, 2 * WIDE), BF16),
+            pltpu.SemaphoreType.DMA((7,)),
+            pltpu.SemaphoreType.DMA((7,)),
+            pltpu.SemaphoreType.DMA((2,)),
+            pltpu.SemaphoreType.DMA((48,)),
+        ],
+        compiler_params=pltpu.CompilerParams(vmem_limit_bytes=50 * 1024 * 1024),
+        cost_estimate=pl.CostEstimate(
+            flops=2 * 1024 * D * WIDE * 3, bytes_accessed=22 * 2**20, transcendentals=0
+        ),
+    )(*x_parts, *c_parts, hidden, grads)
+
+
+def rotary_table():
+    place = np.arange(CAP, dtype=np.float32)[:, None]
+    inverse = np.float32(10000.0) ** (np.arange(32, dtype=np.float32) * np.float32(-2.0 / HDIM))
+    angle = (place * inverse).astype(np.float32)
+    cosine, sine = np.cos(angle), np.sin(angle)
+    zero, one = np.zeros((CAP, 64), np.float32), np.ones((CAP, 64), np.float32)
+    straight = np.concatenate([cosine, cosine] * 5 + [one], axis=1)
+    down = np.concatenate([-sine, zero[:, :32]] * 5 + [zero], axis=1)
+    up = np.concatenate([zero[:, :32], sine] * 5 + [zero], axis=1)
+    table = np.concatenate([straight, down, up], axis=1)
+    high = table.astype(ml_dtypes.bfloat16)
+    rest = (table - high.astype(np.float32)).astype(ml_dtypes.bfloat16)
+    return jnp.asarray(np.stack([high, rest]))
+
+
+def id_copies(parts, ids, sems):
+    copies, spot = [], 0
+    for k, part in enumerate(parts):
+        for j in range(part.shape[0] // 144):
+            copies.append(
+                pltpu.make_async_copy(
+                    part.at[pl.ds(144 * j + CAP, 16), pl.ds(0, CAP)], ids.at[spot], sems.at[spot]
+                )
+            )
+            spot += 1
+    return copies
+
+
+def long_copies(parts, whole, sems):
+    copies, spot = [], 0
+    for part in parts:
+        for j in range(part.shape[0] // 144):
+            copies.append(
+                pltpu.make_async_copy(
+                    part.at[pl.ds(144 * j, CAP)], whole.at[pl.ds(CAP * spot, CAP)], sems.at[spot]
+                )
+            )
+            spot += 1
+    return copies
+
+
+def lane_of(shape, dim):
+    return lax.broadcasted_iota(jnp.int32, shape, dim)
+
+
+def block_tables(ids, table):
+    row = jnp.broadcast_to(ids.astype(F32)[:1], (CAP, CAP))
+    same = row == row.T
+    to, frm = lane_of((CAP, CAP), 0), lane_of((CAP, CAP), 1)
+    place = jnp.sum(jnp.where(same & (frm < to), 1.0, 0.0), axis=1, keepdims=True)
+    chosen = (frm.astype(F32) == place).astype(BF16)
+    factors = dot_nn(chosen, table[0]) + dot_nn(chosen, table[1])
+    return same & (frm <= to), factors
+
+
+def turned(item, factors, sign):
+    other = (
+        pltpu.roll(item, 352, 1) * factors[:, 384:768] + pltpu.roll(item, 32, 1) * factors[:, 768:]
+    )
+    return item * factors[:, :384] + sign * other
+
+
+def stack_heads(item):
+    head = lane_of((CAP, 256), 1) // 64
+    return jnp.concatenate([jnp.where(head == h, item, 0).astype(BF16) for h in range(4)], axis=0)
+
+
+def spreads():
+    lane, own = lane_of((CAP, 256), 1) % 64, lane_of((CAP, 256), 0)
+    return (lane == own).astype(BF16), (lane + 64 == own).astype(BF16)
+
+
+def softmax_heads(queries, keys, allowed):
+    scores = dot_nt(stack_heads(queries), keys) * 0.125
+    out = []
+    for h in range(4):
+        part = jnp.where(allowed, scores[CAP * h : CAP * (h + 1)], -1e30)
+        expo = jnp.exp(part - jnp.max(part, axis=1, keepdims=True))
+        out.append(expo / jnp.sum(expo, axis=1, keepdims=True))
+    return out
+
+
+def attend_kernel(*refs):
+    parts, table, w_hbm, o_hbm = refs[:7], refs[7], refs[8], refs[9]
+    queries, key_values, mixed, far, near = refs[10:15]
+    x, ids, w, o, x_sems, i_sems, w_sems = refs[15:]
+    step = pl.program_id(0)
+    loads = [
+        pltpu.make_async_copy(w_hbm, w, w_sems.at[0]),
+        pltpu.make_async_copy(o_hbm, o, w_sems.at[1]),
+    ]
+
+    @pl.when(step == 0)
+    def _():
+        copies = long_copies(parts, x, x_sems) + id_copies(parts, ids, i_sems) + loads
+        for copy in copies:
+            copy.start()
+        for copy in copies:
+            copy.wait()
+
+    half = 1 - step
+    rows = pl.ds(pl.multiple_of(half * 512, 512), 512)
+    qkv = dot_nn(x[rows, :], w[...])
+    to_key, to_value = spreads()
+    for k in range(4):
+        allowed, factors = block_tables(ids[half * 4 + k], table)
+        block = turned(qkv[CAP * k : CAP * (k + 1)], factors, 1.0).astype(BF16)
+        here = slice(CAP * k, CAP * (k + 1))
+        queries[here, :] = block[:, :256]
+        key_values[here, :] = block[:, 256:]
+        keys = dot_nn(block[:, 256:], to_key).astype(BF16)
+        values = dot_nn(block[:, 256:], to_value).astype(BF16)
+        probs = softmax_heads(block[:, :256], keys, allowed)
+        probs = jnp.concatenate([item.astype(BF16) for item in probs], axis=1)
+        mixed[here, :] = dot_nn(probs, stack_heads(values)).astype(BF16)
+    total = dot_nn(mixed[...], o[...])
+
+    @pl.when(step == 0)
+    def _():
+        far[...] = total.astype(BF16)
+
+    @pl.when(step == 1)
+    def _():
+        near[...] = total
+
+
+def attend(parts, table, qkv_full, out_full):
+    row = lambda i: (1 - i, 0)
+    still = lambda i: (0, 0)
+    return pl.pallas_call(
+        attend_kernel,
+        grid=(2,),
+        in_specs=[ANY] * 7 + [pl.BlockSpec((2, CAP, 1152), lambda i: (0, 0, 0))] + [ANY] * 2,
+        out_specs=[
+            pl.BlockSpec((512, 256), row),
+            pl.BlockSpec((512, CAP), row),
+            pl.BlockSpec((512, 256), row),
+            pl.BlockSpec((512, D), still),
+            pl.BlockSpec((512, D), still),
+        ],
+        out_shape=[
+            jax.ShapeDtypeStruct((1024, 256), BF16),
+            jax.ShapeDtypeStruct((1024, CAP), BF16),
+            jax.ShapeDtypeStruct((1024, 256), BF16),
+            jax.ShapeDtypeStruct((512, D), BF16),
+            jax.ShapeDtypeStruct((512, D), F32),
+        ],
+        scratch_shapes=[
+            pltpu.VMEM((1024, D), BF16),
+            pltpu.VMEM((8, 16, CAP), BF16),
+            pltpu.VMEM((D, 384), BF16),
+            pltpu.VMEM((256, D), BF16),
+            pltpu.SemaphoreType.DMA((8,)),
+            pltpu.SemaphoreType.DMA((8,)),
+            pltpu.SemaphoreType.DMA((2,)),
+        ],
+        compiler_params=pltpu.CompilerParams(vmem_limit_bytes=40 * 1024 * 1024),
+        cost_estimate=pl.CostEstimate(
+            flops=2 * 1024 * D * 640 * 2, bytes_accessed=15 * 2**20, transcendentals=2**19
+        ),
+    )(*parts, table, qkv_full, out_full)
+
+
+def attend_back_kernel(*refs):
+    parts, id_parts, table, w_hbm, o_hbm, queries, key_values = (
+        refs[:7],
+        refs[7:14],
+        refs[14],
+        refs[15],
+        refs[16],
+        refs[17],
+        refs[18],
+    )
+    grads, far, near = refs[19:22]
+    g, ids, w, o, g_sems, i_sems, w_sems = refs[22:]
+    step = pl.program_id(0)
+    loads = [
+        pltpu.make_async_copy(w_hbm, w, w_sems.at[0]),
+        pltpu.make_async_copy(o_hbm, o, w_sems.at[1]),
+    ]
+
+    @pl.when(step == 0)
+    def _():
+        copies = part_copies(parts, g, g_sems) + id_copies(id_parts, ids, i_sems) + loads
+        for copy in copies:
+            copy.start()
+        for copy in copies:
+            copy.wait()
+
+    half = 1 - step
+    rows = pl.ds(pl.multiple_of(half * 512, 512), 512)
+    grad_mixed = dot_nt(g[rows, :], o[...]).astype(BF16)
+    to_key, to_value = spreads()
+    for k in range(4):
+        allowed, factors = block_tables(ids[half * 4 + k], table)
+        here = slice(CAP * k, CAP * (k + 1))
+        query, both = queries[here, :], key_values[here, :]
+        keys = dot_nn(both, to_key).astype(BF16)
+        values = dot_nn(both, to_value).astype(BF16)
+        probs = softmax_heads(query, keys, allowed)
+        grad_heads = stack_heads(grad_mixed[here])
+        grad_probs = dot_nt(grad_heads, values)
+        scores = []
+        for h in range(4):
+            part = grad_probs[CAP * h : CAP * (h + 1)]
+            delta = jnp.sum(probs[h] * part, axis=1, keepdims=True)
+            scores.append((probs[h] * (part - delta)).astype(BF16))
+        grad_query = dot_nn(jnp.concatenate(scores, axis=1), stack_heads(keys)) * 0.125
+        folded = dot_nt(stack_heads(query), to_key).astype(BF16)
+        grad_folded = dot_nt(grad_heads, to_value).astype(BF16)
+        low = jnp.concatenate([item.astype(BF16) for item in probs], axis=0)
+        grad_both = dot_tn(jnp.concatenate(scores, axis=0), folded) * 0.125 + dot_tn(low, grad_folded)
+        item = jnp.concatenate([grad_query, grad_both], axis=1)
+        grads[here, :] = turned(item, factors, -1.0).astype(BF16)
+    total = dot_nt(grads[...], w[...])
+
+    @pl.when(step == 0)
+    def _():
+        far[...] = total.astype(BF16)
+
+    @pl.when(step == 1)
+    def _():
+        near[...] = total
+
+
+def attend_back(parts, id_parts, table, qkv_full, out_full, queries, key_values):
+    row = lambda i: (1 - i, 0)
+    still = lambda i: (0, 0)
+    return pl.pallas_call(
+        attend_back_kernel,
+        grid=(2,),
+        in_specs=[ANY] * 14
+        + [pl.BlockSpec((2, CAP, 1152), lambda i: (0, 0, 0))]
+        + [ANY] * 2
+        + [pl.BlockSpec((512, 256), row), pl.BlockSpec((512, CAP), row)],
+        out_specs=[
+            pl.BlockSpec((512, 384), row),
+            pl.BlockSpec((512, D), still),
+            pl.BlockSpec((512, D), still),
+        ],
+        out_shape=[
+            jax.ShapeDtypeStruct((1024, 384), BF16),
+            jax.ShapeDtypeStruct((512, D), BF16),
+            jax.ShapeDtypeStruct((512, D), F32),
+        ],
+        scratch_shapes=[
+            pltpu.VMEM((1024, D), BF16),
+            pltpu.VMEM((8, 16, CAP), BF16),
+            pltpu.VMEM((D, 384), BF16),
+            pltpu.VMEM((256, D), BF16),
+            pltpu.SemaphoreType.DMA((7,)),
+            pltpu.SemaphoreType.DMA((8,)),
+            pltpu.SemaphoreType.DMA((2,)),
+        ],
+        compiler_params=pltpu.CompilerParams(vmem_limit_bytes=40 * 1024 * 1024),
+        cost_estimate=pl.CostEstimate(
+            flops=2 * 1024 * D * 640 * 2, bytes_accessed=15 * 2**20, transcendentals=2**19
+        ),
+    )(*parts, *id_parts, table, qkv_full, out_full, queries, key_values)
+
+
+def small_grads_kernel(*refs):
+    x_parts, g_parts, mixed_hbm, grads_hbm = refs[:7], refs[7:14], refs[14], refs[15]
+    qkv_term, out_term = refs[16:18]
+    x, g, mixed, grads, x_sems, g_sems, in_sems = refs[18:]
+    first = long_copies(x_parts, x, x_sems)
+    second = part_copies(g_parts, g, g_sems)
+    loads = [
+        pltpu.make_async_copy(grads_hbm, grads, in_sems.at[0]),
+        pltpu.make_async_copy(mixed_hbm, mixed, in_sems.at[1]),
+    ]
+    for copy in first + loads + second:
+        copy.start()
+    for copy in first + loads[:1]:
+        copy.wait()
+    for k in range(8):
+        here = slice(256 * k, 256 * (k + 1))
+        qkv_term[here, :] = dot_tn(x[:, here], grads[...]).astype(BF16)
+    for copy in second + loads[1:]:
+        copy.wait()
+    out_term[...] = dot_tn(mixed[...], g[...]).astype(BF16)
+
+
+def small_grads(x_parts, g_parts, mixed, grads):
+    whole = pl.BlockSpec(memory_space=pltpu.VMEM)
+    return pl.pallas_call(
+        small_grads_kernel,
+        in_specs=[ANY] * 16,
+        out_specs=[whole, whole],
+        out_shape=[jax.ShapeDtypeStruct((D, 384), BF16), jax.ShapeDtypeStruct((256, D), BF16)],
+        scratch_shapes=[
+            pltpu.VMEM((1024, D), BF16),
+            pltpu.VMEM((1024, D), BF16),
+            pltpu.VMEM((1024, 256), BF16),
+            pltpu.VMEM((1024, 384), BF16),
+            pltpu.SemaphoreType.DMA((8,)),
+            pltpu.SemaphoreType.DMA((7,)),
+            pltpu.SemaphoreType.DMA((2,)),
+        ],
+        compiler_params=pltpu.CompilerParams(vmem_limit_bytes=40 * 1024 * 1024),
+        cost_estimate=pl.CostEstimate(
+            flops=2 * 1024 * D * 640, bytes_accessed=12 * 2**20, transcendentals=0
+        ),
+    )(*x_parts, *g_parts, mixed, grads)
 
 
 def times(left, right):
@@ -53,19 +564,6 @@
     )
 
 
-def rotary(ids):
-    order = jnp.arange(CAP)
-    same = ids[:, :, None] == ids[:, None, :]
-    earlier = order[None, :] < order[:, None]
-    place = jnp.sum(jnp.where(same & earlier[None], 1.0, 0.0), axis=2).astype(F32)
-    half = HDIM // 2
-    inverse = 10000.0 ** (jnp.arange(half, dtype=F32) * (-2.0 / HDIM))
-    angle = place[..., None] * inverse
-    angle = jnp.concatenate([angle, angle], axis=-1)
-    allowed = same & (order[None, :] <= order[:, None])[None]
-    return jnp.cos(angle), jnp.sin(angle), allowed
-
-
 def from_ring(item, step):
     return lax.ppermute(item, RING, [(i, (i - step) % 4) for i in range(4)])
 
@@ -78,18 +576,28 @@
     return lax.ppermute(item, axis, SWAP)
 
 
-def share(item):
-    mine = [item] + [from_ring(item, step) for step in (1, 2, 3)]
-    return jnp.concatenate(mine + [swap(part, "c") for part in mine], axis=0)
-
-
-def collect(left, right, product):
-    far = product(left[4 * CAP :], right).astype(BF16)
-    near = product(left[: 4 * CAP], right)
-    near = near + swap(far, "c").astype(F32)
+STEPS = (0, 1, 3, 2)
+
+
+def share_parts(item):
+    one, three, two = (from_ring(item, step) for step in (1, 3, 2))
+    own = swap(item, "c")
+    near = swap(jnp.concatenate([one, three], axis=0), "c")
+    far = swap(two, "c")
+    return [item, one, three, two, own, near, far]
+
+
+def pair_sum(far, near):
+    return near + swap(far, "c").astype(F32)
+
+
+def ring_sum(near):
     total = near[:CAP]
-    for step in (1, 2, 3):
-        total = total + to_ring(near[step * CAP : (step + 1) * CAP].astype(BF16), step).astype(F32)
+    sent = [
+        to_ring(near[spot * CAP : (spot + 1) * CAP].astype(BF16), STEPS[spot]) for spot in (1, 2, 3)
+    ]
+    for item in sent:
+        total = total + item.astype(F32)
     return total
 
 
@@ -131,12 +639,16 @@
 
 
 def gather_four(item, axis, spot, dim):
-    shape = item.shape[:dim] + (4,) + item.shape[dim:]
-    out = jnp.zeros(shape, item.dtype)
-    out = lax.dynamic_update_index_in_dim(out, item, spot, dim)
+    parts = [item]
     for step in (1, 2, 3):
-        came = lax.ppermute(item, axis, [(i, (i - step) % 4) for i in range(4)])
-        out = lax.dynamic_update_index_in_dim(out, came, (spot + step) % 4, dim)
+        parts.append(lax.ppermute(item, axis, [(i, (i - step) % 4) for i in range(4)]))
+    return jnp.stack([pick(parts, (q - spot) % 4) for q in range(4)], axis=dim)
+
+
+def pick(parts, which):
+    out = parts[0]
+    for k in range(1, len(parts)):
+        out = jnp.where(which == k, parts[k], out)
     return out
 
 
@@ -218,16 +730,13 @@
 
     source = 2 * xh + c
     came = swap(out_weight, "c")
-    out_pair = jnp.concatenate(
+    head = jnp.concatenate(
         [jnp.where(c == 0, out_weight, came), jnp.where(c == 0, came, out_weight)], axis=0
     )
-    quarters = out_pair.reshape(4, 16, D)
-    piece = lax.dynamic_index_in_dim(quarters, y, 0, keepdims=False)
+    parts = [head]
     for step in (1, 2, 3):
-        sent = lax.dynamic_index_in_dim(quarters, (y + step) % 4, 0, keepdims=False)
-        came = lax.ppermute(sent, ("xh", "y", "c"), row_pairs(step, False))
-        piece = jnp.where((source + step) % 4 == y, came, piece)
-    out_full = gather_four(gather_four(piece, "y", y, 0), "z", z, 0).reshape(256, D)
+        parts.append(lax.ppermute(head, ("xh", "y", "c"), row_pairs(step, False)))
+    out_full = gather_four(pick(parts, (y - source) % 4), "z", z, 0).reshape(256, D)
 
     wide = jnp.stack([scaled(gate_weight, second_col), scaled(up_weight, second_col)])
     blocks = jnp.concatenate([wide[:, :, 1408 * k : 1408 * (k + 1)] for k in range(4)], axis=0)
@@ -247,95 +756,55 @@
         ]
         for k in range(2)
     ]
-    feed_full = lax.all_gather(spread_columns(chunks, xl, c), ("y", "z"), axis=1, tiled=True)
-    feed_full = feed_full.reshape(D, 2 * WIDE)
     down_half = jnp.where(xh == 0, down_weight[:44], down_weight[44:])
     down_half = jnp.pad(down_half, ((0, 4), (0, 0)))
-    down_full = lax.all_gather(down_half, ("y", "z"), axis=0, tiled=True)
-
-    ids = share(doc_ids[None])
-    cosine, sine, allowed = rotary(ids)
-    cosine = cosine.reshape(TP * CAP, 1, HDIM)
-    sine = sine.reshape(TP * CAP, 1, HDIM)
+    corner = jnp.concatenate(
+        [down_half[16 * k : 16 * (k + 1), 2 * WIDE :] for k in range(3)], axis=1
+    )
+    spread = spread_columns(chunks, xl, c).reshape(128, 2 * WIDE)
+    packed = jnp.concatenate([spread, down_half[:, : 2 * WIDE], corner], axis=0)
+    packed = lax.all_gather(packed, ("y", "z"), axis=0, tiled=True)
+
+    table = rotary_table()
     rows = tokens.astype(F32)
     first_scale = rms_scale(rows)
-    normed = share((rows * first_scale).astype(BF16))
-    upstream = share(after(cotangent, normed))
-    qkv = times(normed, qkv_full)
-    queries = qkv[:, :256].reshape(TP * CAP, LOCAL_HEADS, HDIM)
-    keys = qkv[:, 256:320].reshape(TP * CAP, 1, HDIM)
-    values = qkv[:, 320:].astype(BF16).reshape(TP, CAP, HDIM)
-    rot_queries = (queries * cosine + turn(queries) * sine).astype(BF16)
-    rot_queries = rot_queries.reshape(TP, CAP, LOCAL_HEADS, HDIM)
-    rot_keys = (keys * cosine + turn(keys) * sine).astype(BF16).reshape(TP, CAP, HDIM)
-    scores = jnp.einsum("bigd,bjd->bgij", rot_queries, rot_keys, preferred_element_type=F32)
-    scores = jnp.where(allowed[:, None], scores * HDIM ** (-0.5), -1e30)
-    peak = jnp.max(scores, axis=-1, keepdims=True)
-    expo = jnp.exp(scores - peak)
-    probs = expo / jnp.sum(expo, axis=-1, keepdims=True)
-    probs_low = probs.astype(BF16)
-    mixed = jnp.einsum("bgij,bjd->bigd", probs_low, values, preferred_element_type=F32)
-    mixed = mixed.reshape(TP * CAP, LOCAL_HEADS * HDIM).astype(BF16)
-    midway = rows + collect(mixed, out_full, times)
+    id_rows = jnp.pad(doc_ids.astype(BF16)[None], ((0, 15), (0, D - CAP)))
+    normed = share_parts(jnp.concatenate([(rows * first_scale).astype(BF16), id_rows], axis=0))
+    upstream = share_parts(after(cotangent, *normed[1:4]))
+    queries, key_values, mixed, far, near = attend(normed, table, qkv_full, out_full)
+    midway = rows + ring_sum(pair_sum(far, near))
 
     second_scale = rms_scale(midway)
-    normed_two = share((midway * second_scale).astype(BF16))
-    gate_act = times(normed_two, feed_full[:, :WIDE])
-    up_act = times(normed_two, feed_full[:, WIDE:])
-    sigmoid_gate = jax.nn.sigmoid(gate_act)
-    silu_gate = gate_act * sigmoid_gate
-    hidden = (silu_gate * up_act).astype(BF16)
-    grad_hidden = times_t(upstream, down_full)
-    grad_gate = grad_hidden * up_act * (sigmoid_gate * (1.0 + gate_act * (1.0 - sigmoid_gate)))
-    grad_up = grad_hidden * silu_gate
-    grad_feed = jnp.concatenate([grad_gate.astype(BF16), grad_up.astype(BF16)], axis=1)
-    inner_two = collect(grad_feed, feed_full, times_t)
+    normed_two = share_parts((midway * second_scale).astype(BF16))
+    hidden, grad_feed, far, near = feed_forward(normed_two, upstream, packed)
+    inner_two = ring_sum(pair_sum(far, near))
     grad_mid = cotangent.astype(F32) + norm_back(midway, second_scale, inner_two)
-    feed_term = t_times(normed_two, grad_feed).astype(BF16).reshape(2, 16, 64, 2 * WIDE)
-    feed_term = feed_term.swapaxes(0, 1).reshape(16, 128, 2 * WIDE)
-    down_term = t_times(hidden, upstream).astype(BF16).reshape(16, 48, D)
-    corner = jnp.concatenate(
-        [down_term[:, 16 * k : 16 * (k + 1), 2 * WIDE :] for k in range(3)], axis=2
-    )
-    pack = jnp.concatenate([feed_term, down_term[:, :, : 2 * WIDE], corner], axis=1)
-    pack = pack.reshape(16 * 192, 2 * WIDE)
+    grad_attn = share_parts(grad_mid.astype(BF16))
+
+    pack = feed_grads(normed_two, upstream, hidden, grad_feed)
     pack = lax.psum_scatter(pack, ("y", "z"), scatter_dimension=0, tiled=True)
     feed_part = pack[:128].reshape(2, 64, 2 * WIDE)
     corner = pack[176:]
     corner = jnp.concatenate([corner[:, 512 * k : 512 * (k + 1)] for k in range(3)], axis=0)
     down_part = jnp.concatenate([pack[128:176], corner], axis=1)
 
-    grad_attn = share(grad_mid.astype(BF16))
-    grad_mixed = times_t(grad_attn, out_full).astype(BF16)
-    out_term = t_times(mixed, grad_attn).astype(BF16)
-    out_part = scatter_four(out_term.reshape(4, 4, 16, D), "z", z, 0).astype(BF16)
-    out_part = scatter_four(out_part, "y", y, 0).astype(BF16)
-    output = midway + collect(after(hidden, grad_attn), down_full, times)
-    output = output.astype(BF16)
-    grad_heads = grad_mixed.reshape(TP, CAP, LOCAL_HEADS, HDIM)
-    grad_probs = jnp.einsum("bigd,bjd->bgij", grad_heads, values, preferred_element_type=F32)
-    delta = jnp.sum(probs * grad_probs, axis=-1, keepdims=True)
-    grad_scores = (probs * (grad_probs - delta)).astype(BF16)
-    grad_rot_queries = jnp.einsum("bgij,bjd->bigd", grad_scores, rot_keys, preferred_element_type=F32)
-    grad_rot_keys = jnp.einsum("bgij,bigd->bjd", grad_scores, rot_queries, preferred_element_type=F32)
-    grad_values = jnp.einsum("bgij,bigd->bjd", probs_low, grad_heads, preferred_element_type=F32)
-    grad_rot_queries = (grad_rot_queries * HDIM ** (-0.5)).reshape(TP * CAP, LOCAL_HEADS, HDIM)
-    grad_rot_keys = (grad_rot_keys * HDIM ** (-0.5)).reshape(TP * CAP, 1, HDIM)
-    grad_queries = grad_rot_queries * cosine + turn_back(grad_rot_queries * sine)
-    grad_keys = grad_rot_keys * cosine + turn_back(grad_rot_keys * sine)
-    grad_qkv = jnp.concatenate(
-        [
-            grad_queries.reshape(TP * CAP, LOCAL_HEADS * HDIM).astype(BF16),
-            grad_keys.reshape(TP * CAP, HDIM).astype(BF16),
-            grad_values.reshape(TP * CAP, HDIM).astype(BF16),
-        ],
-        axis=1,
-    )
-    qkv_term = t_times(normed, grad_qkv).astype(BF16).reshape(2, D // 2, 384)
+    blocks = packed.reshape(16, 192, 2 * WIDE)
+    corner = jnp.concatenate(
+        [blocks[:, 176:, 512 * k : 512 * (k + 1)] for k in range(3)], axis=1
+    )
+    down_full = jnp.concatenate([blocks[:, 128:176], corner], axis=2).reshape(WIDE, D)
+    out_sum = pair_sum(times(hidden[512:], down_full).astype(BF16), times(hidden[:512], down_full))
+    output = (midway + ring_sum(after(out_sum, *grad_attn[1:4]))).astype(BF16)
+
+    grad_qkv, far, near = attend_back(
+        grad_attn, normed, table, qkv_full, out_full, queries, key_values
+    )
+    inner_one = ring_sum(pair_sum(far, near))
+    tokens_grad = grad_mid + norm_back(rows, first_scale, inner_one)
+    qkv_term, out_term = small_grads(normed, grad_attn, mixed, grad_qkv)
     qkv_part = scatter_four(qkv_term.reshape(2, 4, 4, 64, 384), "y", y, 1).astype(BF16)
     qkv_part = scatter_four(qkv_part, "z", z, 1).astype(BF16)
-    inner_one = collect(grad_qkv, qkv_full, times_t)
-    tokens_grad = grad_mid + norm_back(rows, first_scale, inner_one)
+    out_part = scatter_four(out_term.reshape(4, 64, D), "z", z, 0)
 
     def with_pair(zero, one):
         pair = zero[:, :, 256:].astype(F32) + one[:, :, 256:].astype(F32)
@@ -386,17 +855,11 @@
         [jnp.where(xh == 0, down_part, came)[:44], jnp.where(xh == 0, came, down_part)[:44]], axis=0
     ).astype(F32)
 
-    parts = [out_part]
+    sent = out_part.astype(BF16)
     for step in (1, 2, 3):
-        parts.append(lax.ppermute(out_part, ("xh", "y", "c"), row_pairs(step, True)))
-    ordered = []
-    for q in range(4):
-        item = parts[0]
-        for step in (1, 2, 3):
-            item = jnp.where((y + step) % 4 == q, parts[step], item)
-        ordered.append(item)
-    low = jnp.concatenate(ordered[:2], axis=0)
-    high = jnp.concatenate(ordered[2:], axis=0)
+        out_part = out_part + lax.ppermute(sent, ("xh", "y", "c"), row_pairs(step, True)).astype(F32)
+    out_part = out_part.astype(BF16)
+    low, high = out_part[:32], out_part[32:]
     came = swap(jnp.where(c == 0, high, low), "c")
     owned = jnp.where(y % 2 == c, jnp.where(c == 0, low, high), came)
     came = swap(owned, "xh")

time: 571 us -> 457 us (0.80)
  Pallas kernels: 0 us -> 84.9 us
  matrix products: 93.5 us -> 9.3 us
  waiting for transfers between devices: 231 us -> 166 us
  local copies, waits for them, and re-layouts: 47.1 us -> 19 us
  other arithmetic: 48.3 us -> 28.5 us
    pallas_call x0 -> x5, Pallas kernels: none -> 84.9 us  [the longest x1 28.5 us: feed_forward(): pl.pallas_call(feed_kernel, grid=(4,), in_specs=[ANY] * 15, out_specs=[pl...]
    dot_general x7 -> x1, matrix products: 34.5 us -> 1.42 us  [times_t(): lax.dot_general(left, right, (((1,), (1,)), ((), ())), preferred_element_...]
    ppermute x18 -> x15, waiting for transfers between devices: 54.5 us -> 23.3 us  [the longest x9 14 us: gather_four(): lax.ppermute(item, axis, [(i, (i - step) % 4) for i in range(4)])]
    dot_general x9 -> x0, matrix products: 25.9 us -> none  [the longest x4 19 us: t_times(): lax.dot_general(left, right, (((0,), (0,)), ((), ())), preferred_element_...]
    dot_general x8 -> x3, matrix products: 29.7 us -> 7.88 us  [times(): return jnp.dot(left, right, preferred_element_type=F32)]
    ppermute x12 -> x9, waiting for transfers between devices: 32.8 us -> 14.6 us  [scatter_four(): lax.ppermute(sent, axis, [(i, (i + step) % 4) for i in range(4)])]
    ppermute x18, waiting for transfers between devices: 84.2 us -> 69 us  [to_ring(): return lax.ppermute(item, RING, [(i, (i + step) % 4) for i in range(4)])]
    unnamed x152 -> x116, local copies, waits for them, and re-layouts: 24.9 us -> 11.4 us
  transfers between devices with their start and end apart: 100 -> 82, of which waited for: 45 -> 33; matrix products, arithmetic and copies ran while one was open for 27% -> 8% of each run, Pallas kernels for 0% -> 8%
where the time goes in v3:
time: 457 us; the launch traced here: 451 us
  waiting for transfers between devices  166 us (36%)
  starting transfers between devices  128 us (28%)
  Pallas kernels  84.9 us (19%)
  other arithmetic  28.5 us (6%)
  local copies, waits for them, and re-layouts  19 us (4%)
  between operations  15.8 us (3%)
  matrix products  9.3 us (2%)
    ppermute x18, waiting for transfers between devices, to_ring(): return lax.ppermute(item, RING, [(i, (i + step) % 4) for i in range(4)])  69 us
    ppermute x26, starting transfers between devices, swap(): return lax.ppermute(item, axis, SWAP)  47.4 us
    ppermute x12, waiting for transfers between devices, from_ring(): return lax.ppermute(item, RING, [(i, (i - step) % 4) for i in range(4)])  41.8 us
    pallas_call x1, Pallas kernels, feed_forward(): pl.pallas_call(feed_kernel, grid=(4,), in_specs=[ANY] * 15, out_specs=[pl...  28.5 us
    ppermute x18, starting transfers between devices, to_ring(): return lax.ppermute(item, RING, [(i, (i + step) % 4) for i in range(4)])  24 us
    pallas_call x1, Pallas kernels, feed_grads(): pl.pallas_call(grads_kernel, in_specs=[ANY] * 16, out_specs=ANY, out_shap...  21 us
    ppermute x9, starting transfers between devices, gather_four(): lax.ppermute(item, axis, [(i, (i - step) % 4) for i in range(4)])  18.6 us
    ppermute x12, starting transfers between devices, from_ring(): return lax.ppermute(item, RING, [(i, (i - step) % 4) for i in range(4)])  18.1 us
  transfers between devices with their start and end apart: 82, of which 33 were waited for; matrix products, arithmetic and copies ran while one was open for 8% of the time, Pallas kernels for 8%

profile of v3, /device:TPU:1, one launch (start us, length us, event | category | flops | bytes accessed | tf_op | source)
XLA Modules:
  0.0 450.7 jit_solution(10342825196268620812)
XLA Ops:
  39.0 7.7 %collective-permute-done.15 = bf16[64,2048]{1,0:T(8,128)(2,1)S(1)} collective-permute-done((bf16[64,2048]{1,0:T(8,128)(2,1)S(1)}, bf16[64,2048]{1,0:T(8,128)(2,1)S(1)}, u32[]{:S(2)}, u32[]{:S(2)}) %collective-permute-start.15) | collective-permute-done | bytes 262176 | tf_op jit(solution)/shard_map/ppermute | solution.py:738
  46.7 7.5 %collective-permute-start.13 = (bf16[2,4,64,384]{3,2,0,1:T(8,128)(2,1)S(1)}, bf16[2,4,64,384]{3,2,0,1:T(8,128)(2,1)S(1)}, u32[]{:S(2)}, u32[]{:S(2)}) collective-permute-start(bf16[2,4,64,384]{3,2,0,1:T(8,128)(2,1)S(1)} %pad_maximum_fusion.10), channel_id=1, source_target_pairs={{0,24},{8,0},{16,8},{24,16},{1,25},{9,1},{17,9},{25,17},{2,26},{10... | collective-permute-start | bytes 1179656 | tf_op jit(solution)/shard_map/ppermute | solution.py:644
  54.4 5.7 %collective-permute-start.2 = (bf16[144,2048]{1,0:T(8,128)(2,1)S(1)}, bf16[144,2048]{1,0:T(8,128)(2,1)S(1)}, u32[]{:S(2)}, u32[]{:S(2)}) collective-permute-start(bf16[144,2048]{1,0:T(8,128)(2,1)S(1)} %fusion.30.refs_0_.refs_7_), channel_id=1, source_target_pairs={{0,64},{32,96},{64,0},{96,32},{1,65},{33,97},{65,1},{97,33},{2,66}... | collective-permute-start | bytes 1769480 | tf_op jit(solution)/shard_map/ppermute | solution.py:568
  67.2 9.7 %collective-permute-done.13 = bf16[2,4,64,384]{3,2,0,1:T(8,128)(2,1)S(1)} collective-permute-done((bf16[2,4,64,384]{3,2,0,1:T(8,128)(2,1)S(1)}, bf16[2,4,64,384]{3,2,0,1:T(8,128)(2,1)S(1)}, u32[]{:S(2)}, u32[]{:S(2)}) %collective-permute-start.13) | collective-permute-done | bytes 393248 | tf_op jit(solution)/shard_map/ppermute | solution.py:644
  84.6 14.0 %shard_map.212 = (bf16[1024,256]{1,0:T(8,128)(2,1)S(1)}, bf16[1024,128]{1,0:T(8,128)(2,1)S(1)}, bf16[1024,256]{1,0:T(8,128)(2,1)S(1)}, bf16[512,2048]{1,0:T(8,128)(2,1)S(1)}, f32[512,2048]{1,0:T(8,128)}) custom-call(bf16[144,2048]{1,0:T(8,128)(2,1)S(1)} %fusion.30.refs_0_.refs_7_, bf16[144,2048]{1,0:T(8,128)(2,1)S(1)} %collective-permute-done.refs_1_.refs_8_, ...), custom_call_target="tpu_custom_call" | custom-call | flops 5368709120 | bytes 15728640 | tf_op jit(solution)/shard_map/pallas_call | solution.py:368
  98.6 6.7 %collective-permute-start.21 = (bf16[512,2048]{1,0:T(8,128)(2,1)S(1)}, bf16[512,2048]{1,0:T(8,128)(2,1)S(1)}, u32[]{:S(2)}, u32[]{:S(2)}) collective-permute-start(bf16[512,2048]{1,0:T(8,128)(2,1)S(1)} %get-tuple-element.28), channel_id=1, source_target_pairs={{0,1},{1,0},{2,3},{3,2},{4,5},{5,4},{6,7},{7,6},{8,9},{9,8},{10,11... | collective-permute-start | bytes 6291464 | tf_op jit(solution)/shard_map/ppermute | solution.py:576
  119.7 8.6 %collective-permute-done.24 = bf16[128,2048]{1,0:T(8,128)(2,1)S(1)} collective-permute-done((bf16[128,2048]{1,0:T(8,128)(2,1)S(1)}, bf16[128,2048]{1,0:T(8,128)(2,1)S(1)}, u32[]{:S(2)}, u32[]{:S(2)}) %collective-permute-start.24) | collective-permute-done | bytes 524320 | tf_op jit(solution)/shard_map/ppermute | solution.py:572
  128.3 12.2 %collective-permute-done.23 = bf16[128,2048]{1,0:T(8,128)(2,1)S(1)} collective-permute-done((bf16[128,2048]{1,0:T(8,128)(2,1)S(1)}, bf16[128,2048]{1,0:T(8,128)(2,1)S(1)}, u32[]{:S(2)}, u32[]{:S(2)}) %collective-permute-start.23) | collective-permute-done | bytes 524320 | tf_op jit(solution)/shard_map/ppermute | solution.py:572
  145.1 6.6 %collective-permute-done.31.refs_8_ = bf16[128,2048]{1,0:T(8,128)(2,1)S(1)} collective-permute-done((bf16[128,2048]{1,0:T(8,128)(2,1)S(1)}, bf16[128,2048]{1,0:T(8,128)(2,1)S(1)}, u32[]{:S(2)}, u32[]{:S(2)}) %collective-permute-start.31) | collective-permute-done | bytes 524320 | tf_op jit(solution)/shard_map/ppermute | solution.py:568
  153.9 9.0 %collective-permute-done.25.refs_1_ = bf16[128,2048]{1,0:T(8,128)(2,1)S(1)} collective-permute-done((bf16[128,2048]{1,0:T(8,128)(2,1)S(1)}, bf16[128,2048]{1,0:T(8,128)(2,1)S(1)}, u32[]{:S(2)}, u32[]{:S(2)}) %collective-permute-start.25) | collective-permute-done | bytes 524320 | tf_op jit(solution)/shard_map/ppermute | solution.py:568
  165.7 7.6 %collective-permute-done.33.refs_10_ = bf16[128,2048]{1,0:T(8,128)(2,1)S(1)} collective-permute-done((bf16[128,2048]{1,0:T(8,128)(2,1)S(1)}, bf16[128,2048]{1,0:T(8,128)(2,1)S(1)}, u32[]{:S(2)}, u32[]{:S(2)}) %collective-permute-start.33) | collective-permute-done | bytes 524320 | tf_op jit(solution)/shard_map/ppermute | solution.py:568
  174.7 9.8 %collective-permute-done.27.refs_3_ = bf16[128,2048]{1,0:T(8,128)(2,1)S(1)} collective-permute-done((bf16[128,2048]{1,0:T(8,128)(2,1)S(1)}, bf16[128,2048]{1,0:T(8,128)(2,1)S(1)}, u32[]{:S(2)}, u32[]{:S(2)}) %collective-permute-start.27) | collective-permute-done | bytes 524320 | tf_op jit(solution)/shard_map/ppermute | solution.py:568
  192.5 28.5 %shard_map.213 = (bf16[1024,768]{1,0:T(8,128)(2,1)}, bf16[1024,1536]{1,0:T(8,128)(2,1)}, bf16[512,2048]{1,0:T(8,128)(2,1)}, f32[512,2048]{1,0:T(8,128)}) custom-call(bf16[128,2048]{1,0:T(8,128)(2,1)S(1)} %multiply_convert_fusion.refs_0_, bf16[128,2048]{1,0:T(8,128)(2,1)S(1)} %collective-permute-done.25.refs_1_, bf16[128,2048]{1,0:T(8,128)(2,1)S(1)} %copy-done.16, ...), custom_call_target="tpu_custom_call" | custom-call | flops 16106127360 | bytes 29360128 | tf_op jit(solution)/shard_map/pallas_call | solution.py:135
  221.0 21.0 %shard_map.216 = bf16[3072,1536]{1,0:T(8,128)(2,1)} custom-call(bf16[128,2048]{1,0:T(8,128)(2,1)S(1)} %multiply_convert_fusion.refs_0_, bf16[128,2048]{1,0:T(8,128)(2,1)S(1)} %collective-permute-done.25.refs_1_, bf16[128,2048]{1,0:T(8,128)(2,1)S(1)} %copy-done.16, bf16[128,2048]{1,0:T(8,128)(2,1)S(1)} %copy-done.18, bf16[128,2048]{1,0:T(8,128)(2,1)S(1)} %copy-done.20, ...), custom_call_target="tpu_custom_call" | custom-call | flops 9663676416 | bytes 23068672 | tf_op jit(solution)/shard_map/pallas_call | solution.py:216
  262.7 12.6 %collective-permute-done.42 = bf16[128,2048]{1,0:T(8,128)(2,1)S(1)} collective-permute-done((bf16[128,2048]{1,0:T(8,128)(2,1)S(1)}, bf16[128,2048]{1,0:T(8,128)(2,1)S(1)}, u32[]{:S(2)}, u32[]{:S(2)}) %collective-permute-start.42) | collective-permute-done | bytes 524320 | tf_op jit(solution)/shard_map/ppermute | solution.py:572
  285.9 5.5 %collective-permute-done.44.refs_1_.refs_8_ = bf16[128,2048]{1,0:T(8,128)(2,1)S(1)} collective-permute-done((bf16[128,2048]{1,0:T(8,128)(2,1)S(1)}, bf16[128,2048]{1,0:T(8,128)(2,1)S(1)}, u32[]{:S(2)}, u32[]{:S(2)}) %collective-permute-start.44) | collective-permute-done | bytes 524320 | tf_op jit(solution)/shard_map/ppermute | solution.py:568
  294.8 11.8 %collective-permute-start.51 = (bf16[256,2048]{1,0:T(8,128)(2,1)S(1)}, bf16[256,2048]{1,0:T(8,128)(2,1)S(1)}, u32[]{:S(2)}, u32[]{:S(2)}) collective-permute-start(bf16[256,2048]{1,0:T(8,128)(2,1)S(1)} %pad_maximum_fusion.5), channel_id=1, source_target_pairs={{0,1},{1,0},{2,3},{3,2},{4,5},{5,4},{6,7},{7,6},{8,9},{9,8},{10,11... | collective-permute-start | bytes 3145736 | tf_op jit(solution)/shard_map/ppermute | solution.py:576
  313.4 16.8 %shard_map.214 = (bf16[1024,384]{1,0:T(8,128)(2,1)S(1)}, bf16[512,2048]{1,0:T(8,128)(2,1)}, f32[512,2048]{1,0:T(8,128)}) custom-call(bf16[128,2048]{1,0:T(8,128)(2,1)S(1)} %get-tuple-element.45.refs_0_.refs_7_, bf16[128,2048]{1,0:T(8,128)(2,1)S(1)} %collective-permute-done.44.refs_1_.refs_8_, bf16[128,2048]{1,0:T(8,128)(2,1)S(1)} %collective-permute-done.45.refs_2_.refs_9_, ...), custom_call_target="tpu_custom_call" | custom-call | flops 5368709120 | bytes 15728640 | tf_op jit(solution)/shard_map/pallas_call | solution.py:467
  335.1 4.8 %collective-permute-start.58 = (bf16[2,4,64,384]{3,2,1,0:T(8,128)(2,1)S(1)}, bf16[2,4,64,384]{3,2,1,0:T(8,128)(2,1)S(1)}, u32[]{:S(2)}, u32[]{:S(2)}) collective-permute-start(bf16[2,4,64,384]{3,2,1,0:T(8,128)(2,1)S(1)} %get-tuple-element.70), channel_id=1, source_target_pairs={{0,16},{8,24},{16,0},{24,8},{1,17},{9,25},{17,1},{25,9},{2,18},{10... | collective-permute-start | bytes 1179656 | tf_op jit(solution)/shard_map/ppermute | solution.py:659
  348.8 9.1 %collective-permute-done.57 = bf16[2,4,64,384]{3,2,1,0:T(8,128)(2,1)S(1)} collective-permute-done((bf16[2,4,64,384]{3,2,1,0:T(8,128)(2,1)S(1)}, bf16[2,4,64,384]{3,2,1,0:T(8,128)(2,1)S(1)}, u32[]{:S(2)}, u32[]{:S(2)}) %collective-permute-start.57) | collective-permute-done | bytes 393248 | tf_op jit(solution)/shard_map/ppermute | solution.py:659
  360.7 7.5 %collective-permute-start.72 = (bf16[64,2048]{1,0:T(8,128)(2,1)S(1)}, bf16[64,2048]{1,0:T(8,128)(2,1)S(1)}, u32[]{:S(2)}, u32[]{:S(2)}) collective-permute-start(bf16[64,2048]{1,0:T(8,128)(2,1)S(1)} %fusion.46), channel_id=1, source_target_pairs={{24,0},{1,9},{72,80},{81,89},{26,2},{3,11},{74,82},{83,91},{28,4},... | collective-permute-start | bytes 786440 | tf_op jit(solution)/shard_map/ppermute | solution.py:860
  391.8 10.1 %collective-permute-done.56 = bf16[128,2048]{1,0:T(8,128)(2,1)S(1)} collective-permute-done((bf16[128,2048]{1,0:T(8,128)(2,1)S(1)}, bf16[128,2048]{1,0:T(8,128)(2,1)S(1)}, u32[]{:S(2)}, u32[]{:S(2)}) %collective-permute-start.56) | collective-permute-done | bytes 524320 | tf_op jit(solution)/shard_map/ppermute | solution.py:572
  401.9 11.4 %collective-permute-done.55 = bf16[128,2048]{1,0:T(8,128)(2,1)S(1)} collective-permute-done((bf16[128,2048]{1,0:T(8,128)(2,1)S(1)}, bf16[128,2048]{1,0:T(8,128)(2,1)S(1)}, u32[]{:S(2)}, u32[]{:S(2)}) %collective-permute-start.55) | collective-permute-done | bytes 524320 | tf_op jit(solution)/shard_map/ppermute | solution.py:572
  432.0 5.5 %collective-permute-done.77 = bf16[32,3072]{1,0:T(8,128)(2,1)S(1)} collective-permute-done((bf16[32,3072]{1,0:T(8,128)(2,1)S(1)}, bf16[32,3072]{1,0:T(8,128)(2,1)S(1)}, u32[]{:S(2)}, u32[]{:S(2)}) %collective-permute-start.77) | collective-permute-done | bytes 196640 | tf_op jit(solution)/shard_map/ppermute | solution.py:572
  (400 shorter events, 185.1 us)
Async XLA Ops:
  7.2 181.2 %all-gather.2.cloned.1.call-start = ((), (), s32[]{:S(2)}) async-start(), calls=%async_computation.1 | async-start | bytes 10027008 | tf_op jit(solution)/shard_map/all_gather | solution.py:766
  20.6 397.1 %reduce-scatter.2.cloned.1.call-start = ((), (), s32[]{:S(2)}) async-start(), calls=%async_computation.2 | async-start | bytes 10027008 | tf_op jit(solution)/shard_map/reduce_scatter | solution.py:785
  24.9 29.4 %collective-permute-start = (bf16[144,2048]{1,0:T(8,128)(2,1)S(1)}, bf16[144,2048]{1,0:T(8,128)(2,1)S(1)}, u32[]{:S(2)}, u32[]{:S(2)}) collective-permute-start(bf16[144,2048]{1,0:T(8,128)(2,1)S(1)} %fusion.30.refs_0_.refs_7_), channel_id=1, source_target_pairs={{0,96},{32,0},{64,32},{96,64},{1,97},{33,1},{65,33},{97,65},{2,98}... | collective-permute-start | bytes 1769480 | tf_op jit(solution)/shard_map/ppermute | solution.py:568
  26.8 33.3 %collective-permute-start.1 = (bf16[144,2048]{1,0:T(8,128)(2,1)S(1)}, bf16[144,2048]{1,0:T(8,128)(2,1)S(1)}, u32[]{:S(2)}, u32[]{:S(2)}) collective-permute-start(bf16[144,2048]{1,0:T(8,128)(2,1)S(1)} %fusion.30.refs_0_.refs_7_), channel_id=1, source_target_pairs={{0,32},{32,64},{64,96},{96,0},{1,33},{33,65},{65,97},{97,1},{2,34}... | collective-permute-start | bytes 1769480 | tf_op jit(solution)/shard_map/ppermute | solution.py:568
  46.7 30.3 %collective-permute-start.13 = (bf16[2,4,64,384]{3,2,0,1:T(8,128)(2,1)S(1)}, bf16[2,4,64,384]{3,2,0,1:T(8,128)(2,1)S(1)}, u32[]{:S(2)}, u32[]{:S(2)}) collective-permute-start(bf16[2,4,64,384]{3,2,0,1:T(8,128)(2,1)S(1)} %pad_maximum_fusion.10), channel_id=1, source_target_pairs={{0,24},{8,0},{16,8},{24,16},{1,25},{9,1},{17,9},{25,17},{2,26},{10... | collective-permute-start | bytes 1179656 | tf_op jit(solution)/shard_map/ppermute | solution.py:644
  54.4 26.8 %collective-permute-start.2 = (bf16[144,2048]{1,0:T(8,128)(2,1)S(1)}, bf16[144,2048]{1,0:T(8,128)(2,1)S(1)}, u32[]{:S(2)}, u32[]{:S(2)}) collective-permute-start(bf16[144,2048]{1,0:T(8,128)(2,1)S(1)} %fusion.30.refs_0_.refs_7_), channel_id=1, source_target_pairs={{0,64},{32,96},{64,0},{96,32},{1,65},{33,97},{65,1},{97,33},{2,66}... | collective-permute-start | bytes 1769480 | tf_op jit(solution)/shard_map/ppermute | solution.py:568
  116.3 24.2 %collective-permute-start.23 = (bf16[128,2048]{1,0:T(8,128)(2,1)S(1)}, bf16[128,2048]{1,0:T(8,128)(2,1)S(1)}, u32[]{:S(2)}, u32[]{:S(2)}) collective-permute-start(bf16[128,2048]{1,0:T(8,128)(2,1)S(1)} %get-tuple-element.67), channel_id=1, source_target_pairs={{0,96},{32,0},{64,32},{96,64},{1,97},{33,1},{65,33},{97,65},{2,98}... | collective-permute-start | bytes 1572872 | tf_op jit(solution)/shard_map/ppermute | solution.py:572
  117.0 23.5 %collective-permute-start.22 = (bf16[128,2048]{1,0:T(8,128)(2,1)S(1)}, bf16[128,2048]{1,0:T(8,128)(2,1)S(1)}, u32[]{:S(2)}, u32[]{:S(2)}) collective-permute-start(bf16[128,2048]{1,0:T(8,128)(2,1)S(1)} %get-tuple-element.65), channel_id=1, source_target_pairs={{0,32},{32,64},{64,96},{96,0},{1,33},{33,65},{65,97},{97,1},{2,34}... | collective-permute-start | bytes 1572872 | tf_op jit(solution)/shard_map/ppermute | solution.py:572
  117.8 34.0 %collective-permute-start.31 = (bf16[128,2048]{1,0:T(8,128)(2,1)S(1)}, bf16[128,2048]{1,0:T(8,128)(2,1)S(1)}, u32[]{:S(2)}, u32[]{:S(2)}) collective-permute-start(bf16[128,2048]{1,0:T(8,128)(2,1)S(1)} %copy-done.12), channel_id=1, source_target_pairs={{0,96},{32,0},{64,32},{96,64},{1,97},{33,1},{65,33},{97,65},{2,98}... | collective-permute-start | bytes 1572872 | tf_op jit(solution)/shard_map/ppermute | solution.py:568
  119.7 34.0 %collective-permute-start.32 = (bf16[128,2048]{1,0:T(8,128)(2,1)S(1)}, bf16[128,2048]{1,0:T(8,128)(2,1)S(1)}, u32[]{:S(2)}, u32[]{:S(2)}) collective-permute-start(bf16[128,2048]{1,0:T(8,128)(2,1)S(1)} %copy-done.12), channel_id=1, source_target_pairs={{0,32},{32,64},{64,96},{96,0},{1,33},{33,65},{65,97},{97,1},{2,34}... | collective-permute-start | bytes 1572872 | tf_op jit(solution)/shard_map/ppermute | solution.py:568
  143.9 29.4 %collective-permute-start.33 = (bf16[128,2048]{1,0:T(8,128)(2,1)S(1)}, bf16[128,2048]{1,0:T(8,128)(2,1)S(1)}, u32[]{:S(2)}, u32[]{:S(2)}) collective-permute-start(bf16[128,2048]{1,0:T(8,128)(2,1)S(1)} %copy-done.12), channel_id=1, source_target_pairs={{0,64},{32,96},{64,0},{96,32},{1,65},{33,97},{65,1},{97,33},{2,66}... | collective-permute-start | bytes 1572872 | tf_op jit(solution)/shard_map/ppermute | solution.py:568
  153.8 32.4 %collective-permute-start.35 = (bf16[256,2048]{1,0:T(8,128)(2,1)S(1)}, bf16[256,2048]{1,0:T(8,128)(2,1)S(1)}, u32[]{:S(2)}, u32[]{:S(2)}) collective-permute-start(bf16[256,2048]{1,0:T(8,128)(2,1)S(1)} %pad_maximum_fusion.4), channel_id=1, source_target_pairs={{0,1},{1,0},{2,3},{3,2},{4,5},{5,4},{6,7},{7,6},{8,9},{9,8},{10,11... | collective-permute-start | bytes 3145736 | tf_op jit(solution)/shard_map/ppermute | solution.py:576
  164.0 24.3 %collective-permute-start.29 = (bf16[256,2048]{1,0:T(8,128)(2,1)S(1)}, bf16[256,2048]{1,0:T(8,128)(2,1)}, u32[]{:S(2)}, u32[]{:S(2)}) collective-permute-start(bf16[256,2048]{1,0:T(8,128)(2,1)S(1)} %pad_maximum_fusion.3), channel_id=1, source_target_pairs={{0,1},{1,0},{2,3},{3,2},{4,5},{5,4},{6,7},{7,6},{8,9},{9,8},{10,11... | collective-permute-start | bytes 3145736 | tf_op jit(solution)/shard_map/ppermute | solution.py:576
  250.7 24.6 %collective-permute-start.42 = (bf16[128,2048]{1,0:T(8,128)(2,1)S(1)}, bf16[128,2048]{1,0:T(8,128)(2,1)S(1)}, u32[]{:S(2)}, u32[]{:S(2)}) collective-permute-start(bf16[128,2048]{1,0:T(8,128)(2,1)S(1)} %get-tuple-element.64), channel_id=1, source_target_pairs={{0,96},{32,0},{64,32},{96,64},{1,97},{33,1},{65,33},{97,65},{2,98}... | collective-permute-start | bytes 1572872 | tf_op jit(solution)/shard_map/ppermute | solution.py:572
  251.5 23.8 %collective-permute-start.41 = (bf16[128,2048]{1,0:T(8,128)(2,1)S(1)}, bf16[128,2048]{1,0:T(8,128)(2,1)S(1)}, u32[]{:S(2)}, u32[]{:S(2)}) collective-permute-start(bf16[128,2048]{1,0:T(8,128)(2,1)S(1)} %get-tuple-element.62), channel_id=1, source_target_pairs={{0,32},{32,64},{64,96},{96,0},{1,33},{33,65},{65,97},{97,1},{2,34}... | collective-permute-start | bytes 1572872 | tf_op jit(solution)/shard_map/ppermute | solution.py:572
  257.5 49.2 %collective-permute-start.39 = (bf16[512,2048]{1,0:T(8,128)(2,1)}, bf16[512,2048]{1,0:T(8,128)(2,1)}, u32[]{:S(2)}, u32[]{:S(2)}) collective-permute-start(bf16[512,2048]{1,0:T(8,128)(2,1)} %convolution_convert_fusion), channel_id=1, source_target_pairs={{0,1},{1,0},{2,3},{3,2},{4,5},{5,4},{6,7},{7,6},{8,9},{9,8},{10,11... | collective-permute-start | bytes 6291464 | tf_op jit(solution)/shard_map/ppermute | solution.py:576
  281.5 25.1 %collective-permute-start.46 = (bf16[128,2048]{1,0:T(8,128)(2,1)S(1)}, bf16[128,2048]{1,0:T(8,128)(2,1)S(1)}, u32[]{:S(2)}, u32[]{:S(2)}) collective-permute-start(bf16[128,2048]{1,0:T(8,128)(2,1)S(1)} %get-tuple-element.45.refs_0_.refs_7_), channel_id=1, source_target_pairs={{0,64},{32,96},{64,0},{96,32},{1,65},{33,97},{65,1},{97,33},{2,66}... | collective-permute-start | bytes 1572872 | tf_op jit(solution)/shard_map/ppermute | solution.py:568
  284.6 26.5 %collective-permute-start.50 = (bf16[128,2048]{1,0:T(8,128)(2,1)S(1)}, bf16[128,2048]{1,0:T(8,128)(2,1)S(1)}, u32[]{:S(2)}, u32[]{:S(2)}) collective-permute-start(bf16[128,2048]{1,0:T(8,128)(2,1)S(1)} %get-tuple-element.45.refs_0_.refs_7_), channel_id=1, source_target_pairs={{0,1},{1,0},{2,3},{3,2},{4,5},{5,4},{6,7},{7,6},{8,9},{9,8},{10,11... | collective-permute-start | bytes 1572872 | tf_op jit(solution)/shard_map/ppermute | solution.py:576
  311.0 28.9 %collective-permute-start.49 = (bf16[128,2048]{1,0:T(8,128)(2,1)S(1)}, bf16[128,2048]{1,0:T(8,128)(2,1)S(1)}, u32[]{:S(2)}, u32[]{:S(2)}) collective-permute-start(bf16[128,2048]{1,0:T(8,128)(2,1)S(1)} %get-tuple-element.60), channel_id=1, source_target_pairs={{0,64},{32,96},{64,0},{96,32},{1,65},{33,97},{65,1},{97,33},{2,66}... | collective-permute-start | bytes 1572872 | tf_op jit(solution)/shard_map/ppermute | solution.py:572
  311.1 29.6 %collective-permute-start.48 = (bf16[128,2048]{1,0:T(8,128)(2,1)S(1)}, bf16[128,2048]{1,0:T(8,128)(2,1)S(1)}, u32[]{:S(2)}, u32[]{:S(2)}) collective-permute-start(bf16[128,2048]{1,0:T(8,128)(2,1)S(1)} %get-tuple-element.61), channel_id=1, source_target_pairs={{0,96},{32,0},{64,32},{96,64},{1,97},{33,1},{65,33},{97,65},{2,98}... | collective-permute-start | bytes 1572872 | tf_op jit(solution)/shard_map/ppermute | solution.py:572
  311.2 29.5 %collective-permute-start.47 = (bf16[128,2048]{1,0:T(8,128)(2,1)S(1)}, bf16[128,2048]{1,0:T(8,128)(2,1)S(1)}, u32[]{:S(2)}, u32[]{:S(2)}) collective-permute-start(bf16[128,2048]{1,0:T(8,128)(2,1)S(1)} %get-tuple-element.59), channel_id=1, source_target_pairs={{0,32},{32,64},{64,96},{96,0},{1,33},{33,65},{65,97},{97,1},{2,34}... | collective-permute-start | bytes 1572872 | tf_op jit(solution)/shard_map/ppermute | solution.py:572
  341.8 44.5 %collective-permute-start.53 = (bf16[512,2048]{1,0:T(8,128)(2,1)S(1)}, bf16[512,2048]{1,0:T(8,128)(2,1)S(1)}, u32[]{:S(2)}, u32[]{:S(2)}) collective-permute-start(bf16[512,2048]{1,0:T(8,128)(2,1)S(1)} %copy-done.50), channel_id=1, source_target_pairs={{0,1},{1,0},{2,3},{3,2},{4,5},{5,4},{6,7},{7,6},{8,9},{9,8},{10,11... | collective-permute-start | bytes 6291464 | tf_op jit(solution)/shard_map/ppermute | solution.py:576
  388.2 25.1 %collective-permute-start.55 = (bf16[128,2048]{1,0:T(8,128)(2,1)S(1)}, bf16[128,2048]{1,0:T(8,128)(2,1)S(1)}, u32[]{:S(2)}, u32[]{:S(2)}) collective-permute-start(bf16[128,2048]{1,0:T(8,128)(2,1)S(1)} %get-tuple-element.58), channel_id=1, source_target_pairs={{0,96},{32,0},{64,32},{96,64},{1,97},{33,1},{65,33},{97,65},{2,98}... | collective-permute-start | bytes 1572872 | tf_op jit(solution)/shard_map/ppermute | solution.py:572
  390.5 25.1 %collective-permute-start.54 = (bf16[128,2048]{1,0:T(8,128)(2,1)S(1)}, bf16[128,2048]{1,0:T(8,128)(2,1)S(1)}, u32[]{:S(2)}, u32[]{:S(2)}) collective-permute-start(bf16[128,2048]{1,0:T(8,128)(2,1)S(1)} %get-tuple-element.56), channel_id=1, source_target_pairs={{0,32},{32,64},{64,96},{96,0},{1,33},{33,65},{65,97},{97,1},{2,34}... | collective-permute-start | bytes 1572872 | tf_op jit(solution)/shard_map/ppermute | solution.py:572
  (116 other events, 1069.2 us)
Sparse Core Ops, SparseCore 0:
  20.7 93.6 all-gather.1
  242.2 87.9 reduce-scatter.1

commit v4 on v3

--- a/solution.py
+++ b/solution.py
@@ -18,6 +18,7 @@
 
 RING = ("xh", "xl")
 SWAP = [(0, 1), (1, 0)]
+STEPS = (0, 1, 3, 2)
 
 
 def dot_nn(left, right):
@@ -32,18 +33,23 @@
     return lax.dot_general(left, right, (((0,), (0,)), ((), ())), preferred_element_type=F32)
 
 
-ANY = pl.BlockSpec(memory_space=pl.ANY)
-
-
-def part_copies(parts, whole, sems):
-    copies, start = [], 0
-    for k, part in enumerate(parts):
-        rows = min(part.shape[0] // CAP, 2) * CAP
-        copies.append(
-            pltpu.make_async_copy(part.at[pl.ds(0, rows)], whole.at[pl.ds(start, rows)], sems.at[k])
+HBM = pl.BlockSpec(memory_space=pltpu.HBM)
+
+
+def block_copies(parts, whole, sems):
+    return [
+        pltpu.make_async_copy(
+            part.at[pl.ds(0, CAP)], whole.at[pl.ds(CAP * spot, CAP)], sems.at[spot]
         )
-        start += rows
-    return copies
+        for spot, part in enumerate(parts)
+    ]
+
+
+def id_copies(parts, ids, sems):
+    return [
+        pltpu.make_async_copy(part.at[pl.ds(CAP, 16), pl.ds(0, CAP)], ids.at[spot], sems.at[spot])
+        for spot, part in enumerate(parts)
+    ]
 
 
 def feed_copies(packed, feed, sems):
@@ -82,16 +88,16 @@
 
 
 def feed_kernel(*refs):
-    x_parts, c_parts, packed = refs[:7], refs[7:14], refs[14]
-    hidden, grads, far, near = refs[15:19]
-    x, c, feed, down, x_sems, c_sems, f_sems, d_sems = refs[19:]
+    x_parts, c_parts, packed = refs[:8], refs[8:16], refs[16]
+    hidden, grads, far, near = refs[17:21]
+    x, c, feed, down, x_sems, c_sems, f_sems, d_sems = refs[21:]
     step = pl.program_id(0)
 
     @pl.when(step == 0)
     def _():
-        first = part_copies(x_parts, x, x_sems)
+        first = block_copies(x_parts, x, x_sems)
         second = feed_copies(packed, feed, f_sems)
-        third = part_copies(c_parts, c, c_sems)
+        third = block_copies(c_parts, c, c_sems)
         fourth = down_copies(packed, down, d_sems)
         for group in (first, second, third, fourth):
             for copy in group:
@@ -106,7 +112,7 @@
 
     @pl.when(step == 0)
     def _():
-        third = part_copies(c_parts, c, c_sems)
+        third = block_copies(c_parts, c, c_sems)
         fourth = down_copies(packed, down, d_sems)
         for copy in third + fourth:
             copy.wait()
@@ -135,7 +141,7 @@
     return pl.pallas_call(
         feed_kernel,
         grid=(4,),
-        in_specs=[ANY] * 15,
+        in_specs=[HBM] * 17,
         out_specs=[
             pl.BlockSpec((256, WIDE), row),
             pl.BlockSpec((256, 2 * WIDE), row),
@@ -153,12 +159,12 @@
             pltpu.VMEM((1024, D), BF16),
             pltpu.VMEM((D, 2 * WIDE), BF16),
             pltpu.VMEM((WIDE, D), BF16),
-            pltpu.SemaphoreType.DMA((7,)),
-            pltpu.SemaphoreType.DMA((7,)),
+            pltpu.SemaphoreType.DMA((8,)),
+            pltpu.SemaphoreType.DMA((8,)),
             pltpu.SemaphoreType.DMA((32,)),
             pltpu.SemaphoreType.DMA((64,)),
         ],
-        compiler_params=pltpu.CompilerParams(vmem_limit_bytes=50 * 1024 * 1024),
+        compiler_params=pltpu.CompilerParams(vmem_limit_bytes=60 * 1024 * 1024),
         cost_estimate=pl.CostEstimate(
             flops=2 * 1024 * D * WIDE * 5, bytes_accessed=28 * 2**20, transcendentals=1024 * WIDE
         ),
@@ -166,11 +172,11 @@
 
 
 def grads_kernel(*refs):
-    x_parts, c_parts, hidden_hbm, grads_hbm = refs[:7], refs[7:14], refs[14], refs[15]
-    out = refs[16]
-    x, c, hidden, grads, pack, x_sems, c_sems, in_sems, sems = refs[17:]
-    first = part_copies(x_parts, x, x_sems)
-    second = part_copies(c_parts, c, c_sems)
+    x_parts, c_parts, hidden_hbm, grads_hbm = refs[:8], refs[8:16], refs[16], refs[17]
+    out = refs[18]
+    x, c, hidden, grads, pack, x_sems, c_sems, in_sems, sems = refs[19:]
+    first = block_copies(x_parts, x, x_sems)
+    second = block_copies(c_parts, c, c_sems)
     loads = [
         pltpu.make_async_copy(grads_hbm, grads, in_sems.at[0]),
         pltpu.make_async_copy(hidden_hbm, hidden, in_sems.at[1]),
@@ -215,8 +221,8 @@
 def feed_grads(x_parts, c_parts, hidden, grads):
     return pl.pallas_call(
         grads_kernel,
-        in_specs=[ANY] * 16,
-        out_specs=ANY,
+        in_specs=[HBM] * 18,
+        out_specs=HBM,
         out_shape=jax.ShapeDtypeStruct((3072, 1536), BF16),
         scratch_shapes=[
             pltpu.VMEM((1024, D), BF16),
@@ -224,16 +230,41 @@
             pltpu.VMEM((1024, WIDE), BF16),
             pltpu.VMEM((1024, 2 * WIDE), BF16),
             pltpu.VMEM((3072, 2 * WIDE), BF16),
-            pltpu.SemaphoreType.DMA((7,)),
-            pltpu.SemaphoreType.DMA((7,)),
+            pltpu.SemaphoreType.DMA((8,)),
+            pltpu.SemaphoreType.DMA((8,)),
             pltpu.SemaphoreType.DMA((2,)),
             pltpu.SemaphoreType.DMA((48,)),
         ],
-        compiler_params=pltpu.CompilerParams(vmem_limit_bytes=50 * 1024 * 1024),
+        compiler_params=pltpu.CompilerParams(vmem_limit_bytes=60 * 1024 * 1024),
         cost_estimate=pl.CostEstimate(
             flops=2 * 1024 * D * WIDE * 3, bytes_accessed=22 * 2**20, transcendentals=0
         ),
     )(*x_parts, *c_parts, hidden, grads)
+
+
+def output_kernel(hidden, packed, far, near, down, sems):
+    copies = down_copies(packed, down, sems)
+    for copy in copies:
+        copy.start()
+    for copy in copies:
+        copy.wait()
+    far[...] = dot_nn(hidden[512:], down[...]).astype(BF16)
+    near[...] = dot_nn(hidden[:512], down[...])
+
+
+def output_product(hidden, packed):
+    whole = pl.BlockSpec(memory_space=pltpu.VMEM)
+    return pl.pallas_call(
+        output_kernel,
+        in_specs=[whole, HBM],
+        out_specs=[whole, whole],
+        out_shape=[jax.ShapeDtypeStruct((512, D), BF16), jax.ShapeDtypeStruct((512, D), F32)],
+        scratch_shapes=[pltpu.VMEM((WIDE, D), BF16), pltpu.SemaphoreType.DMA((64,))],
+        compiler_params=pltpu.CompilerParams(vmem_limit_bytes=60 * 1024 * 1024),
+        cost_estimate=pl.CostEstimate(
+            flops=2 * 1024 * D * WIDE, bytes_accessed=11 * 2**20, transcendentals=0
+        ),
+    )(hidden, packed)
 
 
 def rotary_table():
@@ -251,32 +282,6 @@
     return jnp.asarray(np.stack([high, rest]))
 
 
-def id_copies(parts, ids, sems):
-    copies, spot = [], 0
-    for k, part in enumerate(parts):
-        for j in range(part.shape[0] // 144):
-            copies.append(
-                pltpu.make_async_copy(
-                    part.at[pl.ds(144 * j + CAP, 16), pl.ds(0, CAP)], ids.at[spot], sems.at[spot]
-                )
-            )
-            spot += 1
-    return copies
-
-
-def long_copies(parts, whole, sems):
-    copies, spot = [], 0
-    for part in parts:
-        for j in range(part.shape[0] // 144):
-            copies.append(
-                pltpu.make_async_copy(
-                    part.at[pl.ds(144 * j, CAP)], whole.at[pl.ds(CAP * spot, CAP)], sems.at[spot]
-                )
-            )
-            spot += 1
-    return copies
-
-
 def lane_of(shape, dim):
     return lax.broadcasted_iota(jnp.int32, shape, dim)
 
@@ -319,18 +324,16 @@
 
 
 def attend_kernel(*refs):
-    parts, table, w_hbm, o_hbm = refs[:7], refs[7], refs[8], refs[9]
-    queries, key_values, mixed, far, near = refs[10:15]
-    x, ids, w, o, x_sems, i_sems, w_sems = refs[15:]
+    parts, table, w_hbm, o_hbm = refs[:8], refs[8], refs[9], refs[10]
+    queries, key_values, mixed, far, near = refs[11:16]
+    x, ids, w, o, x_sems, i_sems, w_sems = refs[16:]
     step = pl.program_id(0)
-    loads = [
-        pltpu.make_async_copy(w_hbm, w, w_sems.at[0]),
-        pltpu.make_async_copy(o_hbm, o, w_sems.at[1]),
-    ]
 
     @pl.when(step == 0)
     def _():
-        copies = long_copies(parts, x, x_sems) + id_copies(parts, ids, i_sems) + loads
+        copies = block_copies(parts, x, x_sems) + id_copies(parts, ids, i_sems)
+        copies.append(pltpu.make_async_copy(w_hbm, w, w_sems.at[0]))
+        copies.append(pltpu.make_async_copy(o_hbm, o, w_sems.at[1]))
         for copy in copies:
             copy.start()
         for copy in copies:
@@ -368,7 +371,7 @@
     return pl.pallas_call(
         attend_kernel,
         grid=(2,),
-        in_specs=[ANY] * 7 + [pl.BlockSpec((2, CAP, 1152), lambda i: (0, 0, 0))] + [ANY] * 2,
+        in_specs=[HBM] * 8 + [pl.BlockSpec((2, CAP, 1152), lambda i: (0, 0, 0))] + [HBM] * 2,
         out_specs=[
             pl.BlockSpec((512, 256), row),
             pl.BlockSpec((512, CAP), row),
@@ -392,7 +395,7 @@
             pltpu.SemaphoreType.DMA((8,)),
             pltpu.SemaphoreType.DMA((2,)),
         ],
-        compiler_params=pltpu.CompilerParams(vmem_limit_bytes=40 * 1024 * 1024),
+        compiler_params=pltpu.CompilerParams(vmem_limit_bytes=26 * 1024 * 1024),
         cost_estimate=pl.CostEstimate(
             flops=2 * 1024 * D * 640 * 2, bytes_accessed=15 * 2**20, transcendentals=2**19
         ),
@@ -400,17 +403,10 @@
 
 
 def attend_back_kernel(*refs):
-    parts, id_parts, table, w_hbm, o_hbm, queries, key_values = (
-        refs[:7],
-        refs[7:14],
-        refs[14],
-        refs[15],
-        refs[16],
-        refs[17],
-        refs[18],
-    )
-    grads, far, near = refs[19:22]
-    g, ids, w, o, g_sems, i_sems, w_sems = refs[22:]
+    parts, id_parts, table = refs[:8], refs[8:16], refs[16]
+    w_hbm, o_hbm, queries, key_values = refs[17:21]
+    grads, far, near = refs[21:24]
+    g, ids, w, o, g_sems, i_sems, w_sems = refs[24:]
     step = pl.program_id(0)
     loads = [
         pltpu.make_async_copy(w_hbm, w, w_sems.at[0]),
@@ -419,7 +415,7 @@
 
     @pl.when(step == 0)
     def _():
-        copies = part_copies(parts, g, g_sems) + id_copies(id_parts, ids, i_sems) + loads
+        copies = block_copies(parts, g, g_sems) + id_copies(id_parts, ids, i_sems) + loads
         for copy in copies:
             copy.start()
         for copy in copies:
@@ -463,18 +459,17 @@
 
 def attend_back(parts, id_parts, table, qkv_full, out_full, queries, key_values):
     row = lambda i: (1 - i, 0)
-    still = lambda i: (0, 0)
     return pl.pallas_call(
         attend_back_kernel,
         grid=(2,),
-        in_specs=[ANY] * 14
+        in_specs=[HBM] * 16
         + [pl.BlockSpec((2, CAP, 1152), lambda i: (0, 0, 0))]
-        + [ANY] * 2
+        + [HBM] * 2
         + [pl.BlockSpec((512, 256), row), pl.BlockSpec((512, CAP), row)],
         out_specs=[
             pl.BlockSpec((512, 384), row),
-            pl.BlockSpec((512, D), still),
-            pl.BlockSpec((512, D), still),
+            pl.BlockSpec((512, D), lambda i: (0, 0)),
+            pl.BlockSpec((512, D), lambda i: (0, 0)),
         ],
         out_shape=[
             jax.ShapeDtypeStruct((1024, 384), BF16),
@@ -486,11 +481,11 @@
             pltpu.VMEM((8, 16, CAP), BF16),
             pltpu.VMEM((D, 384), BF16),
             pltpu.VMEM((256, D), BF16),
-            pltpu.SemaphoreType.DMA((7,)),
+            pltpu.SemaphoreType.DMA((8,)),
             pltpu.SemaphoreType.DMA((8,)),
             pltpu.SemaphoreType.DMA((2,)),
         ],
-        compiler_params=pltpu.CompilerParams(vmem_limit_bytes=40 * 1024 * 1024),
+        compiler_params=pltpu.CompilerParams(vmem_limit_bytes=28 * 1024 * 1024),
         cost_estimate=pl.CostEstimate(
             flops=2 * 1024 * D * 640 * 2, bytes_accessed=15 * 2**20, transcendentals=2**19
         ),
@@ -498,11 +493,10 @@
 
 
 def small_grads_kernel(*refs):
-    x_parts, g_parts, mixed_hbm, grads_hbm = refs[:7], refs[7:14], refs[14], refs[15]
-    qkv_term, out_term = refs[16:18]
-    x, g, mixed, grads, x_sems, g_sems, in_sems = refs[18:]
-    first = long_copies(x_parts, x, x_sems)
-    second = part_copies(g_parts, g, g_sems)
+    x_parts, g_parts, mixed_hbm, grads_hbm = refs[:8], refs[8:16], refs[16], refs[17]
+    pack, x, g, mixed, grads, x_sems, g_sems, in_sems = refs[18:]
+    first = block_copies(x_parts, x, x_sems)
+    second = block_copies(g_parts, g, g_sems)
     loads = [
         pltpu.make_async_copy(grads_hbm, grads, in_sems.at[0]),
         pltpu.make_async_copy(mixed_hbm, mixed, in_sems.at[1]),
@@ -512,30 +506,34 @@
     for copy in first + loads[:1]:
         copy.wait()
     for k in range(8):
-        here = slice(256 * k, 256 * (k + 1))
-        qkv_term[here, :] = dot_tn(x[:, here], grads[...]).astype(BF16)
+        tile = dot_tn(x[:, 256 * k : 256 * (k + 1)], grads[...]).astype(BF16)
+        row = 128 * (k % 4) + 64 * (k // 4)
+        for j in range(4):
+            pack[j, row : row + 64, :384] = tile[64 * j : 64 * (j + 1)]
     for copy in second + loads[1:]:
         copy.wait()
-    out_term[...] = dot_tn(mixed[...], g[...]).astype(BF16)
+    for k in range(8):
+        tile = dot_tn(mixed[...], g[:, 256 * k : 256 * (k + 1)]).astype(BF16)
+        for j in range(4):
+            pack[j, 64 * k : 64 * (k + 1), 384:] = tile[64 * j : 64 * (j + 1)]
 
 
 def small_grads(x_parts, g_parts, mixed, grads):
-    whole = pl.BlockSpec(memory_space=pltpu.VMEM)
     return pl.pallas_call(
         small_grads_kernel,
-        in_specs=[ANY] * 16,
-        out_specs=[whole, whole],
-        out_shape=[jax.ShapeDtypeStruct((D, 384), BF16), jax.ShapeDtypeStruct((256, D), BF16)],
+        in_specs=[HBM] * 18,
+        out_specs=pl.BlockSpec(memory_space=pltpu.VMEM),
+        out_shape=jax.ShapeDtypeStruct((4, 512, 640), BF16),
         scratch_shapes=[
             pltpu.VMEM((1024, D), BF16),
             pltpu.VMEM((1024, D), BF16),
             pltpu.VMEM((1024, 256), BF16),
             pltpu.VMEM((1024, 384), BF16),
             pltpu.SemaphoreType.DMA((8,)),
-            pltpu.SemaphoreType.DMA((7,)),
+            pltpu.SemaphoreType.DMA((8,)),
             pltpu.SemaphoreType.DMA((2,)),
         ],
-        compiler_params=pltpu.CompilerParams(vmem_limit_bytes=40 * 1024 * 1024),
+        compiler_params=pltpu.CompilerParams(vmem_limit_bytes=60 * 1024 * 1024),
         cost_estimate=pl.CostEstimate(
             flops=2 * 1024 * D * 640, bytes_accessed=12 * 2**20, transcendentals=0
         ),
@@ -576,29 +574,25 @@
     return lax.ppermute(item, axis, SWAP)
 
 
-STEPS = (0, 1, 3, 2)
-
-
-def share_parts(item):
-    one, three, two = (from_ring(item, step) for step in (1, 3, 2))
+def share_parts(item, *first):
     own = swap(item, "c")
-    near = swap(jnp.concatenate([one, three], axis=0), "c")
-    far = swap(two, "c")
-    return [item, one, three, two, own, near, far]
-
-
-def pair_sum(far, near):
-    return near + swap(far, "c").astype(F32)
-
-
-def ring_sum(near):
-    total = near[:CAP]
-    sent = [
-        to_ring(near[spot * CAP : (spot + 1) * CAP].astype(BF16), STEPS[spot]) for spot in (1, 2, 3)
-    ]
-    for item in sent:
-        total = total + item.astype(F32)
-    return total
+    ring = after(tuple(from_ring(item, step) for step in STEPS[1:]), *first)
+    return [item, *ring, own] + [swap(part, "c") for part in ring]
+
+
+def pair_blocks(near, far, *first):
+    far = after(swap(far, "c"), *first)
+
+    def block(spot):
+        here = slice(spot * CAP, (spot + 1) * CAP)
+        return near[here] + far[here].astype(F32)
+
+    return (block(0),) + tuple(block(spot).astype(BF16) for spot in (1, 2, 3))
+
+
+def ring_sum(blocks, *first):
+    came = tuple(to_ring(blocks[spot], STEPS[spot]) for spot in (1, 2, 3))
+    return blocks[0] + sum(item.astype(F32) for item in after(came, *first))
 
 
 def spread_columns(chunks, xl, c):
@@ -619,25 +613,6 @@
     return jnp.stack([jnp.where(xl == 0, kept, came), jnp.where(xl == 0, came, kept)])
 
 
-def return_columns(item, xh, xl, c, reduce):
-    rows = item.shape[1] // 2
-    mine = jnp.where(c == 0, item[:, :rows], item[:, rows:])
-    came = swap(jnp.where(c == 0, item[:, rows:], item[:, :rows]), "c")
-    both = reduce(jnp.where(c == 0, mine, came), jnp.where(c == 0, came, mine))
-    here = jnp.where(xl == 0, both[0], both[1])
-    there = jnp.where(xl == 0, both[1], both[0])
-    parts = [here, to_ring(there, 1), to_ring(here, 2), to_ring(there, 3)]
-    spot = 2 * xh + xl
-    stacked = jnp.stack(parts)
-    return [
-        [
-            lax.dynamic_index_in_dim(stacked, (spot - (2 * h + k)) % 4, 0, keepdims=False)
-            for h in range(2)
-        ]
-        for k in range(2)
-    ]
-
-
 def gather_four(item, axis, spot, dim):
     parts = [item]
     for step in (1, 2, 3):
@@ -652,12 +627,21 @@
     return out
 
 
-def scatter_four(item, axis, spot, dim):
-    total = lax.dynamic_index_in_dim(item, spot, dim, keepdims=False).astype(F32)
-    for step in (1, 2, 3):
-        sent = lax.dynamic_index_in_dim(item, (spot + step) % 4, dim, keepdims=False)
-        total = total + lax.ppermute(sent, axis, [(i, (i + step) % 4) for i in range(4)]).astype(F32)
-    return total
+def four_pieces(item, spot, dim):
+    return [
+        lax.dynamic_index_in_dim(item, (spot + step) % 4, dim, keepdims=False) for step in range(4)
+    ]
+
+
+def exchange(pieces, axis):
+    return tuple(
+        lax.ppermute(pieces[step], axis, [(i, (i + step) % 4) for i in range(4)])
+        for step in (1, 2, 3)
+    )
+
+
+def four_sum(pieces, came):
+    return pieces[0].astype(F32) + sum(item.astype(F32) for item in came)
 
 
 def row_pairs(step, back):
@@ -672,7 +656,7 @@
 
 
 def after(item, *others):
-    return lax.optimization_barrier((item,) + others)[0]
+    return lax.optimization_barrier((item,) + others)[0] if others else item
 
 
 def order_of_columns(xh):
@@ -726,17 +710,18 @@
         for k in range(2)
     ]
     spread = spread_columns(chunks, xl, c)
-    qkv_full = gather_four(gather_four(spread, "z", z, 1), "y", y, 1).reshape(D, 384)
 
     source = 2 * xh + c
     came = swap(out_weight, "c")
     head = jnp.concatenate(
         [jnp.where(c == 0, out_weight, came), jnp.where(c == 0, came, out_weight)], axis=0
     )
-    parts = [head]
+    lines = [head]
     for step in (1, 2, 3):
-        parts.append(lax.ppermute(head, ("xh", "y", "c"), row_pairs(step, False)))
-    out_full = gather_four(pick(parts, (y - source) % 4), "z", z, 0).reshape(256, D)
+        lines.append(lax.ppermute(head, ("xh", "y", "c"), row_pairs(step, False)))
+    head = pick(lines, (y - source) % 4)
+    out_full = gather_four(head, "z", z, 0).reshape(256, D)
+    qkv_full = lax.all_gather(spread, ("y", "z"), axis=1, tiled=True).reshape(D, 384)
 
     wide = jnp.stack([scaled(gate_weight, second_col), scaled(up_weight, second_col)])
     blocks = jnp.concatenate([wide[:, :, 1408 * k : 1408 * (k + 1)] for k in range(4)], axis=0)
@@ -761,73 +746,127 @@
     corner = jnp.concatenate(
         [down_half[16 * k : 16 * (k + 1), 2 * WIDE :] for k in range(3)], axis=1
     )
-    spread = spread_columns(chunks, xl, c).reshape(128, 2 * WIDE)
-    packed = jnp.concatenate([spread, down_half[:, : 2 * WIDE], corner], axis=0)
-    packed = lax.all_gather(packed, ("y", "z"), axis=0, tiled=True)
+    feed_spread = spread_columns(chunks, xl, c).reshape(128, 2 * WIDE)
+    packed = jnp.concatenate([feed_spread, down_half[:, : 2 * WIDE], corner], axis=0)
 
     table = rotary_table()
     rows = tokens.astype(F32)
     first_scale = rms_scale(rows)
     id_rows = jnp.pad(doc_ids.astype(BF16)[None], ((0, 15), (0, D - CAP)))
-    normed = share_parts(jnp.concatenate([(rows * first_scale).astype(BF16), id_rows], axis=0))
-    upstream = share_parts(after(cotangent, *normed[1:4]))
-    queries, key_values, mixed, far, near = attend(normed, table, qkv_full, out_full)
-    midway = rows + ring_sum(pair_sum(far, near))
+    payload = jnp.concatenate([(rows * first_scale).astype(BF16), id_rows], axis=0)
+    first = share_parts(after(payload, spread, feed_spread))
+    packed = after(packed, qkv_full, out_full, *first[1:4])
+    packed = lax.all_gather(packed, ("y", "z"), axis=0, tiled=True)
+
+    queries, key_values, mixed, far, near = attend(first, table, qkv_full, out_full)
+    shuffle = jnp.concatenate([order_of_columns(0), order_of_columns(1)], axis=1)
+    upstream = share_parts(after(cotangent, *first[1:4]), mixed)
+    far = after(far, upstream[1])
+    midway = rows + ring_sum(pair_blocks(near, far), shuffle)
 
     second_scale = rms_scale(midway)
-    normed_two = share_parts((midway * second_scale).astype(BF16))
-    hidden, grad_feed, far, near = feed_forward(normed_two, upstream, packed)
-    inner_two = ring_sum(pair_sum(far, near))
+    second = share_parts((midway * second_scale).astype(BF16))
+    hidden, grad_feed, far, near = feed_forward(second, upstream, packed)
+    blocks = pair_blocks(near, far)
+    pack = feed_grads(second, upstream, after(hidden, *blocks), grad_feed)
+    inner_two = ring_sum(blocks, pack)
     grad_mid = cotangent.astype(F32) + norm_back(midway, second_scale, inner_two)
-    grad_attn = share_parts(grad_mid.astype(BF16))
-
-    pack = feed_grads(normed_two, upstream, hidden, grad_feed)
-    pack = lax.psum_scatter(pack, ("y", "z"), scatter_dimension=0, tiled=True)
-    feed_part = pack[:128].reshape(2, 64, 2 * WIDE)
-    corner = pack[176:]
-    corner = jnp.concatenate([corner[:, 512 * k : 512 * (k + 1)] for k in range(3)], axis=0)
+    out_far, out_near = output_product(after(hidden, pack), packed)
+    third = share_parts(grad_mid.astype(BF16), out_far)
+    pack = lax.psum_scatter(after(pack, inner_two), ("y", "z"), scatter_dimension=0, tiled=True)
+
+    out_blocks = pair_blocks(out_near, out_far)
+    grad_qkv, far, near = attend_back(
+        third, first, table, qkv_full, out_full, after(queries, *out_blocks), key_values
+    )
+    product = ring_sum(out_blocks, grad_qkv)
+    output = (midway + product).astype(BF16)
+
+    terms = small_grads(first, third, mixed, grad_qkv)
+    blocks = pair_blocks(near, after(far, product), terms)
+    sent = four_pieces(after(terms, *blocks), z, 0)
+    came = exchange(sent, "z")
+    ring_came = (to_ring(blocks[1], STEPS[1]), to_ring(blocks[2], STEPS[2]))
+    came, ring_came = lax.optimization_barrier((came, ring_came))
+    terms = four_sum(sent, came).astype(BF16)
+    head = jnp.concatenate(
+        [
+            jnp.concatenate([terms[64 * k : 64 * (k + 1), 384:] for k in range(h, h + 4)], axis=1)
+            for h in (0, 4)
+        ],
+        axis=0,
+    )
+    lines = terms[:, :384].reshape(4, 128, 384)
+    sent = [jnp.concatenate([item, head], axis=1) for item in four_pieces(lines, y, 0)]
+    came = exchange(sent, "y")
+    last_came = to_ring(after(blocks[3], *ring_came), STEPS[3])
+    corner = jnp.concatenate([pack[176:, 512 * k : 512 * (k + 1)] for k in range(3)], axis=0)
     down_part = jnp.concatenate([pack[128:176], corner], axis=1)
-
-    blocks = packed.reshape(16, 192, 2 * WIDE)
-    corner = jnp.concatenate(
-        [blocks[:, 176:, 512 * k : 512 * (k + 1)] for k in range(3)], axis=1
-    )
-    down_full = jnp.concatenate([blocks[:, 128:176], corner], axis=2).reshape(WIDE, D)
-    out_sum = pair_sum(times(hidden[512:], down_full).astype(BF16), times(hidden[:512], down_full))
-    output = (midway + ring_sum(after(out_sum, *grad_attn[1:4]))).astype(BF16)
-
-    grad_qkv, far, near = attend_back(
-        grad_attn, normed, table, qkv_full, out_full, queries, key_values
-    )
-    inner_one = ring_sum(pair_sum(far, near))
+    down_other = swap(after(down_part, *ring_came), "xh")
+    came, last_came, down_other = lax.optimization_barrier((came, last_came, down_other))
+    total = four_sum(sent, came).astype(BF16)
+    qkv_part = total[:, :384].reshape(2, 64, 384)
+    out_part = jnp.concatenate([total[:64, 384:], total[64:, 384:]], axis=1)
+    inner_one = blocks[0] + sum(item.astype(F32) for item in ring_came + (last_came,))
     tokens_grad = grad_mid + norm_back(rows, first_scale, inner_one)
-    qkv_term, out_term = small_grads(normed, grad_attn, mixed, grad_qkv)
-    qkv_part = scatter_four(qkv_term.reshape(2, 4, 4, 64, 384), "y", y, 1).astype(BF16)
-    qkv_part = scatter_four(qkv_part, "z", z, 1).astype(BF16)
-    out_part = scatter_four(out_term.reshape(4, 64, D), "z", z, 0)
-
-    def with_pair(zero, one):
-        pair = zero[:, :, 256:].astype(F32) + one[:, :, 256:].astype(F32)
-        return jnp.concatenate([zero[:, :, :256], one[:, :, :256], pair.astype(BF16)], axis=2)
-
-    parts = return_columns(qkv_part, xh, xl, c, with_pair)
+    down_grad = jnp.concatenate(
+        [
+            jnp.where(xh == 0, down_part, down_other)[:44],
+            jnp.where(xh == 0, down_other, down_part)[:44],
+        ],
+        axis=0,
+    ).astype(F32)
+
+    wide = jnp.concatenate([pack[:128].reshape(2, 64, 2 * WIDE), qkv_part], axis=2)
+    low, high = wide[:, :32], wide[:, 32:]
+    away = jnp.where(c == 0, out_part[32:], out_part[:32])
+    sent = jnp.concatenate(
+        [
+            jnp.where(c == 0, high, low).reshape(64, 1920),
+            jnp.concatenate([away[:, :1024], away[:, 1024:]], axis=0),
+        ],
+        axis=1,
+    )
+    came = swap(sent, "c")
+    mine, other = jnp.where(c == 0, low, high), came[:, :1920].reshape(2, 32, 1920)
+    zero, one = jnp.where(c == 0, mine, other), jnp.where(c == 0, other, mine)
+    pair = zero[:, :, 1792:].astype(F32) + one[:, :, 1792:].astype(F32)
+    both = jnp.concatenate(
+        [
+            zero[:, :, :1536],
+            one[:, :, :1536],
+            zero[:, :, 1536:1792],
+            one[:, :, 1536:1792],
+            pair.astype(BF16),
+        ],
+        axis=2,
+    )
+    out_half = jnp.where(
+        y % 2 == c,
+        jnp.where(c == 0, out_part[:32], out_part[32:]),
+        jnp.concatenate([came[:32, 1920:], came[32:, 1920:]], axis=1),
+    )
+    here = jnp.where(xl == 0, both[0], both[1])
+    there = jnp.where(xl == 0, both[1], both[0])
+    across = to_ring(jnp.concatenate([here, out_half], axis=1), 2)
+    came = after((to_ring(there, 1), across, to_ring(there, 3)))
+    stacked = [here, came[0], came[1][:, :3712], came[2]]
+    spot = 2 * xh + xl
+    parts = [[pick(stacked, (spot - (2 * h + k)) % 4) for h in range(2)] for k in range(2)]
+    out_grad = jnp.where(y // 2 == xh, out_half, came[1][:, 3712:]).astype(F32)
 
     def joined(start, end):
         return jnp.concatenate(
             [parts[k][h][:, start:end] for k in range(2) for h in range(2)], axis=1
         ).astype(F32)
 
-    query_raw, key_raw, value_raw = joined(0, 512), joined(512, 576), joined(576, 640)
+    query_raw, key_raw, value_raw = joined(3072, 3584), joined(3584, 3648), joined(3648, 3712)
     first_grad = (
         jnp.sum(query_raw * query_weight.astype(F32), axis=1)
         + jnp.sum(key_raw * key_weight.astype(F32), axis=1)
         + jnp.sum(value_raw * value_weight.astype(F32), axis=1)
     )
 
-    parts = return_columns(
-        feed_part, xh, xl, c, lambda zero, one: jnp.concatenate([zero, one], axis=2)
-    )
-    shuffle = jnp.concatenate([order_of_columns(0), order_of_columns(1)], axis=1)
     rows_of = []
     for item in range(2):
         for k in range(2):
@@ -850,21 +889,6 @@
         up_raw * up_weight.astype(F32), axis=1
     )
 
-    came = swap(down_part, "xh")
-    down_grad = jnp.concatenate(
-        [jnp.where(xh == 0, down_part, came)[:44], jnp.where(xh == 0, came, down_part)[:44]], axis=0
-    ).astype(F32)
-
-    sent = out_part.astype(BF16)
-    for step in (1, 2, 3):
-        out_part = out_part + lax.ppermute(sent, ("xh", "y", "c"), row_pairs(step, True)).astype(F32)
-    out_part = out_part.astype(BF16)
-    low, high = out_part[:32], out_part[32:]
-    came = swap(jnp.where(c == 0, high, low), "c")
-    owned = jnp.where(y % 2 == c, jnp.where(c == 0, low, high), came)
-    came = swap(owned, "xh")
-    out_grad = jnp.where(y // 2 == xh, owned, came).astype(F32)
-
     return (
         output,
         tokens_grad,

time: 457 us -> 428 us (0.937)
  starting transfers between devices: 128 us -> 91.3 us
  other arithmetic: 28.5 us -> 44.8 us
  Pallas kernels: 84.9 us -> 95 us
  waiting for transfers between devices: 166 us -> 157 us
  matrix products: 9.3 us -> 2.48 us
  local copies, waits for them, and re-layouts: 19 us -> 13.6 us
    ppermute x12, waiting for transfers between devices: 41.8 us -> 63.7 us  [from_ring(): return lax.ppermute(item, RING, [(i, (i - step) % 4) for i in range(4)])]
    convert_element_type x10 -> x11, other arithmetic: 5.14 us -> 19.5 us  [the longest x4 10.3 us: pair_blocks(): return (block(0),) + tuple((block(spot).astype(BF16) for spot in (1, 2, 3)))]
    ppermute x9 -> x3, waiting for transfers between devices: 14 us -> 0.01 us  [gather_four(): lax.ppermute(item, axis, [(i, (i - step) % 4) for i in range(4)])]
    ppermute x18 -> x15, waiting for transfers between devices: 69 us -> 55.2 us  [to_ring(): return lax.ppermute(item, RING, [(i, (i + step) % 4) for i in range(4)])]
    ppermute x9 -> x3, starting transfers between devices: 18.6 us -> 5.81 us  [gather_four(): lax.ppermute(item, axis, [(i, (i - step) % 4) for i in range(4)])]
    ppermute x26 -> x27, starting transfers between devices: 47.4 us -> 34.6 us  [swap(): return lax.ppermute(item, axis, SWAP)]
    pallas_call x5 -> x6, Pallas kernels: 84.9 us -> 95 us  [the longest x1 31.4 us: feed_forward(): pl.pallas_call(feed_kernel, grid=(4,), in_specs=[HBM] * 17, out_specs=[pl...]
    ppermute x15 -> x9, starting transfers between devices: 19.4 us -> 9.82 us  [the longest x6 7.17 us: exchange(): lax.ppermute(pieces[step], axis, [(i, (i + step) % 4) for i in range(4)])]
  transfers between devices with their start and end apart: 82 -> 69, of which waited for: 33 -> 24; matrix products, arithmetic and copies ran while one was open for 8% -> 8% of each run, Pallas kernels for 8% -> 15%
where the time goes in v4:
time: 428 us; the launch traced here: 420 us
  waiting for transfers between devices  157 us (37%)
  Pallas kernels  95 us (22%)
  starting transfers between devices  91.3 us (21%)
  other arithmetic  44.8 us (10%)
  between operations  15.6 us (4%)
  local copies, waits for them, and re-layouts  13.6 us (3%)
    ppermute x12, waiting for transfers between devices, from_ring(): return lax.ppermute(item, RING, [(i, (i - step) % 4) for i in range(4)])  63.7 us
    ppermute x15, waiting for transfers between devices, to_ring(): return lax.ppermute(item, RING, [(i, (i + step) % 4) for i in range(4)])  55.2 us
    ppermute x27, starting transfers between devices, swap(): return lax.ppermute(item, axis, SWAP)  34.6 us
    pallas_call x1, Pallas kernels, feed_forward(): pl.pallas_call(feed_kernel, grid=(4,), in_specs=[HBM] * 17, out_specs=[pl...  31.4 us
    ppermute x12, starting transfers between devices, from_ring(): return lax.ppermute(item, RING, [(i, (i - step) % 4) for i in range(4)])  24.1 us
    ppermute x6, waiting for transfers between devices, exchange(): lax.ppermute(pieces[step], axis, [(i, (i + step) % 4) for i in range(4)])  23.7 us
    ppermute x15, starting transfers between devices, to_ring(): return lax.ppermute(item, RING, [(i, (i + step) % 4) for i in range(4)])  16.9 us
    pallas_call x1, Pallas kernels, attend_back(): pl.pallas_call(attend_back_kernel, grid=(2,), in_specs=[HBM] * 16 + [pl.B...  16.3 us
  transfers between devices with their start and end apart: 69, of which 24 were waited for; matrix products, arithmetic and copies ran while one was open for 8% of the time, Pallas kernels for 15%

profile of v4, /device:TPU:1, one launch (start us, length us, event | category | flops | bytes accessed | tf_op | source)
XLA Modules:
  0.0 420.0 jit_solution(5729325013439694214)
XLA Ops:
  32.0 9.7 %collective-permute-start.4 = (bf16[144,2048]{1,0:T(8,128)(2,1)S(1)}, bf16[144,2048]{1,0:T(8,128)(2,1)S(1)}, u32[]{:S(2)}, u32[]{:S(2)}) collective-permute-start(bf16[144,2048]{1,0:T(8,128)(2,1)S(1)} %fusion.20.refs_0_.refs_8_), channel_id=1, source_target_pairs={{0,96},{32,0},{64,32},{96,64},{1,97},{33,1},{65,33},{97,65},{2,98}... | collective-permute-start | bytes 1769480 | tf_op jit(solution)/shard_map/ppermute | solution.py:566
  42.6 3.5 collective-permute-start.6
  46.3 21.2 %collective-permute-done.4.refs_1_.refs_9_ = bf16[144,2048]{1,0:T(8,128)(2,1)S(1)} collective-permute-done((bf16[144,2048]{1,0:T(8,128)(2,1)S(1)}, bf16[144,2048]{1,0:T(8,128)(2,1)S(1)}, u32[]{:S(2)}, u32[]{:S(2)}) %collective-permute-start.4) | collective-permute-done | bytes 589856 | tf_op jit(solution)/shard_map/ppermute | solution.py:566
  80.2 12.8 %shard_map.212 = (bf16[1024,256]{1,0:T(8,128)(2,1)S(1)}, bf16[1024,128]{1,0:T(8,128)(2,1)S(1)}, bf16[1024,256]{1,0:T(8,128)(2,1)S(1)}, bf16[512,2048]{1,0:T(8,128)(2,1)S(1)}, f32[512,2048]{1,0:T(8,128)S(1)}) custom-call(bf16[144,2048]{1,0:T(8,128)(2,1)S(1)} %fusion.20.refs_0_.refs_8_, bf16[144,2048]{1,0:T(8,128)(2,1)S(1)} %collective-permute-done.4.refs_1_.refs_9_, ...), custom_call_target="tpu_custom_call" | custom-call | flops 5368709120 | bytes 15728640 | tf_op jit(solution)/shard_map/pallas_call | solution.py:371
  93.1 5.9 %collective-permute-done.20.refs_11_ = bf16[128,2048]{1,0:T(8,128)(2,1)S(1)} collective-permute-done((bf16[128,2048]{1,0:T(8,128)(2,1)}, bf16[128,2048]{1,0:T(8,128)(2,1)S(1)}, u32[]{:S(2)}, u32[]{:S(2)}) %collective-permute-start.20) | collective-permute-done | bytes 524320 | tf_op jit(solution)/shard_map/ppermute | solution.py:566
  100.8 3.8 collective-permute-done.21
  109.0 22.1 %collective-permute-done.22 = bf16[128,2048]{1,0:T(8,128)(2,1)S(1)} collective-permute-done((bf16[128,2048]{1,0:T(8,128)(2,1)S(1)}, bf16[128,2048]{1,0:T(8,128)(2,1)S(1)}, u32[]{:S(2)}, u32[]{:S(2)}) %collective-permute-start.22) | collective-permute-done | bytes 524320 | tf_op jit(solution)/shard_map/ppermute | solution.py:570
  138.6 8.9 %collective-permute-done.25.refs_1_ = bf16[128,2048]{1,0:T(8,128)(2,1)S(1)} collective-permute-done((bf16[128,2048]{1,0:T(8,128)(2,1)S(1)}, bf16[128,2048]{1,0:T(8,128)(2,1)S(1)}, u32[]{:S(2)}, u32[]{:S(2)}) %collective-permute-start.25) | collective-permute-done | bytes 524320 | tf_op jit(solution)/shard_map/ppermute | solution.py:566
  149.3 12.7 %collective-permute-start.30 = (bf16[128,2048]{1,0:T(8,128)(2,1)S(1)}, bf16[128,2048]{1,0:T(8,128)(2,1)S(1)}, u32[]{:S(2)}, u32[]{:S(2)}) collective-permute-start(bf16[128,2048]{1,0:T(8,128)(2,1)S(1)} %collective-permute-done.26.refs_2_), channel_id=1, source_target_pairs={{0,1},{1,0},{2,3},{3,2},{4,5},{5,4},{6,7},{7,6},{8,9},{9,8},{10,11... | collective-permute-start | bytes 1572872 | tf_op jit(solution)/shard_map/ppermute | solution.py:574
  164.6 31.4 %shard_map.213 = (bf16[1024,768]{1,0:T(8,128)(2,1)}, bf16[1024,1536]{1,0:T(8,128)(2,1)}, bf16[512,2048]{1,0:T(8,128)(2,1)}, f32[512,2048]{1,0:T(8,128)}) custom-call(bf16[128,2048]{1,0:T(8,128)(2,1)} %copy-done.49, bf16[128,2048]{1,0:T(8,128)(2,1)} %copy-done.70, bf16[128,2048]{1,0:T(8,128)(2,1)} %copy-done.71, bf16[128,2048]{1,0:T(8,128)(2,1)} %copy-done.72, ...), custom_call_target="tpu_custom_call" | custom-call | flops 16106127360 | bytes 29360128 | tf_op jit(solution)/shard_map/pallas_call | solution.py:141
  196.5 4.0 collective-permute-done.36
  200.5 4.1 add_convert_fusion.7
  207.5 16.2 %shard_map.214 = bf16[3072,1536]{1,0:T(8,128)(2,1)} custom-call(bf16[128,2048]{1,0:T(8,128)(2,1)} %copy-done.49, bf16[128,2048]{1,0:T(8,128)(2,1)} %copy-done.70, bf16[128,2048]{1,0:T(8,128)(2,1)} %copy-done.71, bf16[128,2048]{1,0:T(8,128)(2,1)} %copy-done.72, bf16[128,2048]{1,0:T(8,128)(2,1)} %copy-done.74, bf16[128,2048]{1,0:T(8,128)(2,1)} %copy-done.75, ...), custom_call_target="tpu_custom_call" | custom-call | flops 9663676416 | bytes 23068672 | tf_op jit(solution)/shard_map/pallas_call | solution.py:222
  223.6 6.9 %collective-permute-done.41 = bf16[128,2048]{1,0:T(8,128)(2,1)} collective-permute-done((bf16[128,2048]{1,0:T(8,128)(2,1)}, bf16[128,2048]{1,0:T(8,128)(2,1)}, u32[]{:S(2)}, u32[]{:S(2)}) %collective-permute-start.41) | collective-permute-done | bytes 524320 | tf_op jit(solution)/shard_map/ppermute | solution.py:570
  233.9 9.5 %shard_map.215 = (bf16[512,2048]{1,0:T(8,128)(2,1)}, f32[512,2048]{1,0:T(8,128)}) custom-call(bf16[1024,768]{1,0:T(8,128)(2,1)} %get-tuple-element.81.refs_16_.hidden, bf16[3072,1536]{1,0:T(8,128)(2,1)} %all-gather.5.cloned.1.call-done.refs_16_.packed), custom_call_target="tpu_custom_call" | custom-call | flops 3221225472 | bytes 11534336 | tf_op jit(solution)/shard_map/pallas_call | solution.py:257
  252.4 20.4 %collective-permute-done.44.refs_1_.refs_9_ = bf16[128,2048]{1,0:T(8,128)(2,1)S(1)} collective-permute-done((bf16[128,2048]{1,0:T(8,128)(2,1)S(1)}, bf16[128,2048]{1,0:T(8,128)(2,1)S(1)}, u32[]{:S(2)}, u32[]{:S(2)}) %collective-permute-start.44) | collective-permute-done | bytes 524320 | tf_op jit(solution)/shard_map/ppermute | solution.py:566
  281.7 16.3 %shard_map.216 = (bf16[1024,384]{1,0:T(8,128)(2,1)S(1)}, bf16[512,2048]{1,0:T(8,128)(2,1)}, f32[512,2048]{1,0:T(8,128)S(1)}) custom-call(bf16[128,2048]{1,0:T(8,128)(2,1)S(1)} %get-tuple-element.117.refs_0_.refs_8_, bf16[128,2048]{1,0:T(8,128)(2,1)S(1)} %collective-permute-done.44.refs_1_.refs_9_, ...), custom_call_target="tpu_custom_call" | custom-call | flops 5368709120 | bytes 15728640 | tf_op jit(solution)/shard_map/pallas_call | solution.py:462
  298.9 5.8 %collective-permute-done.38 = bf16[128,2048]{1,0:T(8,128)(2,1)S(1)} collective-permute-done((bf16[128,2048]{1,0:T(8,128)(2,1)S(1)}, bf16[128,2048]{1,0:T(8,128)(2,1)S(1)}, u32[]{:S(2)}, u32[]{:S(2)}) %collective-permute-start.38) | collective-permute-done | bytes 524320 | tf_op jit(solution)/shard_map/ppermute | solution.py:570
  307.2 8.8 %shard_map.217 = bf16[4,512,640]{2,1,0:T(8,128)(2,1)} custom-call(bf16[144,2048]{1,0:T(8,128)(2,1)} %copy-done.1, bf16[144,2048]{1,0:T(8,128)(2,1)} %copy-done.4, bf16[144,2048]{1,0:T(8,128)(2,1)} %copy-done.5, bf16[144,2048]{1,0:T(8,128)(2,1)} %collective-permute-done.6.refs_3_.refs_11_, bf16[144,2048]{1,0:T(8,128)(2,1)} %copy-done.6, ...), custom_call_target="tpu_custom_call" | custom-call | flops 2684354560 | bytes 12582912 | tf_op jit(solution)/shard_map/pallas_call | solution.py:522
  317.3 5.0 %add_convert_fusion = (bf16[128,2048]{1,0:T(8,128)(2,1)}, bf16[128,2048]{1,0:T(8,128)(2,1)}, bf16[128,2048]{1,0:T(8,128)(2,1)}, f32[128,2048]{1,0:T(8,128)}) fusion(f32[512,2048]{1,0:T(8,128)} %copy-done, bf16[512,2048]{1,0:T(8,128)(2,1)} %copy-done.37), kind=kLoop, calls=%fused_computation.27 | loop fusion | flops 2883584 | bytes 8912896 | tf_op jit(solution)/shard_map/convert_element_type | solution.py:590
  331.3 10.2 %collective-permute-done.55 = bf16[128,2048]{1,0:T(8,128)(2,1)} collective-permute-done((bf16[128,2048]{1,0:T(8,128)(2,1)}, bf16[128,2048]{1,0:T(8,128)(2,1)}, u32[]{:S(2)}, u32[]{:S(2)}) %collective-permute-start.55) | collective-permute-done | bytes 524320 | tf_op jit(solution)/shard_map/ppermute | solution.py:570
  341.6 14.4 %collective-permute-done.53 = bf16[512,640]{1,0:T(8,128)(2,1)} collective-permute-done((bf16[512,640]{1,0:T(8,128)(2,1)}, bf16[512,640]{1,0:T(8,128)(2,1)}, u32[]{:S(2)}, u32[]{:S(2)}) %collective-permute-start.53) | collective-permute-done | bytes 655392 | tf_op jit(solution)/shard_map/ppermute | solution.py:638
  370.9 7.6 %collective-permute-done.59 = bf16[128,1408]{1,0:T(8,128)(2,1)} collective-permute-done((bf16[128,1408]{1,0:T(8,128)(2,1)}, bf16[128,1408]{1,0:T(8,128)(2,1)}, u32[]{:S(2)}, u32[]{:S(2)}) %collective-permute-start.59) | collective-permute-done | bytes 360480 | tf_op jit(solution)/shard_map/ppermute | solution.py:638
  394.9 9.3 %collective-permute-done.63 = bf16[32,3712]{1,0:T(8,128)(2,1)S(1)} collective-permute-done((bf16[32,3712]{1,0:T(8,128)(2,1)S(1)}, bf16[32,3712]{1,0:T(8,128)(2,1)S(1)}, u32[]{:S(2)}, u32[]{:S(2)}) %collective-permute-start.63) | collective-permute-done | bytes 237600 | tf_op jit(solution)/shard_map/ppermute | solution.py:570
  (401 shorter events, 134.0 us)
Async XLA Ops:
  7.2 63.5 %all-gather.3.cloned.1.call-start = ((), (), s32[]{:S(2)}) async-start(), calls=%async_computation.1 | async-start | bytes 1671168 | tf_op jit(solution)/shard_map/all_gather | solution.py:724
  18.6 145.9 %all-gather.5.cloned.1.call-start = ((), (), s32[]{:S(2)}) async-start(), calls=%async_computation.2 | async-start | bytes 10027008 | tf_op jit(solution)/shard_map/all_gather | solution.py:759
  32.0 35.5 %collective-permute-start.4 = (bf16[144,2048]{1,0:T(8,128)(2,1)S(1)}, bf16[144,2048]{1,0:T(8,128)(2,1)S(1)}, u32[]{:S(2)}, u32[]{:S(2)}) collective-permute-start(bf16[144,2048]{1,0:T(8,128)(2,1)S(1)} %fusion.20.refs_0_.refs_8_), channel_id=1, source_target_pairs={{0,96},{32,0},{64,32},{96,64},{1,97},{33,1},{65,33},{97,65},{2,98}... | collective-permute-start | bytes 1769480 | tf_op jit(solution)/shard_map/ppermute | solution.py:566
  41.7 29.0 %collective-permute-start.5 = (bf16[144,2048]{1,0:T(8,128)(2,1)S(1)}, bf16[144,2048]{1,0:T(8,128)(2,1)S(1)}, u32[]{:S(2)}, u32[]{:S(2)}) collective-permute-start(bf16[144,2048]{1,0:T(8,128)(2,1)S(1)} %fusion.20.refs_0_.refs_8_), channel_id=1, source_target_pairs={{0,32},{32,64},{64,96},{96,0},{1,33},{33,65},{65,97},{97,1},{2,34}... | collective-permute-start | bytes 1769480 | tf_op jit(solution)/shard_map/ppermute | solution.py:566
  42.6 28.1 %collective-permute-start.6 = (bf16[144,2048]{1,0:T(8,128)(2,1)S(1)}, bf16[144,2048]{1,0:T(8,128)(2,1)}, u32[]{:S(2)}, u32[]{:S(2)}) collective-permute-start(bf16[144,2048]{1,0:T(8,128)(2,1)S(1)} %fusion.20.refs_0_.refs_8_), channel_id=1, source_target_pairs={{0,64},{32,96},{64,0},{96,32},{1,65},{33,97},{65,1},{97,33},{2,66}... | collective-permute-start | bytes 1769480 | tf_op jit(solution)/shard_map/ppermute | solution.py:566
  70.7 293.7 %reduce-scatter.2.cloned.1.call-start = ((), (), s32[]{:S(2)}) async-start(), calls=%async_computation.3 | async-start | bytes 10027008 | tf_op jit(solution)/shard_map/reduce_scatter | solution.py:776
  105.2 25.9 %collective-permute-start.22 = (bf16[128,2048]{1,0:T(8,128)(2,1)S(1)}, bf16[128,2048]{1,0:T(8,128)(2,1)S(1)}, u32[]{:S(2)}, u32[]{:S(2)}) collective-permute-start(bf16[128,2048]{1,0:T(8,128)(2,1)S(1)} %get-tuple-element.137), channel_id=1, source_target_pairs={{0,32},{32,64},{64,96},{96,0},{1,33},{33,65},{65,97},{97,1},{2,34}... | collective-permute-start | bytes 1572872 | tf_op jit(solution)/shard_map/ppermute | solution.py:570
  105.3 26.8 %collective-permute-start.23 = (bf16[128,2048]{1,0:T(8,128)(2,1)S(1)}, bf16[128,2048]{1,0:T(8,128)(2,1)S(1)}, u32[]{:S(2)}, u32[]{:S(2)}) collective-permute-start(bf16[128,2048]{1,0:T(8,128)(2,1)S(1)} %get-tuple-element.136), channel_id=1, source_target_pairs={{0,96},{32,0},{64,32},{96,64},{1,97},{33,1},{65,33},{97,65},{2,98}... | collective-permute-start | bytes 1572872 | tf_op jit(solution)/shard_map/ppermute | solution.py:570
  108.0 27.3 %collective-permute-start.32 = (bf16[128,2048]{1,0:T(8,128)(2,1)S(1)}, bf16[128,2048]{1,0:T(8,128)(2,1)S(1)}, u32[]{:S(2)}, u32[]{:S(2)}) collective-permute-start(bf16[128,2048]{1,0:T(8,128)(2,1)S(1)} %copy-done.47), channel_id=1, source_target_pairs={{0,1},{1,0},{2,3},{3,2},{4,5},{5,4},{6,7},{7,6},{8,9},{9,8},{10,11... | collective-permute-start | bytes 1572872 | tf_op jit(solution)/shard_map/ppermute | solution.py:574
  108.9 27.6 %collective-permute-start.33 = (bf16[128,2048]{1,0:T(8,128)(2,1)S(1)}, bf16[128,2048]{1,0:T(8,128)(2,1)S(1)}, u32[]{:S(2)}, u32[]{:S(2)}) collective-permute-start(bf16[128,2048]{1,0:T(8,128)(2,1)S(1)} %collective-permute-done.18.refs_9_), channel_id=1, source_target_pairs={{0,1},{1,0},{2,3},{3,2},{4,5},{5,4},{6,7},{7,6},{8,9},{9,8},{10,11... | collective-permute-start | bytes 1572872 | tf_op jit(solution)/shard_map/ppermute | solution.py:574
  135.4 26.6 %collective-permute-start.27 = (bf16[128,2048]{1,0:T(8,128)(2,1)S(1)}, bf16[128,2048]{1,0:T(8,128)(2,1)S(1)}, u32[]{:S(2)}, u32[]{:S(2)}) collective-permute-start(bf16[128,2048]{1,0:T(8,128)(2,1)S(1)} %multiply_convert_fusion.refs_0_), channel_id=1, source_target_pairs={{0,64},{32,96},{64,0},{96,32},{1,65},{33,97},{65,1},{97,33},{2,66}... | collective-permute-start | bytes 1572872 | tf_op jit(solution)/shard_map/ppermute | solution.py:566
  136.5 26.1 %collective-permute-start.35 = (bf16[128,2048]{1,0:T(8,128)(2,1)S(1)}, bf16[128,2048]{1,0:T(8,128)(2,1)S(1)}, u32[]{:S(2)}, u32[]{:S(2)}) collective-permute-start(bf16[128,2048]{1,0:T(8,128)(2,1)S(1)} %collective-permute-done.20.refs_11_), channel_id=1, source_target_pairs={{0,1},{1,0},{2,3},{3,2},{4,5},{5,4},{6,7},{7,6},{8,9},{9,8},{10,11... | collective-permute-start | bytes 1572872 | tf_op jit(solution)/shard_map/ppermute | solution.py:574
  204.6 25.9 %collective-permute-start.41 = (bf16[128,2048]{1,0:T(8,128)(2,1)}, bf16[128,2048]{1,0:T(8,128)(2,1)}, u32[]{:S(2)}, u32[]{:S(2)}) collective-permute-start(bf16[128,2048]{1,0:T(8,128)(2,1)} %get-tuple-element.133), channel_id=1, source_target_pairs={{0,32},{32,64},{64,96},{96,0},{1,33},{33,65},{65,97},{97,1},{2,34}... | collective-permute-start | bytes 1572872 | tf_op jit(solution)/shard_map/ppermute | solution.py:570
  204.6 25.9 %collective-permute-start.42 = (bf16[128,2048]{1,0:T(8,128)(2,1)}, bf16[128,2048]{1,0:T(8,128)(2,1)}, u32[]{:S(2)}, u32[]{:S(2)}) collective-permute-start(bf16[128,2048]{1,0:T(8,128)(2,1)} %get-tuple-element.132), channel_id=1, source_target_pairs={{0,96},{32,0},{64,32},{96,64},{1,97},{33,1},{65,33},{97,65},{2,98}... | collective-permute-start | bytes 1572872 | tf_op jit(solution)/shard_map/ppermute | solution.py:570
  243.4 34.6 %collective-permute-start.37 = (bf16[512,2048]{1,0:T(8,128)(2,1)}, bf16[512,2048]{1,0:T(8,128)(2,1)S(1)}, u32[]{:S(2)}, u32[]{:S(2)}) collective-permute-start(bf16[512,2048]{1,0:T(8,128)(2,1)} %get-tuple-element.83), channel_id=1, source_target_pairs={{0,1},{1,0},{2,3},{3,2},{4,5},{5,4},{6,7},{7,6},{8,9},{9,8},{10,11... | collective-permute-start | bytes 6291464 | tf_op jit(solution)/shard_map/ppermute | solution.py:574
  247.7 25.1 %collective-permute-start.44 = (bf16[128,2048]{1,0:T(8,128)(2,1)S(1)}, bf16[128,2048]{1,0:T(8,128)(2,1)S(1)}, u32[]{:S(2)}, u32[]{:S(2)}) collective-permute-start(bf16[128,2048]{1,0:T(8,128)(2,1)S(1)} %get-tuple-element.117.refs_0_.refs_8_), channel_id=1, source_target_pairs={{0,96},{32,0},{64,32},{96,64},{1,97},{33,1},{65,33},{97,65},{2,98}... | collective-permute-start | bytes 1572872 | tf_op jit(solution)/shard_map/ppermute | solution.py:566
  250.4 25.8 %collective-permute-start.45 = (bf16[128,2048]{1,0:T(8,128)(2,1)S(1)}, bf16[128,2048]{1,0:T(8,128)(2,1)S(1)}, u32[]{:S(2)}, u32[]{:S(2)}) collective-permute-start(bf16[128,2048]{1,0:T(8,128)(2,1)S(1)} %get-tuple-element.117.refs_0_.refs_8_), channel_id=1, source_target_pairs={{0,32},{32,64},{64,96},{96,0},{1,33},{33,65},{65,97},{97,1},{2,34}... | collective-permute-start | bytes 1572872 | tf_op jit(solution)/shard_map/ppermute | solution.py:566
  250.6 25.6 %collective-permute-start.46 = (bf16[128,2048]{1,0:T(8,128)(2,1)S(1)}, bf16[128,2048]{1,0:T(8,128)(2,1)S(1)}, u32[]{:S(2)}, u32[]{:S(2)}) collective-permute-start(bf16[128,2048]{1,0:T(8,128)(2,1)S(1)} %get-tuple-element.117.refs_0_.refs_8_), channel_id=1, source_target_pairs={{0,64},{32,96},{64,0},{96,32},{1,65},{33,97},{65,1},{97,33},{2,66}... | collective-permute-start | bytes 1572872 | tf_op jit(solution)/shard_map/ppermute | solution.py:566
  251.8 27.1 %collective-permute-start.47 = (bf16[128,2048]{1,0:T(8,128)(2,1)S(1)}, bf16[128,2048]{1,0:T(8,128)(2,1)S(1)}, u32[]{:S(2)}, u32[]{:S(2)}) collective-permute-start(bf16[128,2048]{1,0:T(8,128)(2,1)S(1)} %get-tuple-element.117.refs_0_.refs_8_), channel_id=1, source_target_pairs={{0,1},{1,0},{2,3},{3,2},{4,5},{5,4},{6,7},{7,6},{8,9},{9,8},{10,11... | collective-permute-start | bytes 1572872 | tf_op jit(solution)/shard_map/ppermute | solution.py:574
  278.8 26.0 %collective-permute-start.38 = (bf16[128,2048]{1,0:T(8,128)(2,1)S(1)}, bf16[128,2048]{1,0:T(8,128)(2,1)S(1)}, u32[]{:S(2)}, u32[]{:S(2)}) collective-permute-start(bf16[128,2048]{1,0:T(8,128)(2,1)S(1)} %get-tuple-element.129), channel_id=1, source_target_pairs={{0,32},{32,64},{64,96},{96,0},{1,33},{33,65},{65,97},{97,1},{2,34}... | collective-permute-start | bytes 1572872 | tf_op jit(solution)/shard_map/ppermute | solution.py:570
  278.9 25.9 %collective-permute-start.39 = (bf16[128,2048]{1,0:T(8,128)(2,1)S(1)}, bf16[128,2048]{1,0:T(8,128)(2,1)S(1)}, u32[]{:S(2)}, u32[]{:S(2)}) collective-permute-start(bf16[128,2048]{1,0:T(8,128)(2,1)S(1)} %get-tuple-element.128), channel_id=1, source_target_pairs={{0,96},{32,0},{64,32},{96,64},{1,97},{33,1},{65,33},{97,65},{2,98}... | collective-permute-start | bytes 1572872 | tf_op jit(solution)/shard_map/ppermute | solution.py:570
  324.4 31.6 %collective-permute-start.53 = (bf16[512,640]{1,0:T(8,128)(2,1)}, bf16[512,640]{1,0:T(8,128)(2,1)}, u32[]{:S(2)}, u32[]{:S(2)}) collective-permute-start(bf16[512,640]{1,0:T(8,128)(2,1)} %get-tuple-element.139), channel_id=1, source_target_pairs={{0,4},{2,6},{4,0},{6,2},{1,5},{3,7},{5,1},{7,3},{8,12},{10,14},{12... | collective-permute-start | bytes 1966088 | tf_op jit(solution)/shard_map/ppermute | solution.py:638
  326.8 29.2 %collective-permute-start.54 = (bf16[512,640]{1,0:T(8,128)(2,1)}, bf16[512,640]{1,0:T(8,128)(2,1)}, u32[]{:S(2)}, u32[]{:S(2)}) collective-permute-start(bf16[512,640]{1,0:T(8,128)(2,1)} %get-tuple-element.138), channel_id=1, source_target_pairs={{0,6},{2,0},{4,2},{6,4},{1,7},{3,1},{5,3},{7,5},{8,14},{10,8},{12,... | collective-permute-start | bytes 1966088 | tf_op jit(solution)/shard_map/ppermute | solution.py:638
  356.0 24.1 %collective-permute-start.60 = (bf16[128,2048]{1,0:T(8,128)(2,1)}, bf16[128,2048]{1,0:T(8,128)(2,1)}, u32[]{:S(2)}, u32[]{:S(2)}) collective-permute-start(bf16[128,2048]{1,0:T(8,128)(2,1)} %get-tuple-element.107), channel_id=1, source_target_pairs={{0,64},{32,96},{64,0},{96,32},{1,65},{33,97},{65,1},{97,33},{2,66}... | collective-permute-start | bytes 1572872 | tf_op jit(solution)/shard_map/ppermute | solution.py:570
  (124 other events, 1842.9 us)
Sparse Core Ops, SparseCore 0:
  18.8 50.2 all-gather.2
  71.8 76.0 all-gather.4
  234.0 86.0 reduce-scatter.1

commit v5 on v4

--- a/solution.py
+++ b/solution.py
@@ -34,6 +34,10 @@
 
 
 HBM = pl.BlockSpec(memory_space=pltpu.HBM)
+
+
+def in_hbm(*items):
+    return [pltpu.with_memory_space_constraint(item, pltpu.HBM) for item in items]
 
 
 def block_copies(parts, whole, sems):
@@ -93,17 +97,24 @@
     x, c, feed, down, x_sems, c_sems, f_sems, d_sems = refs[21:]
     step = pl.program_id(0)
 
+    first, third = block_copies(x_parts, x, x_sems), block_copies(c_parts, c, c_sems)
+
     @pl.when(step == 0)
     def _():
-        first = block_copies(x_parts, x, x_sems)
-        second = feed_copies(packed, feed, f_sems)
-        third = block_copies(c_parts, c, c_sems)
-        fourth = down_copies(packed, down, d_sems)
-        for group in (first, second, third, fourth):
+        second, fourth = feed_copies(packed, feed, f_sems), down_copies(packed, down, d_sems)
+        for group in (first[4:6], second, third[4:6], fourth, first[6:], third[6:], first[:4], third[:4]):
             for copy in group:
                 copy.start()
-        for copy in first + second:
+        for copy in first[4:6] + second:
             copy.wait()
+
+    for k in range(1, 4):
+
+        @pl.when(step == k)
+        def _(k=k):
+            spot = (2 * k + 4) % 8
+            for copy in first[spot : spot + 2] + third[spot : spot + 2]:
+                copy.wait()
 
     rows = pl.ds(pl.multiple_of(((step + 2) % 4) * 256, 256), 256)
     block = x[rows, :]
@@ -112,9 +123,7 @@
 
     @pl.when(step == 0)
     def _():
-        third = block_copies(c_parts, c, c_sems)
-        fourth = down_copies(packed, down, d_sems)
-        for copy in third + fourth:
+        for copy in third[4:6] + down_copies(packed, down, d_sems):
             copy.wait()
 
     back = dot_nt(c[rows, :], down[...])
@@ -133,7 +142,7 @@
 
     @pl.when(step >= 2)
     def _():
-        near[...] = inner
+        near[...] = inner.astype(BF16)
 
 
 def feed_forward(x_parts, c_parts, packed):
@@ -152,7 +161,7 @@
             jax.ShapeDtypeStruct((1024, WIDE), BF16),
             jax.ShapeDtypeStruct((1024, 2 * WIDE), BF16),
             jax.ShapeDtypeStruct((512, D), BF16),
-            jax.ShapeDtypeStruct((512, D), F32),
+            jax.ShapeDtypeStruct((512, D), BF16),
         ],
         scratch_shapes=[
             pltpu.VMEM((1024, D), BF16),
@@ -164,11 +173,11 @@
             pltpu.SemaphoreType.DMA((32,)),
             pltpu.SemaphoreType.DMA((64,)),
         ],
-        compiler_params=pltpu.CompilerParams(vmem_limit_bytes=60 * 1024 * 1024),
+        compiler_params=pltpu.CompilerParams(vmem_limit_bytes=40 * 1024 * 1024),
         cost_estimate=pl.CostEstimate(
             flops=2 * 1024 * D * WIDE * 5, bytes_accessed=28 * 2**20, transcendentals=1024 * WIDE
         ),
-    )(*x_parts, *c_parts, packed)
+    )(*in_hbm(*x_parts, *c_parts, packed))
 
 
 def grads_kernel(*refs):
@@ -239,7 +248,7 @@
         cost_estimate=pl.CostEstimate(
             flops=2 * 1024 * D * WIDE * 3, bytes_accessed=22 * 2**20, transcendentals=0
         ),
-    )(*x_parts, *c_parts, hidden, grads)
+    )(*in_hbm(*x_parts, *c_parts, hidden, grads))
 
 
 def output_kernel(hidden, packed, far, near, down, sems):
@@ -249,7 +258,7 @@
     for copy in copies:
         copy.wait()
     far[...] = dot_nn(hidden[512:], down[...]).astype(BF16)
-    near[...] = dot_nn(hidden[:512], down[...])
+    near[...] = dot_nn(hidden[:512], down[...]).astype(BF16)
 
 
 def output_product(hidden, packed):
@@ -258,13 +267,13 @@
         output_kernel,
         in_specs=[whole, HBM],
         out_specs=[whole, whole],
-        out_shape=[jax.ShapeDtypeStruct((512, D), BF16), jax.ShapeDtypeStruct((512, D), F32)],
+        out_shape=[jax.ShapeDtypeStruct((512, D), BF16), jax.ShapeDtypeStruct((512, D), BF16)],
         scratch_shapes=[pltpu.VMEM((WIDE, D), BF16), pltpu.SemaphoreType.DMA((64,))],
-        compiler_params=pltpu.CompilerParams(vmem_limit_bytes=60 * 1024 * 1024),
+        compiler_params=pltpu.CompilerParams(vmem_limit_bytes=24 * 1024 * 1024),
         cost_estimate=pl.CostEstimate(
             flops=2 * 1024 * D * WIDE, bytes_accessed=11 * 2**20, transcendentals=0
         ),
-    )(hidden, packed)
+    )(hidden, *in_hbm(packed))
 
 
 def rotary_table():
@@ -328,15 +337,22 @@
     queries, key_values, mixed, far, near = refs[11:16]
     x, ids, w, o, x_sems, i_sems, w_sems = refs[16:]
     step = pl.program_id(0)
+    blocks, numbers = block_copies(parts, x, x_sems), id_copies(parts, ids, i_sems)
+    loads = [
+        pltpu.make_async_copy(w_hbm, w, w_sems.at[0]),
+        pltpu.make_async_copy(o_hbm, o, w_sems.at[1]),
+    ]
 
     @pl.when(step == 0)
     def _():
-        copies = block_copies(parts, x, x_sems) + id_copies(parts, ids, i_sems)
-        copies.append(pltpu.make_async_copy(w_hbm, w, w_sems.at[0]))
-        copies.append(pltpu.make_async_copy(o_hbm, o, w_sems.at[1]))
-        for copy in copies:
+        for copy in loads[:1] + blocks[4:] + numbers[4:] + loads[1:] + blocks[:4] + numbers[:4]:
             copy.start()
-        for copy in copies:
+        for copy in loads[:1] + blocks[4:] + numbers[4:]:
+            copy.wait()
+
+    @pl.when(step == 1)
+    def _():
+        for copy in blocks[:4] + numbers[:4]:
             copy.wait()
 
     half = 1 - step
@@ -354,6 +370,11 @@
         probs = softmax_heads(block[:, :256], keys, allowed)
         probs = jnp.concatenate([item.astype(BF16) for item in probs], axis=1)
         mixed[here, :] = dot_nn(probs, stack_heads(values)).astype(BF16)
+
+    @pl.when(step == 0)
+    def _():
+        loads[1].wait()
+
     total = dot_nn(mixed[...], o[...])
 
     @pl.when(step == 0)
@@ -362,7 +383,7 @@
 
     @pl.when(step == 1)
     def _():
-        near[...] = total
+        near[...] = total.astype(BF16)
 
 
 def attend(parts, table, qkv_full, out_full):
@@ -384,7 +405,7 @@
             jax.ShapeDtypeStruct((1024, CAP), BF16),
             jax.ShapeDtypeStruct((1024, 256), BF16),
             jax.ShapeDtypeStruct((512, D), BF16),
-            jax.ShapeDtypeStruct((512, D), F32),
+            jax.ShapeDtypeStruct((512, D), BF16),
         ],
         scratch_shapes=[
             pltpu.VMEM((1024, D), BF16),
@@ -395,11 +416,11 @@
             pltpu.SemaphoreType.DMA((8,)),
             pltpu.SemaphoreType.DMA((2,)),
         ],
-        compiler_params=pltpu.CompilerParams(vmem_limit_bytes=26 * 1024 * 1024),
+        compiler_params=pltpu.CompilerParams(vmem_limit_bytes=32 * 1024 * 1024),
         cost_estimate=pl.CostEstimate(
             flops=2 * 1024 * D * 640 * 2, bytes_accessed=15 * 2**20, transcendentals=2**19
         ),
-    )(*parts, table, qkv_full, out_full)
+    )(*in_hbm(*parts), table, *in_hbm(qkv_full, out_full))
 
 
 def attend_back_kernel(*refs):
@@ -408,17 +429,22 @@
     grads, far, near = refs[21:24]
     g, ids, w, o, g_sems, i_sems, w_sems = refs[24:]
     step = pl.program_id(0)
+    blocks, numbers = block_copies(parts, g, g_sems), id_copies(id_parts, ids, i_sems)
     loads = [
+        pltpu.make_async_copy(o_hbm, o, w_sems.at[1]),
         pltpu.make_async_copy(w_hbm, w, w_sems.at[0]),
-        pltpu.make_async_copy(o_hbm, o, w_sems.at[1]),
     ]
 
     @pl.when(step == 0)
     def _():
-        copies = block_copies(parts, g, g_sems) + id_copies(id_parts, ids, i_sems) + loads
-        for copy in copies:
+        for copy in loads[:1] + blocks[4:] + numbers[4:] + loads[1:] + blocks[:4] + numbers[:4]:
             copy.start()
-        for copy in copies:
+        for copy in loads[:1] + blocks[4:] + numbers[4:]:
+            copy.wait()
+
+    @pl.when(step == 1)
+    def _():
+        for copy in blocks[:4] + numbers[:4]:
             copy.wait()
 
     half = 1 - step
@@ -446,6 +472,11 @@
         grad_both = dot_tn(jnp.concatenate(scores, axis=0), folded) * 0.125 + dot_tn(low, grad_folded)
         item = jnp.concatenate([grad_query, grad_both], axis=1)
         grads[here, :] = turned(item, factors, -1.0).astype(BF16)
+
+    @pl.when(step == 0)
+    def _():
+        loads[1].wait()
+
     total = dot_nt(grads[...], w[...])
 
     @pl.when(step == 0)
@@ -454,7 +485,7 @@
 
     @pl.when(step == 1)
     def _():
-        near[...] = total
+        near[...] = total.astype(BF16)
 
 
 def attend_back(parts, id_parts, table, qkv_full, out_full, queries, key_values):
@@ -474,7 +505,7 @@
         out_shape=[
             jax.ShapeDtypeStruct((1024, 384), BF16),
             jax.ShapeDtypeStruct((512, D), BF16),
-            jax.ShapeDtypeStruct((512, D), F32),
+            jax.ShapeDtypeStruct((512, D), BF16),
         ],
         scratch_shapes=[
             pltpu.VMEM((1024, D), BF16),
@@ -485,59 +516,97 @@
             pltpu.SemaphoreType.DMA((8,)),
             pltpu.SemaphoreType.DMA((2,)),
         ],
-        compiler_params=pltpu.CompilerParams(vmem_limit_bytes=28 * 1024 * 1024),
+        compiler_params=pltpu.CompilerParams(vmem_limit_bytes=32 * 1024 * 1024),
         cost_estimate=pl.CostEstimate(
             flops=2 * 1024 * D * 640 * 2, bytes_accessed=15 * 2**20, transcendentals=2**19
         ),
-    )(*parts, *id_parts, table, qkv_full, out_full, queries, key_values)
-
-
-def small_grads_kernel(*refs):
-    x_parts, g_parts, mixed_hbm, grads_hbm = refs[:8], refs[8:16], refs[16], refs[17]
-    pack, x, g, mixed, grads, x_sems, g_sems, in_sems = refs[18:]
-    first = block_copies(x_parts, x, x_sems)
-    second = block_copies(g_parts, g, g_sems)
-    loads = [
-        pltpu.make_async_copy(grads_hbm, grads, in_sems.at[0]),
-        pltpu.make_async_copy(mixed_hbm, mixed, in_sems.at[1]),
-    ]
-    for copy in first + loads + second:
+    )(*in_hbm(*parts, *id_parts), table, *in_hbm(qkv_full, out_full), queries, key_values)
+
+
+def out_grads_kernel(*refs):
+    parts, mixed_hbm, out, g, mixed, sems, in_sems = refs[:8], *refs[8:]
+    copies = block_copies(parts, g, sems)
+    copies.append(pltpu.make_async_copy(mixed_hbm, mixed, in_sems.at[0]))
+    for copy in copies:
         copy.start()
-    for copy in first + loads[:1]:
+    for copy in copies:
+        copy.wait()
+    out[...] = dot_tn(mixed[...], g[...]).astype(BF16)
+
+
+def out_grads(parts, mixed):
+    return pl.pallas_call(
+        out_grads_kernel,
+        in_specs=[HBM] * 9,
+        out_specs=pl.BlockSpec(memory_space=pltpu.VMEM),
+        out_shape=jax.ShapeDtypeStruct((256, D), BF16),
+        scratch_shapes=[
+            pltpu.VMEM((1024, D), BF16),
+            pltpu.VMEM((1024, 256), BF16),
+            pltpu.SemaphoreType.DMA((8,)),
+            pltpu.SemaphoreType.DMA((1,)),
+        ],
+        compiler_params=pltpu.CompilerParams(vmem_limit_bytes=24 * 1024 * 1024),
+        cost_estimate=pl.CostEstimate(
+            flops=2 * 1024 * D * 256, bytes_accessed=6 * 2**20, transcendentals=0
+        ),
+    )(*in_hbm(*parts, mixed))
+
+
+def qkv_grads_kernel(*refs):
+    parts, grads_hbm, out, x, grads, sems, in_sems = refs[:8], *refs[8:]
+    copies = block_copies(parts, x, sems)
+    copies.append(pltpu.make_async_copy(grads_hbm, grads, in_sems.at[0]))
+    for copy in copies:
+        copy.start()
+    for copy in copies:
         copy.wait()
     for k in range(8):
-        tile = dot_tn(x[:, 256 * k : 256 * (k + 1)], grads[...]).astype(BF16)
-        row = 128 * (k % 4) + 64 * (k // 4)
-        for j in range(4):
-            pack[j, row : row + 64, :384] = tile[64 * j : 64 * (j + 1)]
-    for copy in second + loads[1:]:
-        copy.wait()
-    for k in range(8):
-        tile = dot_tn(mixed[...], g[:, 256 * k : 256 * (k + 1)]).astype(BF16)
-        for j in range(4):
-            pack[j, 64 * k : 64 * (k + 1), 384:] = tile[64 * j : 64 * (j + 1)]
-
-
-def small_grads(x_parts, g_parts, mixed, grads):
+        out[k // 4, k % 4] = dot_tn(x[:, 256 * k : 256 * (k + 1)], grads[...]).astype(BF16)
+
+
+def qkv_grads(parts, grads):
     return pl.pallas_call(
-        small_grads_kernel,
-        in_specs=[HBM] * 18,
+        qkv_grads_kernel,
+        in_specs=[HBM] * 9,
         out_specs=pl.BlockSpec(memory_space=pltpu.VMEM),
-        out_shape=jax.ShapeDtypeStruct((4, 512, 640), BF16),
+        out_shape=jax.ShapeDtypeStruct((2, 4, 256, 384), BF16),
         scratch_shapes=[
             pltpu.VMEM((1024, D), BF16),
-            pltpu.VMEM((1024, D), BF16),
-            pltpu.VMEM((1024, 256), BF16),
             pltpu.VMEM((1024, 384), BF16),
             pltpu.SemaphoreType.DMA((8,)),
-            pltpu.SemaphoreType.DMA((8,)),
-            pltpu.SemaphoreType.DMA((2,)),
-        ],
-        compiler_params=pltpu.CompilerParams(vmem_limit_bytes=60 * 1024 * 1024),
+            pltpu.SemaphoreType.DMA((1,)),
+        ],
+        compiler_params=pltpu.CompilerParams(vmem_limit_bytes=24 * 1024 * 1024),
         cost_estimate=pl.CostEstimate(
-            flops=2 * 1024 * D * 640, bytes_accessed=12 * 2**20, transcendentals=0
+            flops=2 * 1024 * D * 384, bytes_accessed=6 * 2**20, transcendentals=0
         ),
-    )(*x_parts, *g_parts, mixed, grads)
+    )(*in_hbm(*parts, grads))
+
+
+def norm_back_kernel(own, one, two, three, rows, upstream, grad, low):
+    x = rows[...]
+    inner = own[...] + one[...].astype(F32) + two[...].astype(F32) + three[...].astype(F32)
+    scale = lax.rsqrt(jnp.mean(x * x, axis=1, keepdims=True) + norm_eps)
+    slope = jnp.mean(inner * x, axis=1, keepdims=True)
+    total = upstream[...].astype(F32) + scale * inner - x * (scale * scale * scale * slope)
+    grad[...] = total
+    low[...] = total.astype(BF16)
+
+
+def norm_back_sum(own, came, rows, upstream):
+    spec = pl.BlockSpec((32, D), lambda i: (i, 0))
+    return pl.pallas_call(
+        norm_back_kernel,
+        grid=(CAP // 32,),
+        in_specs=[spec] * 6,
+        out_specs=[spec] * 2,
+        out_shape=[jax.ShapeDtypeStruct((CAP, D), F32), jax.ShapeDtypeStruct((CAP, D), BF16)],
+        compiler_params=pltpu.CompilerParams(vmem_limit_bytes=16 * 1024 * 1024),
+        cost_estimate=pl.CostEstimate(
+            flops=20 * CAP * D, bytes_accessed=6 * 2**20, transcendentals=CAP
+        ),
+    )(own, *came, rows, upstream)
 
 
 def times(left, right):
@@ -585,7 +654,7 @@
 
     def block(spot):
         here = slice(spot * CAP, (spot + 1) * CAP)
-        return near[here] + far[here].astype(F32)
+        return near[here].astype(F32) + far[here].astype(F32)
 
     return (block(0),) + tuple(block(spot).astype(BF16) for spot in (1, 2, 3))
 
@@ -711,16 +780,6 @@
     ]
     spread = spread_columns(chunks, xl, c)
 
-    source = 2 * xh + c
-    came = swap(out_weight, "c")
-    head = jnp.concatenate(
-        [jnp.where(c == 0, out_weight, came), jnp.where(c == 0, came, out_weight)], axis=0
-    )
-    lines = [head]
-    for step in (1, 2, 3):
-        lines.append(lax.ppermute(head, ("xh", "y", "c"), row_pairs(step, False)))
-    head = pick(lines, (y - source) % 4)
-    out_full = gather_four(head, "z", z, 0).reshape(256, D)
     qkv_full = lax.all_gather(spread, ("y", "z"), axis=1, tiled=True).reshape(D, 384)
 
     wide = jnp.stack([scaled(gate_weight, second_col), scaled(up_weight, second_col)])
@@ -749,6 +808,17 @@
     feed_spread = spread_columns(chunks, xl, c).reshape(128, 2 * WIDE)
     packed = jnp.concatenate([feed_spread, down_half[:, : 2 * WIDE], corner], axis=0)
 
+    source = 2 * xh + c
+    came = swap(out_weight, "c")
+    head = jnp.concatenate(
+        [jnp.where(c == 0, out_weight, came), jnp.where(c == 0, came, out_weight)], axis=0
+    )
+    lines = [head]
+    for step in (1, 2, 3):
+        lines.append(lax.ppermute(head, ("xh", "y", "c"), row_pairs(step, False)))
+    head = pick(lines, (y - source) % 4)
+    out_full = gather_four(head, "z", z, 0).reshape(256, D)
+
     table = rotary_table()
     rows = tokens.astype(F32)
     first_scale = rms_scale(rows)
@@ -759,9 +829,9 @@
     packed = lax.all_gather(packed, ("y", "z"), axis=0, tiled=True)
 
     queries, key_values, mixed, far, near = attend(first, table, qkv_full, out_full)
-    shuffle = jnp.concatenate([order_of_columns(0), order_of_columns(1)], axis=1)
     upstream = share_parts(after(cotangent, *first[1:4]), mixed)
     far = after(far, upstream[1])
+    shuffle = after(jnp.concatenate([order_of_columns(0), order_of_columns(1)], axis=1), mixed)
     midway = rows + ring_sum(pair_blocks(near, far), shuffle)
 
     second_scale = rms_scale(midway)
@@ -769,46 +839,114 @@
     hidden, grad_feed, far, near = feed_forward(second, upstream, packed)
     blocks = pair_blocks(near, far)
     pack = feed_grads(second, upstream, after(hidden, *blocks), grad_feed)
-    inner_two = ring_sum(blocks, pack)
-    grad_mid = cotangent.astype(F32) + norm_back(midway, second_scale, inner_two)
+    came = tuple(to_ring(blocks[spot], STEPS[spot]) for spot in (1, 2, 3))
+    grad_mid, grad_low = norm_back_sum(blocks[0], after(came, pack), midway, cotangent)
     out_far, out_near = output_product(after(hidden, pack), packed)
-    third = share_parts(grad_mid.astype(BF16), out_far)
-    pack = lax.psum_scatter(after(pack, inner_two), ("y", "z"), scatter_dimension=0, tiled=True)
-
-    out_blocks = pair_blocks(out_near, out_far)
+    third = share_parts(grad_low, out_far)
+    pack = lax.psum_scatter(after(pack, grad_low), ("y", "z"), scatter_dimension=0, tiled=True)
+
+    out_blocks = pair_blocks(out_near, after(out_far, *third[1:4]))
+    out_term = out_grads(third, mixed).reshape(4, 64, D)
+    out_sent = four_pieces(out_term, z, 0)
+    out_came = exchange(out_sent, "z")
     grad_qkv, far, near = attend_back(
-        third, first, table, qkv_full, out_full, after(queries, *out_blocks), key_values
+        third,
+        first,
+        table,
+        qkv_full,
+        out_full,
+        after(queries, *out_sent, *out_blocks),
+        key_values,
     )
     product = ring_sum(out_blocks, grad_qkv)
     output = (midway + product).astype(BF16)
-
-    terms = small_grads(first, third, mixed, grad_qkv)
-    blocks = pair_blocks(near, after(far, product), terms)
-    sent = four_pieces(after(terms, *blocks), z, 0)
-    came = exchange(sent, "z")
+    out_part = four_sum(out_sent, after(out_came, product))
+    far = after(far, out_part)
+    sent = out_part.astype(BF16)
+    out_came = tuple(
+        lax.ppermute(sent, ("xh", "y", "c"), row_pairs(step, True)) for step in (1, 2, 3)
+    )
+    qkv_term = qkv_grads(first, after(grad_qkv, sent))
+    blocks = pair_blocks(near, far, qkv_term)
+    out_came = after(out_came, *blocks)
+    out_part = (out_part + sum(item.astype(F32) for item in out_came)).astype(BF16)
+
+    def halves(item):
+        low, high = item[:, :32], item[:, 32:]
+        return jnp.where(c == 0, low, high), jnp.where(c == 0, high, low)
+
+    sent = four_pieces(after(qkv_term, out_part, *blocks), y, 1)
+    came = exchange(sent, "y")
     ring_came = (to_ring(blocks[1], STEPS[1]), to_ring(blocks[2], STEPS[2]))
-    came, ring_came = lax.optimization_barrier((came, ring_came))
-    terms = four_sum(sent, came).astype(BF16)
-    head = jnp.concatenate(
-        [
-            jnp.concatenate([terms[64 * k : 64 * (k + 1), 384:] for k in range(h, h + 4)], axis=1)
-            for h in (0, 4)
-        ],
-        axis=0,
-    )
-    lines = terms[:, :384].reshape(4, 128, 384)
-    sent = [jnp.concatenate([item, head], axis=1) for item in four_pieces(lines, y, 0)]
-    came = exchange(sent, "y")
-    last_came = to_ring(after(blocks[3], *ring_came), STEPS[3])
     corner = jnp.concatenate([pack[176:, 512 * k : 512 * (k + 1)] for k in range(3)], axis=0)
     down_part = jnp.concatenate([pack[128:176], corner], axis=1)
-    down_other = swap(after(down_part, *ring_came), "xh")
-    came, last_came, down_other = lax.optimization_barrier((came, last_came, down_other))
-    total = four_sum(sent, came).astype(BF16)
-    qkv_part = total[:, :384].reshape(2, 64, 384)
-    out_part = jnp.concatenate([total[:64, 384:], total[64:, 384:]], axis=1)
+    feed_part = pack[:128].reshape(2, 64, 2 * WIDE)
+    feed_mine, feed_away = halves(feed_part)
+    came, ring_came, feed_mine, feed_away, down_part = lax.optimization_barrier(
+        (came, ring_came, feed_mine, feed_away, down_part)
+    )
+    sent = four_pieces(four_sum(sent, came).astype(BF16).reshape(2, 4, 64, 384), z, 1)
+    came = exchange(sent, "z")
+    last_came = to_ring(blocks[3], STEPS[3])
+    feed_came = swap(feed_away, "c")
+    came, last_came, feed_came = lax.optimization_barrier((came, last_came, feed_came))
+
+    def in_order(mine, came):
+        return jnp.where(c == 0, mine, came), jnp.where(c == 0, came, mine)
+
+    def along_ring(both, more):
+        here = jnp.where(xl == 0, both[0], both[1])
+        there = jnp.where(xl == 0, both[1], both[0])
+        across = jnp.concatenate([here, more], axis=1)
+        return here, (to_ring(there, 1), to_ring(across, 2), to_ring(there, 3))
+
+    def by_chip(here, came):
+        width, spot = here.shape[1], 2 * xh + xl
+        stacked = [here, came[0], came[1][:, :width], came[2]]
+        return [[pick(stacked, (spot - (2 * h + k)) % 4) for h in range(2)] for k in range(2)]
+
+    down_wide = jnp.concatenate(
+        [down_part[:32], jnp.concatenate([down_part[32:, :1024], down_part[32:, 1024:]], axis=0)],
+        axis=1,
+    )
+    feed_here, feed_came = along_ring(
+        jnp.concatenate(in_order(feed_mine, feed_came), axis=2), down_wide
+    )
+
+    qkv_part = four_sum(sent, came).astype(BF16)
+    qkv_mine, qkv_away = halves(qkv_part)
+    away = jnp.where(c == 0, out_part[32:], out_part[:32])
+    sent = jnp.concatenate(
+        [
+            qkv_away.reshape(64, 384),
+            jnp.concatenate([away[:, :1024], away[:, 1024:]], axis=0),
+        ],
+        axis=1,
+    )
+    came = swap(sent, "c")
+    zero, one = in_order(qkv_mine, came[:, :384].reshape(2, 32, 384))
+    pair = zero[:, :, 256:].astype(F32) + one[:, :, 256:].astype(F32)
+    both = jnp.concatenate([zero[:, :, :256], one[:, :, :256], pair.astype(BF16)], axis=2)
+    out_half = jnp.where(
+        y % 2 == c,
+        jnp.where(c == 0, out_part[:32], out_part[32:]),
+        jnp.concatenate([came[:32, 384:], came[32:, 384:]], axis=1),
+    )
+    both, out_half = lax.optimization_barrier((both, out_half))
+    qkv_here, came = along_ring(both, out_half)
+    feed_came = after(feed_came, both)
+
     inner_one = blocks[0] + sum(item.astype(F32) for item in ring_came + (last_came,))
     tokens_grad = grad_mid + norm_back(rows, first_scale, inner_one)
+    parts = by_chip(feed_here, feed_came)
+    down_other = feed_came[1][:, 3072:]
+    down_other = jnp.concatenate(
+        [
+            down_other[:, :2048],
+            jnp.concatenate([down_other[:16, 2048:], down_other[16:, 2048:]], axis=1),
+        ],
+        axis=0,
+    )
     down_grad = jnp.concatenate(
         [
             jnp.where(xh == 0, down_part, down_other)[:44],
@@ -816,57 +954,6 @@
         ],
         axis=0,
     ).astype(F32)
-
-    wide = jnp.concatenate([pack[:128].reshape(2, 64, 2 * WIDE), qkv_part], axis=2)
-    low, high = wide[:, :32], wide[:, 32:]
-    away = jnp.where(c == 0, out_part[32:], out_part[:32])
-    sent = jnp.concatenate(
-        [
-            jnp.where(c == 0, high, low).reshape(64, 1920),
-            jnp.concatenate([away[:, :1024], away[:, 1024:]], axis=0),
-        ],
-        axis=1,
-    )
-    came = swap(sent, "c")
-    mine, other = jnp.where(c == 0, low, high), came[:, :1920].reshape(2, 32, 1920)
-    zero, one = jnp.where(c == 0, mine, other), jnp.where(c == 0, other, mine)
-    pair = zero[:, :, 1792:].astype(F32) + one[:, :, 1792:].astype(F32)
-    both = jnp.concatenate(
-        [
-            zero[:, :, :1536],
-            one[:, :, :1536],
-            zero[:, :, 1536:1792],
-            one[:, :, 1536:1792],
-            pair.astype(BF16),
-        ],
-        axis=2,
-    )
-    out_half = jnp.where(
-        y % 2 == c,
-        jnp.where(c == 0, out_part[:32], out_part[32:]),
-        jnp.concatenate([came[:32, 1920:], came[32:, 1920:]], axis=1),
-    )
-    here = jnp.where(xl == 0, both[0], both[1])
-    there = jnp.where(xl == 0, both[1], both[0])
-    across = to_ring(jnp.concatenate([here, out_half], axis=1), 2)
-    came = after((to_ring(there, 1), across, to_ring(there, 3)))
-    stacked = [here, came[0], came[1][:, :3712], came[2]]
-    spot = 2 * xh + xl
-    parts = [[pick(stacked, (spot - (2 * h + k)) % 4) for h in range(2)] for k in range(2)]
-    out_grad = jnp.where(y // 2 == xh, out_half, came[1][:, 3712:]).astype(F32)
-
-    def joined(start, end):
-        return jnp.concatenate(
-            [parts[k][h][:, start:end] for k in range(2) for h in range(2)], axis=1
-        ).astype(F32)
-
-    query_raw, key_raw, value_raw = joined(3072, 3584), joined(3584, 3648), joined(3648, 3712)
-    first_grad = (
-        jnp.sum(query_raw * query_weight.astype(F32), axis=1)
-        + jnp.sum(key_raw * key_weight.astype(F32), axis=1)
-        + jnp.sum(value_raw * value_weight.astype(F32), axis=1)
-    )
-
     rows_of = []
     for item in range(2):
         for k in range(2):
@@ -889,6 +976,21 @@
         up_raw * up_weight.astype(F32), axis=1
     )
 
+    parts = by_chip(qkv_here, came)
+    out_grad = jnp.where(y // 2 == xh, out_half, came[1][:, 640:]).astype(F32)
+
+    def joined(start, end):
+        return jnp.concatenate(
+            [parts[k][h][:, start:end] for k in range(2) for h in range(2)], axis=1
+        ).astype(F32)
+
+    query_raw, key_raw, value_raw = joined(0, 512), joined(512, 576), joined(576, 640)
+    first_grad = (
+        jnp.sum(query_raw * query_weight.astype(F32), axis=1)
+        + jnp.sum(key_raw * key_weight.astype(F32), axis=1)
+        + jnp.sum(value_raw * value_weight.astype(F32), axis=1)
+    )
+
     return (
         output,
         tokens_grad,

time: 428 us -> 400 us (0.935)
  the two profiles are of different devices: /device:TPU:1 before, /device:TPU:16 now
where the time goes in v5:
time: 400 us; the launch traced here: 393 us
  waiting for transfers between devices  141 us (35%)
  Pallas kernels  96.6 us (24%)
  starting transfers between devices  88.5 us (22%)
  other arithmetic  37.7 us (9%)
  between operations  15.6 us (4%)
  local copies, waits for them, and re-layouts  10.5 us (3%)
    ppermute x12, waiting for transfers between devices, from_ring(): return lax.ppermute(item, RING, [(i, (i - step) % 4) for i in range(4)])  59.7 us
    ppermute x18, waiting for transfers between devices, to_ring(): return lax.ppermute(item, RING, [(i, (i + step) % 4) for i in range(4)])  40.5 us
    ppermute x18, starting transfers between devices, to_ring(): return lax.ppermute(item, RING, [(i, (i + step) % 4) for i in range(4)])  30.4 us
    pallas_call x1, Pallas kernels, feed_forward(): pl.pallas_call(feed_kernel, grid=(4,), in_specs=[HBM] * 17, out_specs=[pl...  28.7 us
    ppermute x12, starting transfers between devices, from_ring(): return lax.ppermute(item, RING, [(i, (i - step) % 4) for i in range(4)])  18.8 us
    pallas_call x1, Pallas kernels, attend_back(): pl.pallas_call(attend_back_kernel, grid=(2,), in_specs=[HBM] * 16 + [pl.B...  17.7 us
    ppermute x27, waiting for transfers between devices, swap(): return lax.ppermute(item, axis, SWAP)  16.9 us
    pallas_call x1, Pallas kernels, feed_grads(): pl.pallas_call(grads_kernel, in_specs=[HBM] * 18, out_specs=HBM, out_shap...  16.2 us
  transfers between devices with their start and end apart: 78, of which 34 were waited for; matrix products, arithmetic and copies ran while one was open for 10% of the time, Pallas kernels for 16%

profile of v5, /device:TPU:16, one launch (start us, length us, event | category | flops | bytes accessed | tf_op | source)
XLA Modules:
  0.0 392.8 jit_solution(12328948831295917468)
XLA Ops:
  25.2 4.8 %collective-permute-done.13 = bf16[64,2048]{1,0:T(8,128)(2,1)S(1)} collective-permute-done((bf16[64,2048]{1,0:T(8,128)(2,1)S(1)}, bf16[64,2048]{1,0:T(8,128)(2,1)S(1)}, u32[]{:S(2)}, u32[]{:S(2)}) %collective-permute-start.13) | collective-permute-done | bytes 262176 | tf_op jit(solution)/shard_map/ppermute | solution.py:818
  44.2 5.4 %collective-permute-done.16 = bf16[64,2048]{1,0:T(8,128)(2,1)} collective-permute-done((bf16[64,2048]{1,0:T(8,128)(2,1)S(1)}, bf16[64,2048]{1,0:T(8,128)(2,1)}, u32[]{:S(2)}, u32[]{:S(2)}) %collective-permute-start.16) | collective-permute-done | bytes 262176 | tf_op jit(solution)/shard_map/ppermute | solution.py:688
  55.3 11.2 %collective-permute-done.6.refs_3_.refs_11_ = bf16[144,2048]{1,0:T(8,128)(2,1)} collective-permute-done((bf16[144,2048]{1,0:T(8,128)(2,1)S(1)}, bf16[144,2048]{1,0:T(8,128)(2,1)}, u32[]{:S(2)}, u32[]{:S(2)}) %collective-permute-start.6) | collective-permute-done | bytes 589856 | tf_op jit(solution)/shard_map/ppermute | solution.py:635
  77.2 14.3 %shard_map.212 = (bf16[1024,256]{1,0:T(8,128)(2,1)S(1)}, bf16[1024,128]{1,0:T(8,128)(2,1)S(1)}, bf16[1024,256]{1,0:T(8,128)(2,1)S(1)}, bf16[512,2048]{1,0:T(8,128)(2,1)S(1)}, bf16[512,2048]{1,0:T(8,128)(2,1)S(1)}) custom-call(bf16[144,2048]{1,0:T(8,128)(2,1)} %copy-done.18, bf16[144,2048]{1,0:T(8,128)(2,1)} %collective-permute-done.4.refs_1_.refs_9_, ...), custom_call_target="tpu_custom_call" | custom-call | flops 5368709120 | bytes 15728640 | tf_op jit(solution)/shard_map/pallas_call | solution.py:392
  91.5 3.9 collective-permute-done.18.refs_9_
  110.4 19.7 %collective-permute-done.22 = bf16[128,2048]{1,0:T(8,128)(2,1)S(1)} collective-permute-done((bf16[128,2048]{1,0:T(8,128)(2,1)S(1)}, bf16[128,2048]{1,0:T(8,128)(2,1)S(1)}, u32[]{:S(2)}, u32[]{:S(2)}) %collective-permute-start.22) | collective-permute-done | bytes 524320 | tf_op jit(solution)/shard_map/ppermute | solution.py:639
  136.2 9.5 %collective-permute-done.25.refs_1_ = bf16[128,2048]{1,0:T(8,128)(2,1)S(1)} collective-permute-done((bf16[128,2048]{1,0:T(8,128)(2,1)S(1)}, bf16[128,2048]{1,0:T(8,128)(2,1)S(1)}, u32[]{:S(2)}, u32[]{:S(2)}) %collective-permute-start.25) | collective-permute-done | bytes 524320 | tf_op jit(solution)/shard_map/ppermute | solution.py:635
  145.7 13.3 %collective-permute-done.26.refs_2_ = bf16[128,2048]{1,0:T(8,128)(2,1)S(1)} collective-permute-done((bf16[128,2048]{1,0:T(8,128)(2,1)S(1)}, bf16[128,2048]{1,0:T(8,128)(2,1)S(1)}, u32[]{:S(2)}, u32[]{:S(2)}) %collective-permute-start.26) | collective-permute-done | bytes 524320 | tf_op jit(solution)/shard_map/ppermute | solution.py:635
  161.8 28.7 %shard_map.213 = (bf16[1024,768]{1,0:T(8,128)(2,1)S(1)}, bf16[1024,1536]{1,0:T(8,128)(2,1)S(1)}, bf16[512,2048]{1,0:T(8,128)(2,1)S(1)}, bf16[512,2048]{1,0:T(8,128)(2,1)S(1)}) custom-call(bf16[128,2048]{1,0:T(8,128)(2,1)} %copy-done.27, bf16[128,2048]{1,0:T(8,128)(2,1)} %copy-done.49, bf16[128,2048]{1,0:T(8,128)(2,1)} %copy-done.50, ...), custom_call_target="tpu_custom_call" | custom-call | flops 16106127360 | bytes 29360128 | tf_op jit(solution)/shard_map/pallas_call | solution.py:150
  190.8 4.0 %collective-permute-done.36 = bf16[512,2048]{1,0:T(8,128)(2,1)S(1)} collective-permute-done((bf16[512,2048]{1,0:T(8,128)(2,1)S(1)}, bf16[512,2048]{1,0:T(8,128)(2,1)S(1)}, u32[]{:S(2)}, u32[]{:S(2)}) %collective-permute-start.36) | collective-permute-done | bytes 2097184 | tf_op jit(solution)/shard_map/ppermute | solution.py:643
  199.9 16.2 %shard_map.214 = bf16[3072,1536]{1,0:T(8,128)(2,1)} custom-call(bf16[128,2048]{1,0:T(8,128)(2,1)} %copy-done.27, bf16[128,2048]{1,0:T(8,128)(2,1)} %copy-done.49, bf16[128,2048]{1,0:T(8,128)(2,1)} %copy-done.50, bf16[128,2048]{1,0:T(8,128)(2,1)} %copy-done.51, bf16[128,2048]{1,0:T(8,128)(2,1)} %copy-done.53, bf16[128,2048]{1,0:T(8,128)(2,1)} %copy-done.54, ...), custom_call_target="tpu_custom_call" | custom-call | flops 9663676416 | bytes 23068672 | tf_op jit(solution)/shard_map/pallas_call | solution.py:231
  216.1 7.0 %collective-permute-done.37.one = bf16[128,2048]{1,0:T(8,128)(2,1)S(1)} collective-permute-done((bf16[128,2048]{1,0:T(8,128)(2,1)}, bf16[128,2048]{1,0:T(8,128)(2,1)S(1)}, u32[]{:S(2)}, u32[]{:S(2)}) %collective-permute-start.37) | collective-permute-done | bytes 524320 | tf_op jit(solution)/shard_map/ppermute | solution.py:639
  223.1 3.6 shard_map.216
  233.8 7.2 %shard_map.215 = (bf16[512,2048]{1,0:T(8,128)(2,1)}, bf16[512,2048]{1,0:T(8,128)(2,1)S(1)}) custom-call(bf16[1024,768]{1,0:T(8,128)(2,1)S(1)} %copy-done.12, bf16[3072,1536]{1,0:T(8,128)(2,1)} %all-gather.5.cloned.1.call-done.refs_16_.packed), custom_call_target="tpu_custom_call" | custom-call | flops 3221225472 | bytes 11534336 | tf_op jit(solution)/shard_map/pallas_call | solution.py:266
  241.0 11.8 %collective-permute-done.40.refs_1_ = bf16[128,2048]{1,0:T(8,128)(2,1)} collective-permute-done((bf16[128,2048]{1,0:T(8,128)(2,1)}, bf16[128,2048]{1,0:T(8,128)(2,1)}, u32[]{:S(2)}, u32[]{:S(2)}) %collective-permute-start.40) | collective-permute-done | bytes 524320 | tf_op jit(solution)/shard_map/ppermute | solution.py:635
  257.7 4.1 %collective-permute-done.47.refs_4_ = bf16[128,2048]{1,0:T(8,128)(2,1)} collective-permute-done((bf16[128,2048]{1,0:T(8,128)(2,1)}, bf16[128,2048]{1,0:T(8,128)(2,1)}, u32[]{:S(2)}, u32[]{:S(2)}) %collective-permute-start.47) | collective-permute-done | bytes 524320 | tf_op jit(solution)/shard_map/ppermute | solution.py:643
  264.1 4.0 %shard_map.217 = bf16[256,2048]{1,0:T(8,128)(2,1)S(1)} custom-call(bf16[128,2048]{1,0:T(8,128)(2,1)} %get-tuple-element.105.refs_0_, bf16[128,2048]{1,0:T(8,128)(2,1)} %collective-permute-done.40.refs_1_, bf16[128,2048]{1,0:T(8,128)(2,1)} %collective-permute-done.41.refs_2_, bf16[128,2048]{1,0:T(8,128)(2,1)} %collective-permute-done.42.refs_3_, ...), custom_call_target="tpu_custom_call" | custom-call | flops 1073741824 | bytes 6291456 | tf_op jit(solution)/shard_map/pallas_call | solution.py:538
  276.5 17.7 %shard_map.218 = (bf16[1024,384]{1,0:T(8,128)(2,1)S(1)}, bf16[512,2048]{1,0:T(8,128)(2,1)}, bf16[512,2048]{1,0:T(8,128)(2,1)S(1)}) custom-call(bf16[128,2048]{1,0:T(8,128)(2,1)} %get-tuple-element.105.refs_0_, bf16[128,2048]{1,0:T(8,128)(2,1)} %collective-permute-done.40.refs_1_, bf16[128,2048]{1,0:T(8,128)(2,1)} %collective-permute-done.41.refs_2_, ...), custom_call_target="tpu_custom_call" | custom-call | flops 5368709120 | bytes 15728640 | tf_op jit(solution)/shard_map/pallas_call | solution.py:493
  304.9 3.9 %collective-permute-start.56 = (bf16[64,2048]{1,0:T(8,128)(2,1)S(1)}, bf16[64,2048]{1,0:T(8,128)(2,1)S(1)}, u32[]{:S(2)}, u32[]{:S(2)}) collective-permute-start(bf16[64,2048]{1,0:T(8,128)(2,1)S(1)} %get-tuple-element.149), channel_id=1, source_target_pairs={{16,0},{25,9},{64,80},{73,89},{18,2},{27,11},{66,82},{75,91},{20,4... | collective-permute-start | bytes 786440 | tf_op jit(solution)/shard_map/ppermute | solution.py:867
  309.5 5.0 %shard_map.219 = bf16[2,4,256,384]{3,2,1,0:T(8,128)(2,1)S(1)} custom-call(bf16[144,2048]{1,0:T(8,128)(2,1)} %copy-done.18, bf16[144,2048]{1,0:T(8,128)(2,1)} %collective-permute-done.4.refs_1_.refs_9_, bf16[144,2048]{1,0:T(8,128)(2,1)} %collective-permute-done.5.refs_2_.refs_10_, bf16[144,2048]{1,0:T(8,128)(2,1)} %collective-permute-done.6.refs_3_.refs_11_, ...), custom_call_target="tpu_custom_call" | custom-call | flops 1610612736 | bytes 6291456 | tf_op jit(solution)/shard_map/pallas_call | solution.py:569
  334.5 7.5 %collective-permute-start.66 = (bf16[128,2048]{1,0:T(8,128)(2,1)}, bf16[128,2048]{1,0:T(8,128)(2,1)S(1)}, u32[]{:S(2)}, u32[]{:S(2)}) collective-permute-start(bf16[128,2048]{1,0:T(8,128)(2,1)} %get-tuple-element.155), channel_id=1, source_target_pairs={{0,64},{32,96},{64,0},{96,32},{1,65},{33,97},{65,1},{97,33},{2,66}... | collective-permute-start | bytes 1572872 | tf_op jit(solution)/shard_map/ppermute | solution.py:639
  343.8 4.2 %collective-permute-start.64 = (bf16[2,64,384]{2,1,0:T(8,128)(2,1)S(1)}, bf16[2,64,384]{2,1,0:T(8,128)(2,1)S(1)}, u32[]{:S(2)}, u32[]{:S(2)}) collective-permute-start(bf16[2,64,384]{2,1,0:T(8,128)(2,1)S(1)} %get-tuple-element.212), channel_id=1, source_target_pairs={{0,4},{2,6},{4,0},{6,2},{1,5},{3,7},{5,1},{7,3},{8,12},{10,14},{12... | collective-permute-start | bytes 294920 | tf_op jit(solution)/shard_map/ppermute | solution.py:707
  352.8 3.8 collective-permute-start.74
  367.1 10.6 %collective-permute-done.71 = bf16[32,640]{1,0:T(8,128)(2,1)S(1)} collective-permute-done((bf16[32,640]{1,0:T(8,128)(2,1)S(1)}, bf16[32,640]{1,0:T(8,128)(2,1)S(1)}, u32[]{:S(2)}, u32[]{:S(2)}) %collective-permute-start.71) | collective-permute-done | bytes 40992 | tf_op jit(solution)/shard_map/ppermute | solution.py:639
  (389 shorter events, 155.9 us)
Async XLA Ops:
  7.2 61.6 %all-gather.3.cloned.1.call-start = ((), (), s32[]{:S(2)}) async-start(), calls=%async_computation.1 | async-start | bytes 1671168 | tf_op jit(solution)/shard_map/all_gather | solution.py:783
  18.9 142.9 %all-gather.5.cloned.1.call-start = ((), (), s32[]{:S(2)}) async-start(), calls=%async_computation.2 | async-start | bytes 10027008 | tf_op jit(solution)/shard_map/all_gather | solution.py:829
  68.8 260.7 %reduce-scatter.2.cloned.1.call-start = ((), (), s32[]{:S(2)}) async-start(), calls=%async_computation.3 | async-start | bytes 10027008 | tf_op jit(solution)/shard_map/reduce_scatter | solution.py:846
  69.9 25.4 %collective-permute-start.18 = (bf16[128,2048]{1,0:T(8,128)(2,1)S(1)}, bf16[128,2048]{1,0:T(8,128)(2,1)S(1)}, u32[]{:S(2)}, u32[]{:S(2)}) collective-permute-start(bf16[128,2048]{1,0:T(8,128)(2,1)S(1)} %copy-done.6), channel_id=1, source_target_pairs={{0,96},{32,0},{64,32},{96,64},{1,97},{33,1},{65,33},{97,65},{2,98}... | collective-permute-start | bytes 1572872 | tf_op jit(solution)/shard_map/ppermute | solution.py:635
  72.6 26.1 %collective-permute-start.19 = (bf16[128,2048]{1,0:T(8,128)(2,1)S(1)}, bf16[128,2048]{1,0:T(8,128)(2,1)S(1)}, u32[]{:S(2)}, u32[]{:S(2)}) collective-permute-start(bf16[128,2048]{1,0:T(8,128)(2,1)S(1)} %copy-done.6), channel_id=1, source_target_pairs={{0,32},{32,64},{64,96},{96,0},{1,33},{33,65},{65,97},{97,1},{2,34}... | collective-permute-start | bytes 1572872 | tf_op jit(solution)/shard_map/ppermute | solution.py:635
  72.6 26.1 %collective-permute-start.20 = (bf16[128,2048]{1,0:T(8,128)(2,1)S(1)}, bf16[128,2048]{1,0:T(8,128)(2,1)S(1)}, u32[]{:S(2)}, u32[]{:S(2)}) collective-permute-start(bf16[128,2048]{1,0:T(8,128)(2,1)S(1)} %copy-done.6), channel_id=1, source_target_pairs={{0,64},{32,96},{64,0},{96,32},{1,65},{33,97},{65,1},{97,33},{2,66}... | collective-permute-start | bytes 1572872 | tf_op jit(solution)/shard_map/ppermute | solution.py:635
  103.6 26.5 %collective-permute-start.22 = (bf16[128,2048]{1,0:T(8,128)(2,1)S(1)}, bf16[128,2048]{1,0:T(8,128)(2,1)S(1)}, u32[]{:S(2)}, u32[]{:S(2)}) collective-permute-start(bf16[128,2048]{1,0:T(8,128)(2,1)S(1)} %get-tuple-element.167), channel_id=1, source_target_pairs={{0,32},{32,64},{64,96},{96,0},{1,33},{33,65},{65,97},{97,1},{2,34}... | collective-permute-start | bytes 1572872 | tf_op jit(solution)/shard_map/ppermute | solution.py:639
  103.7 26.4 %collective-permute-start.23 = (bf16[128,2048]{1,0:T(8,128)(2,1)S(1)}, bf16[128,2048]{1,0:T(8,128)(2,1)S(1)}, u32[]{:S(2)}, u32[]{:S(2)}) collective-permute-start(bf16[128,2048]{1,0:T(8,128)(2,1)S(1)} %get-tuple-element.166), channel_id=1, source_target_pairs={{0,96},{32,0},{64,32},{96,64},{1,97},{33,1},{65,33},{97,65},{2,98}... | collective-permute-start | bytes 1572872 | tf_op jit(solution)/shard_map/ppermute | solution.py:639
  109.9 25.6 %collective-permute-start.33 = (bf16[128,2048]{1,0:T(8,128)(2,1)S(1)}, bf16[128,2048]{1,0:T(8,128)(2,1)S(1)}, u32[]{:S(2)}, u32[]{:S(2)}) collective-permute-start(bf16[128,2048]{1,0:T(8,128)(2,1)S(1)} %collective-permute-done.18.refs_9_), channel_id=1, source_target_pairs={{0,1},{1,0},{2,3},{3,2},{4,5},{5,4},{6,7},{7,6},{8,9},{9,8},{10,11... | collective-permute-start | bytes 1572872 | tf_op jit(solution)/shard_map/ppermute | solution.py:643
  133.9 25.1 %collective-permute-start.26 = (bf16[128,2048]{1,0:T(8,128)(2,1)S(1)}, bf16[128,2048]{1,0:T(8,128)(2,1)S(1)}, u32[]{:S(2)}, u32[]{:S(2)}) collective-permute-start(bf16[128,2048]{1,0:T(8,128)(2,1)S(1)} %multiply_convert_fusion.refs_0_), channel_id=1, source_target_pairs={{0,32},{32,64},{64,96},{96,0},{1,33},{33,65},{65,97},{97,1},{2,34}... | collective-permute-start | bytes 1572872 | tf_op jit(solution)/shard_map/ppermute | solution.py:635
  133.9 25.1 %collective-permute-start.27 = (bf16[128,2048]{1,0:T(8,128)(2,1)S(1)}, bf16[128,2048]{1,0:T(8,128)(2,1)S(1)}, u32[]{:S(2)}, u32[]{:S(2)}) collective-permute-start(bf16[128,2048]{1,0:T(8,128)(2,1)S(1)} %multiply_convert_fusion.refs_0_), channel_id=1, source_target_pairs={{0,64},{32,96},{64,0},{96,32},{1,65},{33,97},{65,1},{97,33},{2,66}... | collective-permute-start | bytes 1572872 | tf_op jit(solution)/shard_map/ppermute | solution.py:635
  196.5 26.6 %collective-permute-start.37 = (bf16[128,2048]{1,0:T(8,128)(2,1)}, bf16[128,2048]{1,0:T(8,128)(2,1)S(1)}, u32[]{:S(2)}, u32[]{:S(2)}) collective-permute-start(bf16[128,2048]{1,0:T(8,128)(2,1)} %get-tuple-element.163), channel_id=1, source_target_pairs={{0,32},{32,64},{64,96},{96,0},{1,33},{33,65},{65,97},{97,1},{2,34}... | collective-permute-start | bytes 1572872 | tf_op jit(solution)/shard_map/ppermute | solution.py:639
  196.5 26.6 %collective-permute-start.38 = (bf16[128,2048]{1,0:T(8,128)(2,1)}, bf16[128,2048]{1,0:T(8,128)(2,1)}, u32[]{:S(2)}, u32[]{:S(2)}) collective-permute-start(bf16[128,2048]{1,0:T(8,128)(2,1)} %get-tuple-element.162), channel_id=1, source_target_pairs={{0,96},{32,0},{64,32},{96,64},{1,97},{33,1},{65,33},{97,65},{2,98}... | collective-permute-start | bytes 1572872 | tf_op jit(solution)/shard_map/ppermute | solution.py:639
  227.7 25.0 %collective-permute-start.40 = (bf16[128,2048]{1,0:T(8,128)(2,1)}, bf16[128,2048]{1,0:T(8,128)(2,1)}, u32[]{:S(2)}, u32[]{:S(2)}) collective-permute-start(bf16[128,2048]{1,0:T(8,128)(2,1)} %get-tuple-element.105.refs_0_), channel_id=1, source_target_pairs={{0,96},{32,0},{64,32},{96,64},{1,97},{33,1},{65,33},{97,65},{2,98}... | collective-permute-start | bytes 1572872 | tf_op jit(solution)/shard_map/ppermute | solution.py:635
  230.9 25.3 %collective-permute-start.41 = (bf16[128,2048]{1,0:T(8,128)(2,1)}, bf16[128,2048]{1,0:T(8,128)(2,1)}, u32[]{:S(2)}, u32[]{:S(2)}) collective-permute-start(bf16[128,2048]{1,0:T(8,128)(2,1)} %get-tuple-element.105.refs_0_), channel_id=1, source_target_pairs={{0,32},{32,64},{64,96},{96,0},{1,33},{33,65},{65,97},{97,1},{2,34}... | collective-permute-start | bytes 1572872 | tf_op jit(solution)/shard_map/ppermute | solution.py:635
  230.9 25.3 %collective-permute-start.42 = (bf16[128,2048]{1,0:T(8,128)(2,1)}, bf16[128,2048]{1,0:T(8,128)(2,1)}, u32[]{:S(2)}, u32[]{:S(2)}) collective-permute-start(bf16[128,2048]{1,0:T(8,128)(2,1)} %get-tuple-element.105.refs_0_), channel_id=1, source_target_pairs={{0,64},{32,96},{64,0},{96,32},{1,65},{33,97},{65,1},{97,33},{2,66}... | collective-permute-start | bytes 1572872 | tf_op jit(solution)/shard_map/ppermute | solution.py:635
  270.1 26.2 %collective-permute-start.44 = (bf16[128,2048]{1,0:T(8,128)(2,1)S(1)}, bf16[128,2048]{1,0:T(8,128)(2,1)S(1)}, u32[]{:S(2)}, u32[]{:S(2)}) collective-permute-start(bf16[128,2048]{1,0:T(8,128)(2,1)S(1)} %get-tuple-element.160), channel_id=1, source_target_pairs={{0,32},{32,64},{64,96},{96,0},{1,33},{33,65},{65,97},{97,1},{2,34}... | collective-permute-start | bytes 1572872 | tf_op jit(solution)/shard_map/ppermute | solution.py:639
  270.2 27.6 %collective-permute-start.45 = (bf16[128,2048]{1,0:T(8,128)(2,1)S(1)}, bf16[128,2048]{1,0:T(8,128)(2,1)S(1)}, u32[]{:S(2)}, u32[]{:S(2)}) collective-permute-start(bf16[128,2048]{1,0:T(8,128)(2,1)S(1)} %get-tuple-element.159), channel_id=1, source_target_pairs={{0,96},{32,0},{64,32},{96,64},{1,97},{33,1},{65,33},{97,65},{2,98}... | collective-permute-start | bytes 1572872 | tf_op jit(solution)/shard_map/ppermute | solution.py:639
  273.6 26.6 %collective-permute-start.51 = (bf16[64,2048]{1,0:T(8,128)(2,1)S(1)}, bf16[64,2048]{1,0:T(8,128)(2,1)S(1)}, u32[]{:S(2)}, u32[]{:S(2)}) collective-permute-start(bf16[64,2048]{1,0:T(8,128)(2,1)S(1)} %get-tuple-element.181), channel_id=1, source_target_pairs={{0,2},{2,4},{4,6},{6,0},{1,3},{3,5},{5,7},{7,1},{8,10},{10,12},{12... | collective-permute-start | bytes 786440 | tf_op jit(solution)/shard_map/ppermute | solution.py:707
  273.7 26.5 %collective-permute-start.52 = (bf16[64,2048]{1,0:T(8,128)(2,1)S(1)}, bf16[64,2048]{1,0:T(8,128)(2,1)S(1)}, u32[]{:S(2)}, u32[]{:S(2)}) collective-permute-start(bf16[64,2048]{1,0:T(8,128)(2,1)S(1)} %get-tuple-element.180), channel_id=1, source_target_pairs={{0,4},{2,6},{4,0},{6,2},{1,5},{3,7},{5,1},{7,3},{8,12},{10,14},{12... | collective-permute-start | bytes 786440 | tf_op jit(solution)/shard_map/ppermute | solution.py:707
  317.4 24.8 %collective-permute-start.61 = (bf16[128,2048]{1,0:T(8,128)(2,1)}, bf16[128,2048]{1,0:T(8,128)(2,1)S(1)}, u32[]{:S(2)}, u32[]{:S(2)}) collective-permute-start(bf16[128,2048]{1,0:T(8,128)(2,1)} %get-tuple-element.157), channel_id=1, source_target_pairs={{0,32},{32,64},{64,96},{96,0},{1,33},{33,65},{65,97},{97,1},{2,34}... | collective-permute-start | bytes 1572872 | tf_op jit(solution)/shard_map/ppermute | solution.py:639
  317.4 24.8 %collective-permute-start.62 = (bf16[128,2048]{1,0:T(8,128)(2,1)}, bf16[128,2048]{1,0:T(8,128)(2,1)S(1)}, u32[]{:S(2)}, u32[]{:S(2)}) collective-permute-start(bf16[128,2048]{1,0:T(8,128)(2,1)} %get-tuple-element.156), channel_id=1, source_target_pairs={{0,96},{32,0},{64,32},{96,64},{1,97},{33,1},{65,33},{97,65},{2,98}... | collective-permute-start | bytes 1572872 | tf_op jit(solution)/shard_map/ppermute | solution.py:639
  352.7 28.4 %collective-permute-start.72 = (bf16[32,3072]{1,0:T(8,128)(2,1)S(1)}, bf16[32,3072]{1,0:T(8,128)(2,1)S(1)}, u32[]{:S(2)}, u32[]{:S(2)}) collective-permute-start(bf16[32,3072]{1,0:T(8,128)(2,1)S(1)} %get-tuple-element.208), channel_id=1, source_target_pairs={{0,32},{32,64},{64,96},{96,0},{1,33},{33,65},{65,97},{97,1},{2,34}... | collective-permute-start | bytes 589832 | tf_op jit(solution)/shard_map/ppermute | solution.py:639
  352.8 28.3 %collective-permute-start.74 = (bf16[32,3072]{1,0:T(8,128)(2,1)S(1)}, bf16[32,3072]{1,0:T(8,128)(2,1)S(1)}, u32[]{:S(2)}, u32[]{:S(2)}) collective-permute-start(bf16[32,3072]{1,0:T(8,128)(2,1)S(1)} %get-tuple-element.208), channel_id=1, source_target_pairs={{0,96},{32,0},{64,32},{96,64},{1,97},{33,1},{65,33},{97,65},{2,98}... | collective-permute-start | bytes 589832 | tf_op jit(solution)/shard_map/ppermute | solution.py:639
  (115 other events, 1267.3 us)
Sparse Core Ops, SparseCore 0:
  19.0 49.6 all-gather.2
  70.9 75.7 all-gather.4
  227.9 94.7 reduce-scatter.1

commit v6 on v5

--- a/solution.py
+++ b/solution.py
@@ -91,20 +91,59 @@
     return copies
 
 
+def back_kernel(*refs):
+    parts, packed, out, c, down, c_sems, d_sems = refs[:8], *refs[8:]
+    step = pl.program_id(0)
+    loads = block_copies(parts, c, c_sems)
+
+    @pl.when(step == 0)
+    def _():
+        rows = down_copies(packed, down, d_sems)
+        for copy in loads[:4] + rows + loads[4:]:
+            copy.start()
+        for copy in loads[:4] + rows:
+            copy.wait()
+
+    @pl.when(step == 1)
+    def _():
+        for copy in loads[4:]:
+            copy.wait()
+
+    rows = pl.ds(pl.multiple_of(step * 512, 512), 512)
+    out[...] = dot_nt(c[rows, :], down[...])
+
+
+def feed_back(c_parts, packed):
+    return pl.pallas_call(
+        back_kernel,
+        grid=(2,),
+        in_specs=[HBM] * 9,
+        out_specs=pl.BlockSpec((512, WIDE), lambda i: (i, 0)),
+        out_shape=jax.ShapeDtypeStruct((1024, WIDE), F32),
+        scratch_shapes=[
+            pltpu.VMEM((1024, D), BF16),
+            pltpu.VMEM((WIDE, D), BF16),
+            pltpu.SemaphoreType.DMA((8,)),
+            pltpu.SemaphoreType.DMA((64,)),
+        ],
+        compiler_params=pltpu.CompilerParams(vmem_limit_bytes=24 * 1024 * 1024),
+        cost_estimate=pl.CostEstimate(
+            flops=2 * 1024 * D * WIDE, bytes_accessed=10 * 2**20, transcendentals=0
+        ),
+    )(*in_hbm(*c_parts, packed))
+
+
 def feed_kernel(*refs):
-    x_parts, c_parts, packed = refs[:8], refs[8:16], refs[16]
-    hidden, grads, far, near = refs[17:21]
-    x, c, feed, down, x_sems, c_sems, f_sems, d_sems = refs[21:]
+    x_parts, packed, back = refs[:8], refs[8], refs[9]
+    hidden, grads, far, near, x, feed, x_sems, f_sems = refs[10:]
     step = pl.program_id(0)
-
-    first, third = block_copies(x_parts, x, x_sems), block_copies(c_parts, c, c_sems)
+    first = block_copies(x_parts, x, x_sems)
 
     @pl.when(step == 0)
     def _():
-        second, fourth = feed_copies(packed, feed, f_sems), down_copies(packed, down, d_sems)
-        for group in (first[4:6], second, third[4:6], fourth, first[6:], third[6:], first[:4], third[:4]):
-            for copy in group:
-                copy.start()
+        second = feed_copies(packed, feed, f_sems)
+        for copy in first[4:6] + second + first[6:] + first[:4]:
+            copy.start()
         for copy in first[4:6] + second:
             copy.wait()
 
@@ -113,27 +152,21 @@
         @pl.when(step == k)
         def _(k=k):
             spot = (2 * k + 4) % 8
-            for copy in first[spot : spot + 2] + third[spot : spot + 2]:
+            for copy in first[spot : spot + 2]:
                 copy.wait()
 
     rows = pl.ds(pl.multiple_of(((step + 2) % 4) * 256, 256), 256)
     block = x[rows, :]
-    gate = dot_nn(block, feed[:, :WIDE])
-    up = dot_nn(block, feed[:, WIDE:])
-
-    @pl.when(step == 0)
-    def _():
-        for copy in third[4:6] + down_copies(packed, down, d_sems):
-            copy.wait()
-
-    back = dot_nt(c[rows, :], down[...])
-    sig = jax.nn.sigmoid(gate)
-    silu = gate * sig
-    hidden[...] = (silu * up).astype(BF16)
-    grad_gate = (back * up * (sig * (1.0 + gate * (1.0 - sig)))).astype(BF16)
-    grad_up = (back * silu).astype(BF16)
-    grads[:, :WIDE] = grad_gate
-    grads[:, WIDE:] = grad_up
+    for k in range(0, WIDE, 256):
+        here, beside = slice(k, k + 256), slice(WIDE + k, WIDE + k + 256)
+        gate = dot_nn(block, feed[:, here])
+        up = dot_nn(block, feed[:, beside])
+        slope = back[:, here]
+        sig = jax.nn.sigmoid(gate)
+        silu = gate * sig
+        hidden[:, here] = (silu * up).astype(BF16)
+        grads[:, here] = (slope * up * (sig * (1.0 + gate * (1.0 - sig)))).astype(BF16)
+        grads[:, beside] = (slope * silu).astype(BF16)
     inner = dot_nt(grads[...], feed[...])
 
     @pl.when(step < 2)
@@ -145,12 +178,12 @@
         near[...] = inner.astype(BF16)
 
 
-def feed_forward(x_parts, c_parts, packed):
+def feed_forward(x_parts, packed, back):
     row = lambda i: ((i + 2) % 4, 0)
     return pl.pallas_call(
         feed_kernel,
         grid=(4,),
-        in_specs=[HBM] * 17,
+        in_specs=[HBM] * 9 + [pl.BlockSpec((256, WIDE), row)],
         out_specs=[
             pl.BlockSpec((256, WIDE), row),
             pl.BlockSpec((256, 2 * WIDE), row),
@@ -165,19 +198,15 @@
         ],
         scratch_shapes=[
             pltpu.VMEM((1024, D), BF16),
-            pltpu.VMEM((1024, D), BF16),
             pltpu.VMEM((D, 2 * WIDE), BF16),
-            pltpu.VMEM((WIDE, D), BF16),
-            pltpu.SemaphoreType.DMA((8,)),
             pltpu.SemaphoreType.DMA((8,)),
             pltpu.SemaphoreType.DMA((32,)),
-            pltpu.SemaphoreType.DMA((64,)),
-        ],
-        compiler_params=pltpu.CompilerParams(vmem_limit_bytes=40 * 1024 * 1024),
+        ],
+        compiler_params=pltpu.CompilerParams(vmem_limit_bytes=36 * 1024 * 1024),
         cost_estimate=pl.CostEstimate(
-            flops=2 * 1024 * D * WIDE * 5, bytes_accessed=28 * 2**20, transcendentals=1024 * WIDE
+            flops=2 * 1024 * D * WIDE * 4, bytes_accessed=24 * 2**20, transcendentals=1024 * WIDE
         ),
-    )(*in_hbm(*x_parts, *c_parts, packed))
+    )(*in_hbm(*x_parts, packed), back)
 
 
 def grads_kernel(*refs):
@@ -251,29 +280,40 @@
     )(*in_hbm(*x_parts, *c_parts, hidden, grads))
 
 
-def output_kernel(hidden, packed, far, near, down, sems):
+def output_kernel(hidden_hbm, packed, far, near, hidden, down, total, sems, out_sems):
     copies = down_copies(packed, down, sems)
+    copies.append(pltpu.make_async_copy(hidden_hbm, hidden, sems.at[64]))
     for copy in copies:
         copy.start()
     for copy in copies:
         copy.wait()
-    far[...] = dot_nn(hidden[512:], down[...]).astype(BF16)
-    near[...] = dot_nn(hidden[:512], down[...]).astype(BF16)
+    stores = []
+    for k, out in ((1, far), (0, near)):
+        total[k] = dot_nn(hidden[512 * k : 512 * (k + 1)], down[...]).astype(BF16)
+        stores.append(pltpu.make_async_copy(total.at[k], out, out_sems.at[k]))
+        stores[-1].start()
+    for copy in stores:
+        copy.wait()
 
 
 def output_product(hidden, packed):
-    whole = pl.BlockSpec(memory_space=pltpu.VMEM)
     return pl.pallas_call(
         output_kernel,
-        in_specs=[whole, HBM],
-        out_specs=[whole, whole],
-        out_shape=[jax.ShapeDtypeStruct((512, D), BF16), jax.ShapeDtypeStruct((512, D), BF16)],
-        scratch_shapes=[pltpu.VMEM((WIDE, D), BF16), pltpu.SemaphoreType.DMA((64,))],
+        in_specs=[HBM, HBM],
+        out_specs=[HBM, HBM],
+        out_shape=[pltpu.HBM((512, D), BF16), pltpu.HBM((512, D), BF16)],
+        scratch_shapes=[
+            pltpu.VMEM((1024, WIDE), BF16),
+            pltpu.VMEM((WIDE, D), BF16),
+            pltpu.VMEM((2, 512, D), BF16),
+            pltpu.SemaphoreType.DMA((65,)),
+            pltpu.SemaphoreType.DMA((2,)),
+        ],
         compiler_params=pltpu.CompilerParams(vmem_limit_bytes=24 * 1024 * 1024),
         cost_estimate=pl.CostEstimate(
             flops=2 * 1024 * D * WIDE, bytes_accessed=11 * 2**20, transcendentals=0
         ),
-    )(hidden, *in_hbm(packed))
+    )(*in_hbm(hidden, packed))
 
 
 def rotary_table():
@@ -282,10 +322,12 @@
     angle = (place * inverse).astype(np.float32)
     cosine, sine = np.cos(angle), np.sin(angle)
     zero, one = np.zeros((CAP, 64), np.float32), np.ones((CAP, 64), np.float32)
-    straight = np.concatenate([cosine, cosine] * 5 + [one], axis=1)
-    down = np.concatenate([-sine, zero[:, :32]] * 5 + [zero], axis=1)
-    up = np.concatenate([zero[:, :32], sine] * 5 + [zero], axis=1)
-    table = np.concatenate([straight, down, up], axis=1)
+    ahead = np.concatenate([-sine, zero[:, :32]], axis=1)
+    behind = np.concatenate([zero[:, :32], sine], axis=1)
+    cosine = np.concatenate([cosine, cosine], axis=1)
+    table = np.concatenate(
+        [cosine, cosine, ahead, ahead, behind, behind, cosine, one, ahead, zero, behind, zero], axis=1
+    )
     high = table.astype(ml_dtypes.bfloat16)
     rest = (table - high.astype(np.float32)).astype(ml_dtypes.bfloat16)
     return jnp.asarray(np.stack([high, rest]))
@@ -306,10 +348,12 @@
 
 
 def turned(item, factors, sign):
-    other = (
-        pltpu.roll(item, 352, 1) * factors[:, 384:768] + pltpu.roll(item, 32, 1) * factors[:, 768:]
-    )
-    return item * factors[:, :384] + sign * other
+    def three(k):
+        pair = factors[:, CAP * k : CAP * (k + 1)]
+        return jnp.concatenate([pair, pair, factors[:, CAP * (k + 3) : CAP * (k + 4)]], axis=1)
+
+    other = pltpu.roll(item, 352, 1) * three(1) + pltpu.roll(item, 32, 1) * three(2)
+    return item * three(0) + sign * other
 
 
 def stack_heads(item):
@@ -392,7 +436,7 @@
     return pl.pallas_call(
         attend_kernel,
         grid=(2,),
-        in_specs=[HBM] * 8 + [pl.BlockSpec((2, CAP, 1152), lambda i: (0, 0, 0))] + [HBM] * 2,
+        in_specs=[HBM] * 8 + [pl.BlockSpec((2, CAP, 768), lambda i: (0, 0, 0))] + [HBM] * 2,
         out_specs=[
             pl.BlockSpec((512, 256), row),
             pl.BlockSpec((512, CAP), row),
@@ -423,80 +467,116 @@
     )(*in_hbm(*parts), table, *in_hbm(qkv_full, out_full))
 
 
+def prepare_kernel(*refs):
+    parts, table, queries, key_values = refs[:8], *refs[8:11]
+    probs, keys, values, folded, factors, ids, i_sems = refs[11:]
+    step = pl.program_id(0)
+
+    @pl.when(step == 0)
+    def _():
+        copies = id_copies(parts, ids, i_sems)
+        for copy in copies:
+            copy.start()
+        for copy in copies:
+            copy.wait()
+
+    to_key, to_value = spreads()
+    allowed, around = block_tables(ids[step], table)
+    factors[...] = around
+    both = key_values[...]
+    keys[...] = dot_nn(both, to_key).astype(BF16)
+    values[...] = dot_nn(both, to_value).astype(BF16)
+    folded[...] = dot_nt(stack_heads(queries[...]), to_key).astype(BF16)
+    for h, item in enumerate(softmax_heads(queries[...], keys[...], allowed)):
+        probs[CAP * h : CAP * (h + 1), :] = item
+
+
+def prepare_back(id_parts, table, queries, key_values):
+    row = lambda i: (i, 0)
+    sizes = ((512, CAP, F32), (CAP, 256, BF16), (CAP, 256, BF16), (512, CAP, BF16), (CAP, 768, F32))
+    return pl.pallas_call(
+        prepare_kernel,
+        grid=(8,),
+        in_specs=[HBM] * 8
+        + [pl.BlockSpec((2, CAP, 768), lambda i: (0, 0, 0))]
+        + [pl.BlockSpec((CAP, 256), row), pl.BlockSpec((CAP, CAP), row)],
+        out_specs=[pl.BlockSpec((rows, lanes), row) for rows, lanes, _ in sizes],
+        out_shape=[jax.ShapeDtypeStruct((8 * rows, lanes), kind) for rows, lanes, kind in sizes],
+        scratch_shapes=[pltpu.VMEM((8, 16, CAP), BF16), pltpu.SemaphoreType.DMA((8,))],
+        compiler_params=pltpu.CompilerParams(vmem_limit_bytes=20 * 1024 * 1024),
+        cost_estimate=pl.CostEstimate(
+            flops=2**30, bytes_accessed=9 * 2**20, transcendentals=2**19
+        ),
+    )(*in_hbm(*id_parts), table, queries, key_values)
+
+
 def attend_back_kernel(*refs):
-    parts, id_parts, table = refs[:8], refs[8:16], refs[16]
-    w_hbm, o_hbm, queries, key_values = refs[17:21]
-    grads, far, near = refs[21:24]
-    g, ids, w, o, g_sems, i_sems, w_sems = refs[24:]
+    parts, w_hbm, o_hbm = refs[:8], refs[8], refs[9]
+    probs, keys, values, folded, factors = refs[10:15]
+    grads, far, near, g, w, o, g_sems, w_sems = refs[15:]
     step = pl.program_id(0)
-    blocks, numbers = block_copies(parts, g, g_sems), id_copies(id_parts, ids, i_sems)
+    blocks = block_copies(parts, g, g_sems)
     loads = [
-        pltpu.make_async_copy(o_hbm, o, w_sems.at[1]),
-        pltpu.make_async_copy(w_hbm, w, w_sems.at[0]),
+        pltpu.make_async_copy(o_hbm, o, w_sems.at[0]),
+        pltpu.make_async_copy(w_hbm, w, w_sems.at[1]),
     ]
 
     @pl.when(step == 0)
     def _():
-        for copy in loads[:1] + blocks[4:] + numbers[4:] + loads[1:] + blocks[:4] + numbers[:4]:
+        for copy in loads[:1] + blocks[4:] + loads[1:] + blocks[:4]:
             copy.start()
-        for copy in loads[:1] + blocks[4:] + numbers[4:]:
+        for copy in loads[:1] + blocks[4:]:
             copy.wait()
 
     @pl.when(step == 1)
     def _():
-        for copy in blocks[:4] + numbers[:4]:
+        for copy in blocks[:4]:
             copy.wait()
 
-    half = 1 - step
-    rows = pl.ds(pl.multiple_of(half * 512, 512), 512)
+    rows = pl.ds(pl.multiple_of((1 - step) * 512, 512), 512)
     grad_mixed = dot_nt(g[rows, :], o[...]).astype(BF16)
-    to_key, to_value = spreads()
+    to_value = spreads()[1]
     for k in range(4):
-        allowed, factors = block_tables(ids[half * 4 + k], table)
-        here = slice(CAP * k, CAP * (k + 1))
-        query, both = queries[here, :], key_values[here, :]
-        keys = dot_nn(both, to_key).astype(BF16)
-        values = dot_nn(both, to_value).astype(BF16)
-        probs = softmax_heads(query, keys, allowed)
+        here, heads = slice(CAP * k, CAP * (k + 1)), slice(512 * k, 512 * (k + 1))
         grad_heads = stack_heads(grad_mixed[here])
-        grad_probs = dot_nt(grad_heads, values)
-        scores = []
-        for h in range(4):
-            part = grad_probs[CAP * h : CAP * (h + 1)]
-            delta = jnp.sum(probs[h] * part, axis=1, keepdims=True)
-            scores.append((probs[h] * (part - delta)).astype(BF16))
-        grad_query = dot_nn(jnp.concatenate(scores, axis=1), stack_heads(keys)) * 0.125
-        folded = dot_nt(stack_heads(query), to_key).astype(BF16)
+        part = dot_nt(grad_heads, values[here, :])
+        prob = probs[heads, :]
+        scores = (prob * (part - jnp.sum(prob * part, axis=1, keepdims=True))).astype(BF16)
+        beside = jnp.concatenate([scores[CAP * h : CAP * (h + 1)] for h in range(4)], axis=1)
+        grad_query = dot_nn(beside, stack_heads(keys[here, :])) * 0.125
         grad_folded = dot_nt(grad_heads, to_value).astype(BF16)
-        low = jnp.concatenate([item.astype(BF16) for item in probs], axis=0)
-        grad_both = dot_tn(jnp.concatenate(scores, axis=0), folded) * 0.125 + dot_tn(low, grad_folded)
+        grad_both = dot_tn(scores, folded[heads, :]) * 0.125 + dot_tn(prob.astype(BF16), grad_folded)
         item = jnp.concatenate([grad_query, grad_both], axis=1)
-        grads[here, :] = turned(item, factors, -1.0).astype(BF16)
+        grads[here, :] = turned(item, factors[here, :], -1.0).astype(BF16)
 
     @pl.when(step == 0)
     def _():
         loads[1].wait()
 
-    total = dot_nt(grads[...], w[...])
+    total = dot_nt(grads[...], w[...]).astype(BF16)
 
     @pl.when(step == 0)
     def _():
-        far[...] = total.astype(BF16)
+        far[...] = total
 
     @pl.when(step == 1)
     def _():
-        near[...] = total.astype(BF16)
-
-
-def attend_back(parts, id_parts, table, qkv_full, out_full, queries, key_values):
+        near[...] = total
+
+
+def attend_back(parts, qkv_full, out_full, prepared):
     row = lambda i: (1 - i, 0)
     return pl.pallas_call(
         attend_back_kernel,
         grid=(2,),
-        in_specs=[HBM] * 16
-        + [pl.BlockSpec((2, CAP, 1152), lambda i: (0, 0, 0))]
-        + [HBM] * 2
-        + [pl.BlockSpec((512, 256), row), pl.BlockSpec((512, CAP), row)],
+        in_specs=[HBM] * 10
+        + [
+            pl.BlockSpec((2048, CAP), row),
+            pl.BlockSpec((512, 256), row),
+            pl.BlockSpec((512, 256), row),
+            pl.BlockSpec((2048, CAP), row),
+            pl.BlockSpec((512, 768), row),
+        ],
         out_specs=[
             pl.BlockSpec((512, 384), row),
             pl.BlockSpec((512, D), lambda i: (0, 0)),
@@ -509,18 +589,16 @@
         ],
         scratch_shapes=[
             pltpu.VMEM((1024, D), BF16),
-            pltpu.VMEM((8, 16, CAP), BF16),
             pltpu.VMEM((D, 384), BF16),
             pltpu.VMEM((256, D), BF16),
             pltpu.SemaphoreType.DMA((8,)),
-            pltpu.SemaphoreType.DMA((8,)),
             pltpu.SemaphoreType.DMA((2,)),
         ],
-        compiler_params=pltpu.CompilerParams(vmem_limit_bytes=32 * 1024 * 1024),
+        compiler_params=pltpu.CompilerParams(vmem_limit_bytes=36 * 1024 * 1024),
         cost_estimate=pl.CostEstimate(
-            flops=2 * 1024 * D * 640 * 2, bytes_accessed=15 * 2**20, transcendentals=2**19
+            flops=2 * 1024 * D * 640 * 2, bytes_accessed=15 * 2**20, transcendentals=0
         ),
-    )(*in_hbm(*parts, *id_parts), table, *in_hbm(qkv_full, out_full), queries, key_values)
+    )(*in_hbm(*parts, qkv_full, out_full), *prepared)
 
 
 def out_grads_kernel(*refs):
@@ -601,12 +679,12 @@
         grid=(CAP // 32,),
         in_specs=[spec] * 6,
         out_specs=[spec] * 2,
-        out_shape=[jax.ShapeDtypeStruct((CAP, D), F32), jax.ShapeDtypeStruct((CAP, D), BF16)],
+        out_shape=[pltpu.HBM((CAP, D), F32), pltpu.HBM((CAP, D), BF16)],
         compiler_params=pltpu.CompilerParams(vmem_limit_bytes=16 * 1024 * 1024),
         cost_estimate=pl.CostEstimate(
             flops=20 * CAP * D, bytes_accessed=6 * 2**20, transcendentals=CAP
         ),
-    )(own, *came, rows, upstream)
+    )(*in_hbm(own, *came, rows, upstream))
 
 
 def times(left, right):
@@ -702,11 +780,12 @@
     ]
 
 
+def shifted(item, axis, step):
+    return lax.ppermute(item, axis, [(i, (i + step) % 4) for i in range(4)])
+
+
 def exchange(pieces, axis):
-    return tuple(
-        lax.ppermute(pieces[step], axis, [(i, (i + step) % 4) for i in range(4)])
-        for step in (1, 2, 3)
-    )
+    return tuple(shifted(pieces[step], axis, step) for step in (1, 2, 3))
 
 
 def four_sum(pieces, came):
@@ -832,34 +911,32 @@
     upstream = share_parts(after(cotangent, *first[1:4]), mixed)
     far = after(far, upstream[1])
     shuffle = after(jnp.concatenate([order_of_columns(0), order_of_columns(1)], axis=1), mixed)
-    midway = rows + ring_sum(pair_blocks(near, far), shuffle)
+    blocks = pair_blocks(near, far)
+    prepared = prepare_back(first, table, after(queries, *blocks), key_values)
+    midway = rows + ring_sum(blocks, shuffle, *prepared)
 
     second_scale = rms_scale(midway)
-    second = share_parts((midway * second_scale).astype(BF16))
-    hidden, grad_feed, far, near = feed_forward(second, upstream, packed)
+    back = feed_back(upstream, packed)
+    second = share_parts((midway * second_scale).astype(BF16), back)
+    hidden, grad_feed, far, near = feed_forward(second, packed, back)
     blocks = pair_blocks(near, far)
     pack = feed_grads(second, upstream, after(hidden, *blocks), grad_feed)
     came = tuple(to_ring(blocks[spot], STEPS[spot]) for spot in (1, 2, 3))
-    grad_mid, grad_low = norm_back_sum(blocks[0], after(came, pack), midway, cotangent)
     out_far, out_near = output_product(after(hidden, pack), packed)
-    third = share_parts(grad_low, out_far)
-    pack = lax.psum_scatter(after(pack, grad_low), ("y", "z"), scatter_dimension=0, tiled=True)
-
-    out_blocks = pair_blocks(out_near, after(out_far, *third[1:4]))
+    grad_mid, grad_low = norm_back_sum(blocks[0], after(came, pack, out_far), midway, cotangent)
+    out_blocks = pair_blocks(out_near, after(out_far, grad_low))
+    third = share_parts(grad_low, *out_blocks)
+    pack = lax.psum_scatter(after(pack, *came, out_far), ("y", "z"), scatter_dimension=0, tiled=True)
+
     out_term = out_grads(third, mixed).reshape(4, 64, D)
     out_sent = four_pieces(out_term, z, 0)
-    out_came = exchange(out_sent, "z")
+    out_came = tuple(shifted(out_sent[step], "z", step) for step in (1, 2))
     grad_qkv, far, near = attend_back(
-        third,
-        first,
-        table,
-        qkv_full,
-        out_full,
-        after(queries, *out_sent, *out_blocks),
-        key_values,
+        third, qkv_full, after(out_full, *out_sent, *out_blocks), prepared
     )
     product = ring_sum(out_blocks, grad_qkv)
     output = (midway + product).astype(BF16)
+    out_came += (shifted(after(out_sent[3], grad_qkv), "z", 3),)
     out_part = four_sum(out_sent, after(out_came, product))
     far = after(far, out_part)
     sent = out_part.astype(BF16)

time: 400 us -> 387 us (0.968)
  the two profiles are of different devices: /device:TPU:16 before, /device:TPU:1 now
where the time goes in v6:
time: 387 us; the launch traced here: 380 us
  waiting for transfers between devices  121 us (31%)
  Pallas kernels  99.6 us (26%)
  starting transfers between devices  95.4 us (25%)
  other arithmetic  36.4 us (9%)
  between operations  15.7 us (4%)
  local copies, waits for them, and re-layouts  8.78 us (2%)
    ppermute x12, waiting for transfers between devices, from_ring(): return lax.ppermute(item, RING, [(i, (i - step) % 4) for i in range(4)])  59.4 us
    ppermute x12, starting transfers between devices, from_ring(): return lax.ppermute(item, RING, [(i, (i - step) % 4) for i in range(4)])  26.6 us
    ppermute x27, starting transfers between devices, swap(): return lax.ppermute(item, axis, SWAP)  24.3 us
    ppermute x18, waiting for transfers between devices, to_ring(): return lax.ppermute(item, RING, [(i, (i + step) % 4) for i in range(4)])  20.1 us
    pallas_call x1, Pallas kernels, feed_forward(): pl.pallas_call(feed_kernel, grid=(4,), in_specs=[HBM] * 9 + [pl.BlockSpec...  18.5 us
    ppermute x18, starting transfers between devices, to_ring(): return lax.ppermute(item, RING, [(i, (i + step) % 4) for i in range(4)])  18.4 us
    pallas_call x1, Pallas kernels, feed_grads(): pl.pallas_call(grads_kernel, in_specs=[HBM] * 18, out_specs=HBM, out_shap...  16.1 us
    pallas_call x1, Pallas kernels, attend_back(): pl.pallas_call(attend_back_kernel, grid=(2,), in_specs=[HBM] * 10 + [pl.B...  14.4 us
  transfers between devices with their start and end apart: 78, of which 28 were waited for; matrix products, arithmetic and copies ran while one was open for 10% of the time, Pallas kernels for 21%

profile of v6, /device:TPU:1, one launch (start us, length us, event | category | flops | bytes accessed | tf_op | source)
XLA Modules:
  0.0 379.7 jit_solution(11341625548038107449)
XLA Ops:
  31.7 9.7 %collective-permute-start.4 = (bf16[144,2048]{1,0:T(8,128)(2,1)S(1)}, bf16[144,2048]{1,0:T(8,128)(2,1)S(1)}, u32[]{:S(2)}, u32[]{:S(2)}) collective-permute-start(bf16[144,2048]{1,0:T(8,128)(2,1)S(1)} %fusion.16.refs_0_), channel_id=1, source_target_pairs={{0,96},{32,0},{64,32},{96,64},{1,97},{33,1},{65,33},{97,65},{2,98}... | collective-permute-start | bytes 1769480 | tf_op jit(solution)/shard_map/ppermute | solution.py:713
  48.1 18.8 %collective-permute-done.4.refs_1_ = bf16[144,2048]{1,0:T(8,128)(2,1)S(1)} collective-permute-done((bf16[144,2048]{1,0:T(8,128)(2,1)S(1)}, bf16[144,2048]{1,0:T(8,128)(2,1)S(1)}, u32[]{:S(2)}, u32[]{:S(2)}) %collective-permute-start.4) | collective-permute-done | bytes 589856 | tf_op jit(solution)/shard_map/ppermute | solution.py:713
  77.7 14.0 %shard_map.212 = (bf16[1024,256]{1,0:T(8,128)(2,1)S(1)}, bf16[1024,128]{1,0:T(8,128)(2,1)S(1)}, bf16[1024,256]{1,0:T(8,128)(2,1)S(1)}, bf16[512,2048]{1,0:T(8,128)(2,1)S(1)}, bf16[512,2048]{1,0:T(8,128)(2,1)S(1)}) custom-call(bf16[144,2048]{1,0:T(8,128)(2,1)} %copy-done.21, bf16[144,2048]{1,0:T(8,128)(2,1)} %copy-done.22, bf16[144,2048]{1,0:T(8,128)(2,1)} %copy-done.23, ...), custom_call_target="tpu_custom_call" | custom-call | flops 5368709120 | bytes 15728640 | tf_op jit(solution)/shard_map/pallas_call | solution.py:436
  91.7 7.2 %collective-permute-done.20.refs_3_.refs_11_ = bf16[128,2048]{1,0:T(8,128)(2,1)S(1)} collective-permute-done((bf16[128,2048]{1,0:T(8,128)(2,1)}, bf16[128,2048]{1,0:T(8,128)(2,1)S(1)}, u32[]{:S(2)}, u32[]{:S(2)}) %collective-permute-start.20) | collective-permute-done | bytes 524320 | tf_op jit(solution)/shard_map/ppermute | solution.py:713
  111.8 7.6 %shard_map.213 = (f32[4096,128]{1,0:T(8,128)S(1)}, bf16[1024,256]{1,0:T(8,128)(2,1)S(1)}, bf16[1024,256]{1,0:T(8,128)(2,1)S(1)}, bf16[4096,128]{1,0:T(8,128)(2,1)S(1)}, f32[1024,768]{1,0:T(8,128)S(1)}) custom-call(bf16[144,2048]{1,0:T(8,128)(2,1)} %copy-done.21, bf16[144,2048]{1,0:T(8,128)(2,1)} %copy-done.22, bf16[144,2048]{1,0:T(8,128)(2,1)} %copy-done.23, ...), custom_call_target="tpu_custom_call" | custom-call | flops 1073741824 | bytes 9437184 | tf_op jit(solution)/shard_map/pallas_call | solution.py:497
  119.4 11.5 %collective-permute-done.22 = bf16[128,2048]{1,0:T(8,128)(2,1)S(1)} collective-permute-done((bf16[128,2048]{1,0:T(8,128)(2,1)S(1)}, bf16[128,2048]{1,0:T(8,128)(2,1)S(1)}, u32[]{:S(2)}, u32[]{:S(2)}) %collective-permute-start.22) | collective-permute-done | bytes 524320 | tf_op jit(solution)/shard_map/ppermute | solution.py:717
  139.7 7.3 %all-gather.5.cloned.1.call-done.refs_8_.packed = bf16[3072,1536]{1,0:T(8,128)(2,1)} async-done(((bf16[192,1536]{1,0:T(8,128)(2,1)}), bf16[3072,1536]{1,0:T(8,128)(2,1)}) %all-gather.5.cloned.1.call-update) | async-done | bytes 9437200 | tf_op jit(solution)/shard_map/all_gather | solution.py:908
  147.0 7.2 %shard_map.214.refs_9_ = f32[1024,768]{1,0:T(8,128)S(1)} custom-call(bf16[128,2048]{1,0:T(8,128)(2,1)} %upstream.1, bf16[128,2048]{1,0:T(8,128)(2,1)} %copy-done.36, bf16[128,2048]{1,0:T(8,128)(2,1)} %copy-done.37, bf16[128,2048]{1,0:T(8,128)(2,1)} %copy-done.38, bf16[128,2048]{1,0:T(8,128)(2,1)} %copy-done.39, bf16[128,2048]{1,0:T(8,128)(2,1)} %copy-done.40, ...), custom_call_target="tpu_custom_call" | custom-call | flops 3221225472 | bytes 10485760 | tf_op jit(solution)/shard_map/pallas_call | solution.py:117
  154.3 5.7 %collective-permute-done.25.refs_1_ = bf16[128,2048]{1,0:T(8,128)(2,1)} collective-permute-done((bf16[128,2048]{1,0:T(8,128)(2,1)}, bf16[128,2048]{1,0:T(8,128)(2,1)}, u32[]{:S(2)}, u32[]{:S(2)}) %collective-permute-start.25) | collective-permute-done | bytes 524320 | tf_op jit(solution)/shard_map/ppermute | solution.py:713
  168.8 18.5 %shard_map.215 = (bf16[1024,768]{1,0:T(8,128)(2,1)S(1)}, bf16[1024,1536]{1,0:T(8,128)(2,1)S(1)}, bf16[512,2048]{1,0:T(8,128)(2,1)S(1)}, bf16[512,2048]{1,0:T(8,128)(2,1)S(1)}) custom-call(bf16[128,2048]{1,0:T(8,128)(2,1)} %multiply_convert_fusion.refs_0_, bf16[128,2048]{1,0:T(8,128)(2,1)} %collective-permute-done.25.refs_1_, ...), custom_call_target="tpu_custom_call" | custom-call | flops 12884901888 | bytes 25165824 | tf_op jit(solution)/shard_map/pallas_call | solution.py:183
  196.5 16.1 %shard_map.216 = bf16[3072,1536]{1,0:T(8,128)(2,1)} custom-call(bf16[128,2048]{1,0:T(8,128)(2,1)} %multiply_convert_fusion.refs_0_, bf16[128,2048]{1,0:T(8,128)(2,1)} %collective-permute-done.25.refs_1_, bf16[128,2048]{1,0:T(8,128)(2,1)} %collective-permute-done.26.refs_2_, bf16[128,2048]{1,0:T(8,128)(2,1)} %collective-permute-done.27.refs_3_, ...), custom_call_target="tpu_custom_call" | custom-call | flops 9663676416 | bytes 23068672 | tf_op jit(solution)/shard_map/pallas_call | solution.py:260
  212.6 7.9 %shard_map.217 = (bf16[512,2048]{1,0:T(8,128)(2,1)}, bf16[512,2048]{1,0:T(8,128)(2,1)}) custom-call(bf16[1024,768]{1,0:T(8,128)(2,1)} %copy-done.14, bf16[3072,1536]{1,0:T(8,128)(2,1)} %all-gather.5.cloned.1.call-done.refs_8_.packed), custom_call_target="tpu_custom_call" | custom-call | flops 3221225472 | bytes 11534336 | tf_op jit(solution)/shard_map/pallas_call | solution.py:300
  220.6 4.7 %shard_map.218 = (f32[128,2048]{1,0:T(8,128)}, bf16[128,2048]{1,0:T(8,128)(2,1)}) custom-call(f32[128,2048]{1,0:T(8,128)} %get-tuple-element.184.own, bf16[128,2048]{1,0:T(8,128)(2,1)} %collective-permute-done.37.one, bf16[128,2048]{1,0:T(8,128)(2,1)} %collective-permute-done.38.two, bf16[128,2048]{1,0:T(8,128)(2,1)} %collective-permute-done.39.three, ...), custom_call_target="tpu_custom_call" | custom-call | flops 5242880 | bytes 6291456 | tf_op jit(solution)/shard_map/pallas_call | solution.py:677
  233.9 6.2 %collective-permute-done.44.refs_1_ = bf16[128,2048]{1,0:T(8,128)(2,1)} collective-permute-done((bf16[128,2048]{1,0:T(8,128)(2,1)}, bf16[128,2048]{1,0:T(8,128)(2,1)}, u32[]{:S(2)}, u32[]{:S(2)}) %collective-permute-start.44) | collective-permute-done | bytes 524320 | tf_op jit(solution)/shard_map/ppermute | solution.py:713
  242.9 11.3 %collective-permute-done.46.refs_3_ = bf16[128,2048]{1,0:T(8,128)(2,1)} collective-permute-done((bf16[128,2048]{1,0:T(8,128)(2,1)}, bf16[128,2048]{1,0:T(8,128)(2,1)}, u32[]{:S(2)}, u32[]{:S(2)}) %collective-permute-start.46) | collective-permute-done | bytes 524320 | tf_op jit(solution)/shard_map/ppermute | solution.py:713
  258.8 3.9 %shard_map.219 = bf16[256,2048]{1,0:T(8,128)(2,1)S(1)} custom-call(bf16[128,2048]{1,0:T(8,128)(2,1)} %get-tuple-element.126.refs_0_, bf16[128,2048]{1,0:T(8,128)(2,1)} %collective-permute-done.44.refs_1_, bf16[128,2048]{1,0:T(8,128)(2,1)} %collective-permute-done.45.refs_2_, bf16[128,2048]{1,0:T(8,128)(2,1)} %collective-permute-done.46.refs_3_, ...), custom_call_target="tpu_custom_call" | custom-call | flops 1073741824 | bytes 6291456 | tf_op jit(solution)/shard_map/pallas_call | solution.py:616
  266.1 14.4 %shard_map.220 = (bf16[1024,384]{1,0:T(8,128)(2,1)S(1)}, bf16[512,2048]{1,0:T(8,128)(2,1)}, bf16[512,2048]{1,0:T(8,128)(2,1)S(1)}) custom-call(bf16[128,2048]{1,0:T(8,128)(2,1)} %get-tuple-element.126.refs_0_, bf16[128,2048]{1,0:T(8,128)(2,1)} %collective-permute-done.44.refs_1_, bf16[128,2048]{1,0:T(8,128)(2,1)} %collective-permute-done.45.refs_2_, ...), custom_call_target="tpu_custom_call" | custom-call | flops 5368709120 | bytes 15728640 | tf_op jit(solution)/shard_map/pallas_call | solution.py:569
  286.7 4.6 %collective-permute-done.53 = bf16[64,2048]{1,0:T(8,128)(2,1)S(1)} collective-permute-done((bf16[64,2048]{1,0:T(8,128)(2,1)S(1)}, bf16[64,2048]{1,0:T(8,128)(2,1)S(1)}, u32[]{:S(2)}, u32[]{:S(2)}) %collective-permute-start.53) | collective-permute-done | bytes 262176 | tf_op jit(solution)/shard_map/ppermute | solution.py:784
  294.2 4.1 %collective-permute-start.57 = (bf16[64,2048]{1,0:T(8,128)(2,1)S(1)}, bf16[64,2048]{1,0:T(8,128)(2,1)S(1)}, u32[]{:S(2)}, u32[]{:S(2)}) collective-permute-start(bf16[64,2048]{1,0:T(8,128)(2,1)S(1)} %get-tuple-element.169), channel_id=1, source_target_pairs={{24,0},{1,9},{72,80},{81,89},{26,2},{3,11},{74,82},{83,91},{28,4},... | collective-permute-start | bytes 786440 | tf_op jit(solution)/shard_map/ppermute | solution.py:944
  298.4 5.2 %shard_map.221 = bf16[2,4,256,384]{3,2,1,0:T(8,128)(2,1)S(1)} custom-call(bf16[144,2048]{1,0:T(8,128)(2,1)} %copy-done.21, bf16[144,2048]{1,0:T(8,128)(2,1)} %copy-done.22, bf16[144,2048]{1,0:T(8,128)(2,1)} %copy-done.23, bf16[144,2048]{1,0:T(8,128)(2,1)} %copy-done.24, bf16[144,2048]{1,0:T(8,128)(2,1)} %copy-done.25, bf16[144,2048]{1,0:T(8,128)(2,1)} %copy-done.27, ...), custom_call_target="tpu_custom_call" | custom-call | flops 1610612736 | bytes 6291456 | tf_op jit(solution)/shard_map/pallas_call | solution.py:647
  313.5 9.1 %reduce-scatter.2.cloned.1.call-done = bf16[192,1536]{1,0:T(8,128)(2,1)} async-done(((bf16[3072,1536]{1,0:T(8,128)(2,1)}), bf16[192,1536]{1,0:T(8,128)(2,1)}) %reduce-scatter.2.cloned.1.call-update) | async-done | bytes 589840 | tf_op jit(solution)/shard_map/reduce_scatter | solution.py:929
  325.5 5.1 %collective-permute-done.59 = bf16[2,256,384]{2,1,0:T(8,128)(2,1)} collective-permute-done((bf16[2,256,384]{2,1,0:T(8,128)(2,1)}, bf16[2,256,384]{2,1,0:T(8,128)(2,1)}, u32[]{:S(2)}, u32[]{:S(2)}) %collective-permute-start.59) | collective-permute-done | bytes 393248 | tf_op jit(solution)/shard_map/ppermute | solution.py:784
  344.0 4.2 %collective-permute-start.68 = (bf16[64,1408]{1,0:T(8,128)(2,1)S(1)}, bf16[64,1408]{1,0:T(8,128)(2,1)S(1)}, u32[]{:S(2)}, u32[]{:S(2)}) collective-permute-start(bf16[64,1408]{1,0:T(8,128)(2,1)S(1)} %maximum_maximum_fusion.4), channel_id=1, source_target_pairs={{0,1},{1,0},{2,3},{3,2},{4,5},{5,4},{6,7},{7,6},{8,9},{9,8},{10,11... | collective-permute-start | bytes 540680 | tf_op jit(solution)/shard_map/ppermute | solution.py:721
  362.3 5.5 %collective-permute-done.73 = bf16[32,6144]{1,0:T(8,128)(2,1)S(1)} collective-permute-done((bf16[32,6144]{1,0:T(8,128)(2,1)S(1)}, bf16[32,6144]{1,0:T(8,128)(2,1)S(1)}, u32[]{:S(2)}, u32[]{:S(2)}) %collective-permute-start.73) | collective-permute-done | bytes 393248 | tf_op jit(solution)/shard_map/ppermute | solution.py:717
  (399 shorter events, 154.0 us)
Async XLA Ops:
  7.2 63.4 %all-gather.3.cloned.1.call-start = ((), (), s32[]{:S(2)}) async-start(), calls=%async_computation.1 | async-start | bytes 1671168 | tf_op jit(solution)/shard_map/all_gather | solution.py:862
  18.3 128.7 %all-gather.5.cloned.1.call-start = ((), (), s32[]{:S(2)}) async-start(), calls=%async_computation.2 | async-start | bytes 10027008 | tf_op jit(solution)/shard_map/all_gather | solution.py:908
  31.7 35.2 %collective-permute-start.4 = (bf16[144,2048]{1,0:T(8,128)(2,1)S(1)}, bf16[144,2048]{1,0:T(8,128)(2,1)S(1)}, u32[]{:S(2)}, u32[]{:S(2)}) collective-permute-start(bf16[144,2048]{1,0:T(8,128)(2,1)S(1)} %fusion.16.refs_0_), channel_id=1, source_target_pairs={{0,96},{32,0},{64,32},{96,64},{1,97},{33,1},{65,33},{97,65},{2,98}... | collective-permute-start | bytes 1769480 | tf_op jit(solution)/shard_map/ppermute | solution.py:713
  41.4 29.2 %collective-permute-start.5 = (bf16[144,2048]{1,0:T(8,128)(2,1)S(1)}, bf16[144,2048]{1,0:T(8,128)(2,1)S(1)}, u32[]{:S(2)}, u32[]{:S(2)}) collective-permute-start(bf16[144,2048]{1,0:T(8,128)(2,1)S(1)} %fusion.16.refs_0_), channel_id=1, source_target_pairs={{0,32},{32,64},{64,96},{96,0},{1,33},{33,65},{65,97},{97,1},{2,34}... | collective-permute-start | bytes 1769480 | tf_op jit(solution)/shard_map/ppermute | solution.py:713
  42.3 28.3 %collective-permute-start.6 = (bf16[144,2048]{1,0:T(8,128)(2,1)S(1)}, bf16[144,2048]{1,0:T(8,128)(2,1)S(1)}, u32[]{:S(2)}, u32[]{:S(2)}) collective-permute-start(bf16[144,2048]{1,0:T(8,128)(2,1)S(1)} %fusion.16.refs_0_), channel_id=1, source_target_pairs={{0,64},{32,96},{64,0},{96,32},{1,65},{33,97},{65,1},{97,33},{2,66}... | collective-permute-start | bytes 1769480 | tf_op jit(solution)/shard_map/ppermute | solution.py:713
  70.6 252.0 %reduce-scatter.2.cloned.1.call-start = ((), (), s32[]{:S(2)}) async-start(), calls=%async_computation.3 | async-start | bytes 10027008 | tf_op jit(solution)/shard_map/reduce_scatter | solution.py:929
  105.1 25.8 %collective-permute-start.22 = (bf16[128,2048]{1,0:T(8,128)(2,1)S(1)}, bf16[128,2048]{1,0:T(8,128)(2,1)S(1)}, u32[]{:S(2)}, u32[]{:S(2)}) collective-permute-start(bf16[128,2048]{1,0:T(8,128)(2,1)S(1)} %get-tuple-element.187), channel_id=1, source_target_pairs={{0,32},{32,64},{64,96},{96,0},{1,33},{33,65},{65,97},{97,1},{2,34}... | collective-permute-start | bytes 1572872 | tf_op jit(solution)/shard_map/ppermute | solution.py:717
  105.2 26.8 %collective-permute-start.23 = (bf16[128,2048]{1,0:T(8,128)(2,1)S(1)}, bf16[128,2048]{1,0:T(8,128)(2,1)S(1)}, u32[]{:S(2)}, u32[]{:S(2)}) collective-permute-start(bf16[128,2048]{1,0:T(8,128)(2,1)S(1)} %get-tuple-element.186), channel_id=1, source_target_pairs={{0,96},{32,0},{64,32},{96,64},{1,97},{33,1},{65,33},{97,65},{2,98}... | collective-permute-start | bytes 1572872 | tf_op jit(solution)/shard_map/ppermute | solution.py:717
  110.8 26.4 %collective-permute-start.28 = (bf16[128,2048]{1,0:T(8,128)(2,1)}, bf16[128,2048]{1,0:T(8,128)(2,1)S(1)}, u32[]{:S(2)}, u32[]{:S(2)}) collective-permute-start(bf16[128,2048]{1,0:T(8,128)(2,1)} %upstream.1), channel_id=1, source_target_pairs={{0,1},{1,0},{2,3},{3,2},{4,5},{5,4},{6,7},{7,6},{8,9},{9,8},{10,11... | collective-permute-start | bytes 1572872 | tf_op jit(solution)/shard_map/ppermute | solution.py:721
  111.8 25.9 %collective-permute-start.29 = (bf16[128,2048]{1,0:T(8,128)(2,1)S(1)}, bf16[128,2048]{1,0:T(8,128)(2,1)S(1)}, u32[]{:S(2)}, u32[]{:S(2)}) collective-permute-start(bf16[128,2048]{1,0:T(8,128)(2,1)S(1)} %collective-permute-done.18.refs_1_.refs_9_), channel_id=1, source_target_pairs={{0,1},{1,0},{2,3},{3,2},{4,5},{5,4},{6,7},{7,6},{8,9},{9,8},{10,11... | collective-permute-start | bytes 1572872 | tf_op jit(solution)/shard_map/ppermute | solution.py:721
  134.7 25.3 %collective-permute-start.25 = (bf16[128,2048]{1,0:T(8,128)(2,1)}, bf16[128,2048]{1,0:T(8,128)(2,1)}, u32[]{:S(2)}, u32[]{:S(2)}) collective-permute-start(bf16[128,2048]{1,0:T(8,128)(2,1)} %multiply_convert_fusion.refs_0_), channel_id=1, source_target_pairs={{0,96},{32,0},{64,32},{96,64},{1,97},{33,1},{65,33},{97,65},{2,98}... | collective-permute-start | bytes 1572872 | tf_op jit(solution)/shard_map/ppermute | solution.py:713
  137.3 26.4 %collective-permute-start.26 = (bf16[128,2048]{1,0:T(8,128)(2,1)}, bf16[128,2048]{1,0:T(8,128)(2,1)}, u32[]{:S(2)}, u32[]{:S(2)}) collective-permute-start(bf16[128,2048]{1,0:T(8,128)(2,1)} %multiply_convert_fusion.refs_0_), channel_id=1, source_target_pairs={{0,32},{32,64},{64,96},{96,0},{1,33},{33,65},{65,97},{97,1},{2,34}... | collective-permute-start | bytes 1572872 | tf_op jit(solution)/shard_map/ppermute | solution.py:713
  137.7 26.0 %collective-permute-start.27 = (bf16[128,2048]{1,0:T(8,128)(2,1)}, bf16[128,2048]{1,0:T(8,128)(2,1)}, u32[]{:S(2)}, u32[]{:S(2)}) collective-permute-start(bf16[128,2048]{1,0:T(8,128)(2,1)} %multiply_convert_fusion.refs_0_), channel_id=1, source_target_pairs={{0,64},{32,96},{64,0},{96,32},{1,65},{33,97},{65,1},{97,33},{2,66}... | collective-permute-start | bytes 1572872 | tf_op jit(solution)/shard_map/ppermute | solution.py:713
  138.9 26.3 %collective-permute-start.32 = (bf16[128,2048]{1,0:T(8,128)(2,1)}, bf16[128,2048]{1,0:T(8,128)(2,1)}, u32[]{:S(2)}, u32[]{:S(2)}) collective-permute-start(bf16[128,2048]{1,0:T(8,128)(2,1)} %multiply_convert_fusion.refs_0_), channel_id=1, source_target_pairs={{0,1},{1,0},{2,3},{3,2},{4,5},{5,4},{6,7},{7,6},{8,9},{9,8},{10,11... | collective-permute-start | bytes 1572872 | tf_op jit(solution)/shard_map/ppermute | solution.py:721
  193.6 26.9 %collective-permute-start.37 = (bf16[128,2048]{1,0:T(8,128)(2,1)}, bf16[128,2048]{1,0:T(8,128)(2,1)}, u32[]{:S(2)}, u32[]{:S(2)}) collective-permute-start(bf16[128,2048]{1,0:T(8,128)(2,1)} %get-tuple-element.183), channel_id=1, source_target_pairs={{0,32},{32,64},{64,96},{96,0},{1,33},{33,65},{65,97},{97,1},{2,34}... | collective-permute-start | bytes 1572872 | tf_op jit(solution)/shard_map/ppermute | solution.py:717
  193.6 26.9 %collective-permute-start.38 = (bf16[128,2048]{1,0:T(8,128)(2,1)}, bf16[128,2048]{1,0:T(8,128)(2,1)}, u32[]{:S(2)}, u32[]{:S(2)}) collective-permute-start(bf16[128,2048]{1,0:T(8,128)(2,1)} %get-tuple-element.182), channel_id=1, source_target_pairs={{0,96},{32,0},{64,32},{96,64},{1,97},{33,1},{65,33},{97,65},{2,98}... | collective-permute-start | bytes 1572872 | tf_op jit(solution)/shard_map/ppermute | solution.py:717
  228.2 26.0 %collective-permute-start.46 = (bf16[128,2048]{1,0:T(8,128)(2,1)}, bf16[128,2048]{1,0:T(8,128)(2,1)}, u32[]{:S(2)}, u32[]{:S(2)}) collective-permute-start(bf16[128,2048]{1,0:T(8,128)(2,1)} %get-tuple-element.126.refs_0_), channel_id=1, source_target_pairs={{0,64},{32,96},{64,0},{96,32},{1,65},{33,97},{65,1},{97,33},{2,66}... | collective-permute-start | bytes 1572872 | tf_op jit(solution)/shard_map/ppermute | solution.py:713
  255.9 26.3 %collective-permute-start.41 = (bf16[128,2048]{1,0:T(8,128)(2,1)}, bf16[128,2048]{1,0:T(8,128)(2,1)S(1)}, u32[]{:S(2)}, u32[]{:S(2)}) collective-permute-start(bf16[128,2048]{1,0:T(8,128)(2,1)} %get-tuple-element.180), channel_id=1, source_target_pairs={{0,32},{32,64},{64,96},{96,0},{1,33},{33,65},{65,97},{97,1},{2,34}... | collective-permute-start | bytes 1572872 | tf_op jit(solution)/shard_map/ppermute | solution.py:717
  255.9 28.3 %collective-permute-start.42 = (bf16[128,2048]{1,0:T(8,128)(2,1)}, bf16[128,2048]{1,0:T(8,128)(2,1)S(1)}, u32[]{:S(2)}, u32[]{:S(2)}) collective-permute-start(bf16[128,2048]{1,0:T(8,128)(2,1)} %get-tuple-element.179), channel_id=1, source_target_pairs={{0,96},{32,0},{64,32},{96,64},{1,97},{33,1},{65,33},{97,65},{2,98}... | collective-permute-start | bytes 1572872 | tf_op jit(solution)/shard_map/ppermute | solution.py:717
  258.6 25.6 %collective-permute-start.43 = (bf16[128,2048]{1,0:T(8,128)(2,1)}, bf16[128,2048]{1,0:T(8,128)(2,1)S(1)}, u32[]{:S(2)}, u32[]{:S(2)}) collective-permute-start(bf16[128,2048]{1,0:T(8,128)(2,1)} %get-tuple-element.178), channel_id=1, source_target_pairs={{0,64},{32,96},{64,0},{96,32},{1,65},{33,97},{65,1},{97,33},{2,66}... | collective-permute-start | bytes 1572872 | tf_op jit(solution)/shard_map/ppermute | solution.py:717
  262.8 28.6 %collective-permute-start.51 = (bf16[64,2048]{1,0:T(8,128)(2,1)S(1)}, bf16[64,2048]{1,0:T(8,128)(2,1)S(1)}, u32[]{:S(2)}, u32[]{:S(2)}) collective-permute-start(bf16[64,2048]{1,0:T(8,128)(2,1)S(1)} %get-tuple-element.201), channel_id=1, source_target_pairs={{0,2},{2,4},{4,6},{6,0},{1,3},{3,5},{5,7},{7,1},{8,10},{10,12},{12... | collective-permute-start | bytes 786440 | tf_op jit(solution)/shard_map/ppermute | solution.py:784
  263.6 27.7 %collective-permute-start.52 = (bf16[64,2048]{1,0:T(8,128)(2,1)S(1)}, bf16[64,2048]{1,0:T(8,128)(2,1)S(1)}, u32[]{:S(2)}, u32[]{:S(2)}) collective-permute-start(bf16[64,2048]{1,0:T(8,128)(2,1)S(1)} %get-tuple-element.200), channel_id=1, source_target_pairs={{0,4},{2,6},{4,0},{6,2},{1,5},{3,7},{5,1},{7,3},{8,12},{10,14},{12... | collective-permute-start | bytes 786440 | tf_op jit(solution)/shard_map/ppermute | solution.py:784
  306.5 25.6 %collective-permute-start.61 = (bf16[128,2048]{1,0:T(8,128)(2,1)}, bf16[128,2048]{1,0:T(8,128)(2,1)S(1)}, u32[]{:S(2)}, u32[]{:S(2)}) collective-permute-start(bf16[128,2048]{1,0:T(8,128)(2,1)} %get-tuple-element.177), channel_id=1, source_target_pairs={{0,32},{32,64},{64,96},{96,0},{1,33},{33,65},{65,97},{97,1},{2,34}... | collective-permute-start | bytes 1572872 | tf_op jit(solution)/shard_map/ppermute | solution.py:717
  306.5 25.6 %collective-permute-start.62 = (bf16[128,2048]{1,0:T(8,128)(2,1)}, bf16[128,2048]{1,0:T(8,128)(2,1)S(1)}, u32[]{:S(2)}, u32[]{:S(2)}) collective-permute-start(bf16[128,2048]{1,0:T(8,128)(2,1)} %get-tuple-element.176), channel_id=1, source_target_pairs={{0,96},{32,0},{64,32},{96,64},{1,97},{33,1},{65,33},{97,65},{2,98}... | collective-permute-start | bytes 1572872 | tf_op jit(solution)/shard_map/ppermute | solution.py:717
  (119 other events, 1124.6 us)
Sparse Core Ops, SparseCore 0:
  18.4 50.2 all-gather.2
  70.9 76.0 all-gather.4
  220.7 101.8 reduce-scatter.1

commit v7 on v6

--- a/solution.py
+++ b/solution.py
@@ -92,9 +92,10 @@
 
 
 def back_kernel(*refs):
-    parts, packed, out, c, down, c_sems, d_sems = refs[:8], *refs[8:]
+    parts, packed, out, down_out, c, down, c_sems, d_sems, out_sems = refs[:8], *refs[8:]
     step = pl.program_id(0)
     loads = block_copies(parts, c, c_sems)
+    keep = pltpu.make_async_copy(down, down_out, out_sems.at[0])
 
     @pl.when(step == 0)
     def _():
@@ -103,6 +104,7 @@
             copy.start()
         for copy in loads[:4] + rows:
             copy.wait()
+        keep.start()
 
     @pl.when(step == 1)
     def _():
@@ -111,6 +113,10 @@
 
     rows = pl.ds(pl.multiple_of(step * 512, 512), 512)
     out[...] = dot_nt(c[rows, :], down[...])
+
+    @pl.when(step == 1)
+    def _():
+        keep.wait()
 
 
 def feed_back(c_parts, packed):
@@ -118,13 +124,14 @@
         back_kernel,
         grid=(2,),
         in_specs=[HBM] * 9,
-        out_specs=pl.BlockSpec((512, WIDE), lambda i: (i, 0)),
-        out_shape=jax.ShapeDtypeStruct((1024, WIDE), F32),
+        out_specs=[pl.BlockSpec((512, WIDE), lambda i: (i, 0)), HBM],
+        out_shape=[jax.ShapeDtypeStruct((1024, WIDE), F32), pltpu.HBM((WIDE, D), BF16)],
         scratch_shapes=[
             pltpu.VMEM((1024, D), BF16),
             pltpu.VMEM((WIDE, D), BF16),
             pltpu.SemaphoreType.DMA((8,)),
             pltpu.SemaphoreType.DMA((64,)),
+            pltpu.SemaphoreType.DMA((1,)),
         ],
         compiler_params=pltpu.CompilerParams(vmem_limit_bytes=24 * 1024 * 1024),
         cost_estimate=pl.CostEstimate(
@@ -280,9 +287,11 @@
     )(*in_hbm(*x_parts, *c_parts, hidden, grads))
 
 
-def output_kernel(hidden_hbm, packed, far, near, hidden, down, total, sems, out_sems):
-    copies = down_copies(packed, down, sems)
-    copies.append(pltpu.make_async_copy(hidden_hbm, hidden, sems.at[64]))
+def output_kernel(hidden_hbm, down_hbm, far, near, hidden, down, total, sems, out_sems):
+    copies = [
+        pltpu.make_async_copy(down_hbm, down, sems.at[0]),
+        pltpu.make_async_copy(hidden_hbm, hidden, sems.at[1]),
+    ]
     for copy in copies:
         copy.start()
     for copy in copies:
@@ -296,7 +305,7 @@
         copy.wait()
 
 
-def output_product(hidden, packed):
+def output_product(hidden, down_full):
     return pl.pallas_call(
         output_kernel,
         in_specs=[HBM, HBM],
@@ -306,14 +315,14 @@
             pltpu.VMEM((1024, WIDE), BF16),
             pltpu.VMEM((WIDE, D), BF16),
             pltpu.VMEM((2, 512, D), BF16),
-            pltpu.SemaphoreType.DMA((65,)),
+            pltpu.SemaphoreType.DMA((2,)),
             pltpu.SemaphoreType.DMA((2,)),
         ],
         compiler_params=pltpu.CompilerParams(vmem_limit_bytes=24 * 1024 * 1024),
         cost_estimate=pl.CostEstimate(
             flops=2 * 1024 * D * WIDE, bytes_accessed=11 * 2**20, transcendentals=0
         ),
-    )(*in_hbm(hidden, packed))
+    )(*in_hbm(hidden, down_full))
 
 
 def rotary_table():
@@ -685,6 +694,55 @@
             flops=20 * CAP * D, bytes_accessed=6 * 2**20, transcendentals=CAP
         ),
     )(*in_hbm(own, *came, rows, upstream))
+
+
+def finish_kernel(place, here, one, two, three, gain, *refs):
+    query_weight, key_weight, value_weight, half, query, key, value, gain_grad, out = refs
+    stacked = [here[...], one[...], two[:, :640], three[...]]
+    scale = gain[...]
+    lane = lane_of((32, CAP), 1)
+    parts = []
+    for chip in (0, 2, 1, 3):
+        which = lax.rem(place[0] - chip + 4, 4)
+        item = stacked[0]
+        for k in range(1, 4):
+            item = jnp.where(which == k, stacked[k], item)
+        parts.append(item.astype(F32))
+    total = jnp.zeros((32, 1), F32)
+    for k, item in enumerate(parts):
+        side = slice(512 * k, 512 * (k + 1))
+        raw = item[:, :512]
+        query[:, side] = raw * scale
+        total += jnp.sum(raw * query_weight[:, side].astype(F32), axis=1, keepdims=True)
+    for k in range(2):
+        side = slice(CAP * k, CAP * (k + 1))
+        low, high = parts[2 * k][:, 512:], parts[2 * k + 1][:, 512:]
+        raw = jnp.where(lane < HDIM, low, pltpu.roll(high, HDIM, 1))
+        key[:, side] = raw * scale
+        total += jnp.sum(raw * key_weight[:, side].astype(F32), axis=1, keepdims=True)
+        raw = jnp.where(lane < HDIM, pltpu.roll(low, HDIM, 1), high)
+        value[:, side] = raw * scale
+        total += jnp.sum(raw * value_weight[:, side].astype(F32), axis=1, keepdims=True)
+    gain_grad[...] = total
+    out[...] = jnp.where(place[1] == 1, half[...], two[:, 640:]).astype(F32)
+
+
+def finish(place, here, came, gain, weights, half):
+    whole = pl.BlockSpec(memory_space=pltpu.VMEM)
+    return pl.pallas_call(
+        finish_kernel,
+        in_specs=[pl.BlockSpec(memory_space=pltpu.SMEM)] + [whole] * 9,
+        out_specs=[whole] * 5,
+        out_shape=[
+            jax.ShapeDtypeStruct((32, D), F32),
+            jax.ShapeDtypeStruct((32, 256), F32),
+            jax.ShapeDtypeStruct((32, 256), F32),
+            jax.ShapeDtypeStruct((32, 1), F32),
+            jax.ShapeDtypeStruct((32, D), F32),
+        ],
+        compiler_params=pltpu.CompilerParams(vmem_limit_bytes=16 * 1024 * 1024),
+        cost_estimate=pl.CostEstimate(flops=2**19, bytes_accessed=2**20, transcendentals=0),
+    )(place, here, *came, gain, *weights, half)
 
 
 def times(left, right):
@@ -916,13 +974,13 @@
     midway = rows + ring_sum(blocks, shuffle, *prepared)
 
     second_scale = rms_scale(midway)
-    back = feed_back(upstream, packed)
+    back, down_full = feed_back(upstream, packed)
     second = share_parts((midway * second_scale).astype(BF16), back)
     hidden, grad_feed, far, near = feed_forward(second, packed, back)
     blocks = pair_blocks(near, far)
     pack = feed_grads(second, upstream, after(hidden, *blocks), grad_feed)
     came = tuple(to_ring(blocks[spot], STEPS[spot]) for spot in (1, 2, 3))
-    out_far, out_near = output_product(after(hidden, pack), packed)
+    out_far, out_near = output_product(after(hidden, pack), down_full)
     grad_mid, grad_low = norm_back_sum(blocks[0], after(came, pack, out_far), midway, cotangent)
     out_blocks = pair_blocks(out_near, after(out_far, grad_low))
     third = share_parts(grad_low, *out_blocks)
@@ -1053,28 +1111,20 @@
         up_raw * up_weight.astype(F32), axis=1
     )
 
-    parts = by_chip(qkv_here, came)
-    out_grad = jnp.where(y // 2 == xh, out_half, came[1][:, 640:]).astype(F32)
-
-    def joined(start, end):
-        return jnp.concatenate(
-            [parts[k][h][:, start:end] for k in range(2) for h in range(2)], axis=1
-        ).astype(F32)
-
-    query_raw, key_raw, value_raw = joined(0, 512), joined(512, 576), joined(576, 640)
-    first_grad = (
-        jnp.sum(query_raw * query_weight.astype(F32), axis=1)
-        + jnp.sum(key_raw * key_weight.astype(F32), axis=1)
-        + jnp.sum(value_raw * value_weight.astype(F32), axis=1)
+    place = jnp.stack([2 * xh + xl, (y // 2 == xh).astype(jnp.int32)]).astype(jnp.int32)
+    weights = (query_weight, key_weight, value_weight)
+    came = after(came, gate_raw, up_raw, second_grad, down_grad)
+    query_grad, key_grad, value_grad, first_grad, out_grad = finish(
+        place, qkv_here, came, first_col, weights, out_half
     )
 
     return (
         output,
         tokens_grad,
-        first_grad,
-        query_raw * first_col,
-        key_raw * first_col,
-        value_raw * first_col,
+        first_grad[:, 0],
+        query_grad,
+        key_grad,
+        value_grad,
         out_grad,
         second_grad,
         gate_raw * second_col,

time: 387 us -> 383 us (0.990)
  the two profiles are of different devices: /device:TPU:1 before, /device:TPU:30 now
where the time goes in v7:
time: 383 us; the launch traced here: 376 us
  waiting for transfers between devices  132 us (34%)
  Pallas kernels  99.8 us (26%)
  starting transfers between devices  81 us (21%)
  other arithmetic  33.4 us (9%)
  between operations  15.8 us (4%)
  local copies, waits for them, and re-layouts  11.7 us (3%)
    ppermute x12, waiting for transfers between devices, from_ring(): return lax.ppermute(item, RING, [(i, (i - step) % 4) for i in range(4)])  47 us
    ppermute x18, starting transfers between devices, to_ring(): return lax.ppermute(item, RING, [(i, (i + step) % 4) for i in range(4)])  31.3 us
    ppermute x18, waiting for transfers between devices, to_ring(): return lax.ppermute(item, RING, [(i, (i + step) % 4) for i in range(4)])  28 us
    pallas_call x1, Pallas kernels, feed_forward(): pl.pallas_call(feed_kernel, grid=(4,), in_specs=[HBM] * 9 + [pl.BlockSpec...  18.5 us
    ppermute x12, starting transfers between devices, from_ring(): return lax.ppermute(item, RING, [(i, (i - step) % 4) for i in range(4)])  17.2 us
    pallas_call x1, Pallas kernels, feed_grads(): pl.pallas_call(grads_kernel, in_specs=[HBM] * 18, out_specs=HBM, out_shap...  16.1 us
    pallas_call x1, Pallas kernels, attend_back(): pl.pallas_call(attend_back_kernel, grid=(2,), in_specs=[HBM] * 10 + [pl.B...  14.3 us
    pallas_call x1, Pallas kernels, attend(): pl.pallas_call(attend_kernel, grid=(2,), in_specs=[HBM] * 8 + [pl.BlockSp...  14 us
  transfers between devices with their start and end apart: 78, of which 31 were waited for; matrix products, arithmetic and copies ran while one was open for 10% of the time, Pallas kernels for 21%

profile of v7, /device:TPU:30, one launch (start us, length us, event | category | flops | bytes accessed | tf_op | source)
XLA Modules:
  0.0 375.8 jit_solution(13686709255746239160)
XLA Ops:
  22.1 7.8 %collective-permute-done.14 = bf16[64,2048]{1,0:T(8,128)(2,1)S(1)} collective-permute-done((bf16[64,2048]{1,0:T(8,128)(2,1)S(1)}, bf16[64,2048]{1,0:T(8,128)(2,1)S(1)}, u32[]{:S(2)}, u32[]{:S(2)}) %collective-permute-start.14) | collective-permute-done | bytes 262176 | tf_op jit(solution)/shard_map/ppermute | solution.py:955
  43.2 4.3 %collective-permute-done.16 = bf16[64,2048]{1,0:T(8,128)(2,1)} collective-permute-done((bf16[64,2048]{1,0:T(8,128)(2,1)S(1)}, bf16[64,2048]{1,0:T(8,128)(2,1)}, u32[]{:S(2)}, u32[]{:S(2)}) %collective-permute-start.16) | collective-permute-done | bytes 262176 | tf_op jit(solution)/shard_map/ppermute | solution.py:824
  49.9 13.8 %collective-permute-done.4.refs_1_ = bf16[144,2048]{1,0:T(8,128)(2,1)S(1)} collective-permute-done((bf16[144,2048]{1,0:T(8,128)(2,1)S(1)}, bf16[144,2048]{1,0:T(8,128)(2,1)S(1)}, u32[]{:S(2)}, u32[]{:S(2)}) %collective-permute-start.4) | collective-permute-done | bytes 589856 | tf_op jit(solution)/shard_map/ppermute | solution.py:771
  63.7 4.3 %all-gather.3.cloned.1.call-done = bf16[2,1024,384]{2,1,0:T(8,128)(2,1)} async-done(((bf16[2,64,384]{2,1,0:T(8,128)(2,1)}), bf16[2,1024,384]{2,1,0:T(8,128)(2,1)}) %all-gather.3.cloned.1.call-update) | async-done | bytes 1572880 | tf_op jit(solution)/shard_map/all_gather | solution.py:920
  75.3 14.0 %shard_map.212 = (bf16[1024,256]{1,0:T(8,128)(2,1)S(1)}, bf16[1024,128]{1,0:T(8,128)(2,1)S(1)}, bf16[1024,256]{1,0:T(8,128)(2,1)S(1)}, bf16[512,2048]{1,0:T(8,128)(2,1)S(1)}, bf16[512,2048]{1,0:T(8,128)(2,1)S(1)}) custom-call(bf16[144,2048]{1,0:T(8,128)(2,1)} %copy-done.18, bf16[144,2048]{1,0:T(8,128)(2,1)} %copy-done.19, bf16[144,2048]{1,0:T(8,128)(2,1)} %copy-done.20, ...), custom_call_target="tpu_custom_call" | custom-call | flops 5368709120 | bytes 15728640 | tf_op jit(solution)/shard_map/pallas_call | solution.py:445
  89.3 6.4 %collective-permute-done.18.refs_1_.refs_9_ = bf16[128,2048]{1,0:T(8,128)(2,1)S(1)} collective-permute-done((bf16[128,2048]{1,0:T(8,128)(2,1)}, bf16[128,2048]{1,0:T(8,128)(2,1)S(1)}, u32[]{:S(2)}, u32[]{:S(2)}) %collective-permute-start.18) | collective-permute-done | bytes 524320 | tf_op jit(solution)/shard_map/ppermute | solution.py:771
  108.6 7.5 %shard_map.213 = (f32[4096,128]{1,0:T(8,128)S(1)}, bf16[1024,256]{1,0:T(8,128)(2,1)S(1)}, bf16[1024,256]{1,0:T(8,128)(2,1)S(1)}, bf16[4096,128]{1,0:T(8,128)(2,1)S(1)}, f32[1024,768]{1,0:T(8,128)S(1)}) custom-call(bf16[144,2048]{1,0:T(8,128)(2,1)} %copy-done.18, bf16[144,2048]{1,0:T(8,128)(2,1)} %copy-done.19, bf16[144,2048]{1,0:T(8,128)(2,1)} %copy-done.20, ...), custom_call_target="tpu_custom_call" | custom-call | flops 1073741824 | bytes 9437184 | tf_op jit(solution)/shard_map/pallas_call | solution.py:506
  117.5 8.9 %collective-permute-done.22 = bf16[128,2048]{1,0:T(8,128)(2,1)S(1)} collective-permute-done((bf16[128,2048]{1,0:T(8,128)(2,1)S(1)}, bf16[128,2048]{1,0:T(8,128)(2,1)S(1)}, u32[]{:S(2)}, u32[]{:S(2)}) %collective-permute-start.22) | collective-permute-done | bytes 524320 | tf_op jit(solution)/shard_map/ppermute | solution.py:775
  136.3 9.5 %all-gather.5.cloned.1.call-done.refs_8_ = bf16[3072,1536]{1,0:T(8,128)(2,1)} async-done(((bf16[192,1536]{1,0:T(8,128)(2,1)}), bf16[3072,1536]{1,0:T(8,128)(2,1)}) %all-gather.5.cloned.1.call-update) | async-done | bytes 9437200 | tf_op jit(solution)/shard_map/all_gather | solution.py:966
  145.8 7.2 %shard_map.214 = (f32[1024,768]{1,0:T(8,128)S(1)}, bf16[768,2048]{1,0:T(8,128)(2,1)}) custom-call(bf16[128,2048]{1,0:T(8,128)(2,1)} %upstream.1, bf16[128,2048]{1,0:T(8,128)(2,1)} %copy-done.33, bf16[128,2048]{1,0:T(8,128)(2,1)} %copy-done.34, bf16[128,2048]{1,0:T(8,128)(2,1)} %copy-done.35, bf16[128,2048]{1,0:T(8,128)(2,1)} %copy-done.36, ...), custom_call_target="tpu_custom_call" | custom-call | flops 3221225472 | bytes 10485760 | tf_op jit(solution)/shard_map/pallas_call | solution.py:123
  153.0 5.6 %collective-permute-done.25.refs_1_ = bf16[128,2048]{1,0:T(8,128)(2,1)} collective-permute-done((bf16[128,2048]{1,0:T(8,128)(2,1)S(1)}, bf16[128,2048]{1,0:T(8,128)(2,1)}, u32[]{:S(2)}, u32[]{:S(2)}) %collective-permute-start.25) | collective-permute-done | bytes 524320 | tf_op jit(solution)/shard_map/ppermute | solution.py:771
  163.0 18.5 %shard_map.215 = (bf16[1024,768]{1,0:T(8,128)(2,1)S(1)}, bf16[1024,1536]{1,0:T(8,128)(2,1)S(1)}, bf16[512,2048]{1,0:T(8,128)(2,1)S(1)}, bf16[512,2048]{1,0:T(8,128)(2,1)S(1)}) custom-call(bf16[128,2048]{1,0:T(8,128)(2,1)} %copy-done.31, bf16[128,2048]{1,0:T(8,128)(2,1)} %collective-permute-done.25.refs_1_, ...), custom_call_target="tpu_custom_call" | custom-call | flops 12884901888 | bytes 25165824 | tf_op jit(solution)/shard_map/pallas_call | solution.py:190
  181.8 4.0 %collective-permute-done.36 = bf16[512,2048]{1,0:T(8,128)(2,1)S(1)} collective-permute-done((bf16[512,2048]{1,0:T(8,128)(2,1)S(1)}, bf16[512,2048]{1,0:T(8,128)(2,1)S(1)}, u32[]{:S(2)}, u32[]{:S(2)}) %collective-permute-start.36) | collective-permute-done | bytes 2097184 | tf_op jit(solution)/shard_map/ppermute | solution.py:779
  192.9 16.1 %shard_map.216 = bf16[3072,1536]{1,0:T(8,128)(2,1)} custom-call(bf16[128,2048]{1,0:T(8,128)(2,1)} %copy-done.31, bf16[128,2048]{1,0:T(8,128)(2,1)} %collective-permute-done.25.refs_1_, bf16[128,2048]{1,0:T(8,128)(2,1)} %collective-permute-done.26.refs_2_, bf16[128,2048]{1,0:T(8,128)(2,1)} %collective-permute-done.27.refs_3_, ...), custom_call_target="tpu_custom_call" | custom-call | flops 9663676416 | bytes 23068672 | tf_op jit(solution)/shard_map/pallas_call | solution.py:267
  209.0 7.1 %shard_map.217 = (bf16[512,2048]{1,0:T(8,128)(2,1)}, bf16[512,2048]{1,0:T(8,128)(2,1)}) custom-call(bf16[1024,768]{1,0:T(8,128)(2,1)} %copy-done.13, bf16[768,2048]{1,0:T(8,128)(2,1)} %get-tuple-element.132.down_hbm), custom_call_target="tpu_custom_call" | custom-call | flops 3221225472 | bytes 11534336 | tf_op jit(solution)/shard_map/pallas_call | solution.py:309
  217.7 4.7 %shard_map.218 = (f32[128,2048]{1,0:T(8,128)}, bf16[128,2048]{1,0:T(8,128)(2,1)}) custom-call(f32[128,2048]{1,0:T(8,128)} %get-tuple-element.204.own, bf16[128,2048]{1,0:T(8,128)(2,1)} %copy-done.32, bf16[128,2048]{1,0:T(8,128)(2,1)} %collective-permute-done.38.two, bf16[128,2048]{1,0:T(8,128)(2,1)} %collective-permute-done.39.three, ...), custom_call_target="tpu_custom_call" | custom-call | flops 5242880 | bytes 6291456 | tf_op jit(solution)/shard_map/pallas_call | solution.py:686
  228.4 21.2 %collective-permute-done.44.refs_1_ = bf16[128,2048]{1,0:T(8,128)(2,1)} collective-permute-done((bf16[128,2048]{1,0:T(8,128)(2,1)}, bf16[128,2048]{1,0:T(8,128)(2,1)}, u32[]{:S(2)}, u32[]{:S(2)}) %collective-permute-start.44) | collective-permute-done | bytes 524320 | tf_op jit(solution)/shard_map/ppermute | solution.py:771
  261.2 14.3 %shard_map.220 = (bf16[1024,384]{1,0:T(8,128)(2,1)S(1)}, bf16[512,2048]{1,0:T(8,128)(2,1)}, bf16[512,2048]{1,0:T(8,128)(2,1)S(1)}) custom-call(bf16[128,2048]{1,0:T(8,128)(2,1)} %get-tuple-element.138.refs_0_, bf16[128,2048]{1,0:T(8,128)(2,1)} %collective-permute-done.44.refs_1_, bf16[128,2048]{1,0:T(8,128)(2,1)} %collective-permute-done.45.refs_2_, ...), custom_call_target="tpu_custom_call" | custom-call | flops 5368709120 | bytes 15728640 | tf_op jit(solution)/shard_map/pallas_call | solution.py:578
  282.3 4.4 %collective-permute-done.53 = bf16[64,2048]{1,0:T(8,128)(2,1)S(1)} collective-permute-done((bf16[64,2048]{1,0:T(8,128)(2,1)S(1)}, bf16[64,2048]{1,0:T(8,128)(2,1)S(1)}, u32[]{:S(2)}, u32[]{:S(2)}) %collective-permute-start.53) | collective-permute-done | bytes 262176 | tf_op jit(solution)/shard_map/ppermute | solution.py:842
  291.5 4.9 %shard_map.221 = bf16[2,4,256,384]{3,2,1,0:T(8,128)(2,1)S(1)} custom-call(bf16[144,2048]{1,0:T(8,128)(2,1)} %copy-done.18, bf16[144,2048]{1,0:T(8,128)(2,1)} %copy-done.19, bf16[144,2048]{1,0:T(8,128)(2,1)} %copy-done.20, bf16[144,2048]{1,0:T(8,128)(2,1)} %collective-permute-done.6.refs_3_, bf16[144,2048]{1,0:T(8,128)(2,1)} %copy-done.21, ...), custom_call_target="tpu_custom_call" | custom-call | flops 1610612736 | bytes 6291456 | tf_op jit(solution)/shard_map/pallas_call | solution.py:656
  299.3 4.5 %collective-permute-start.61 = (bf16[128,2048]{1,0:T(8,128)(2,1)}, bf16[128,2048]{1,0:T(8,128)(2,1)}, u32[]{:S(2)}, u32[]{:S(2)}) collective-permute-start(bf16[128,2048]{1,0:T(8,128)(2,1)} %get-tuple-element.197), channel_id=1, source_target_pairs={{0,32},{32,64},{64,96},{96,0},{1,33},{33,65},{65,97},{97,1},{2,34}... | collective-permute-start | bytes 1572872 | tf_op jit(solution)/shard_map/ppermute | solution.py:775
  310.5 9.0 %reduce-scatter.2.cloned.1.call-done = bf16[192,1536]{1,0:T(8,128)(2,1)} async-done(((bf16[3072,1536]{1,0:T(8,128)(2,1)}), bf16[192,1536]{1,0:T(8,128)(2,1)}) %reduce-scatter.2.cloned.1.call-update) | async-done | bytes 589840 | tf_op jit(solution)/shard_map/reduce_scatter | solution.py:987
  322.3 4.6 %collective-permute-start.66 = (bf16[128,2048]{1,0:T(8,128)(2,1)}, bf16[128,2048]{1,0:T(8,128)(2,1)S(1)}, u32[]{:S(2)}, u32[]{:S(2)}) collective-permute-start(bf16[128,2048]{1,0:T(8,128)(2,1)} %get-tuple-element.195), channel_id=1, source_target_pairs={{0,64},{32,96},{64,0},{96,32},{1,65},{33,97},{65,1},{97,33},{2,66}... | collective-permute-start | bytes 1572872 | tf_op jit(solution)/shard_map/ppermute | solution.py:775
  353.8 7.1 %collective-permute-done.74 = bf16[32,3072]{1,0:T(8,128)(2,1)S(1)} collective-permute-done((bf16[32,3072]{1,0:T(8,128)(2,1)S(1)}, bf16[32,3072]{1,0:T(8,128)(2,1)S(1)}, u32[]{:S(2)}, u32[]{:S(2)}) %collective-permute-start.74) | collective-permute-done | bytes 196640 | tf_op jit(solution)/shard_map/ppermute | solution.py:775
  (361 shorter events, 150.4 us)
Async XLA Ops:
  7.2 60.8 %all-gather.3.cloned.1.call-start = ((), (), s32[]{:S(2)}) async-start(), calls=%async_computation.1 | async-start | bytes 1671168 | tf_op jit(solution)/shard_map/all_gather | solution.py:920
  18.2 127.6 %all-gather.5.cloned.1.call-start = ((), (), s32[]{:S(2)}) async-start(), calls=%async_computation.2 | async-start | bytes 10027008 | tf_op jit(solution)/shard_map/all_gather | solution.py:966
  36.7 27.0 %collective-permute-start.4 = (bf16[144,2048]{1,0:T(8,128)(2,1)S(1)}, bf16[144,2048]{1,0:T(8,128)(2,1)S(1)}, u32[]{:S(2)}, u32[]{:S(2)}) collective-permute-start(bf16[144,2048]{1,0:T(8,128)(2,1)S(1)} %fusion.16.refs_0_), channel_id=1, source_target_pairs={{0,96},{32,0},{64,32},{96,64},{1,97},{33,1},{65,33},{97,65},{2,98}... | collective-permute-start | bytes 1769480 | tf_op jit(solution)/shard_map/ppermute | solution.py:771
  37.6 26.1 %collective-permute-start.5 = (bf16[144,2048]{1,0:T(8,128)(2,1)S(1)}, bf16[144,2048]{1,0:T(8,128)(2,1)S(1)}, u32[]{:S(2)}, u32[]{:S(2)}) collective-permute-start(bf16[144,2048]{1,0:T(8,128)(2,1)S(1)} %fusion.16.refs_0_), channel_id=1, source_target_pairs={{0,32},{32,64},{64,96},{96,0},{1,33},{33,65},{65,97},{97,1},{2,34}... | collective-permute-start | bytes 1769480 | tf_op jit(solution)/shard_map/ppermute | solution.py:771
  68.0 251.5 %reduce-scatter.2.cloned.1.call-start = ((), (), s32[]{:S(2)}) async-start(), calls=%async_computation.3 | async-start | bytes 10027008 | tf_op jit(solution)/shard_map/reduce_scatter | solution.py:987
  69.2 26.6 %collective-permute-start.18 = (bf16[128,2048]{1,0:T(8,128)(2,1)}, bf16[128,2048]{1,0:T(8,128)(2,1)S(1)}, u32[]{:S(2)}, u32[]{:S(2)}) collective-permute-start(bf16[128,2048]{1,0:T(8,128)(2,1)} %upstream.1), channel_id=1, source_target_pairs={{0,96},{32,0},{64,32},{96,64},{1,97},{33,1},{65,33},{97,65},{2,98}... | collective-permute-start | bytes 1572872 | tf_op jit(solution)/shard_map/ppermute | solution.py:771
  70.2 25.6 %collective-permute-start.19 = (bf16[128,2048]{1,0:T(8,128)(2,1)}, bf16[128,2048]{1,0:T(8,128)(2,1)S(1)}, u32[]{:S(2)}, u32[]{:S(2)}) collective-permute-start(bf16[128,2048]{1,0:T(8,128)(2,1)} %upstream.1), channel_id=1, source_target_pairs={{0,32},{32,64},{64,96},{96,0},{1,33},{33,65},{65,97},{97,1},{2,34}... | collective-permute-start | bytes 1572872 | tf_op jit(solution)/shard_map/ppermute | solution.py:771
  100.7 25.7 %collective-permute-start.22 = (bf16[128,2048]{1,0:T(8,128)(2,1)S(1)}, bf16[128,2048]{1,0:T(8,128)(2,1)S(1)}, u32[]{:S(2)}, u32[]{:S(2)}) collective-permute-start(bf16[128,2048]{1,0:T(8,128)(2,1)S(1)} %get-tuple-element.207), channel_id=1, source_target_pairs={{0,32},{32,64},{64,96},{96,0},{1,33},{33,65},{65,97},{97,1},{2,34}... | collective-permute-start | bytes 1572872 | tf_op jit(solution)/shard_map/ppermute | solution.py:775
  103.7 26.1 %collective-permute-start.23 = (bf16[128,2048]{1,0:T(8,128)(2,1)S(1)}, bf16[128,2048]{1,0:T(8,128)(2,1)S(1)}, u32[]{:S(2)}, u32[]{:S(2)}) collective-permute-start(bf16[128,2048]{1,0:T(8,128)(2,1)S(1)} %get-tuple-element.206), channel_id=1, source_target_pairs={{0,96},{32,0},{64,32},{96,64},{1,97},{33,1},{65,33},{97,65},{2,98}... | collective-permute-start | bytes 1572872 | tf_op jit(solution)/shard_map/ppermute | solution.py:775
  103.7 26.1 %collective-permute-start.24 = (bf16[128,2048]{1,0:T(8,128)(2,1)S(1)}, bf16[128,2048]{1,0:T(8,128)(2,1)S(1)}, u32[]{:S(2)}, u32[]{:S(2)}) collective-permute-start(bf16[128,2048]{1,0:T(8,128)(2,1)S(1)} %get-tuple-element.205), channel_id=1, source_target_pairs={{0,64},{32,96},{64,0},{96,32},{1,65},{33,97},{65,1},{97,33},{2,66}... | collective-permute-start | bytes 1572872 | tf_op jit(solution)/shard_map/ppermute | solution.py:775
  108.1 27.2 %collective-permute-start.29 = (bf16[128,2048]{1,0:T(8,128)(2,1)S(1)}, bf16[128,2048]{1,0:T(8,128)(2,1)S(1)}, u32[]{:S(2)}, u32[]{:S(2)}) collective-permute-start(bf16[128,2048]{1,0:T(8,128)(2,1)S(1)} %collective-permute-done.18.refs_1_.refs_9_), channel_id=1, source_target_pairs={{0,1},{1,0},{2,3},{3,2},{4,5},{5,4},{6,7},{7,6},{8,9},{9,8},{10,11... | collective-permute-start | bytes 1572872 | tf_op jit(solution)/shard_map/ppermute | solution.py:779
  131.6 27.0 %collective-permute-start.25 = (bf16[128,2048]{1,0:T(8,128)(2,1)S(1)}, bf16[128,2048]{1,0:T(8,128)(2,1)}, u32[]{:S(2)}, u32[]{:S(2)}) collective-permute-start(bf16[128,2048]{1,0:T(8,128)(2,1)S(1)} %multiply_convert_fusion.refs_0_), channel_id=1, source_target_pairs={{0,96},{32,0},{64,32},{96,64},{1,97},{33,1},{65,33},{97,65},{2,98}... | collective-permute-start | bytes 1572872 | tf_op jit(solution)/shard_map/ppermute | solution.py:771
  131.7 26.8 %collective-permute-start.26 = (bf16[128,2048]{1,0:T(8,128)(2,1)S(1)}, bf16[128,2048]{1,0:T(8,128)(2,1)}, u32[]{:S(2)}, u32[]{:S(2)}) collective-permute-start(bf16[128,2048]{1,0:T(8,128)(2,1)S(1)} %multiply_convert_fusion.refs_0_), channel_id=1, source_target_pairs={{0,32},{32,64},{64,96},{96,0},{1,33},{33,65},{65,97},{97,1},{2,34}... | collective-permute-start | bytes 1572872 | tf_op jit(solution)/shard_map/ppermute | solution.py:771
  187.9 28.3 %collective-permute-start.37 = (bf16[128,2048]{1,0:T(8,128)(2,1)}, bf16[128,2048]{1,0:T(8,128)(2,1)S(1)}, u32[]{:S(2)}, u32[]{:S(2)}) collective-permute-start(bf16[128,2048]{1,0:T(8,128)(2,1)} %get-tuple-element.203), channel_id=1, source_target_pairs={{0,32},{32,64},{64,96},{96,0},{1,33},{33,65},{65,97},{97,1},{2,34}... | collective-permute-start | bytes 1572872 | tf_op jit(solution)/shard_map/ppermute | solution.py:775
  191.2 26.4 %collective-permute-start.38 = (bf16[128,2048]{1,0:T(8,128)(2,1)}, bf16[128,2048]{1,0:T(8,128)(2,1)}, u32[]{:S(2)}, u32[]{:S(2)}) collective-permute-start(bf16[128,2048]{1,0:T(8,128)(2,1)} %get-tuple-element.202), channel_id=1, source_target_pairs={{0,96},{32,0},{64,32},{96,64},{1,97},{33,1},{65,33},{97,65},{2,98}... | collective-permute-start | bytes 1572872 | tf_op jit(solution)/shard_map/ppermute | solution.py:775
  191.2 26.4 %collective-permute-start.39 = (bf16[128,2048]{1,0:T(8,128)(2,1)}, bf16[128,2048]{1,0:T(8,128)(2,1)}, u32[]{:S(2)}, u32[]{:S(2)}) collective-permute-start(bf16[128,2048]{1,0:T(8,128)(2,1)} %get-tuple-element.201), channel_id=1, source_target_pairs={{0,64},{32,96},{64,0},{96,32},{1,65},{33,97},{65,1},{97,33},{2,66}... | collective-permute-start | bytes 1572872 | tf_op jit(solution)/shard_map/ppermute | solution.py:775
  222.5 27.1 %collective-permute-start.44 = (bf16[128,2048]{1,0:T(8,128)(2,1)}, bf16[128,2048]{1,0:T(8,128)(2,1)}, u32[]{:S(2)}, u32[]{:S(2)}) collective-permute-start(bf16[128,2048]{1,0:T(8,128)(2,1)} %get-tuple-element.138.refs_0_), channel_id=1, source_target_pairs={{0,96},{32,0},{64,32},{96,64},{1,97},{33,1},{65,33},{97,65},{2,98}... | collective-permute-start | bytes 1572872 | tf_op jit(solution)/shard_map/ppermute | solution.py:771
  226.5 26.6 %collective-permute-start.47 = (bf16[128,2048]{1,0:T(8,128)(2,1)}, bf16[128,2048]{1,0:T(8,128)(2,1)}, u32[]{:S(2)}, u32[]{:S(2)}) collective-permute-start(bf16[128,2048]{1,0:T(8,128)(2,1)} %get-tuple-element.138.refs_0_), channel_id=1, source_target_pairs={{0,1},{1,0},{2,3},{3,2},{4,5},{5,4},{6,7},{7,6},{8,9},{9,8},{10,11... | collective-permute-start | bytes 1572872 | tf_op jit(solution)/shard_map/ppermute | solution.py:779
  250.2 26.3 %collective-permute-start.41 = (bf16[128,2048]{1,0:T(8,128)(2,1)}, bf16[128,2048]{1,0:T(8,128)(2,1)S(1)}, u32[]{:S(2)}, u32[]{:S(2)}) collective-permute-start(bf16[128,2048]{1,0:T(8,128)(2,1)} %get-tuple-element.200), channel_id=1, source_target_pairs={{0,32},{32,64},{64,96},{96,0},{1,33},{33,65},{65,97},{97,1},{2,34}... | collective-permute-start | bytes 1572872 | tf_op jit(solution)/shard_map/ppermute | solution.py:775
  253.1 26.7 %collective-permute-start.42 = (bf16[128,2048]{1,0:T(8,128)(2,1)}, bf16[128,2048]{1,0:T(8,128)(2,1)S(1)}, u32[]{:S(2)}, u32[]{:S(2)}) collective-permute-start(bf16[128,2048]{1,0:T(8,128)(2,1)} %get-tuple-element.199), channel_id=1, source_target_pairs={{0,96},{32,0},{64,32},{96,64},{1,97},{33,1},{65,33},{97,65},{2,98}... | collective-permute-start | bytes 1572872 | tf_op jit(solution)/shard_map/ppermute | solution.py:775
  253.1 26.7 %collective-permute-start.43 = (bf16[128,2048]{1,0:T(8,128)(2,1)S(1)}, bf16[128,2048]{1,0:T(8,128)(2,1)S(1)}, u32[]{:S(2)}, u32[]{:S(2)}) collective-permute-start(bf16[128,2048]{1,0:T(8,128)(2,1)S(1)} %get-tuple-element.198), channel_id=1, source_target_pairs={{0,64},{32,96},{64,0},{96,32},{1,65},{33,97},{65,1},{97,33},{2,66}... | collective-permute-start | bytes 1572872 | tf_op jit(solution)/shard_map/ppermute | solution.py:775
  258.8 27.9 %collective-permute-start.51 = (bf16[64,2048]{1,0:T(8,128)(2,1)S(1)}, bf16[64,2048]{1,0:T(8,128)(2,1)S(1)}, u32[]{:S(2)}, u32[]{:S(2)}) collective-permute-start(bf16[64,2048]{1,0:T(8,128)(2,1)S(1)} %get-tuple-element.221), channel_id=1, source_target_pairs={{0,2},{2,4},{4,6},{6,0},{1,3},{3,5},{5,7},{7,1},{8,10},{10,12},{12... | collective-permute-start | bytes 786440 | tf_op jit(solution)/shard_map/ppermute | solution.py:842
  258.9 27.8 %collective-permute-start.52 = (bf16[64,2048]{1,0:T(8,128)(2,1)S(1)}, bf16[64,2048]{1,0:T(8,128)(2,1)S(1)}, u32[]{:S(2)}, u32[]{:S(2)}) collective-permute-start(bf16[64,2048]{1,0:T(8,128)(2,1)S(1)} %get-tuple-element.220), channel_id=1, source_target_pairs={{0,4},{2,6},{4,0},{6,2},{1,5},{3,7},{5,1},{7,3},{8,12},{10,14},{12... | collective-permute-start | bytes 786440 | tf_op jit(solution)/shard_map/ppermute | solution.py:842
  299.3 27.9 %collective-permute-start.61 = (bf16[128,2048]{1,0:T(8,128)(2,1)}, bf16[128,2048]{1,0:T(8,128)(2,1)}, u32[]{:S(2)}, u32[]{:S(2)}) collective-permute-start(bf16[128,2048]{1,0:T(8,128)(2,1)} %get-tuple-element.197), channel_id=1, source_target_pairs={{0,32},{32,64},{64,96},{96,0},{1,33},{33,65},{65,97},{97,1},{2,34}... | collective-permute-start | bytes 1572872 | tf_op jit(solution)/shard_map/ppermute | solution.py:775
  (104 other events, 1035.3 us)
Sparse Core Ops, SparseCore 0:
  18.3 49.6 all-gather.2
  70.2 75.5 all-gather.4
  217.8 101.6 reduce-scatter.1

commit v8 on v7

--- a/solution.py
+++ b/solution.py
@@ -745,6 +745,57 @@
     )(place, here, *came, gain, *weights, half)
 
 
+def feed_finish_kernel(place, here, one, two, three, shuffle, gain, *refs):
+    weights, grads, gain_grad = refs[:2], refs[2:4], refs[4]
+    stacked = [here[...], one[...], two[:, : 4 * WIDE], three[...]]
+    scale = gain[...]
+
+    def part(chip):
+        which = lax.rem(place[0] - chip + 4, 4)
+        item = stacked[0]
+        for k in range(1, 4):
+            item = jnp.where(which == k, stacked[k], item)
+        return item
+
+    parts = [[part(2 * h + k) for h in range(2)] for k in range(2)]
+    rows = []
+    for item in range(2):
+        for k in range(2):
+            for half in range(2):
+                start = item * WIDE + half * 384
+                pieces = [
+                    parts[k][h][:, 2 * WIDE * e + start : 2 * WIDE * e + start + 384]
+                    for h in range(2)
+                    for e in range(2)
+                ]
+                rows.append(jnp.concatenate(pieces, axis=1))
+    raw = dot_nt(jnp.concatenate(rows, axis=0), shuffle[...])
+    total = jnp.zeros((32, 1), F32)
+    for item in range(2):
+        for k in range(4):
+            side = slice(1408 * k, 1408 * (k + 1))
+            block = raw[32 * (4 * item + k) : 32 * (4 * item + k + 1)]
+            grads[item][:, side] = block * scale
+            total += jnp.sum(block * weights[item][:, side].astype(F32), axis=1, keepdims=True)
+    gain_grad[...] = total
+
+
+def feed_finish(place, here, came, shuffle, gain, gate_weight, up_weight):
+    whole = pl.BlockSpec(memory_space=pltpu.VMEM)
+    return pl.pallas_call(
+        feed_finish_kernel,
+        in_specs=[pl.BlockSpec(memory_space=pltpu.SMEM)] + [whole] * 8,
+        out_specs=[whole] * 3,
+        out_shape=[
+            jax.ShapeDtypeStruct((32, 5632), F32),
+            jax.ShapeDtypeStruct((32, 5632), F32),
+            jax.ShapeDtypeStruct((32, 1), F32),
+        ],
+        compiler_params=pltpu.CompilerParams(vmem_limit_bytes=20 * 1024 * 1024),
+        cost_estimate=pl.CostEstimate(flops=2**30, bytes_accessed=2**23, transcendentals=0),
+    )(place, here, *came, shuffle, gain, gate_weight, up_weight)
+
+
 def times(left, right):
     return jnp.dot(left, right, preferred_element_type=F32)
 
@@ -1035,11 +1086,6 @@
         across = jnp.concatenate([here, more], axis=1)
         return here, (to_ring(there, 1), to_ring(across, 2), to_ring(there, 3))
 
-    def by_chip(here, came):
-        width, spot = here.shape[1], 2 * xh + xl
-        stacked = [here, came[0], came[1][:, :width], came[2]]
-        return [[pick(stacked, (spot - (2 * h + k)) % 4) for h in range(2)] for k in range(2)]
-
     down_wide = jnp.concatenate(
         [down_part[:32], jnp.concatenate([down_part[32:, :1024], down_part[32:, 1024:]], axis=0)],
         axis=1,
@@ -1073,7 +1119,6 @@
 
     inner_one = blocks[0] + sum(item.astype(F32) for item in ring_came + (last_came,))
     tokens_grad = grad_mid + norm_back(rows, first_scale, inner_one)
-    parts = by_chip(feed_here, feed_came)
     down_other = feed_came[1][:, 3072:]
     down_other = jnp.concatenate(
         [
@@ -1089,31 +1134,12 @@
         ],
         axis=0,
     ).astype(F32)
-    rows_of = []
-    for item in range(2):
-        for k in range(2):
-            for half in range(2):
-                start = item * WIDE + half * 384
-                rows_of.append(
-                    jnp.concatenate(
-                        [
-                            parts[k][h][:, e * 2 * WIDE + start : e * 2 * WIDE + start + 384]
-                            for h in range(2)
-                            for e in range(2)
-                        ],
-                        axis=1,
-                    )
-                )
-    unsorted = times_t(jnp.concatenate(rows_of, axis=0), shuffle).reshape(2, 4, 32, 1408)
-    gate_raw = jnp.concatenate([unsorted[0, k] for k in range(4)], axis=1)
-    up_raw = jnp.concatenate([unsorted[1, k] for k in range(4)], axis=1)
-    second_grad = jnp.sum(gate_raw * gate_weight.astype(F32), axis=1) + jnp.sum(
-        up_raw * up_weight.astype(F32), axis=1
-    )
-
     place = jnp.stack([2 * xh + xl, (y // 2 == xh).astype(jnp.int32)]).astype(jnp.int32)
+    gate_grad, up_grad, second_grad = feed_finish(
+        place, feed_here, feed_came, shuffle, second_col, gate_weight, up_weight
+    )
     weights = (query_weight, key_weight, value_weight)
-    came = after(came, gate_raw, up_raw, second_grad, down_grad)
+    came = after(came, gate_grad, up_grad, second_grad, down_grad)
     query_grad, key_grad, value_grad, first_grad, out_grad = finish(
         place, qkv_here, came, first_col, weights, out_half
     )
@@ -1126,9 +1152,9 @@
         key_grad,
         value_grad,
         out_grad,
-        second_grad,
-        gate_raw * second_col,
-        up_raw * second_col,
+        second_grad[:, 0],
+        gate_grad,
+        up_grad,
         down_grad,
     )
 

time: 383 us -> 382 us (level)
  transfers between devices with their start and end apart: 78 -> 78, of which waited for: 31 -> 30; matrix products, arithmetic and copies ran while one was open for 10% -> 9% of each run, Pallas kernels for 21% -> 22%
where the time goes in v8:
time: 382 us; the launch traced here: 375 us
  waiting for transfers between devices  131 us (34%)
  Pallas kernels  103 us (27%)
  starting transfers between devices  81.4 us (21%)
  other arithmetic  31.9 us (8%)
  between operations  15.5 us (4%)
  local copies, waits for them, and re-layouts  10.6 us (3%)
    ppermute x12, waiting for transfers between devices, from_ring(): return lax.ppermute(item, RING, [(i, (i - step) % 4) for i in range(4)])  47 us
    ppermute x18, starting transfers between devices, to_ring(): return lax.ppermute(item, RING, [(i, (i + step) % 4) for i in range(4)])  31.5 us
    ppermute x18, waiting for transfers between devices, to_ring(): return lax.ppermute(item, RING, [(i, (i + step) % 4) for i in range(4)])  29.3 us
    pallas_call x1, Pallas kernels, feed_forward(): pl.pallas_call(feed_kernel, grid=(4,), in_specs=[HBM] * 9 + [pl.BlockSpec...  18.5 us
    ppermute x12, starting transfers between devices, from_ring(): return lax.ppermute(item, RING, [(i, (i - step) % 4) for i in range(4)])  17.1 us
    pallas_call x1, Pallas kernels, feed_grads(): pl.pallas_call(grads_kernel, in_specs=[HBM] * 18, out_specs=HBM, out_shap...  16.1 us
    pallas_call x1, Pallas kernels, attend_back(): pl.pallas_call(attend_back_kernel, grid=(2,), in_specs=[HBM] * 10 + [pl.B...  14.3 us
    pallas_call x1, Pallas kernels, attend(): pl.pallas_call(attend_kernel, grid=(2,), in_specs=[HBM] * 8 + [pl.BlockSp...  14 us
  transfers between devices with their start and end apart: 78, of which 30 were waited for; matrix products, arithmetic and copies ran while one was open for 9% of the time, Pallas kernels for 22%

profile of v8, /device:TPU:30, one launch (start us, length us, event | category | flops | bytes accessed | tf_op | source)
XLA Modules:
  0.0 374.6 jit_solution(10424682249901891272)
XLA Ops:
  22.1 7.8 %collective-permute-done.14 = bf16[64,2048]{1,0:T(8,128)(2,1)S(1)} collective-permute-done((bf16[64,2048]{1,0:T(8,128)(2,1)S(1)}, bf16[64,2048]{1,0:T(8,128)(2,1)S(1)}, u32[]{:S(2)}, u32[]{:S(2)}) %collective-permute-start.14) | collective-permute-done | bytes 262176 | tf_op jit(solution)/shard_map/ppermute | solution.py:1006
  43.2 4.3 %collective-permute-done.16 = bf16[64,2048]{1,0:T(8,128)(2,1)} collective-permute-done((bf16[64,2048]{1,0:T(8,128)(2,1)S(1)}, bf16[64,2048]{1,0:T(8,128)(2,1)}, u32[]{:S(2)}, u32[]{:S(2)}) %collective-permute-start.16) | collective-permute-done | bytes 262176 | tf_op jit(solution)/shard_map/ppermute | solution.py:875
  49.9 13.8 %collective-permute-done.4.refs_1_ = bf16[144,2048]{1,0:T(8,128)(2,1)S(1)} collective-permute-done((bf16[144,2048]{1,0:T(8,128)(2,1)S(1)}, bf16[144,2048]{1,0:T(8,128)(2,1)S(1)}, u32[]{:S(2)}, u32[]{:S(2)}) %collective-permute-start.4) | collective-permute-done | bytes 589856 | tf_op jit(solution)/shard_map/ppermute | solution.py:822
  63.7 4.3 %all-gather.3.cloned.1.call-done = bf16[2,1024,384]{2,1,0:T(8,128)(2,1)} async-done(((bf16[2,64,384]{2,1,0:T(8,128)(2,1)}), bf16[2,1024,384]{2,1,0:T(8,128)(2,1)}) %all-gather.3.cloned.1.call-update) | async-done | bytes 1572880 | tf_op jit(solution)/shard_map/all_gather | solution.py:971
  75.3 14.0 %shard_map.212 = (bf16[1024,256]{1,0:T(8,128)(2,1)S(1)}, bf16[1024,128]{1,0:T(8,128)(2,1)S(1)}, bf16[1024,256]{1,0:T(8,128)(2,1)S(1)}, bf16[512,2048]{1,0:T(8,128)(2,1)S(1)}, bf16[512,2048]{1,0:T(8,128)(2,1)S(1)}) custom-call(bf16[144,2048]{1,0:T(8,128)(2,1)} %copy-done.20, bf16[144,2048]{1,0:T(8,128)(2,1)} %copy-done.21, bf16[144,2048]{1,0:T(8,128)(2,1)} %copy-done.22, ...), custom_call_target="tpu_custom_call" | custom-call | flops 5368709120 | bytes 15728640 | tf_op jit(solution)/shard_map/pallas_call | solution.py:445
  89.3 6.4 %collective-permute-done.18.refs_1_.refs_9_ = bf16[128,2048]{1,0:T(8,128)(2,1)S(1)} collective-permute-done((bf16[128,2048]{1,0:T(8,128)(2,1)}, bf16[128,2048]{1,0:T(8,128)(2,1)S(1)}, u32[]{:S(2)}, u32[]{:S(2)}) %collective-permute-start.18) | collective-permute-done | bytes 524320 | tf_op jit(solution)/shard_map/ppermute | solution.py:822
  108.6 7.5 %shard_map.213 = (f32[4096,128]{1,0:T(8,128)S(1)}, bf16[1024,256]{1,0:T(8,128)(2,1)S(1)}, bf16[1024,256]{1,0:T(8,128)(2,1)S(1)}, bf16[4096,128]{1,0:T(8,128)(2,1)S(1)}, f32[1024,768]{1,0:T(8,128)S(1)}) custom-call(bf16[144,2048]{1,0:T(8,128)(2,1)} %copy-done.20, bf16[144,2048]{1,0:T(8,128)(2,1)} %copy-done.21, bf16[144,2048]{1,0:T(8,128)(2,1)} %copy-done.22, ...), custom_call_target="tpu_custom_call" | custom-call | flops 1073741824 | bytes 9437184 | tf_op jit(solution)/shard_map/pallas_call | solution.py:506
  117.5 8.9 %collective-permute-done.22 = bf16[128,2048]{1,0:T(8,128)(2,1)S(1)} collective-permute-done((bf16[128,2048]{1,0:T(8,128)(2,1)S(1)}, bf16[128,2048]{1,0:T(8,128)(2,1)S(1)}, u32[]{:S(2)}, u32[]{:S(2)}) %collective-permute-start.22) | collective-permute-done | bytes 524320 | tf_op jit(solution)/shard_map/ppermute | solution.py:826
  136.3 9.5 %all-gather.5.cloned.1.call-done.refs_8_ = bf16[3072,1536]{1,0:T(8,128)(2,1)} async-done(((bf16[192,1536]{1,0:T(8,128)(2,1)}), bf16[3072,1536]{1,0:T(8,128)(2,1)}) %all-gather.5.cloned.1.call-update) | async-done | bytes 9437200 | tf_op jit(solution)/shard_map/all_gather | solution.py:1017
  145.8 7.2 %shard_map.214 = (f32[1024,768]{1,0:T(8,128)S(1)}, bf16[768,2048]{1,0:T(8,128)(2,1)}) custom-call(bf16[128,2048]{1,0:T(8,128)(2,1)} %upstream.1, bf16[128,2048]{1,0:T(8,128)(2,1)} %copy-done.33, bf16[128,2048]{1,0:T(8,128)(2,1)} %copy-done.34, bf16[128,2048]{1,0:T(8,128)(2,1)} %copy-done.35, bf16[128,2048]{1,0:T(8,128)(2,1)} %copy-done.36, ...), custom_call_target="tpu_custom_call" | custom-call | flops 3221225472 | bytes 10485760 | tf_op jit(solution)/shard_map/pallas_call | solution.py:123
  153.0 5.6 %collective-permute-done.25.refs_1_ = bf16[128,2048]{1,0:T(8,128)(2,1)} collective-permute-done((bf16[128,2048]{1,0:T(8,128)(2,1)S(1)}, bf16[128,2048]{1,0:T(8,128)(2,1)}, u32[]{:S(2)}, u32[]{:S(2)}) %collective-permute-start.25) | collective-permute-done | bytes 524320 | tf_op jit(solution)/shard_map/ppermute | solution.py:822
  163.0 18.5 %shard_map.215 = (bf16[1024,768]{1,0:T(8,128)(2,1)S(1)}, bf16[1024,1536]{1,0:T(8,128)(2,1)S(1)}, bf16[512,2048]{1,0:T(8,128)(2,1)S(1)}, bf16[512,2048]{1,0:T(8,128)(2,1)S(1)}) custom-call(bf16[128,2048]{1,0:T(8,128)(2,1)} %copy-done.31, bf16[128,2048]{1,0:T(8,128)(2,1)} %collective-permute-done.25.refs_1_, ...), custom_call_target="tpu_custom_call" | custom-call | flops 12884901888 | bytes 25165824 | tf_op jit(solution)/shard_map/pallas_call | solution.py:190
  181.8 4.0 %collective-permute-done.36 = bf16[512,2048]{1,0:T(8,128)(2,1)S(1)} collective-permute-done((bf16[512,2048]{1,0:T(8,128)(2,1)S(1)}, bf16[512,2048]{1,0:T(8,128)(2,1)S(1)}, u32[]{:S(2)}, u32[]{:S(2)}) %collective-permute-start.36) | collective-permute-done | bytes 2097184 | tf_op jit(solution)/shard_map/ppermute | solution.py:830
  192.9 16.1 %shard_map.216 = bf16[3072,1536]{1,0:T(8,128)(2,1)} custom-call(bf16[128,2048]{1,0:T(8,128)(2,1)} %copy-done.31, bf16[128,2048]{1,0:T(8,128)(2,1)} %collective-permute-done.25.refs_1_, bf16[128,2048]{1,0:T(8,128)(2,1)} %collective-permute-done.26.refs_2_, bf16[128,2048]{1,0:T(8,128)(2,1)} %collective-permute-done.27.refs_3_, ...), custom_call_target="tpu_custom_call" | custom-call | flops 9663676416 | bytes 23068672 | tf_op jit(solution)/shard_map/pallas_call | solution.py:267
  209.0 7.1 %shard_map.217 = (bf16[512,2048]{1,0:T(8,128)(2,1)}, bf16[512,2048]{1,0:T(8,128)(2,1)}) custom-call(bf16[1024,768]{1,0:T(8,128)(2,1)} %copy-done.15, bf16[768,2048]{1,0:T(8,128)(2,1)} %get-tuple-element.135.down_hbm), custom_call_target="tpu_custom_call" | custom-call | flops 3221225472 | bytes 11534336 | tf_op jit(solution)/shard_map/pallas_call | solution.py:309
  217.7 4.7 %shard_map.218 = (f32[128,2048]{1,0:T(8,128)}, bf16[128,2048]{1,0:T(8,128)(2,1)}) custom-call(f32[128,2048]{1,0:T(8,128)} %get-tuple-element.210.own, bf16[128,2048]{1,0:T(8,128)(2,1)} %copy-done.32, bf16[128,2048]{1,0:T(8,128)(2,1)} %collective-permute-done.38.two, bf16[128,2048]{1,0:T(8,128)(2,1)} %collective-permute-done.39.three, ...), custom_call_target="tpu_custom_call" | custom-call | flops 5242880 | bytes 6291456 | tf_op jit(solution)/shard_map/pallas_call | solution.py:686
  228.4 21.2 %collective-permute-done.44.refs_1_ = bf16[128,2048]{1,0:T(8,128)(2,1)} collective-permute-done((bf16[128,2048]{1,0:T(8,128)(2,1)}, bf16[128,2048]{1,0:T(8,128)(2,1)}, u32[]{:S(2)}, u32[]{:S(2)}) %collective-permute-start.44) | collective-permute-done | bytes 524320 | tf_op jit(solution)/shard_map/ppermute | solution.py:822
  261.3 14.3 %shard_map.220 = (bf16[1024,384]{1,0:T(8,128)(2,1)S(1)}, bf16[512,2048]{1,0:T(8,128)(2,1)}, bf16[512,2048]{1,0:T(8,128)(2,1)S(1)}) custom-call(bf16[128,2048]{1,0:T(8,128)(2,1)} %get-tuple-element.141.refs_0_, bf16[128,2048]{1,0:T(8,128)(2,1)} %collective-permute-done.44.refs_1_, bf16[128,2048]{1,0:T(8,128)(2,1)} %collective-permute-done.45.refs_2_, ...), custom_call_target="tpu_custom_call" | custom-call | flops 5368709120 | bytes 15728640 | tf_op jit(solution)/shard_map/pallas_call | solution.py:578
  282.3 4.4 %collective-permute-done.53 = bf16[64,2048]{1,0:T(8,128)(2,1)S(1)} collective-permute-done((bf16[64,2048]{1,0:T(8,128)(2,1)S(1)}, bf16[64,2048]{1,0:T(8,128)(2,1)S(1)}, u32[]{:S(2)}, u32[]{:S(2)}) %collective-permute-start.53) | collective-permute-done | bytes 262176 | tf_op jit(solution)/shard_map/ppermute | solution.py:893
  291.5 4.9 %shard_map.221 = bf16[2,4,256,384]{3,2,1,0:T(8,128)(2,1)S(1)} custom-call(bf16[144,2048]{1,0:T(8,128)(2,1)} %copy-done.20, bf16[144,2048]{1,0:T(8,128)(2,1)} %copy-done.21, bf16[144,2048]{1,0:T(8,128)(2,1)} %copy-done.22, bf16[144,2048]{1,0:T(8,128)(2,1)} %collective-permute-done.6.refs_3_, bf16[144,2048]{1,0:T(8,128)(2,1)} %copy-done.23, ...), custom_call_target="tpu_custom_call" | custom-call | flops 1610612736 | bytes 6291456 | tf_op jit(solution)/shard_map/pallas_call | solution.py:656
  299.3 4.5 %collective-permute-start.61 = (bf16[128,2048]{1,0:T(8,128)(2,1)}, bf16[128,2048]{1,0:T(8,128)(2,1)}, u32[]{:S(2)}, u32[]{:S(2)}) collective-permute-start(bf16[128,2048]{1,0:T(8,128)(2,1)} %get-tuple-element.203), channel_id=1, source_target_pairs={{0,32},{32,64},{64,96},{96,0},{1,33},{33,65},{65,97},{97,1},{2,34}... | collective-permute-start | bytes 1572872 | tf_op jit(solution)/shard_map/ppermute | solution.py:826
  310.5 9.0 %reduce-scatter.2.cloned.1.call-done = bf16[192,1536]{1,0:T(8,128)(2,1)} async-done(((bf16[3072,1536]{1,0:T(8,128)(2,1)}), bf16[192,1536]{1,0:T(8,128)(2,1)}) %reduce-scatter.2.cloned.1.call-update) | async-done | bytes 589840 | tf_op jit(solution)/shard_map/reduce_scatter | solution.py:1038
  322.3 4.8 %collective-permute-start.66 = (bf16[128,2048]{1,0:T(8,128)(2,1)}, bf16[128,2048]{1,0:T(8,128)(2,1)S(1)}, u32[]{:S(2)}, u32[]{:S(2)}) collective-permute-start(bf16[128,2048]{1,0:T(8,128)(2,1)} %get-tuple-element.201), channel_id=1, source_target_pairs={{0,64},{32,96},{64,0},{96,32},{1,65},{33,97},{65,1},{97,33},{2,66}... | collective-permute-start | bytes 1572872 | tf_op jit(solution)/shard_map/ppermute | solution.py:826
  353.7 7.1 %collective-permute-done.74.three = bf16[32,3072]{1,0:T(8,128)(2,1)S(1)} collective-permute-done((bf16[32,3072]{1,0:T(8,128)(2,1)S(1)}, bf16[32,3072]{1,0:T(8,128)(2,1)S(1)}, u32[]{:S(2)}, u32[]{:S(2)}) %collective-permute-start.74) | collective-permute-done | bytes 196640 | tf_op jit(solution)/shard_map/ppermute | solution.py:826
  (347 shorter events, 149.3 us)
Async XLA Ops:
  7.2 60.8 %all-gather.3.cloned.1.call-start = ((), (), s32[]{:S(2)}) async-start(), calls=%async_computation.1 | async-start | bytes 1671168 | tf_op jit(solution)/shard_map/all_gather | solution.py:971
  18.2 127.6 %all-gather.5.cloned.1.call-start = ((), (), s32[]{:S(2)}) async-start(), calls=%async_computation.2 | async-start | bytes 10027008 | tf_op jit(solution)/shard_map/all_gather | solution.py:1017
  36.7 27.0 %collective-permute-start.4 = (bf16[144,2048]{1,0:T(8,128)(2,1)S(1)}, bf16[144,2048]{1,0:T(8,128)(2,1)S(1)}, u32[]{:S(2)}, u32[]{:S(2)}) collective-permute-start(bf16[144,2048]{1,0:T(8,128)(2,1)S(1)} %fusion.12.refs_0_), channel_id=1, source_target_pairs={{0,96},{32,0},{64,32},{96,64},{1,97},{33,1},{65,33},{97,65},{2,98}... | collective-permute-start | bytes 1769480 | tf_op jit(solution)/shard_map/ppermute | solution.py:822
  37.6 26.1 %collective-permute-start.5 = (bf16[144,2048]{1,0:T(8,128)(2,1)S(1)}, bf16[144,2048]{1,0:T(8,128)(2,1)S(1)}, u32[]{:S(2)}, u32[]{:S(2)}) collective-permute-start(bf16[144,2048]{1,0:T(8,128)(2,1)S(1)} %fusion.12.refs_0_), channel_id=1, source_target_pairs={{0,32},{32,64},{64,96},{96,0},{1,33},{33,65},{65,97},{97,1},{2,34}... | collective-permute-start | bytes 1769480 | tf_op jit(solution)/shard_map/ppermute | solution.py:822
  68.0 251.5 %reduce-scatter.2.cloned.1.call-start = ((), (), s32[]{:S(2)}) async-start(), calls=%async_computation.3 | async-start | bytes 10027008 | tf_op jit(solution)/shard_map/reduce_scatter | solution.py:1038
  69.2 26.6 %collective-permute-start.18 = (bf16[128,2048]{1,0:T(8,128)(2,1)}, bf16[128,2048]{1,0:T(8,128)(2,1)S(1)}, u32[]{:S(2)}, u32[]{:S(2)}) collective-permute-start(bf16[128,2048]{1,0:T(8,128)(2,1)} %upstream.1), channel_id=1, source_target_pairs={{0,96},{32,0},{64,32},{96,64},{1,97},{33,1},{65,33},{97,65},{2,98}... | collective-permute-start | bytes 1572872 | tf_op jit(solution)/shard_map/ppermute | solution.py:822
  70.2 25.6 %collective-permute-start.19 = (bf16[128,2048]{1,0:T(8,128)(2,1)}, bf16[128,2048]{1,0:T(8,128)(2,1)S(1)}, u32[]{:S(2)}, u32[]{:S(2)}) collective-permute-start(bf16[128,2048]{1,0:T(8,128)(2,1)} %upstream.1), channel_id=1, source_target_pairs={{0,32},{32,64},{64,96},{96,0},{1,33},{33,65},{65,97},{97,1},{2,34}... | collective-permute-start | bytes 1572872 | tf_op jit(solution)/shard_map/ppermute | solution.py:822
  100.7 25.7 %collective-permute-start.22 = (bf16[128,2048]{1,0:T(8,128)(2,1)S(1)}, bf16[128,2048]{1,0:T(8,128)(2,1)S(1)}, u32[]{:S(2)}, u32[]{:S(2)}) collective-permute-start(bf16[128,2048]{1,0:T(8,128)(2,1)S(1)} %get-tuple-element.213), channel_id=1, source_target_pairs={{0,32},{32,64},{64,96},{96,0},{1,33},{33,65},{65,97},{97,1},{2,34}... | collective-permute-start | bytes 1572872 | tf_op jit(solution)/shard_map/ppermute | solution.py:826
  103.7 26.1 %collective-permute-start.23 = (bf16[128,2048]{1,0:T(8,128)(2,1)S(1)}, bf16[128,2048]{1,0:T(8,128)(2,1)S(1)}, u32[]{:S(2)}, u32[]{:S(2)}) collective-permute-start(bf16[128,2048]{1,0:T(8,128)(2,1)S(1)} %get-tuple-element.212), channel_id=1, source_target_pairs={{0,96},{32,0},{64,32},{96,64},{1,97},{33,1},{65,33},{97,65},{2,98}... | collective-permute-start | bytes 1572872 | tf_op jit(solution)/shard_map/ppermute | solution.py:826
  103.7 26.1 %collective-permute-start.24 = (bf16[128,2048]{1,0:T(8,128)(2,1)S(1)}, bf16[128,2048]{1,0:T(8,128)(2,1)S(1)}, u32[]{:S(2)}, u32[]{:S(2)}) collective-permute-start(bf16[128,2048]{1,0:T(8,128)(2,1)S(1)} %get-tuple-element.211), channel_id=1, source_target_pairs={{0,64},{32,96},{64,0},{96,32},{1,65},{33,97},{65,1},{97,33},{2,66}... | collective-permute-start | bytes 1572872 | tf_op jit(solution)/shard_map/ppermute | solution.py:826
  108.1 27.2 %collective-permute-start.29 = (bf16[128,2048]{1,0:T(8,128)(2,1)S(1)}, bf16[128,2048]{1,0:T(8,128)(2,1)S(1)}, u32[]{:S(2)}, u32[]{:S(2)}) collective-permute-start(bf16[128,2048]{1,0:T(8,128)(2,1)S(1)} %collective-permute-done.18.refs_1_.refs_9_), channel_id=1, source_target_pairs={{0,1},{1,0},{2,3},{3,2},{4,5},{5,4},{6,7},{7,6},{8,9},{9,8},{10,11... | collective-permute-start | bytes 1572872 | tf_op jit(solution)/shard_map/ppermute | solution.py:830
  131.6 27.0 %collective-permute-start.25 = (bf16[128,2048]{1,0:T(8,128)(2,1)S(1)}, bf16[128,2048]{1,0:T(8,128)(2,1)}, u32[]{:S(2)}, u32[]{:S(2)}) collective-permute-start(bf16[128,2048]{1,0:T(8,128)(2,1)S(1)} %multiply_convert_fusion.refs_0_), channel_id=1, source_target_pairs={{0,96},{32,0},{64,32},{96,64},{1,97},{33,1},{65,33},{97,65},{2,98}... | collective-permute-start | bytes 1572872 | tf_op jit(solution)/shard_map/ppermute | solution.py:822
  131.7 26.8 %collective-permute-start.26 = (bf16[128,2048]{1,0:T(8,128)(2,1)S(1)}, bf16[128,2048]{1,0:T(8,128)(2,1)}, u32[]{:S(2)}, u32[]{:S(2)}) collective-permute-start(bf16[128,2048]{1,0:T(8,128)(2,1)S(1)} %multiply_convert_fusion.refs_0_), channel_id=1, source_target_pairs={{0,32},{32,64},{64,96},{96,0},{1,33},{33,65},{65,97},{97,1},{2,34}... | collective-permute-start | bytes 1572872 | tf_op jit(solution)/shard_map/ppermute | solution.py:822
  187.9 28.3 %collective-permute-start.37 = (bf16[128,2048]{1,0:T(8,128)(2,1)}, bf16[128,2048]{1,0:T(8,128)(2,1)S(1)}, u32[]{:S(2)}, u32[]{:S(2)}) collective-permute-start(bf16[128,2048]{1,0:T(8,128)(2,1)} %get-tuple-element.209), channel_id=1, source_target_pairs={{0,32},{32,64},{64,96},{96,0},{1,33},{33,65},{65,97},{97,1},{2,34}... | collective-permute-start | bytes 1572872 | tf_op jit(solution)/shard_map/ppermute | solution.py:826
  191.2 26.4 %collective-permute-start.38 = (bf16[128,2048]{1,0:T(8,128)(2,1)}, bf16[128,2048]{1,0:T(8,128)(2,1)}, u32[]{:S(2)}, u32[]{:S(2)}) collective-permute-start(bf16[128,2048]{1,0:T(8,128)(2,1)} %get-tuple-element.208), channel_id=1, source_target_pairs={{0,96},{32,0},{64,32},{96,64},{1,97},{33,1},{65,33},{97,65},{2,98}... | collective-permute-start | bytes 1572872 | tf_op jit(solution)/shard_map/ppermute | solution.py:826
  191.2 26.4 %collective-permute-start.39 = (bf16[128,2048]{1,0:T(8,128)(2,1)}, bf16[128,2048]{1,0:T(8,128)(2,1)}, u32[]{:S(2)}, u32[]{:S(2)}) collective-permute-start(bf16[128,2048]{1,0:T(8,128)(2,1)} %get-tuple-element.207), channel_id=1, source_target_pairs={{0,64},{32,96},{64,0},{96,32},{1,65},{33,97},{65,1},{97,33},{2,66}... | collective-permute-start | bytes 1572872 | tf_op jit(solution)/shard_map/ppermute | solution.py:826
  222.5 27.1 %collective-permute-start.44 = (bf16[128,2048]{1,0:T(8,128)(2,1)}, bf16[128,2048]{1,0:T(8,128)(2,1)}, u32[]{:S(2)}, u32[]{:S(2)}) collective-permute-start(bf16[128,2048]{1,0:T(8,128)(2,1)} %get-tuple-element.141.refs_0_), channel_id=1, source_target_pairs={{0,96},{32,0},{64,32},{96,64},{1,97},{33,1},{65,33},{97,65},{2,98}... | collective-permute-start | bytes 1572872 | tf_op jit(solution)/shard_map/ppermute | solution.py:822
  226.5 26.6 %collective-permute-start.47 = (bf16[128,2048]{1,0:T(8,128)(2,1)}, bf16[128,2048]{1,0:T(8,128)(2,1)}, u32[]{:S(2)}, u32[]{:S(2)}) collective-permute-start(bf16[128,2048]{1,0:T(8,128)(2,1)} %get-tuple-element.141.refs_0_), channel_id=1, source_target_pairs={{0,1},{1,0},{2,3},{3,2},{4,5},{5,4},{6,7},{7,6},{8,9},{9,8},{10,11... | collective-permute-start | bytes 1572872 | tf_op jit(solution)/shard_map/ppermute | solution.py:830
  250.2 26.3 %collective-permute-start.41 = (bf16[128,2048]{1,0:T(8,128)(2,1)}, bf16[128,2048]{1,0:T(8,128)(2,1)S(1)}, u32[]{:S(2)}, u32[]{:S(2)}) collective-permute-start(bf16[128,2048]{1,0:T(8,128)(2,1)} %get-tuple-element.206), channel_id=1, source_target_pairs={{0,32},{32,64},{64,96},{96,0},{1,33},{33,65},{65,97},{97,1},{2,34}... | collective-permute-start | bytes 1572872 | tf_op jit(solution)/shard_map/ppermute | solution.py:826
  253.1 26.7 %collective-permute-start.42 = (bf16[128,2048]{1,0:T(8,128)(2,1)}, bf16[128,2048]{1,0:T(8,128)(2,1)S(1)}, u32[]{:S(2)}, u32[]{:S(2)}) collective-permute-start(bf16[128,2048]{1,0:T(8,128)(2,1)} %get-tuple-element.205), channel_id=1, source_target_pairs={{0,96},{32,0},{64,32},{96,64},{1,97},{33,1},{65,33},{97,65},{2,98}... | collective-permute-start | bytes 1572872 | tf_op jit(solution)/shard_map/ppermute | solution.py:826
  253.1 26.7 %collective-permute-start.43 = (bf16[128,2048]{1,0:T(8,128)(2,1)S(1)}, bf16[128,2048]{1,0:T(8,128)(2,1)S(1)}, u32[]{:S(2)}, u32[]{:S(2)}) collective-permute-start(bf16[128,2048]{1,0:T(8,128)(2,1)S(1)} %get-tuple-element.204), channel_id=1, source_target_pairs={{0,64},{32,96},{64,0},{96,32},{1,65},{33,97},{65,1},{97,33},{2,66}... | collective-permute-start | bytes 1572872 | tf_op jit(solution)/shard_map/ppermute | solution.py:826
  258.8 27.9 %collective-permute-start.51 = (bf16[64,2048]{1,0:T(8,128)(2,1)S(1)}, bf16[64,2048]{1,0:T(8,128)(2,1)S(1)}, u32[]{:S(2)}, u32[]{:S(2)}) collective-permute-start(bf16[64,2048]{1,0:T(8,128)(2,1)S(1)} %get-tuple-element.219), channel_id=1, source_target_pairs={{0,2},{2,4},{4,6},{6,0},{1,3},{3,5},{5,7},{7,1},{8,10},{10,12},{12... | collective-permute-start | bytes 786440 | tf_op jit(solution)/shard_map/ppermute | solution.py:893
  258.9 27.8 %collective-permute-start.52 = (bf16[64,2048]{1,0:T(8,128)(2,1)S(1)}, bf16[64,2048]{1,0:T(8,128)(2,1)S(1)}, u32[]{:S(2)}, u32[]{:S(2)}) collective-permute-start(bf16[64,2048]{1,0:T(8,128)(2,1)S(1)} %get-tuple-element.218), channel_id=1, source_target_pairs={{0,4},{2,6},{4,0},{6,2},{1,5},{3,7},{5,1},{7,3},{8,12},{10,14},{12... | collective-permute-start | bytes 786440 | tf_op jit(solution)/shard_map/ppermute | solution.py:893
  299.3 27.9 %collective-permute-start.61 = (bf16[128,2048]{1,0:T(8,128)(2,1)}, bf16[128,2048]{1,0:T(8,128)(2,1)}, u32[]{:S(2)}, u32[]{:S(2)}) collective-permute-start(bf16[128,2048]{1,0:T(8,128)(2,1)} %get-tuple-element.203), channel_id=1, source_target_pairs={{0,32},{32,64},{64,96},{96,0},{1,33},{33,65},{65,97},{97,1},{2,34}... | collective-permute-start | bytes 1572872 | tf_op jit(solution)/shard_map/ppermute | solution.py:826
  (104 other events, 1055.9 us)
Sparse Core Ops, SparseCore 0:
  18.3 49.6 all-gather.2
  70.2 75.5 all-gather.4
  217.8 101.6 reduce-scatter.1

commit v9 on v8

--- a/solution.py
+++ b/solution.py
@@ -693,7 +693,7 @@
         cost_estimate=pl.CostEstimate(
             flops=20 * CAP * D, bytes_accessed=6 * 2**20, transcendentals=CAP
         ),
-    )(*in_hbm(own, *came, rows, upstream))
+    )(*in_hbm(own, *came), rows, upstream)
 
 
 def finish_kernel(place, here, one, two, three, gain, *refs):

time: 382 us -> 384 us (level)
  transfers between devices with their start and end apart: 78 -> 78, of which waited for: 30 -> 31; matrix products, arithmetic and copies ran while one was open for 9% -> 10% of each run, Pallas kernels for 22% -> 22%
where the time goes in v9:
time: 384 us; the launch traced here: 377 us
  waiting for transfers between devices  133 us (35%)
  Pallas kernels  103 us (27%)
  starting transfers between devices  79.2 us (21%)
  other arithmetic  33.6 us (9%)
  between operations  15.5 us (4%)
  local copies, waits for them, and re-layouts  11.4 us (3%)
    ppermute x12, waiting for transfers between devices, from_ring(): return lax.ppermute(item, RING, [(i, (i - step) % 4) for i in range(4)])  46.5 us
    ppermute x18, starting transfers between devices, to_ring(): return lax.ppermute(item, RING, [(i, (i + step) % 4) for i in range(4)])  30.4 us
    ppermute x18, waiting for transfers between devices, to_ring(): return lax.ppermute(item, RING, [(i, (i + step) % 4) for i in range(4)])  28.3 us
    pallas_call x1, Pallas kernels, feed_forward(): pl.pallas_call(feed_kernel, grid=(4,), in_specs=[HBM] * 9 + [pl.BlockSpec...  18.6 us
    pallas_call x1, Pallas kernels, feed_grads(): pl.pallas_call(grads_kernel, in_specs=[HBM] * 18, out_specs=HBM, out_shap...  16.2 us
    ppermute x12, starting transfers between devices, from_ring(): return lax.ppermute(item, RING, [(i, (i - step) % 4) for i in range(4)])  16.1 us
    pallas_call x1, Pallas kernels, attend_back(): pl.pallas_call(attend_back_kernel, grid=(2,), in_specs=[HBM] * 10 + [pl.B...  14.2 us
    pallas_call x1, Pallas kernels, attend(): pl.pallas_call(attend_kernel, grid=(2,), in_specs=[HBM] * 8 + [pl.BlockSp...  14 us
  transfers between devices with their start and end apart: 78, of which 31 were waited for; matrix products, arithmetic and copies ran while one was open for 10% of the time, Pallas kernels for 22%

profile of v9, /device:TPU:30, one launch (start us, length us, event | category | flops | bytes accessed | tf_op | source)
XLA Modules:
  0.0 376.6 jit_solution(116749252791190034)
XLA Ops:
  22.1 7.8 %collective-permute-done.14 = bf16[64,2048]{1,0:T(8,128)(2,1)S(1)} collective-permute-done((bf16[64,2048]{1,0:T(8,128)(2,1)S(1)}, bf16[64,2048]{1,0:T(8,128)(2,1)S(1)}, u32[]{:S(2)}, u32[]{:S(2)}) %collective-permute-start.14) | collective-permute-done | bytes 262176 | tf_op jit(solution)/shard_map/ppermute | solution.py:1006
  43.8 4.3 %collective-permute-done.16 = bf16[64,2048]{1,0:T(8,128)(2,1)} collective-permute-done((bf16[64,2048]{1,0:T(8,128)(2,1)}, bf16[64,2048]{1,0:T(8,128)(2,1)}, u32[]{:S(2)}, u32[]{:S(2)}) %collective-permute-start.16) | collective-permute-done | bytes 262176 | tf_op jit(solution)/shard_map/ppermute | solution.py:875
  50.6 13.8 %collective-permute-done.4.refs_1_ = bf16[144,2048]{1,0:T(8,128)(2,1)S(1)} collective-permute-done((bf16[144,2048]{1,0:T(8,128)(2,1)S(1)}, bf16[144,2048]{1,0:T(8,128)(2,1)S(1)}, u32[]{:S(2)}, u32[]{:S(2)}) %collective-permute-start.4) | collective-permute-done | bytes 589856 | tf_op jit(solution)/shard_map/ppermute | solution.py:822
  64.4 4.3 %all-gather.3.cloned.1.call-done = bf16[2,1024,384]{2,1,0:T(8,128)(2,1)} async-done(((bf16[2,64,384]{2,1,0:T(8,128)(2,1)}), bf16[2,1024,384]{2,1,0:T(8,128)(2,1)}) %all-gather.3.cloned.1.call-update) | async-done | bytes 1572880 | tf_op jit(solution)/shard_map/all_gather | solution.py:971
  75.7 14.0 %shard_map.212 = (bf16[1024,256]{1,0:T(8,128)(2,1)S(1)}, bf16[1024,128]{1,0:T(8,128)(2,1)S(1)}, bf16[1024,256]{1,0:T(8,128)(2,1)S(1)}, bf16[512,2048]{1,0:T(8,128)(2,1)S(1)}, bf16[512,2048]{1,0:T(8,128)(2,1)S(1)}) custom-call(bf16[144,2048]{1,0:T(8,128)(2,1)} %copy-done.24, bf16[144,2048]{1,0:T(8,128)(2,1)} %copy-done.25, bf16[144,2048]{1,0:T(8,128)(2,1)} %copy-done.26, ...), custom_call_target="tpu_custom_call" | custom-call | flops 5368709120 | bytes 15728640 | tf_op jit(solution)/shard_map/pallas_call | solution.py:445
  89.7 6.5 %collective-permute-done.18.refs_1_.refs_9_ = bf16[128,2048]{1,0:T(8,128)(2,1)S(1)} collective-permute-done((bf16[128,2048]{1,0:T(8,128)(2,1)S(1)}, bf16[128,2048]{1,0:T(8,128)(2,1)S(1)}, u32[]{:S(2)}, u32[]{:S(2)}) %collective-permute-start.18) | collective-permute-done | bytes 524320 | tf_op jit(solution)/shard_map/ppermute | solution.py:822
  109.1 7.6 %shard_map.213 = (f32[4096,128]{1,0:T(8,128)S(1)}, bf16[1024,256]{1,0:T(8,128)(2,1)S(1)}, bf16[1024,256]{1,0:T(8,128)(2,1)S(1)}, bf16[4096,128]{1,0:T(8,128)(2,1)S(1)}, f32[1024,768]{1,0:T(8,128)S(1)}) custom-call(bf16[144,2048]{1,0:T(8,128)(2,1)} %copy-done.24, bf16[144,2048]{1,0:T(8,128)(2,1)} %copy-done.25, bf16[144,2048]{1,0:T(8,128)(2,1)} %copy-done.26, ...), custom_call_target="tpu_custom_call" | custom-call | flops 1073741824 | bytes 9437184 | tf_op jit(solution)/shard_map/pallas_call | solution.py:506
  118.1 8.7 %collective-permute-done.22 = bf16[128,2048]{1,0:T(8,128)(2,1)S(1)} collective-permute-done((bf16[128,2048]{1,0:T(8,128)(2,1)S(1)}, bf16[128,2048]{1,0:T(8,128)(2,1)S(1)}, u32[]{:S(2)}, u32[]{:S(2)}) %collective-permute-start.22) | collective-permute-done | bytes 524320 | tf_op jit(solution)/shard_map/ppermute | solution.py:826
  136.4 9.8 %all-gather.5.cloned.1.call-done.refs_8_ = bf16[3072,1536]{1,0:T(8,128)(2,1)} async-done(((bf16[192,1536]{1,0:T(8,128)(2,1)}), bf16[3072,1536]{1,0:T(8,128)(2,1)}) %all-gather.5.cloned.1.call-update) | async-done | bytes 9437200 | tf_op jit(solution)/shard_map/all_gather | solution.py:1017
  146.2 7.2 %shard_map.214 = (f32[1024,768]{1,0:T(8,128)S(1)}, bf16[768,2048]{1,0:T(8,128)(2,1)}) custom-call(bf16[128,2048]{1,0:T(8,128)(2,1)} %upstream.1, bf16[128,2048]{1,0:T(8,128)(2,1)} %copy-done.37, bf16[128,2048]{1,0:T(8,128)(2,1)} %copy-done.38, bf16[128,2048]{1,0:T(8,128)(2,1)} %copy-done.39, bf16[128,2048]{1,0:T(8,128)(2,1)} %copy-done.40, ...), custom_call_target="tpu_custom_call" | custom-call | flops 3221225472 | bytes 10485760 | tf_op jit(solution)/shard_map/pallas_call | solution.py:123
  153.4 5.4 %collective-permute-done.25.refs_1_ = bf16[128,2048]{1,0:T(8,128)(2,1)} collective-permute-done((bf16[128,2048]{1,0:T(8,128)(2,1)}, bf16[128,2048]{1,0:T(8,128)(2,1)}, u32[]{:S(2)}, u32[]{:S(2)}) %collective-permute-start.25) | collective-permute-done | bytes 524320 | tf_op jit(solution)/shard_map/ppermute | solution.py:822
  164.0 18.6 %shard_map.215 = (bf16[1024,768]{1,0:T(8,128)(2,1)S(1)}, bf16[1024,1536]{1,0:T(8,128)(2,1)S(1)}, bf16[512,2048]{1,0:T(8,128)(2,1)S(1)}, bf16[512,2048]{1,0:T(8,128)(2,1)S(1)}) custom-call(bf16[128,2048]{1,0:T(8,128)(2,1)} %multiply_convert_fusion.refs_0_, bf16[128,2048]{1,0:T(8,128)(2,1)} %collective-permute-done.25.refs_1_, bf16[128,2048]{1,0:T(8,128)(2,1)} %copy-done.47, ...), custom_call_target="tpu_custom_call" | custom-call | flops 12884901888 | bytes 25165824 | tf_op jit(solution)/shard_map/pallas_call | solution.py:190
  182.8 4.0 %collective-permute-done.36 = bf16[512,2048]{1,0:T(8,128)(2,1)S(1)} collective-permute-done((bf16[512,2048]{1,0:T(8,128)(2,1)S(1)}, bf16[512,2048]{1,0:T(8,128)(2,1)S(1)}, u32[]{:S(2)}, u32[]{:S(2)}) %collective-permute-start.36) | collective-permute-done | bytes 2097184 | tf_op jit(solution)/shard_map/ppermute | solution.py:830
  193.7 16.2 %shard_map.216 = bf16[3072,1536]{1,0:T(8,128)(2,1)} custom-call(bf16[128,2048]{1,0:T(8,128)(2,1)} %multiply_convert_fusion.refs_0_, bf16[128,2048]{1,0:T(8,128)(2,1)} %collective-permute-done.25.refs_1_, bf16[128,2048]{1,0:T(8,128)(2,1)} %copy-done.47, bf16[128,2048]{1,0:T(8,128)(2,1)} %collective-permute-done.27.refs_3_, ...), custom_call_target="tpu_custom_call" | custom-call | flops 9663676416 | bytes 23068672 | tf_op jit(solution)/shard_map/pallas_call | solution.py:267
  209.9 7.2 %shard_map.217 = (bf16[512,2048]{1,0:T(8,128)(2,1)}, bf16[512,2048]{1,0:T(8,128)(2,1)}) custom-call(bf16[1024,768]{1,0:T(8,128)(2,1)} %copy-done.19, bf16[768,2048]{1,0:T(8,128)(2,1)} %get-tuple-element.135.down_hbm), custom_call_target="tpu_custom_call" | custom-call | flops 3221225472 | bytes 11534336 | tf_op jit(solution)/shard_map/pallas_call | solution.py:309
  219.5 4.3 %shard_map.218 = (f32[128,2048]{1,0:T(8,128)}, bf16[128,2048]{1,0:T(8,128)(2,1)}) custom-call(f32[128,2048]{1,0:T(8,128)} %get-tuple-element.210.own, bf16[128,2048]{1,0:T(8,128)(2,1)} %copy-done.36, bf16[128,2048]{1,0:T(8,128)(2,1)} %collective-permute-done.38.two, bf16[128,2048]{1,0:T(8,128)(2,1)} %collective-permute-done.39.three, ...), custom_call_target="tpu_custom_call" | custom-call | flops 5242880 | bytes 6291456 | tf_op jit(solution)/shard_map/pallas_call | solution.py:686
  230.1 20.7 %collective-permute-done.44.refs_1_ = bf16[128,2048]{1,0:T(8,128)(2,1)S(1)} collective-permute-done((bf16[128,2048]{1,0:T(8,128)(2,1)}, bf16[128,2048]{1,0:T(8,128)(2,1)S(1)}, u32[]{:S(2)}, u32[]{:S(2)}) %collective-permute-start.44) | collective-permute-done | bytes 524320 | tf_op jit(solution)/shard_map/ppermute | solution.py:822
  256.2 4.0 %shard_map.219 = bf16[256,2048]{1,0:T(8,128)(2,1)S(1)} custom-call(bf16[128,2048]{1,0:T(8,128)(2,1)} %get-tuple-element.141.refs_0_, bf16[128,2048]{1,0:T(8,128)(2,1)} %copy-done.35, bf16[128,2048]{1,0:T(8,128)(2,1)} %collective-permute-done.45.refs_2_, bf16[128,2048]{1,0:T(8,128)(2,1)} %collective-permute-done.46.refs_3_, ...), custom_call_target="tpu_custom_call" | custom-call | flops 1073741824 | bytes 6291456 | tf_op jit(solution)/shard_map/pallas_call | solution.py:625
  263.0 14.2 %shard_map.220 = (bf16[1024,384]{1,0:T(8,128)(2,1)S(1)}, bf16[512,2048]{1,0:T(8,128)(2,1)}, bf16[512,2048]{1,0:T(8,128)(2,1)S(1)}) custom-call(bf16[128,2048]{1,0:T(8,128)(2,1)} %get-tuple-element.141.refs_0_, bf16[128,2048]{1,0:T(8,128)(2,1)} %copy-done.35, bf16[128,2048]{1,0:T(8,128)(2,1)} %collective-permute-done.45.refs_2_, ...), custom_call_target="tpu_custom_call" | custom-call | flops 5368709120 | bytes 15728640 | tf_op jit(solution)/shard_map/pallas_call | solution.py:578
  283.8 4.1 %collective-permute-done.53 = bf16[64,2048]{1,0:T(8,128)(2,1)S(1)} collective-permute-done((bf16[64,2048]{1,0:T(8,128)(2,1)S(1)}, bf16[64,2048]{1,0:T(8,128)(2,1)S(1)}, u32[]{:S(2)}, u32[]{:S(2)}) %collective-permute-start.53) | collective-permute-done | bytes 262176 | tf_op jit(solution)/shard_map/ppermute | solution.py:893
  293.0 4.9 %shard_map.221 = bf16[2,4,256,384]{3,2,1,0:T(8,128)(2,1)S(1)} custom-call(bf16[144,2048]{1,0:T(8,128)(2,1)} %copy-done.24, bf16[144,2048]{1,0:T(8,128)(2,1)} %copy-done.25, bf16[144,2048]{1,0:T(8,128)(2,1)} %copy-done.26, bf16[144,2048]{1,0:T(8,128)(2,1)} %copy-done.27, bf16[144,2048]{1,0:T(8,128)(2,1)} %copy-done.28, bf16[144,2048]{1,0:T(8,128)(2,1)} %copy-done.30, ...), custom_call_target="tpu_custom_call" | custom-call | flops 1610612736 | bytes 6291456 | tf_op jit(solution)/shard_map/pallas_call | solution.py:656
  300.8 4.7 %collective-permute-start.61 = (bf16[128,2048]{1,0:T(8,128)(2,1)}, bf16[128,2048]{1,0:T(8,128)(2,1)S(1)}, u32[]{:S(2)}, u32[]{:S(2)}) collective-permute-start(bf16[128,2048]{1,0:T(8,128)(2,1)} %get-tuple-element.203), channel_id=1, source_target_pairs={{0,32},{32,64},{64,96},{96,0},{1,33},{33,65},{65,97},{97,1},{2,34}... | collective-permute-start | bytes 1572872 | tf_op jit(solution)/shard_map/ppermute | solution.py:826
  312.0 10.4 %reduce-scatter.2.cloned.1.call-done = bf16[192,1536]{1,0:T(8,128)(2,1)} async-done(((bf16[3072,1536]{1,0:T(8,128)(2,1)}), bf16[192,1536]{1,0:T(8,128)(2,1)}) %reduce-scatter.2.cloned.1.call-update) | async-done | bytes 589840 | tf_op jit(solution)/shard_map/reduce_scatter | solution.py:1038
  355.6 7.1 %collective-permute-done.74.three = bf16[32,3072]{1,0:T(8,128)(2,1)S(1)} collective-permute-done((bf16[32,3072]{1,0:T(8,128)(2,1)S(1)}, bf16[32,3072]{1,0:T(8,128)(2,1)S(1)}, u32[]{:S(2)}, u32[]{:S(2)}) %collective-permute-start.74) | collective-permute-done | bytes 196640 | tf_op jit(solution)/shard_map/ppermute | solution.py:826
  (357 shorter events, 151.4 us)
Async XLA Ops:
  7.2 61.5 %all-gather.3.cloned.1.call-start = ((), (), s32[]{:S(2)}) async-start(), calls=%async_computation.1 | async-start | bytes 1671168 | tf_op jit(solution)/shard_map/all_gather | solution.py:971
  18.2 128.0 %all-gather.5.cloned.1.call-start = ((), (), s32[]{:S(2)}) async-start(), calls=%async_computation.2 | async-start | bytes 10027008 | tf_op jit(solution)/shard_map/all_gather | solution.py:1017
  37.4 27.0 %collective-permute-start.4 = (bf16[144,2048]{1,0:T(8,128)(2,1)S(1)}, bf16[144,2048]{1,0:T(8,128)(2,1)S(1)}, u32[]{:S(2)}, u32[]{:S(2)}) collective-permute-start(bf16[144,2048]{1,0:T(8,128)(2,1)S(1)} %fusion.12.refs_0_), channel_id=1, source_target_pairs={{0,96},{32,0},{64,32},{96,64},{1,97},{33,1},{65,33},{97,65},{2,98}... | collective-permute-start | bytes 1769480 | tf_op jit(solution)/shard_map/ppermute | solution.py:822
  38.3 26.1 %collective-permute-start.5 = (bf16[144,2048]{1,0:T(8,128)(2,1)S(1)}, bf16[144,2048]{1,0:T(8,128)(2,1)S(1)}, u32[]{:S(2)}, u32[]{:S(2)}) collective-permute-start(bf16[144,2048]{1,0:T(8,128)(2,1)S(1)} %fusion.12.refs_0_), channel_id=1, source_target_pairs={{0,32},{32,64},{64,96},{96,0},{1,33},{33,65},{65,97},{97,1},{2,34}... | collective-permute-start | bytes 1769480 | tf_op jit(solution)/shard_map/ppermute | solution.py:822
  68.7 253.7 %reduce-scatter.2.cloned.1.call-start = ((), (), s32[]{:S(2)}) async-start(), calls=%async_computation.3 | async-start | bytes 10027008 | tf_op jit(solution)/shard_map/reduce_scatter | solution.py:1038
  69.8 26.4 %collective-permute-start.18 = (bf16[128,2048]{1,0:T(8,128)(2,1)S(1)}, bf16[128,2048]{1,0:T(8,128)(2,1)S(1)}, u32[]{:S(2)}, u32[]{:S(2)}) collective-permute-start(bf16[128,2048]{1,0:T(8,128)(2,1)S(1)} %copy-done.3), channel_id=1, source_target_pairs={{0,96},{32,0},{64,32},{96,64},{1,97},{33,1},{65,33},{97,65},{2,98}... | collective-permute-start | bytes 1572872 | tf_op jit(solution)/shard_map/ppermute | solution.py:822
  70.8 25.4 %collective-permute-start.19 = (bf16[128,2048]{1,0:T(8,128)(2,1)S(1)}, bf16[128,2048]{1,0:T(8,128)(2,1)S(1)}, u32[]{:S(2)}, u32[]{:S(2)}) collective-permute-start(bf16[128,2048]{1,0:T(8,128)(2,1)S(1)} %copy-done.3), channel_id=1, source_target_pairs={{0,32},{32,64},{64,96},{96,0},{1,33},{33,65},{65,97},{97,1},{2,34}... | collective-permute-start | bytes 1572872 | tf_op jit(solution)/shard_map/ppermute | solution.py:822
  101.1 25.7 %collective-permute-start.22 = (bf16[128,2048]{1,0:T(8,128)(2,1)S(1)}, bf16[128,2048]{1,0:T(8,128)(2,1)S(1)}, u32[]{:S(2)}, u32[]{:S(2)}) collective-permute-start(bf16[128,2048]{1,0:T(8,128)(2,1)S(1)} %get-tuple-element.213), channel_id=1, source_target_pairs={{0,32},{32,64},{64,96},{96,0},{1,33},{33,65},{65,97},{97,1},{2,34}... | collective-permute-start | bytes 1572872 | tf_op jit(solution)/shard_map/ppermute | solution.py:826
  104.1 26.1 %collective-permute-start.23 = (bf16[128,2048]{1,0:T(8,128)(2,1)S(1)}, bf16[128,2048]{1,0:T(8,128)(2,1)S(1)}, u32[]{:S(2)}, u32[]{:S(2)}) collective-permute-start(bf16[128,2048]{1,0:T(8,128)(2,1)S(1)} %get-tuple-element.212), channel_id=1, source_target_pairs={{0,96},{32,0},{64,32},{96,64},{1,97},{33,1},{65,33},{97,65},{2,98}... | collective-permute-start | bytes 1572872 | tf_op jit(solution)/shard_map/ppermute | solution.py:826
  104.1 26.1 %collective-permute-start.24 = (bf16[128,2048]{1,0:T(8,128)(2,1)S(1)}, bf16[128,2048]{1,0:T(8,128)(2,1)S(1)}, u32[]{:S(2)}, u32[]{:S(2)}) collective-permute-start(bf16[128,2048]{1,0:T(8,128)(2,1)S(1)} %get-tuple-element.211), channel_id=1, source_target_pairs={{0,64},{32,96},{64,0},{96,32},{1,65},{33,97},{65,1},{97,33},{2,66}... | collective-permute-start | bytes 1572872 | tf_op jit(solution)/shard_map/ppermute | solution.py:826
  108.6 26.8 %collective-permute-start.29 = (bf16[128,2048]{1,0:T(8,128)(2,1)S(1)}, bf16[128,2048]{1,0:T(8,128)(2,1)S(1)}, u32[]{:S(2)}, u32[]{:S(2)}) collective-permute-start(bf16[128,2048]{1,0:T(8,128)(2,1)S(1)} %collective-permute-done.18.refs_1_.refs_9_), channel_id=1, source_target_pairs={{0,1},{1,0},{2,3},{3,2},{4,5},{5,4},{6,7},{7,6},{8,9},{9,8},{10,11... | collective-permute-start | bytes 1572872 | tf_op jit(solution)/shard_map/ppermute | solution.py:830
  131.8 27.1 %collective-permute-start.25 = (bf16[128,2048]{1,0:T(8,128)(2,1)}, bf16[128,2048]{1,0:T(8,128)(2,1)}, u32[]{:S(2)}, u32[]{:S(2)}) collective-permute-start(bf16[128,2048]{1,0:T(8,128)(2,1)} %multiply_convert_fusion.refs_0_), channel_id=1, source_target_pairs={{0,96},{32,0},{64,32},{96,64},{1,97},{33,1},{65,33},{97,65},{2,98}... | collective-permute-start | bytes 1572872 | tf_op jit(solution)/shard_map/ppermute | solution.py:822
  131.8 27.1 %collective-permute-start.26 = (bf16[128,2048]{1,0:T(8,128)(2,1)}, bf16[128,2048]{1,0:T(8,128)(2,1)S(1)}, u32[]{:S(2)}, u32[]{:S(2)}) collective-permute-start(bf16[128,2048]{1,0:T(8,128)(2,1)} %multiply_convert_fusion.refs_0_), channel_id=1, source_target_pairs={{0,32},{32,64},{64,96},{96,0},{1,33},{33,65},{65,97},{97,1},{2,34}... | collective-permute-start | bytes 1572872 | tf_op jit(solution)/shard_map/ppermute | solution.py:822
  188.9 28.2 %collective-permute-start.37 = (bf16[128,2048]{1,0:T(8,128)(2,1)}, bf16[128,2048]{1,0:T(8,128)(2,1)S(1)}, u32[]{:S(2)}, u32[]{:S(2)}) collective-permute-start(bf16[128,2048]{1,0:T(8,128)(2,1)} %get-tuple-element.209), channel_id=1, source_target_pairs={{0,32},{32,64},{64,96},{96,0},{1,33},{33,65},{65,97},{97,1},{2,34}... | collective-permute-start | bytes 1572872 | tf_op jit(solution)/shard_map/ppermute | solution.py:826
  192.0 26.4 %collective-permute-start.38 = (bf16[128,2048]{1,0:T(8,128)(2,1)}, bf16[128,2048]{1,0:T(8,128)(2,1)}, u32[]{:S(2)}, u32[]{:S(2)}) collective-permute-start(bf16[128,2048]{1,0:T(8,128)(2,1)} %get-tuple-element.208), channel_id=1, source_target_pairs={{0,96},{32,0},{64,32},{96,64},{1,97},{33,1},{65,33},{97,65},{2,98}... | collective-permute-start | bytes 1572872 | tf_op jit(solution)/shard_map/ppermute | solution.py:826
  192.0 26.4 %collective-permute-start.39 = (bf16[128,2048]{1,0:T(8,128)(2,1)}, bf16[128,2048]{1,0:T(8,128)(2,1)}, u32[]{:S(2)}, u32[]{:S(2)}) collective-permute-start(bf16[128,2048]{1,0:T(8,128)(2,1)} %get-tuple-element.207), channel_id=1, source_target_pairs={{0,64},{32,96},{64,0},{96,32},{1,65},{33,97},{65,1},{97,33},{2,66}... | collective-permute-start | bytes 1572872 | tf_op jit(solution)/shard_map/ppermute | solution.py:826
  223.9 27.0 %collective-permute-start.44 = (bf16[128,2048]{1,0:T(8,128)(2,1)}, bf16[128,2048]{1,0:T(8,128)(2,1)S(1)}, u32[]{:S(2)}, u32[]{:S(2)}) collective-permute-start(bf16[128,2048]{1,0:T(8,128)(2,1)} %get-tuple-element.141.refs_0_), channel_id=1, source_target_pairs={{0,96},{32,0},{64,32},{96,64},{1,97},{33,1},{65,33},{97,65},{2,98}... | collective-permute-start | bytes 1572872 | tf_op jit(solution)/shard_map/ppermute | solution.py:822
  228.1 26.6 %collective-permute-start.47 = (bf16[128,2048]{1,0:T(8,128)(2,1)}, bf16[128,2048]{1,0:T(8,128)(2,1)}, u32[]{:S(2)}, u32[]{:S(2)}) collective-permute-start(bf16[128,2048]{1,0:T(8,128)(2,1)} %get-tuple-element.141.refs_0_), channel_id=1, source_target_pairs={{0,1},{1,0},{2,3},{3,2},{4,5},{5,4},{6,7},{7,6},{8,9},{9,8},{10,11... | collective-permute-start | bytes 1572872 | tf_op jit(solution)/shard_map/ppermute | solution.py:830
  251.6 26.5 %collective-permute-start.41 = (bf16[128,2048]{1,0:T(8,128)(2,1)}, bf16[128,2048]{1,0:T(8,128)(2,1)S(1)}, u32[]{:S(2)}, u32[]{:S(2)}) collective-permute-start(bf16[128,2048]{1,0:T(8,128)(2,1)} %get-tuple-element.206), channel_id=1, source_target_pairs={{0,32},{32,64},{64,96},{96,0},{1,33},{33,65},{65,97},{97,1},{2,34}... | collective-permute-start | bytes 1572872 | tf_op jit(solution)/shard_map/ppermute | solution.py:826
  254.6 26.7 %collective-permute-start.42 = (bf16[128,2048]{1,0:T(8,128)(2,1)}, bf16[128,2048]{1,0:T(8,128)(2,1)S(1)}, u32[]{:S(2)}, u32[]{:S(2)}) collective-permute-start(bf16[128,2048]{1,0:T(8,128)(2,1)} %get-tuple-element.205), channel_id=1, source_target_pairs={{0,96},{32,0},{64,32},{96,64},{1,97},{33,1},{65,33},{97,65},{2,98}... | collective-permute-start | bytes 1572872 | tf_op jit(solution)/shard_map/ppermute | solution.py:826
  254.7 26.7 %collective-permute-start.43 = (bf16[128,2048]{1,0:T(8,128)(2,1)}, bf16[128,2048]{1,0:T(8,128)(2,1)S(1)}, u32[]{:S(2)}, u32[]{:S(2)}) collective-permute-start(bf16[128,2048]{1,0:T(8,128)(2,1)} %get-tuple-element.204), channel_id=1, source_target_pairs={{0,64},{32,96},{64,0},{96,32},{1,65},{33,97},{65,1},{97,33},{2,66}... | collective-permute-start | bytes 1572872 | tf_op jit(solution)/shard_map/ppermute | solution.py:826
  260.4 27.5 %collective-permute-start.51 = (bf16[64,2048]{1,0:T(8,128)(2,1)S(1)}, bf16[64,2048]{1,0:T(8,128)(2,1)S(1)}, u32[]{:S(2)}, u32[]{:S(2)}) collective-permute-start(bf16[64,2048]{1,0:T(8,128)(2,1)S(1)} %get-tuple-element.219), channel_id=1, source_target_pairs={{0,2},{2,4},{4,6},{6,0},{1,3},{3,5},{5,7},{7,1},{8,10},{10,12},{12... | collective-permute-start | bytes 786440 | tf_op jit(solution)/shard_map/ppermute | solution.py:893
  260.5 27.5 %collective-permute-start.52 = (bf16[64,2048]{1,0:T(8,128)(2,1)S(1)}, bf16[64,2048]{1,0:T(8,128)(2,1)S(1)}, u32[]{:S(2)}, u32[]{:S(2)}) collective-permute-start(bf16[64,2048]{1,0:T(8,128)(2,1)S(1)} %get-tuple-element.218), channel_id=1, source_target_pairs={{0,4},{2,6},{4,0},{6,2},{1,5},{3,7},{5,1},{7,3},{8,12},{10,14},{12... | collective-permute-start | bytes 786440 | tf_op jit(solution)/shard_map/ppermute | solution.py:893
  300.8 28.3 %collective-permute-start.61 = (bf16[128,2048]{1,0:T(8,128)(2,1)}, bf16[128,2048]{1,0:T(8,128)(2,1)S(1)}, u32[]{:S(2)}, u32[]{:S(2)}) collective-permute-start(bf16[128,2048]{1,0:T(8,128)(2,1)} %get-tuple-element.203), channel_id=1, source_target_pairs={{0,32},{32,64},{64,96},{96,0},{1,33},{33,65},{65,97},{97,1},{2,34}... | collective-permute-start | bytes 1572872 | tf_op jit(solution)/shard_map/ppermute | solution.py:826
  (109 other events, 1114.2 us)
Sparse Core Ops, SparseCore 0:
  18.3 50.3 all-gather.2
  70.8 75.3 all-gather.4
  218.6 103.7 reduce-scatter.1
